TPU v7x, 256 devices: a whole 4x4x8 slice. The times are simulated.
256 devices in a mesh: layer: 4 (over z_lo, core), latent: 64 (over x, z_hi, y).
Axes of the slice: x: 4, y: 4, z: 8 (z_hi: 4, z_lo: 2; z = z_hi * 2 + z_lo), core: 2. Of those that a mesh axis runs over, the one named last changes fastest.
Arguments:
- acts: bfloat16 [4, 512, 2048], P('layer', None, 'latent'), may hold values from -6 to 6
- w_enc: bfloat16 [4, 2048, 32768], P('layer', None, 'latent'), may hold values from -0.0625 to 0.0625
- b_enc: float32 [32768], P('latent'), may hold values from -3 to 3
- w_dec: bfloat16 [4, 32768, 2048], P('layer', 'latent'), may hold values from -0.09375 to 0.09375
- b_dec: bfloat16 [4, 2048], P('layer', 'latent'), may hold values from -3 to 3
Outputs:
- grad_enc: bfloat16 [4, 2048, 32768], P('layer', None, 'latent')
- grad_dec: bfloat16 [4, 32768, 2048], P('layer', 'latent')
- grad_benc: float32 [32768], P('latent')
- grad_bdec: float32 [4, 2048], P('layer', 'latent')
All inputs are finite; a program needn't handle non-finite values.
Results may differ from a plain program's by a relative error of at most 0.014.
Values may be sent and summed in bfloat16 or wider, within the bound.
No kernel may reach another device: no remote copies, remote signals or barrier semaphores. Data moves between devices by JAX's collectives and lax.ppermute only.
A program may use at most 64 MiB of HBM per device.

v0:
```python
import jax
import jax.numpy as jnp
from jax import lax
from jax.sharding import Mesh
from jax.sharding import PartitionSpec as P

LATENT = ("latent_0", "latent_1", "latent_2")


def turned_gather(arrays, axis, dims):
    turned = [jnp.moveaxis(a, dim, 0) for a, dim in zip(arrays, dims)]
    widths = [t[0].size for t in turned]
    both = jnp.concatenate([t.reshape(-1, w) for t, w in zip(turned, widths)], axis=1)
    whole = lax.all_gather(both, axis, axis=0, tiled=True)
    blocks = jnp.split(whole, [sum(widths[:k]) for k in range(1, len(widths))], axis=1)
    return tuple(
        (
            jnp.moveaxis(b.reshape(-1, *t.shape[1:]), 0, dim)
            for b, t, dim in zip(blocks, turned, dims)
        )
    )


def sent_to_all(x, axis):
    peers = lax.axis_size(axis)
    return lax.all_to_all(jnp.broadcast_to(x[None], (peers, *x.shape)), axis, 0, 0, tiled=True)


def over_copies(x, axis):
    everything = sent_to_all(x, axis)
    return jnp.sum(everything, axis=0)


def sum_in_order(blocks, axes, order):
    inside = blocks.shape[1:]
    blocks = blocks.reshape(*(lax.axis_size(a) for a in axes), *inside)
    blocks = jnp.moveaxis(blocks, order, range(len(axes))).reshape(-1, *inside)
    for k in order:
        blocks = lax.psum_scatter(blocks, axes[k], scatter_dimension=0, tiled=True)
    return blocks[0]


def in_blocks(x, dim, peers):
    before, after = (x.shape[:dim], x.shape[dim + 1 :])
    return jnp.moveaxis(x.reshape(*before, peers, -1, *after), dim, 0)


def summed_rows(x, axes, order, dim):
    peers = lax.axis_size(axes)
    return sum_in_order(in_blocks(x, dim, peers), axes, order)


def taken_together(x, axis):
    everything = sent_to_all(x, axis)
    return jnp.sum(everything.astype(jnp.float32), axis=0)


def body(acts, w_enc, b_enc, w_dec, b_dec):
    local = acts[0]
    width_own = local.shape[1]
    enc_own = w_enc[0]
    dec_own = w_dec[0]
    full, bias_full = turned_gather((local, b_dec), LATENT, (1, 1))
    tokens_all = full.shape[0]
    scale = tokens_all ** (-0.5)
    part = jnp.dot(full, enc_own, preferred_element_type=jnp.float32)
    pre = over_copies(part, "layer") + b_enc[None, :]
    feat = (jax.nn.softplus(4.0 * pre) / 4.0).astype(jnp.bfloat16)
    rows = tokens_all // lax.axis_size(LATENT)
    recon = summed_rows(
        jnp.dot(feat, dec_own, preferred_element_type=jnp.float32), LATENT, (0, 2, 1), 0
    )
    position = lax.axis_index(LATENT)
    own_rows = lax.dynamic_slice_in_dim(full, position * rows, rows, 0)
    err_rows = (recon + bias_full.astype(jnp.float32) - own_rows.astype(jnp.float32)).astype(
        jnp.bfloat16
    )
    err = lax.all_gather(err_rows, LATENT, axis=0, tiled=True)
    bias_grad_full = scale * jnp.sum(err.astype(jnp.float32), axis=0)
    grad_bdec = lax.dynamic_slice_in_dim(bias_grad_full, position * width_own, width_own, 0)
    dec_prod = lax.dot_general(
        feat, err, (((0,), (0,)), ((), ())), preferred_element_type=jnp.float32
    )
    grad_dec = (scale * dec_prod).astype(jnp.bfloat16)
    feat_term = lax.dot_general(
        err, dec_own, (((1,), (1,)), ((), ())), preferred_element_type=jnp.float32
    )
    grad_feat = scale * taken_together(feat_term.astype(jnp.bfloat16), "layer").astype(jnp.float32)
    grad_pre = grad_feat * jax.nn.sigmoid(4.0 * pre)
    grad_benc = jnp.sum(grad_pre, axis=0)
    grad_pre_b = grad_pre.astype(jnp.bfloat16)
    enc_prod = lax.dot_general(
        full, grad_pre_b, (((0,), (0,)), ((), ())), preferred_element_type=jnp.float32
    )
    grad_enc = enc_prod.astype(jnp.bfloat16)
    return (grad_enc[None], grad_dec[None], grad_benc, grad_bdec[None])


def solution(mesh):
    finer = Mesh(
        mesh.devices.reshape(mesh.shape["layer"], 4, 4, 4),
        ("layer", "latent_0", "latent_1", "latent_2"),
    )
    placed = (
        P("layer", None, LATENT),
        P("layer", None, LATENT),
        P(LATENT),
        P("layer", LATENT, None),
        P("layer", LATENT),
    )
    return jax.shard_map(
        body,
        mesh=finer,
        in_specs=placed,
        out_specs=(
            P("layer", None, LATENT),
            P("layer", LATENT, None),
            P(LATENT),
            P("layer", LATENT),
        ),
        check_vma=False,
    )
```

profile of v0, /device:TPU:1, one launch (start us, length us, event | category | flops | bytes accessed | tf_op | source)
XLA Modules:
  0.0 392.8 jit_solution(11635537470442020400)
XLA Ops:
  7.2 0.9 copy.15
  8.1 1.4 pad_maximum_fusion
  9.5 0.0 reduce-scatter.4.cloned.1.call-start
  9.6 86.1 %all-gather.3.cloned.1.call-done = bf16[2048,513]{1,0:T(8,128)(2,1)} async-done(((bf16[32,513]{1,0:T(8,128)(2,1)}), bf16[2048,513]{1,0:T(8,128)(2,1)}) %all-gather.3.cloned.1.call-update) | async-done | bytes 2101264 | tf_op jit(solution)/shard_map/all_gather | solution.py:14
  95.7 3.5 fusion.5
  99.2 0.5 broadcast_in_dim.10
  99.7 52.5 %all_to_all.10 = f32[4,512,512]{2,1,0:T(8,128)} all-to-all(f32[4,512,512]{2,1,0:T(8,128)S(1)} %broadcast_in_dim.10), channel_id=1, replica_groups=mesh['layer'=4,'latent_0'=4,'latent_1'=4,'latent_2'=4] {'layer'}, dimensions={0} | all-to-all | bytes 8388608 | tf_op jit(solution)/shard_map/all_to_all | solution.py:26
  152.2 2.8 reduce_sum.36
  155.0 0.7 fusion.11
  155.8 0.8 copy-done.3
  156.6 1.2 convolution_bitcast_fusion
  157.8 2.2 copy.17
  160.1 47.6 %reduce-scatter.4.cloned.1.call-done = f32[16,8,2048]{2,1,0:T(8,128)} async-done(((f32[64,8,2048]{2,1,0:T(8,128)}), f32[16,8,2048]{2,1,0:T(8,128)}) %reduce-scatter.4.cloned.1.call-update) | async-done | bytes 1048592 | tf_op jit(solution)/shard_map/reduce_scatter | solution.py:39
  207.7 26.4 %reduce-scatter.6.cloned.1.call-done = f32[4,8,2048]{2,1,0:T(8,128)} async-done(((f32[16,8,2048]{2,1,0:T(8,128)}), f32[4,8,2048]{2,1,0:T(8,128)}) %reduce-scatter.6.cloned.1.call-update) | async-done | bytes 262160 | tf_op jit(solution)/shard_map/reduce_scatter | solution.py:39
  234.2 1.6 slice-done
  235.8 1.0 constant_dynamic-slice_fusion
  236.8 1.2 copy.20
  238.0 1.3 convert_reduce_fusion.2
  239.3 22.5 %reduce-scatter.8.cloned.1.call-done = f32[1,8,2048]{2,1,0:T(8,128)} async-done(((f32[4,8,2048]{2,1,0:T(8,128)}), f32[1,8,2048]{2,1,0:T(8,128)}) %reduce-scatter.8.cloned.1.call-update) | async-done | bytes 65552 | tf_op jit(solution)/shard_map/reduce_scatter | solution.py:39
  261.8 1.5 fusion.13
  263.3 80.6 %all-gather.5.cloned.1.call-done = bf16[512,2048]{1,0:T(8,128)(2,1)} async-done(((bf16[8,2048]{1,0:T(8,128)(2,1)}), bf16[512,2048]{1,0:T(8,128)(2,1)}) %all-gather.5.cloned.1.call-update) | async-done | bytes 2097168 | tf_op jit(solution)/shard_map/all_gather | solution.py:78
  343.9 2.9 fusion.7
  346.8 1.5 broadcast_in_dim.11
  348.3 6.7 %all-to-all-start.1 = ((bf16[4,512,512]{2,1,0:T(8,128)(2,1)}), bf16[4,512,512]{2,1,0:T(8,128)(2,1)}, u32[]{:S(2)}, u32[]{:S(2)}) async-start(bf16[4,512,512]{2,1,0:T(8,128)(2,1)} %broadcast_in_dim.11), calls=%async_computation.4 | async-start | bytes 4194304 | tf_op jit(solution)/shard_map/all_to_all | solution.py:26
  355.0 2.1 convert_reduce_fusion
  357.1 0.6 fusion.14
  357.7 3.7 fusion.1
  361.3 18.6 %all-to-all-done.1 = bf16[4,512,512]{2,1,0:T(8,128)(2,1)} async-done(((bf16[4,512,512]{2,1,0:T(8,128)(2,1)}), bf16[4,512,512]{2,1,0:T(8,128)(2,1)}, u32[]{:S(2)}, u32[]{:S(2)}) %all-to-all-start.1) | async-done | bytes 2097184 | tf_op jit(solution)/shard_map/all_to_all | solution.py:26
  379.9 2.0 convert_reduce_fusion.1
  382.0 0.9 fusion.17
  382.9 0.8 copy-done.1
  383.7 2.6 fusion
  (18 shorter events, 0.3 us)
Async XLA Ops:
  7.2 149.4 %copy-start = (bf16[1,512,2048]{2,1,0:T(8,128)(2,1)S(1)}, bf16[1,512,2048]{2,1,0:T(8,128)(2,1)}, u32[]{:S(2)}) copy-start(bf16[1,512,2048]{2,1,0:T(8,128)(2,1)} %param.8) | copy-start | bytes 6291460
  7.2 88.5 %all-gather.3.cloned.1.call-start = ((), (), s32[]{:S(2)}) async-start(), calls=%async_computation.5 | async-start | bytes 2662400 | tf_op jit(solution)/shard_map/all_gather | solution.py:14
  9.5 198.1 %reduce-scatter.4.cloned.1.call-start = ((), (), s32[]{:S(2)}) async-start(), calls=%async_computation.6 | async-start | bytes 5242880 | tf_op jit(solution)/shard_map/reduce_scatter | solution.py:39
  152.2 2.8 copy-start.4
  155.8 0.8 copy-start.3
  160.1 74.1 %reduce-scatter.6.cloned.1.call-start = ((), (), s32[]{:S(2)}) async-start(), calls=%async_computation.7 | async-start | bytes 1310720 | tf_op jit(solution)/shard_map/reduce_scatter | solution.py:39
  207.7 54.1 %reduce-scatter.8.cloned.1.call-start = ((), (), s32[]{:S(2)}) async-start(), calls=%async_computation.8 | async-start | bytes 327680 | tf_op jit(solution)/shard_map/reduce_scatter | solution.py:39
  234.2 109.7 %all-gather.5.cloned.1.call-start = ((), (), s32[]{:S(2)}) async-start(), calls=%async_computation.9 | async-start | bytes 2129920 | tf_op jit(solution)/shard_map/all_gather | solution.py:78
  234.2 1.6 slice-start
  348.3 31.7 %all-to-all-start.1 = ((bf16[4,512,512]{2,1,0:T(8,128)(2,1)}), bf16[4,512,512]{2,1,0:T(8,128)(2,1)}, u32[]{:S(2)}, u32[]{:S(2)}) async-start(bf16[4,512,512]{2,1,0:T(8,128)(2,1)} %broadcast_in_dim.11), calls=%async_computation.4 | async-start | bytes 4194304 | tf_op jit(solution)/shard_map/all_to_all | solution.py:26
  355.0 2.7 copy-start.2
  381.9 1.7 copy-start.1
Sparse Core Ops, SparseCore 0:
  11.9 83.7 all-gather.2
  160.2 47.4 reduce-scatter.3
  210.4 23.7 reduce-scatter.5
  236.5 25.2 reduce-scatter.7
  266.0 77.8 all-gather.4
where the time goes:
time: 393 us
  waiting for transfers between devices  282 us (72%)
  blocking collectives  52.5 us (13%)
  between operations  13.9 us (4%)
  matrix products  13.8 us (4%)
  other arithmetic  13.2 us (3%)
  local copies, waits for them, and re-layouts  10.5 us (3%)
  starting transfers between devices  6.93 us (2%)
    reduce_scatter x3, waiting for transfers between devices, sum_in_order(): blocks = lax.psum_scatter(blocks, axes[k], scatter_dimension=0, tiled=True)  96.4 us
    all_gather x1, waiting for transfers between devices, turned_gather(): whole = lax.all_gather(both, axis, axis=0, tiled=True)  86.1 us
    all_gather x1, waiting for transfers between devices, body(): err = lax.all_gather(err_rows, LATENT, axis=0, tiled=True)  80.6 us
    all_to_all x1, blocking collectives, sent_to_all(): lax.all_to_all(jnp.broadcast_to(x[None], (peers, *x.shape)), axis, 0, 0,...  52.5 us
    all_to_all x1, waiting for transfers between devices, sent_to_all(): lax.all_to_all(jnp.broadcast_to(x[None], (peers, *x.shape)), axis, 0, 0,...  18.6 us
  transfers between devices with their start and end apart: 6, of which 6 were waited for; matrix products, arithmetic and copies ran while one was open for 2% of the time, Pallas kernels for 0%

commit v1 on v0

v1 whole, which is shorter than its diff:
```python
import jax
import jax.numpy as jnp
import numpy as np
from jax import lax
from jax.experimental import pallas as pl
from jax.experimental.pallas import tpu as pltpu
from jax.sharding import Mesh
from jax.sharding import PartitionSpec as P

AXES = ("z_lo", "core", "x", "z_hi", "y")
LATENT = ("x", "z_hi", "y")
PLANE = ("core", "x", "y")
ORDER = (2, 1, 3)
BLOCK = 32

VMEM = pl.BlockSpec(memory_space=pltpu.VMEM)
SMEM = pl.BlockSpec(memory_space=pltpu.SMEM)
PARAMS = pltpu.CompilerParams(vmem_limit_bytes=32 * 1024 * 1024)


def other_core(x):
    return lax.ppermute(x, "core", [(0, 1), (1, 0)])


def other_layer(x):
    return lax.ppermute(x, "z_lo", [(0, 1), (1, 0)])


def along_z(x, k):
    return lax.ppermute(x, "z_hi", [(i, i ^ k) for i in range(4)])


def in_plane(x, k, x_core):
    pairs = []
    for c in range(2):
        for i in range(4):
            for j in range(4):
                a, b = (i ^ k, j) if c == x_core else (i, j ^ k)
                pairs.append((c * 16 + i * 4 + j, c * 16 + a * 4 + b))
    return lax.ppermute(x, PLANE, pairs)


def first(x, k):
    return in_plane(x, k, 0)


def second(x, k):
    return in_plane(x, k, 1)


def received(pieces, send):
    got = {k: send(pieces[k], k) for k in ORDER}
    return [pieces[0], got[1], got[2], got[3]]


def gathered(x):
    for send in (along_z, first):
        x = jnp.concatenate(received([x] * 4, send), axis=0)
    return received([x] * 4, second)


def scattered(pieces):
    total = sum(p.astype(jnp.float32) for p in received(pieces, second))
    for send in (first, along_z):
        pieces = jnp.split(total.astype(jnp.bfloat16), 4, axis=0)
        total = sum(p.astype(jnp.float32) for p in received(pieces, send))
    return total


def block_rows():
    c = lax.axis_index("core")
    x, z, y = (lax.axis_index(a) for a in LATENT)
    k = np.arange(64)
    far, near, up = k // 16, (k // 4) % 4, k % 4
    bx = jnp.where(c == 0, near ^ x, far ^ x)
    by = jnp.where(c == 0, far ^ y, near ^ y)
    return (BLOCK * (bx * 16 + (up ^ z) * 4 + by)).astype(jnp.int32)


def assemble(rows, pieces, own, other):
    for k in range(64):
        at = pl.ds(pl.multiple_of(rows[k], BLOCK), BLOCK)
        piece, src = pieces[k // 16], (k % 16) * 2 * BLOCK
        own[at, :] = piece[src : src + BLOCK, :]
        other[at, :] = piece[src + BLOCK : src + 2 * BLOCK, :]


def gathered_dot_kernel(rows, p0, p1, p2, p3, w_own, w_other, own, other, out):
    assemble(rows, (p0, p1, p2, p3), own, other)
    out[...] = (
        jnp.dot(w_own[...], own[...], preferred_element_type=jnp.float32)
        + jnp.dot(w_other[...], other[...], preferred_element_type=jnp.float32)
    ).astype(out.dtype)


def gathered_dot(rows, pieces, w_own, w_other):
    n, depth = w_own.shape
    tokens = pieces[0].shape[1]
    whole = jax.ShapeDtypeStruct((depth, tokens), jnp.bfloat16)
    return pl.pallas_call(
        gathered_dot_kernel,
        out_shape=(whole, whole, jax.ShapeDtypeStruct((n, tokens), jnp.bfloat16)),
        in_specs=[SMEM] + [VMEM] * 6,
        out_specs=(VMEM,) * 3,
        compiler_params=PARAMS,
        cost_estimate=pl.CostEstimate(
            flops=4 * n * depth * tokens, bytes_accessed=8 << 20, transcendentals=0
        ),
    )(rows, *pieces, w_own, w_other)


def blocked_dot_kernel(rows, w_own, w_other, feat, p0, p1, p2, p3, own, other):
    own[...] = jnp.dot(w_own[...], feat[...], preferred_element_type=jnp.float32).astype(own.dtype)
    other[...] = jnp.dot(w_other[...], feat[...], preferred_element_type=jnp.float32).astype(
        own.dtype
    )
    pieces = (p0, p1, p2, p3)
    for k in range(64):
        at = pl.ds(pl.multiple_of(rows[k], BLOCK), BLOCK)
        piece, dst = pieces[k // 16], (k % 16) * 2 * BLOCK
        piece[dst : dst + BLOCK, :] = own[at, :]
        piece[dst + BLOCK : dst + 2 * BLOCK, :] = other[at, :]


def blocked_dot(rows, w_own, w_other, feat):
    width, n = w_own.shape
    tokens = feat.shape[1]
    piece = jax.ShapeDtypeStruct((width // 2, tokens), jnp.bfloat16)
    return pl.pallas_call(
        blocked_dot_kernel,
        out_shape=(piece,) * 4,
        in_specs=[SMEM] + [VMEM] * 3,
        out_specs=(VMEM,) * 4,
        scratch_shapes=[pltpu.VMEM((width, tokens), jnp.bfloat16)] * 2,
        compiler_params=PARAMS,
        cost_estimate=pl.CostEstimate(
            flops=4 * n * width * tokens, bytes_accessed=7 << 20, transcendentals=0
        ),
    )(rows, w_own, w_other, feat)


def outer_kernel(scale, a0, b0, a1, b1, out):
    dims = (((1,), (1,)), ((), ()))
    out[...] = (
        scale
        * (
            lax.dot_general(a0[...], b0[...], dims, preferred_element_type=jnp.float32)
            + lax.dot_general(a1[...], b1[...], dims, preferred_element_type=jnp.float32)
        )
    ).astype(out.dtype)


def outer(a0, b0, a1, b1, scale):
    m, tokens = a0.shape
    n = b0.shape[0]
    tile = m // 4

    def kernel(*refs):
        outer_kernel(scale, *refs)

    rows = pl.BlockSpec((tile, tokens), lambda i: (i, 0))
    whole = pl.BlockSpec((n, tokens), lambda i: (0, 0))
    return pl.pallas_call(
        kernel,
        out_shape=jax.ShapeDtypeStruct((m, n), jnp.bfloat16),
        grid=(4,),
        in_specs=[rows, whole, rows, whole],
        out_specs=pl.BlockSpec((tile, n), lambda i: (i, 0)),
        compiler_params=PARAMS,
        cost_estimate=pl.CostEstimate(
            flops=4 * m * n * tokens, bytes_accessed=5 << 20, transcendentals=0
        ),
    )(a0, b0, a1, b1)


def body(acts, w_enc, b_enc, w_dec, b_dec):
    tokens_all = acts.shape[1]
    half = tokens_all // 2
    scale = tokens_all ** (-0.5)
    core = lax.axis_index("core")
    rows = block_rows()

    local = acts[0].T
    bias = jnp.broadcast_to(b_dec[0][:, None], (local.shape[0], 128))
    mine = lax.dynamic_slice_in_dim(local, core * half, half, 1)
    theirs = lax.dynamic_slice_in_dim(local, (1 - core) * half, half, 1)
    swapped = other_core(jnp.concatenate([theirs, bias], axis=1))
    start = jnp.concatenate([mine, swapped[:, :half]], axis=0)
    bias_both = jnp.concatenate([bias[:, :1], swapped[:, half : half + 1]], axis=0)

    enc_t = w_enc[0].T
    dec = w_dec[0]
    dec_t = dec.T
    enc_t, dec, dec_t = lax.optimization_barrier((enc_t, dec, dec_t))
    enc_t_other, dec_t_other, dec_other = (other_core(w) for w in (enc_t, dec_t, dec))

    acts_own, acts_other, part = gathered_dot(rows, gathered(start), enc_t, enc_t_other)
    part_b = other_layer(part)
    pre = part.astype(jnp.float32) + part_b.astype(jnp.float32) + b_enc[:, None]
    feat = (jax.nn.softplus(4.0 * pre) / 4.0).astype(jnp.bfloat16)
    feat_b = other_core(feat)
    acts_b = other_core(acts_other)

    recon = scattered(blocked_dot(rows, dec_t, dec_t_other, feat))
    err = (recon + bias_both.astype(jnp.float32) - start.astype(jnp.float32)).astype(jnp.bfloat16)
    sums = jnp.sum(err.astype(jnp.float32), axis=1)
    width = sums.shape[0] // 2
    grad_bdec = scale * (sums[:width] + other_core(sums[width:]))

    err_own, err_other, term = gathered_dot(rows, gathered(err), dec, dec_other)
    term_b = other_layer(term)
    err_b = other_core(err_other)
    grad_dec = outer(feat, err_own, feat_b, err_b, scale)

    grad_feat = scale * (term.astype(jnp.float32) + term_b.astype(jnp.float32))
    grad_pre = grad_feat * jax.nn.sigmoid(4.0 * pre)
    grad_pre_b = grad_pre.astype(jnp.bfloat16)
    grad_pre_o = other_core(grad_pre_b)
    part_benc = jnp.sum(grad_pre, axis=1)
    grad_benc = part_benc + other_core(part_benc)
    grad_enc = outer(acts_own, grad_pre_b, acts_b, grad_pre_o, 1.0)
    return (grad_enc[None], grad_dec[None], grad_benc, grad_bdec[None])


def solution(mesh):
    finer = Mesh(mesh.devices.reshape(2, 2, 4, 4, 4), AXES)
    layer = ("z_lo", "core")
    return jax.shard_map(
        body,
        mesh=finer,
        in_specs=(
            P(layer, None, LATENT),
            P(layer, None, LATENT),
            P(LATENT),
            P(layer, LATENT, None),
            P(layer, LATENT),
        ),
        out_specs=(
            P(layer, None, LATENT),
            P(layer, LATENT, None),
            P(LATENT),
            P(layer, LATENT),
        ),
        check_vma=False,
    )
```

time: 393 us -> 190 us (0.48)
  waiting for transfers between devices: 282 us -> 58.4 us
  starting transfers between devices: 6.93 us -> 91.6 us
  blocking collectives: 52.5 us -> 0 us
  Pallas kernels: 0 us -> 14.3 us
  matrix products: 13.8 us -> 0 us
  between operations: 13.9 us -> 0.93 us
  local copies, waits for them, and re-layouts: 10.5 us -> 20.3 us
  other arithmetic: 13.2 us -> 4.43 us
    all_gather x2 -> x0, waiting for transfers between devices: 167 us -> none  [the longest x1 86.1 us: turned_gather(): whole = lax.all_gather(both, axis, axis=0, tiled=True)]
    reduce_scatter x3 -> x0, waiting for transfers between devices: 96.4 us -> none  [sum_in_order(): blocks = lax.psum_scatter(blocks, axes[k], scatter_dimension=0, tiled=True)]
    ppermute x0 -> x39, starting transfers between devices: none -> 91.6 us  [the longest x10 47.8 us: other_core(): return lax.ppermute(x, 'core', [(0, 1), (1, 0)])]
    ppermute x0 -> x39, waiting for transfers between devices: none -> 58.4 us  [the longest x18 36.7 us: in_plane(): return lax.ppermute(x, PLANE, pairs)]
    all_to_all x1 -> x0, blocking collectives: 52.5 us -> none  [sent_to_all(): lax.all_to_all(jnp.broadcast_to(x[None], (peers, *x.shape)), axis, 0, 0,...]
    all_to_all x1 -> x0, waiting for transfers between devices: 18.6 us -> none  [sent_to_all(): lax.all_to_all(jnp.broadcast_to(x[None], (peers, *x.shape)), axis, 0, 0,...]
    pallas_call x0 -> x5, Pallas kernels: none -> 14.3 us  [the longest x2 7.07 us: outer(): pl.pallas_call(kernel, out_shape=jax.ShapeDtypeStruct((m, n), jnp.bfloat1...]
    dot_general x5 -> x0, matrix products: 13.8 us -> none  [the longest x1 3.65 us: body(): lax.dot_general(feat, err, (((0,), (0,)), ((), ())), preferred_element_ty...]
  transfers between devices with their start and end apart: 6 -> 39, of which waited for: 6 -> 20; matrix products, arithmetic and copies ran while one was open for 2% -> 5% of each run, Pallas kernels for 0% -> 4%
where the time goes in v1:
time: 190 us
  starting transfers between devices  91.6 us (48%)
  waiting for transfers between devices  58.4 us (31%)
  local copies, waits for them, and re-layouts  20.3 us (11%)
  Pallas kernels  14.3 us (8%)
  other arithmetic  4.43 us (2%)
    ppermute x10, starting transfers between devices, other_core(): return lax.ppermute(x, 'core', [(0, 1), (1, 0)])  47.8 us
    ppermute x18, waiting for transfers between devices, in_plane(): return lax.ppermute(x, PLANE, pairs)  36.7 us
    ppermute x18, starting transfers between devices, in_plane(): return lax.ppermute(x, PLANE, pairs)  24.4 us
    ppermute x9, starting transfers between devices, along_z(): return lax.ppermute(x, 'z_hi', [(i, i ^ k) for i in range(4)])  17.9 us
    unnamed x46, local copies, waits for them, and re-layouts  13.6 us
    ppermute x9, waiting for transfers between devices, along_z(): return lax.ppermute(x, 'z_hi', [(i, i ^ k) for i in range(4)])  11 us
    pallas_call x2, Pallas kernels, outer(): pl.pallas_call(kernel, out_shape=jax.ShapeDtypeStruct((m, n), jnp.bfloat1...  7.07 us
    ppermute x2, waiting for transfers between devices, other_layer(): return lax.ppermute(x, 'z_lo', [(0, 1), (1, 0)])  6.74 us
  transfers between devices with their start and end apart: 39, of which 20 were waited for; matrix products, arithmetic and copies ran while one was open for 5% of the time, Pallas kernels for 4%

profile of v1, /device:TPU:1, one launch (start us, length us, event | category | flops | bytes accessed | tf_op | source)
XLA Modules:
  0.0 190.0 jit_solution(18432339118276962028)
XLA Ops:
  0.7 4.1 %copy.15 = bf16[1,2048,512]{1,2,0:T(8,128)(2,1)} copy(bf16[1,2048,512]{2,1,0:T(8,128)(2,1)} %param.9) | data formatting | bytes 4194304 | tf_op args[1]
  4.8 3.2 %collective-permute-start.10 = (bf16[512,2048]{1,0:T(8,128)(2,1)}, bf16[512,2048]{1,0:T(8,128)(2,1)}, u32[]{:S(2)}, u32[]{:S(2)}) collective-permute-start(bf16[512,2048]{1,0:T(8,128)(2,1)} %bitcast.24), channel_id=1, source_target_pairs={{0,64},{64,0},{1,65},{65,1},{2,66},{66,2},{3,67},{67,3},{4,68},{68... | collective-permute-start | bytes 6291464 | tf_op jit(solution)/shard_map/ppermute | solution.py:22
  8.6 3.1 %collective-permute-done = bf16[32,384]{1,0:T(8,128)(2,1)S(1)} collective-permute-done((bf16[32,384]{1,0:T(8,128)(2,1)S(1)}, bf16[32,384]{1,0:T(8,128)(2,1)S(1)}, u32[]{:S(2)}, u32[]{:S(2)}) %collective-permute-start) | collective-permute-done | bytes 24608 | tf_op jit(solution)/shard_map/ppermute | solution.py:22
  13.1 5.1 %collective-permute-start.2 = (bf16[64,256]{1,0:T(8,128)(2,1)S(1)}, bf16[64,256]{1,0:T(8,128)(2,1)S(1)}, u32[]{:S(2)}, u32[]{:S(2)}) collective-permute-start(bf16[64,256]{1,0:T(8,128)(2,1)S(1)} %pad_maximum_fusion.1), channel_id=1, source_target_pairs={{0,8},{4,12},{8,0},{12,4},{1,9},{5,13},{9,1},{13,5},{2,10},{6,14},... | collective-permute-start | bytes 98312 | tf_op jit(solution)/shard_map/ppermute | solution.py:30
  20.1 3.0 %collective-permute-done.3 = bf16[64,256]{1,0:T(8,128)(2,1)S(1)} collective-permute-done((bf16[64,256]{1,0:T(8,128)(2,1)S(1)}, bf16[64,256]{1,0:T(8,128)(2,1)S(1)}, u32[]{:S(2)}, u32[]{:S(2)}) %collective-permute-start.3) | collective-permute-done | bytes 32800 | tf_op jit(solution)/shard_map/ppermute | solution.py:30
  24.4 2.6 %collective-permute-start.5 = (bf16[256,256]{1,0:T(8,128)(2,1)S(1)}, bf16[256,256]{1,0:T(8,128)(2,1)S(1)}, u32[]{:S(2)}, u32[]{:S(2)}) collective-permute-start(bf16[256,256]{1,0:T(8,128)(2,1)S(1)} %get-tuple-element.42), channel_id=1, source_target_pairs={{0,32},{1,33},{2,34},{3,35},{16,48},{17,49},{18,50},{19,51},{32,0}... | collective-permute-start | bytes 393224 | tf_op jit(solution)/shard_map/ppermute | solution.py:40
  27.0 3.7 %collective-permute-done.5 = bf16[256,256]{1,0:T(8,128)(2,1)S(1)} collective-permute-done((bf16[256,256]{1,0:T(8,128)(2,1)S(1)}, bf16[256,256]{1,0:T(8,128)(2,1)S(1)}, u32[]{:S(2)}, u32[]{:S(2)}) %collective-permute-start.5) | collective-permute-done | bytes 131104 | tf_op jit(solution)/shard_map/ppermute | solution.py:40
  33.5 2.7 %collective-permute-start.8 = (bf16[1024,256]{1,0:T(8,128)(2,1)S(1)}, bf16[1024,256]{1,0:T(8,128)(2,1)}, u32[]{:S(2)}, u32[]{:S(2)}) collective-permute-start(bf16[1024,256]{1,0:T(8,128)(2,1)S(1)} %constant_dynamic-update-slice_fusion.5.p0), channel_id=1, source_target_pairs={{0,2},{1,3},{2,0},{3,1},{16,18},{17,19},{18,16},{19,17},{32,34},{3... | collective-permute-start | bytes 1572872 | tf_op jit(solution)/shard_map/ppermute | solution.py:40
  37.2 3.7 %collective-permute-done.7.p1 = bf16[1024,256]{1,0:T(8,128)(2,1)S(1)} collective-permute-done((bf16[1024,256]{1,0:T(8,128)(2,1)S(1)}, bf16[1024,256]{1,0:T(8,128)(2,1)S(1)}, u32[]{:S(2)}, u32[]{:S(2)}) %collective-permute-start.7) | collective-permute-done | bytes 524320 | tf_op jit(solution)/shard_map/ppermute | solution.py:40
  41.7 7.2 %collective-permute-done.8.p2 = bf16[1024,256]{1,0:T(8,128)(2,1)} collective-permute-done((bf16[1024,256]{1,0:T(8,128)(2,1)S(1)}, bf16[1024,256]{1,0:T(8,128)(2,1)}, u32[]{:S(2)}, u32[]{:S(2)}) %collective-permute-start.8) | collective-permute-done | bytes 524320 | tf_op jit(solution)/shard_map/ppermute | solution.py:40
  48.8 2.6 %collective-permute-done.9.p3 = bf16[1024,256]{1,0:T(8,128)(2,1)} collective-permute-done((bf16[1024,256]{1,0:T(8,128)(2,1)S(1)}, bf16[1024,256]{1,0:T(8,128)(2,1)}, u32[]{:S(2)}, u32[]{:S(2)}) %collective-permute-start.9) | collective-permute-done | bytes 524320 | tf_op jit(solution)/shard_map/ppermute | solution.py:40
  55.1 3.3 %shard_map.111 = (bf16[2048,256]{1,0:T(8,128)(2,1)S(1)}, bf16[2048,256]{1,0:T(8,128)(2,1)S(1)}, bf16[512,256]{1,0:T(8,128)(2,1)S(1)}) custom-call(s32[64]{0:T(128)S(1)} %fusion.5.rows, bf16[1024,256]{1,0:T(8,128)(2,1)S(1)} %copy-done.5, bf16[1024,256]{1,0:T(8,128)(2,1)S(1)} %copy-done.7, bf16[1024,256]{1,0:T(8,128)(2,1)} %collective-permute-done.8.p2, ...), custom_call_target="tpu_custom_call" | custom-call | flops 1073741824 | bytes 8388608 | tf_op jit(solution)/shard_map/pallas_call | solution.py:100
  60.2 2.5 %copy.16.w_own = bf16[2048,512]{1,0:T(8,128)(2,1)} copy(bf16[2048,512]{0,1:T(8,128)(2,1)S(1)} %bitcast.21) | data formatting | bytes 4194304 | tf_op jit(solution)/shard_map/optimization_barrier | solution.py:194
  62.7 3.9 %copy.17.w_other = bf16[2048,512]{1,0:T(8,128)(2,1)} copy(bf16[2048,512]{0,1:T(8,128)(2,1)} %collective-permute-done.11) | data formatting | bytes 4194304 | tf_op jit(solution)/shard_map/ppermute | solution.py:22
  74.6 2.5 %collective-permute-start.15 = (bf16[1024,256]{1,0:T(8,128)(2,1)S(1)}, bf16[1024,256]{1,0:T(8,128)(2,1)S(1)}, u32[]{:S(2)}, u32[]{:S(2)}) collective-permute-start(bf16[1024,256]{1,0:T(8,128)(2,1)S(1)} %get-tuple-element.24), channel_id=1, source_target_pairs={{0,3},{1,2},{2,1},{3,0},{16,19},{17,18},{18,17},{19,16},{32,35},{3... | collective-permute-start | bytes 1572872 | tf_op jit(solution)/shard_map/ppermute | solution.py:40
  77.1 4.5 %collective-permute-done.13 = bf16[1024,256]{1,0:T(8,128)(2,1)S(1)} collective-permute-done((bf16[1024,256]{1,0:T(8,128)(2,1)S(1)}, bf16[1024,256]{1,0:T(8,128)(2,1)S(1)}, u32[]{:S(2)}, u32[]{:S(2)}) %collective-permute-start.13) | collective-permute-done | bytes 524320 | tf_op jit(solution)/shard_map/ppermute | solution.py:40
  81.6 5.6 %collective-permute-done.14 = bf16[1024,256]{1,0:T(8,128)(2,1)S(1)} collective-permute-done((bf16[1024,256]{1,0:T(8,128)(2,1)S(1)}, bf16[1024,256]{1,0:T(8,128)(2,1)S(1)}, u32[]{:S(2)}, u32[]{:S(2)}) %collective-permute-start.14) | collective-permute-done | bytes 524320 | tf_op jit(solution)/shard_map/ppermute | solution.py:40
  87.1 2.6 %collective-permute-done.15 = bf16[1024,256]{1,0:T(8,128)(2,1)S(1)} collective-permute-done((bf16[1024,256]{1,0:T(8,128)(2,1)S(1)}, bf16[1024,256]{1,0:T(8,128)(2,1)S(1)}, u32[]{:S(2)}, u32[]{:S(2)}) %collective-permute-start.15) | collective-permute-done | bytes 524320 | tf_op jit(solution)/shard_map/ppermute | solution.py:40
  92.0 2.0 %collective-permute-start.18 = (bf16[256,256]{1,0:T(8,128)(2,1)S(1)}, bf16[256,256]{1,0:T(8,128)(2,1)S(1)}, u32[]{:S(2)}, u32[]{:S(2)}) collective-permute-start(bf16[256,256]{1,0:T(8,128)(2,1)S(1)} %get-tuple-element.37), channel_id=1, source_target_pairs={{0,48},{1,49},{2,50},{3,51},{16,32},{17,33},{18,34},{19,35},{32,16... | collective-permute-start | bytes 393224 | tf_op jit(solution)/shard_map/ppermute | solution.py:40
  94.0 8.8 %collective-permute-start.31 = (bf16[512,2048]{1,0:T(8,128)(2,1)S(1)}, bf16[512,2048]{1,0:T(8,128)(2,1)S(1)}, u32[]{:S(2)}, u32[]{:S(2)}) collective-permute-start(bf16[512,2048]{1,0:T(8,128)(2,1)S(1)} %bitcast.22), channel_id=1, source_target_pairs={{0,64},{64,0},{1,65},{65,1},{2,66},{66,2},{3,67},{67,3},{4,68},{68... | collective-permute-start | bytes 6291464 | tf_op jit(solution)/shard_map/ppermute | solution.py:22
  106.3 2.5 %collective-permute-start.21 = (bf16[64,256]{1,0:T(8,128)(2,1)S(1)}, bf16[64,256]{1,0:T(8,128)(2,1)S(1)}, u32[]{:S(2)}, u32[]{:S(2)}) collective-permute-start(bf16[64,256]{1,0:T(8,128)(2,1)S(1)} %get-tuple-element.40), channel_id=1, source_target_pairs={{0,12},{4,8},{8,4},{12,0},{1,13},{5,9},{9,5},{13,1},{2,14},{6,10},... | collective-permute-start | bytes 98312 | tf_op jit(solution)/shard_map/ppermute | solution.py:30
  108.9 2.4 %collective-permute-done.20 = bf16[64,256]{1,0:T(8,128)(2,1)S(1)} collective-permute-done((bf16[64,256]{1,0:T(8,128)(2,1)S(1)}, bf16[64,256]{1,0:T(8,128)(2,1)S(1)}, u32[]{:S(2)}, u32[]{:S(2)}) %collective-permute-start.20) | collective-permute-done | bytes 32800 | tf_op jit(solution)/shard_map/ppermute | solution.py:30
  113.7 2.3 %collective-permute-start.23 = (bf16[64,256]{1,0:T(8,128)(2,1)S(1)}, bf16[64,256]{1,0:T(8,128)(2,1)S(1)}, u32[]{:S(2)}, u32[]{:S(2)}) collective-permute-start(bf16[64,256]{1,0:T(8,128)(2,1)S(1)} %get-tuple-element.31), channel_id=1, source_target_pairs={{0,8},{4,12},{8,0},{12,4},{1,9},{5,13},{9,1},{13,5},{2,10},{6,14},... | collective-permute-start | bytes 98312 | tf_op jit(solution)/shard_map/ppermute | solution.py:30
  117.7 2.7 %collective-permute-done.23 = bf16[64,256]{1,0:T(8,128)(2,1)S(1)} collective-permute-done((bf16[64,256]{1,0:T(8,128)(2,1)S(1)}, bf16[64,256]{1,0:T(8,128)(2,1)S(1)}, u32[]{:S(2)}, u32[]{:S(2)}) %collective-permute-start.23) | collective-permute-done | bytes 32800 | tf_op jit(solution)/shard_map/ppermute | solution.py:30
  121.0 4.6 %collective-permute-start.26 = (bf16[256,256]{1,0:T(8,128)(2,1)S(1)}, bf16[256,256]{1,0:T(8,128)(2,1)S(1)}, u32[]{:S(2)}, u32[]{:S(2)}) collective-permute-start(bf16[256,256]{1,0:T(8,128)(2,1)S(1)} %pad_maximum_fusion), channel_id=1, source_target_pairs={{0,32},{1,33},{2,34},{3,35},{16,48},{17,49},{18,50},{19,51},{32,0}... | collective-permute-start | bytes 393224 | tf_op jit(solution)/shard_map/ppermute | solution.py:40
  125.7 3.7 %collective-permute-done.26 = bf16[256,256]{1,0:T(8,128)(2,1)S(1)} collective-permute-done((bf16[256,256]{1,0:T(8,128)(2,1)S(1)}, bf16[256,256]{1,0:T(8,128)(2,1)S(1)}, u32[]{:S(2)}, u32[]{:S(2)}) %collective-permute-start.26) | collective-permute-done | bytes 131104 | tf_op jit(solution)/shard_map/ppermute | solution.py:40
  131.8 3.0 %collective-permute-start.30 = (bf16[1024,256]{1,0:T(8,128)(2,1)S(1)}, bf16[1024,256]{1,0:T(8,128)(2,1)S(1)}, u32[]{:S(2)}, u32[]{:S(2)}) collective-permute-start(bf16[1024,256]{1,0:T(8,128)(2,1)S(1)} %constant_dynamic-update-slice_fusion.13.p0), channel_id=1, source_target_pairs={{0,3},{1,2},{2,1},{3,0},{16,19},{17,18},{18,17},{19,16},{32,35},{3... | collective-permute-start | bytes 1572872 | tf_op jit(solution)/shard_map/ppermute | solution.py:40
  134.7 17.0 %collective-permute-start.33 = (bf16[2048,256]{1,0:T(8,128)(2,1)S(1)}, bf16[2048,256]{1,0:T(8,128)(2,1)S(1)}, u32[]{:S(2)}, u32[]{:S(2)}) collective-permute-start(bf16[2048,256]{1,0:T(8,128)(2,1)S(1)} %copy-done.9), channel_id=1, source_target_pairs={{0,64},{64,0},{1,65},{65,1},{2,66},{66,2},{3,67},{67,3},{4,68},{68... | collective-permute-start | bytes 3145736 | tf_op jit(solution)/shard_map/ppermute | solution.py:22
  153.7 16.1 %collective-permute-start.36 = (bf16[2048,256]{1,0:T(8,128)(2,1)S(1)}, bf16[2048,256]{1,0:T(8,128)(2,1)S(1)}, u32[]{:S(2)}, u32[]{:S(2)}) collective-permute-start(bf16[2048,256]{1,0:T(8,128)(2,1)S(1)} %get-tuple-element.29), channel_id=1, source_target_pairs={{0,64},{64,0},{1,65},{65,1},{2,66},{66,2},{3,67},{67,3},{4,68},{68... | collective-permute-start | bytes 3145736 | tf_op jit(solution)/shard_map/ppermute | solution.py:22
  170.6 6.7 %collective-permute-done.32 = bf16[512,256]{1,0:T(8,128)(2,1)S(1)} collective-permute-done((bf16[512,256]{1,0:T(8,128)(2,1)S(1)}, bf16[512,256]{1,0:T(8,128)(2,1)S(1)}, u32[]{:S(2)}, u32[]{:S(2)}) %collective-permute-start.32) | collective-permute-done | bytes 262176 | tf_op jit(solution)/shard_map/ppermute | solution.py:26
  182.9 3.0 %shard_map.114 = bf16[2048,512]{1,0:T(8,128)(2,1)} custom-call(bf16[2048,256]{1,0:T(8,128)(2,1)S(1)} %get-tuple-element.18.refs_0_, bf16[512,256]{1,0:T(8,128)(2,1)S(1)} %get-tuple-element.33.refs_1_, bf16[2048,256]{1,0:T(8,128)(2,1)S(1)} %collective-permute-done.33.refs_2_, bf16[512,256]{1,0:T(8,128)(2,1)S(1)} %collective-permute-done.34.refs_3_), custom_call_target="tpu_custom_call" | custom-call | flops 1073741824 | bytes 5242880 | tf_op jit(solution)/shard_map/pallas_call | solution.py:163
  185.9 4.1 %shard_map.115 = bf16[512,2048]{1,0:T(8,128)(2,1)} custom-call(bf16[512,256]{1,0:T(8,128)(2,1)S(1)} %fusion.1.feat.refs_0_, bf16[2048,256]{1,0:T(8,128)(2,1)S(1)} %get-tuple-element.28.refs_1_, bf16[512,256]{1,0:T(8,128)(2,1)S(1)} %collective-permute-done.35.refs_2_, bf16[2048,256]{1,0:T(8,128)(2,1)S(1)} %collective-permute-done.36.refs_3_), custom_call_target="tpu_custom_call" | custom-call | flops 1073741824 | bytes 5242880 | tf_op jit(solution)/shard_map/pallas_call | solution.py:163
  (120 shorter events, 44.2 us)
Async XLA Ops:
  4.8 46.7 %collective-permute-start.10 = (bf16[512,2048]{1,0:T(8,128)(2,1)}, bf16[512,2048]{1,0:T(8,128)(2,1)}, u32[]{:S(2)}, u32[]{:S(2)}) collective-permute-start(bf16[512,2048]{1,0:T(8,128)(2,1)} %bitcast.24), channel_id=1, source_target_pairs={{0,64},{64,0},{1,65},{65,1},{2,66},{66,2},{3,67},{67,3},{4,68},{68... | collective-permute-start | bytes 6291464 | tf_op jit(solution)/shard_map/ppermute | solution.py:22
  8.1 54.5 %collective-permute-start.11 = (bf16[2048,512]{0,1:T(8,128)(2,1)S(1)}, bf16[2048,512]{0,1:T(8,128)(2,1)}, u32[]{:S(2)}, u32[]{:S(2)}) collective-permute-start(bf16[2048,512]{0,1:T(8,128)(2,1)S(1)} %bitcast.20), channel_id=1, source_target_pairs={{0,64},{64,0},{1,65},{65,1},{2,66},{66,2},{3,67},{67,3},{4,68},{68... | collective-permute-start | bytes 6291464 | tf_op jit(solution)/shard_map/ppermute | solution.py:22
  11.7 6.5 %collective-permute-start.1 = (bf16[64,256]{1,0:T(8,128)(2,1)S(1)}, bf16[64,256]{1,0:T(8,128)(2,1)S(1)}, u32[]{:S(2)}, u32[]{:S(2)}) collective-permute-start(bf16[64,256]{1,0:T(8,128)(2,1)S(1)} %pad_maximum_fusion.1), channel_id=1, source_target_pairs={{0,4},{4,0},{8,12},{12,8},{1,5},{5,1},{9,13},{13,9},{2,6},{6,2},{1... | collective-permute-start | bytes 98312 | tf_op jit(solution)/shard_map/ppermute | solution.py:30
  13.1 7.0 %collective-permute-start.2 = (bf16[64,256]{1,0:T(8,128)(2,1)S(1)}, bf16[64,256]{1,0:T(8,128)(2,1)S(1)}, u32[]{:S(2)}, u32[]{:S(2)}) collective-permute-start(bf16[64,256]{1,0:T(8,128)(2,1)S(1)} %pad_maximum_fusion.1), channel_id=1, source_target_pairs={{0,8},{4,12},{8,0},{12,4},{1,9},{5,13},{9,1},{13,5},{2,10},{6,14},... | collective-permute-start | bytes 98312 | tf_op jit(solution)/shard_map/ppermute | solution.py:30
  24.4 6.4 %collective-permute-start.5 = (bf16[256,256]{1,0:T(8,128)(2,1)S(1)}, bf16[256,256]{1,0:T(8,128)(2,1)S(1)}, u32[]{:S(2)}, u32[]{:S(2)}) collective-permute-start(bf16[256,256]{1,0:T(8,128)(2,1)S(1)} %get-tuple-element.42), channel_id=1, source_target_pairs={{0,32},{1,33},{2,34},{3,35},{16,48},{17,49},{18,50},{19,51},{32,0}... | collective-permute-start | bytes 393224 | tf_op jit(solution)/shard_map/ppermute | solution.py:40
  27.0 5.5 %collective-permute-start.6 = (bf16[256,256]{1,0:T(8,128)(2,1)S(1)}, bf16[256,256]{1,0:T(8,128)(2,1)S(1)}, u32[]{:S(2)}, u32[]{:S(2)}) collective-permute-start(bf16[256,256]{1,0:T(8,128)(2,1)S(1)} %get-tuple-element.42), channel_id=1, source_target_pairs={{0,48},{1,49},{2,50},{3,51},{16,32},{17,33},{18,34},{19,35},{32,16... | collective-permute-start | bytes 393224 | tf_op jit(solution)/shard_map/ppermute | solution.py:40
  32.5 8.4 %collective-permute-start.7 = (bf16[1024,256]{1,0:T(8,128)(2,1)S(1)}, bf16[1024,256]{1,0:T(8,128)(2,1)S(1)}, u32[]{:S(2)}, u32[]{:S(2)}) collective-permute-start(bf16[1024,256]{1,0:T(8,128)(2,1)S(1)} %constant_dynamic-update-slice_fusion.5.p0), channel_id=1, source_target_pairs={{0,1},{1,0},{2,3},{3,2},{16,17},{17,16},{18,19},{19,18},{32,33},{3... | collective-permute-start | bytes 1572872 | tf_op jit(solution)/shard_map/ppermute | solution.py:40
  33.5 15.4 %collective-permute-start.8 = (bf16[1024,256]{1,0:T(8,128)(2,1)S(1)}, bf16[1024,256]{1,0:T(8,128)(2,1)}, u32[]{:S(2)}, u32[]{:S(2)}) collective-permute-start(bf16[1024,256]{1,0:T(8,128)(2,1)S(1)} %constant_dynamic-update-slice_fusion.5.p0), channel_id=1, source_target_pairs={{0,2},{1,3},{2,0},{3,1},{16,18},{17,19},{18,16},{19,17},{32,34},{3... | collective-permute-start | bytes 1572872 | tf_op jit(solution)/shard_map/ppermute | solution.py:40
  36.2 15.3 %collective-permute-start.9 = (bf16[1024,256]{1,0:T(8,128)(2,1)S(1)}, bf16[1024,256]{1,0:T(8,128)(2,1)}, u32[]{:S(2)}, u32[]{:S(2)}) collective-permute-start(bf16[1024,256]{1,0:T(8,128)(2,1)S(1)} %constant_dynamic-update-slice_fusion.5.p0), channel_id=1, source_target_pairs={{0,3},{1,2},{2,1},{3,0},{16,19},{17,18},{18,17},{19,16},{32,35},{3... | collective-permute-start | bytes 1572872 | tf_op jit(solution)/shard_map/ppermute | solution.py:40
  59.5 7.2 %collective-permute-start.12 = (bf16[512,256]{1,0:T(8,128)(2,1)S(1)}, bf16[512,256]{1,0:T(8,128)(2,1)}, u32[]{:S(2)}, u32[]{:S(2)}) collective-permute-start(bf16[512,256]{1,0:T(8,128)(2,1)S(1)} %get-tuple-element.20), channel_id=1, source_target_pairs={{0,128},{128,0},{1,129},{129,1},{2,130},{130,2},{3,131},{131,3},{4... | collective-permute-start | bytes 786440 | tf_op jit(solution)/shard_map/ppermute | solution.py:26
  73.1 8.4 %collective-permute-start.13 = (bf16[1024,256]{1,0:T(8,128)(2,1)S(1)}, bf16[1024,256]{1,0:T(8,128)(2,1)S(1)}, u32[]{:S(2)}, u32[]{:S(2)}) collective-permute-start(bf16[1024,256]{1,0:T(8,128)(2,1)S(1)} %get-tuple-element.22), channel_id=1, source_target_pairs={{0,1},{1,0},{2,3},{3,2},{16,17},{17,16},{18,19},{19,18},{32,33},{3... | collective-permute-start | bytes 1572872 | tf_op jit(solution)/shard_map/ppermute | solution.py:40
  73.2 13.9 %collective-permute-start.14 = (bf16[1024,256]{1,0:T(8,128)(2,1)S(1)}, bf16[1024,256]{1,0:T(8,128)(2,1)S(1)}, u32[]{:S(2)}, u32[]{:S(2)}) collective-permute-start(bf16[1024,256]{1,0:T(8,128)(2,1)S(1)} %get-tuple-element.23), channel_id=1, source_target_pairs={{0,2},{1,3},{2,0},{3,1},{16,18},{17,19},{18,16},{19,17},{32,34},{3... | collective-permute-start | bytes 1572872 | tf_op jit(solution)/shard_map/ppermute | solution.py:40
  74.6 15.2 %collective-permute-start.15 = (bf16[1024,256]{1,0:T(8,128)(2,1)S(1)}, bf16[1024,256]{1,0:T(8,128)(2,1)S(1)}, u32[]{:S(2)}, u32[]{:S(2)}) collective-permute-start(bf16[1024,256]{1,0:T(8,128)(2,1)S(1)} %get-tuple-element.24), channel_id=1, source_target_pairs={{0,3},{1,2},{2,1},{3,0},{16,19},{17,18},{18,17},{19,16},{32,35},{3... | collective-permute-start | bytes 1572872 | tf_op jit(solution)/shard_map/ppermute | solution.py:40
  90.1 12.9 %collective-permute-start.16 = (bf16[256,256]{1,0:T(8,128)(2,1)S(1)}, bf16[256,256]{1,0:T(8,128)(2,1)S(1)}, u32[]{:S(2)}, u32[]{:S(2)}) collective-permute-start(bf16[256,256]{1,0:T(8,128)(2,1)S(1)} %get-tuple-element.36), channel_id=1, source_target_pairs={{0,16},{1,17},{2,18},{3,19},{16,0},{17,1},{18,2},{19,3},{32,48},{3... | collective-permute-start | bytes 393224 | tf_op jit(solution)/shard_map/ppermute | solution.py:40
  90.2 12.8 %collective-permute-start.17 = (bf16[256,256]{1,0:T(8,128)(2,1)S(1)}, bf16[256,256]{1,0:T(8,128)(2,1)S(1)}, u32[]{:S(2)}, u32[]{:S(2)}) collective-permute-start(bf16[256,256]{1,0:T(8,128)(2,1)S(1)} %get-tuple-element.38), channel_id=1, source_target_pairs={{0,32},{1,33},{2,34},{3,35},{16,48},{17,49},{18,50},{19,51},{32,0}... | collective-permute-start | bytes 393224 | tf_op jit(solution)/shard_map/ppermute | solution.py:40
  92.0 11.0 %collective-permute-start.18 = (bf16[256,256]{1,0:T(8,128)(2,1)S(1)}, bf16[256,256]{1,0:T(8,128)(2,1)S(1)}, u32[]{:S(2)}, u32[]{:S(2)}) collective-permute-start(bf16[256,256]{1,0:T(8,128)(2,1)S(1)} %get-tuple-element.37), channel_id=1, source_target_pairs={{0,48},{1,49},{2,50},{3,51},{16,32},{17,33},{18,34},{19,35},{32,16... | collective-permute-start | bytes 393224 | tf_op jit(solution)/shard_map/ppermute | solution.py:40
  94.0 57.8 %collective-permute-start.31 = (bf16[512,2048]{1,0:T(8,128)(2,1)S(1)}, bf16[512,2048]{1,0:T(8,128)(2,1)S(1)}, u32[]{:S(2)}, u32[]{:S(2)}) collective-permute-start(bf16[512,2048]{1,0:T(8,128)(2,1)S(1)} %bitcast.22), channel_id=1, source_target_pairs={{0,64},{64,0},{1,65},{65,1},{2,66},{66,2},{3,67},{67,3},{4,68},{68... | collective-permute-start | bytes 6291464 | tf_op jit(solution)/shard_map/ppermute | solution.py:22
  103.1 5.8 %collective-permute-start.19 = (bf16[64,256]{1,0:T(8,128)(2,1)S(1)}, bf16[64,256]{1,0:T(8,128)(2,1)S(1)}, u32[]{:S(2)}, u32[]{:S(2)}) collective-permute-start(bf16[64,256]{1,0:T(8,128)(2,1)S(1)} %get-tuple-element.39), channel_id=1, source_target_pairs={{0,4},{4,0},{8,12},{12,8},{1,5},{5,1},{9,13},{13,9},{2,6},{6,2},{1... | collective-permute-start | bytes 98312 | tf_op jit(solution)/shard_map/ppermute | solution.py:30
  104.3 7.0 %collective-permute-start.20 = (bf16[64,256]{1,0:T(8,128)(2,1)S(1)}, bf16[64,256]{1,0:T(8,128)(2,1)S(1)}, u32[]{:S(2)}, u32[]{:S(2)}) collective-permute-start(bf16[64,256]{1,0:T(8,128)(2,1)S(1)} %get-tuple-element.41), channel_id=1, source_target_pairs={{0,8},{4,12},{8,0},{12,4},{1,9},{5,13},{9,1},{13,5},{2,10},{6,14},... | collective-permute-start | bytes 98312 | tf_op jit(solution)/shard_map/ppermute | solution.py:30
  106.3 5.5 %collective-permute-start.21 = (bf16[64,256]{1,0:T(8,128)(2,1)S(1)}, bf16[64,256]{1,0:T(8,128)(2,1)S(1)}, u32[]{:S(2)}, u32[]{:S(2)}) collective-permute-start(bf16[64,256]{1,0:T(8,128)(2,1)S(1)} %get-tuple-element.40), channel_id=1, source_target_pairs={{0,12},{4,8},{8,4},{12,0},{1,13},{5,9},{9,5},{13,1},{2,14},{6,10},... | collective-permute-start | bytes 98312 | tf_op jit(solution)/shard_map/ppermute | solution.py:30
  112.0 5.8 %collective-permute-start.22 = (bf16[64,256]{1,0:T(8,128)(2,1)S(1)}, bf16[64,256]{1,0:T(8,128)(2,1)S(1)}, u32[]{:S(2)}, u32[]{:S(2)}) collective-permute-start(bf16[64,256]{1,0:T(8,128)(2,1)S(1)} %get-tuple-element.31), channel_id=1, source_target_pairs={{0,4},{4,0},{8,12},{12,8},{1,5},{5,1},{9,13},{13,9},{2,6},{6,2},{1... | collective-permute-start | bytes 98312 | tf_op jit(solution)/shard_map/ppermute | solution.py:30
  113.7 6.7 %collective-permute-start.23 = (bf16[64,256]{1,0:T(8,128)(2,1)S(1)}, bf16[64,256]{1,0:T(8,128)(2,1)S(1)}, u32[]{:S(2)}, u32[]{:S(2)}) collective-permute-start(bf16[64,256]{1,0:T(8,128)(2,1)S(1)} %get-tuple-element.31), channel_id=1, source_target_pairs={{0,8},{4,12},{8,0},{12,4},{1,9},{5,13},{9,1},{13,5},{2,10},{6,14},... | collective-permute-start | bytes 98312 | tf_op jit(solution)/shard_map/ppermute | solution.py:30
  116.0 4.9 %collective-permute-start.24 = (bf16[64,256]{1,0:T(8,128)(2,1)S(1)}, bf16[64,256]{1,0:T(8,128)(2,1)S(1)}, u32[]{:S(2)}, u32[]{:S(2)}) collective-permute-start(bf16[64,256]{1,0:T(8,128)(2,1)S(1)} %get-tuple-element.31), channel_id=1, source_target_pairs={{0,12},{4,8},{8,4},{12,0},{1,13},{5,9},{9,5},{13,1},{2,14},{6,10},... | collective-permute-start | bytes 98312 | tf_op jit(solution)/shard_map/ppermute | solution.py:30
  121.0 8.3 %collective-permute-start.26 = (bf16[256,256]{1,0:T(8,128)(2,1)S(1)}, bf16[256,256]{1,0:T(8,128)(2,1)S(1)}, u32[]{:S(2)}, u32[]{:S(2)}) collective-permute-start(bf16[256,256]{1,0:T(8,128)(2,1)S(1)} %pad_maximum_fusion), channel_id=1, source_target_pairs={{0,32},{1,33},{2,34},{3,35},{16,48},{17,49},{18,50},{19,51},{32,0}... | collective-permute-start | bytes 393224 | tf_op jit(solution)/shard_map/ppermute | solution.py:40
  125.6 5.2 %collective-permute-start.27 = (bf16[256,256]{1,0:T(8,128)(2,1)S(1)}, bf16[256,256]{1,0:T(8,128)(2,1)S(1)}, u32[]{:S(2)}, u32[]{:S(2)}) collective-permute-start(bf16[256,256]{1,0:T(8,128)(2,1)S(1)} %pad_maximum_fusion), channel_id=1, source_target_pairs={{0,48},{1,49},{2,50},{3,51},{16,32},{17,33},{18,34},{19,35},{32,16... | collective-permute-start | bytes 393224 | tf_op jit(solution)/shard_map/ppermute | solution.py:40
  130.8 21.0 %collective-permute-start.28 = (bf16[1024,256]{1,0:T(8,128)(2,1)S(1)}, bf16[1024,256]{1,0:T(8,128)(2,1)S(1)}, u32[]{:S(2)}, u32[]{:S(2)}) collective-permute-start(bf16[1024,256]{1,0:T(8,128)(2,1)S(1)} %constant_dynamic-update-slice_fusion.13.p0), channel_id=1, source_target_pairs={{0,1},{1,0},{2,3},{3,2},{16,17},{17,16},{18,19},{19,18},{32,33},{3... | collective-permute-start | bytes 1572872 | tf_op jit(solution)/shard_map/ppermute | solution.py:40
  130.9 20.9 %collective-permute-start.29 = (bf16[1024,256]{1,0:T(8,128)(2,1)S(1)}, bf16[1024,256]{1,0:T(8,128)(2,1)S(1)}, u32[]{:S(2)}, u32[]{:S(2)}) collective-permute-start(bf16[1024,256]{1,0:T(8,128)(2,1)S(1)} %constant_dynamic-update-slice_fusion.13.p0), channel_id=1, source_target_pairs={{0,2},{1,3},{2,0},{3,1},{16,18},{17,19},{18,16},{19,17},{32,34},{3... | collective-permute-start | bytes 1572872 | tf_op jit(solution)/shard_map/ppermute | solution.py:40
  131.8 20.0 %collective-permute-start.30 = (bf16[1024,256]{1,0:T(8,128)(2,1)S(1)}, bf16[1024,256]{1,0:T(8,128)(2,1)S(1)}, u32[]{:S(2)}, u32[]{:S(2)}) collective-permute-start(bf16[1024,256]{1,0:T(8,128)(2,1)S(1)} %constant_dynamic-update-slice_fusion.13.p0), channel_id=1, source_target_pairs={{0,3},{1,2},{2,1},{3,0},{16,19},{17,18},{18,17},{19,16},{32,35},{3... | collective-permute-start | bytes 1572872 | tf_op jit(solution)/shard_map/ppermute | solution.py:40
  134.7 48.1 %collective-permute-start.33 = (bf16[2048,256]{1,0:T(8,128)(2,1)S(1)}, bf16[2048,256]{1,0:T(8,128)(2,1)S(1)}, u32[]{:S(2)}, u32[]{:S(2)}) collective-permute-start(bf16[2048,256]{1,0:T(8,128)(2,1)S(1)} %copy-done.9), channel_id=1, source_target_pairs={{0,64},{64,0},{1,65},{65,1},{2,66},{66,2},{3,67},{67,3},{4,68},{68... | collective-permute-start | bytes 3145736 | tf_op jit(solution)/shard_map/ppermute | solution.py:22
  153.7 32.1 %collective-permute-start.36 = (bf16[2048,256]{1,0:T(8,128)(2,1)S(1)}, bf16[2048,256]{1,0:T(8,128)(2,1)S(1)}, u32[]{:S(2)}, u32[]{:S(2)}) collective-permute-start(bf16[2048,256]{1,0:T(8,128)(2,1)S(1)} %get-tuple-element.29), channel_id=1, source_target_pairs={{0,64},{64,0},{1,65},{65,1},{2,66},{66,2},{3,67},{67,3},{4,68},{68... | collective-permute-start | bytes 3145736 | tf_op jit(solution)/shard_map/ppermute | solution.py:22
  169.8 7.6 %collective-permute-start.32 = (bf16[512,256]{1,0:T(8,128)(2,1)S(1)}, bf16[512,256]{1,0:T(8,128)(2,1)S(1)}, u32[]{:S(2)}, u32[]{:S(2)}) collective-permute-start(bf16[512,256]{1,0:T(8,128)(2,1)S(1)} %get-tuple-element.26), channel_id=1, source_target_pairs={{0,128},{128,0},{1,129},{129,1},{2,130},{130,2},{3,131},{131,3},{4... | collective-permute-start | bytes 786440 | tf_op jit(solution)/shard_map/ppermute | solution.py:26
  180.0 5.8 %collective-permute-start.35 = (bf16[512,256]{1,0:T(8,128)(2,1)S(1)}, bf16[512,256]{1,0:T(8,128)(2,1)S(1)}, u32[]{:S(2)}, u32[]{:S(2)}) collective-permute-start(bf16[512,256]{1,0:T(8,128)(2,1)S(1)} %fusion.1.feat.refs_0_), channel_id=1, source_target_pairs={{0,64},{64,0},{1,65},{65,1},{2,66},{66,2},{3,67},{67,3},{4,68},{68... | collective-permute-start | bytes 786440 | tf_op jit(solution)/shard_map/ppermute | solution.py:22
  (23 other events, 213.5 us)

commit v2 on v1

v2 whole, which is shorter than its diff:
```python
import jax
import jax.numpy as jnp
import numpy as np
from jax import lax
from jax.experimental import pallas as pl
from jax.experimental.pallas import tpu as pltpu
from jax.sharding import Mesh
from jax.sharding import PartitionSpec as P

AXES = ("z_lo", "core", "x", "z_hi", "y")
LATENT = ("x", "z_hi", "y")
PLANE = ("core", "x", "y")
ORDER = (2, 1, 3)
BLOCK = 32

VMEM = pl.BlockSpec(memory_space=pltpu.VMEM)
FAR = pl.BlockSpec(memory_space=pltpu.HBM)
SMEM = pl.BlockSpec(memory_space=pltpu.SMEM)
PARAMS = pltpu.CompilerParams(vmem_limit_bytes=16 * 1024 * 1024)


def other_core(x):
    return lax.ppermute(x, "core", [(0, 1), (1, 0)])


def other_layer(x):
    return lax.ppermute(x, "z_lo", [(0, 1), (1, 0)])


def along_z(x, k):
    return lax.ppermute(x, "z_hi", [(i, i ^ k) for i in range(4)])


def in_plane(x, k, x_core):
    pairs = []
    for c in range(2):
        for i in range(4):
            for j in range(4):
                a, b = (i ^ k, j) if c == x_core else (i, j ^ k)
                pairs.append((c * 16 + i * 4 + j, c * 16 + a * 4 + b))
    return lax.ppermute(x, PLANE, pairs)


def first(x, k):
    return in_plane(x, k, 0)


def second(x, k):
    return in_plane(x, k, 1)


def received(pieces, send):
    got = {k: send(pieces[k], k) for k in ORDER}
    return [pieces[0], got[1], got[2], got[3]]


def gathered(x, beside=()):
    for send in (along_z, first):
        x = jnp.concatenate(received([x] * 4, send), axis=0)
    x, beside = lax.optimization_barrier((x, beside))
    return received([x] * 4, second), beside


def scattered(pieces):
    total = sum(p.astype(jnp.float32) for p in received(pieces, second))
    for send in (first, along_z):
        pieces = jnp.split(total.astype(jnp.bfloat16), 4, axis=0)
        total = sum(p.astype(jnp.float32) for p in received(pieces, send))
    return total


def block_rows():
    c = lax.axis_index("core")
    x, z, y = (lax.axis_index(a) for a in LATENT)
    k = np.arange(64)
    far, near, up = k // 16, (k // 4) % 4, k % 4
    bx = jnp.where(c == 0, near ^ x, far ^ x)
    by = jnp.where(c == 0, far ^ y, near ^ y)
    return (BLOCK * (bx * 16 + (up ^ z) * 4 + by)).astype(jnp.int32)


def relative_enc_kernel(rows, own, other, out, blocks):
    step = pl.program_id(0)
    for k in range(16):
        at = pl.ds(pl.multiple_of(rows[step * 16 + k], BLOCK), BLOCK)
        blocks[2 * k * BLOCK : (2 * k + 1) * BLOCK, :] = own[at, :]
        blocks[(2 * k + 1) * BLOCK : (2 * k + 2) * BLOCK, :] = other[at, :]
    out[0] = blocks[...].T


def relative_enc(rows, own, other):
    depth, n = own.shape
    whole = pl.BlockSpec((depth, n), lambda i: (0, 0))
    return pl.pallas_call(
        relative_enc_kernel,
        out_shape=jax.ShapeDtypeStruct((4, n, depth // 2), jnp.bfloat16),
        grid=(4,),
        in_specs=[SMEM, whole, whole],
        out_specs=pl.BlockSpec((1, n, depth // 2), lambda i: (i, 0, 0)),
        scratch_shapes=[pltpu.VMEM((depth // 2, n), jnp.bfloat16)],
        compiler_params=PARAMS,
        cost_estimate=pl.CostEstimate(flops=1 << 20, bytes_accessed=16 << 20, transcendentals=0),
    )(rows, own, other)


def relative_dec_kernel(rows, own, other, out, own_t, other_t):
    @pl.when(pl.program_id(0) == 0)
    def _():
        width = own.shape[1]
        for j in range(0, width, 512):
            own_t[j : j + 512, :] = own[:, j : j + 512].T
            other_t[j : j + 512, :] = other[:, j : j + 512].T

    step = pl.program_id(0)
    for k in range(16):
        at = pl.ds(pl.multiple_of(rows[step * 16 + k], BLOCK), BLOCK)
        out[0, 2 * k * BLOCK : (2 * k + 1) * BLOCK, :] = own_t[at, :]
        out[0, (2 * k + 1) * BLOCK : (2 * k + 2) * BLOCK, :] = other_t[at, :]


def relative_dec(rows, own, other):
    n, width = own.shape
    whole = pl.BlockSpec((n, width), lambda i: (0, 0))
    return pl.pallas_call(
        relative_dec_kernel,
        out_shape=jax.ShapeDtypeStruct((4, width // 2, n), jnp.bfloat16),
        grid=(4,),
        in_specs=[SMEM, whole, whole],
        out_specs=pl.BlockSpec((1, width // 2, n), lambda i: (i, 0, 0)),
        scratch_shapes=[pltpu.VMEM((width, n), jnp.bfloat16)] * 2,
        compiler_params=PARAMS,
        cost_estimate=pl.CostEstimate(flops=1 << 20, bytes_accessed=16 << 20, transcendentals=0),
    )(rows, own, other)


def turned_kernel(x, out):
    out[0] = x[0].T


def turned(x):
    m, n = x.shape[1:]
    return pl.pallas_call(
        turned_kernel,
        out_shape=jax.ShapeDtypeStruct((4, n, m), jnp.bfloat16),
        grid=(4,),
        in_specs=[pl.BlockSpec((1, m, n), lambda i: (i, 0, 0))],
        out_specs=pl.BlockSpec((1, n, m), lambda i: (i, 0, 0)),
        compiler_params=PARAMS,
        cost_estimate=pl.CostEstimate(flops=1 << 20, bytes_accessed=16 << 20, transcendentals=0),
    )(x)


def gathered_dot_kernel(w, p0, p1, p2, p3, out, held, sems):
    copies = [pltpu.make_async_copy(w.at[k], held.at[k], sems.at[k]) for k in range(4)]
    for copy in copies:
        copy.start()
    total = None
    for k, piece in enumerate((p0, p1, p2, p3)):
        copies[k].wait()
        term = jnp.dot(held[k], piece[...], preferred_element_type=jnp.float32)
        total = term if total is None else total + term
    out[...] = total.astype(out.dtype)


def gathered_dot(w, pieces):
    _, n, depth = w.shape
    tokens = pieces[0].shape[1]
    return pl.pallas_call(
        gathered_dot_kernel,
        out_shape=jax.ShapeDtypeStruct((n, tokens), jnp.bfloat16),
        in_specs=[FAR] + [VMEM] * 4,
        out_specs=VMEM,
        scratch_shapes=[pltpu.VMEM(w.shape, jnp.bfloat16), pltpu.SemaphoreType.DMA((4,))],
        compiler_params=PARAMS,
        cost_estimate=pl.CostEstimate(
            flops=8 * n * depth * tokens, bytes_accessed=8 << 20, transcendentals=0
        ),
    )(w, *pieces)


def blocked_dot_kernel(w, feat, p0, p1, p2, p3, held, sems):
    order = ((2, p2), (1, p1), (3, p3), (0, p0))
    copies = {k: pltpu.make_async_copy(w.at[k], held.at[k], sems.at[k]) for k, _ in order}
    for k, _ in order:
        copies[k].start()
    for k, piece in order:
        copies[k].wait()
        piece[...] = jnp.dot(held[k], feat[...], preferred_element_type=jnp.float32).astype(
            piece.dtype
        )


def blocked_dot(w, feat):
    _, width, n = w.shape
    tokens = feat.shape[1]
    piece = jax.ShapeDtypeStruct((width, tokens), jnp.bfloat16)
    return pl.pallas_call(
        blocked_dot_kernel,
        out_shape=(piece,) * 4,
        in_specs=[FAR, VMEM],
        out_specs=(VMEM,) * 4,
        scratch_shapes=[pltpu.VMEM(w.shape, jnp.bfloat16), pltpu.SemaphoreType.DMA((4,))],
        compiler_params=PARAMS,
        cost_estimate=pl.CostEstimate(
            flops=8 * n * width * tokens, bytes_accessed=7 << 20, transcendentals=0
        ),
    )(w, feat)


def placed_kernel(rows, p0, p1, p2, p3, own, other):
    for k in range(64):
        at = pl.ds(pl.multiple_of(rows[k], BLOCK), BLOCK)
        piece, src = (p0, p1, p2, p3)[k // 16], (k % 16) * 2 * BLOCK
        own[at, :] = piece[src : src + BLOCK, :]
        other[at, :] = piece[src + BLOCK : src + 2 * BLOCK, :]


def placed(rows, pieces):
    depth, tokens = pieces[0].shape
    whole = jax.ShapeDtypeStruct((2 * depth, tokens), jnp.bfloat16)
    return pl.pallas_call(
        placed_kernel,
        out_shape=(whole, whole),
        in_specs=[SMEM] + [VMEM] * 4,
        out_specs=(VMEM,) * 2,
        compiler_params=PARAMS,
        cost_estimate=pl.CostEstimate(flops=1 << 20, bytes_accessed=4 << 20, transcendentals=0),
    )(rows, *pieces)


def outer_kernel(scale, a0, b0, a1, b1, out):
    dims = (((1,), (1,)), ((), ()))
    out[...] = (
        scale
        * (
            lax.dot_general(a0[...], b0[...], dims, preferred_element_type=jnp.float32)
            + lax.dot_general(a1[...], b1[...], dims, preferred_element_type=jnp.float32)
        )
    ).astype(out.dtype)


def outer(a0, b0, a1, b1, scale):
    m, tokens = a0.shape
    n = b0.shape[0]
    tile = 512

    def kernel(*refs):
        outer_kernel(scale, *refs)

    if m > n:
        left = pl.BlockSpec((tile, tokens), lambda i: (i, 0))
        right = pl.BlockSpec((n, tokens), lambda i: (0, 0))
        out = pl.BlockSpec((tile, n), lambda i: (i, 0))
    else:
        left = pl.BlockSpec((m, tokens), lambda i: (0, 0))
        right = pl.BlockSpec((tile, tokens), lambda i: (i, 0))
        out = pl.BlockSpec((m, tile), lambda i: (0, i))
    return pl.pallas_call(
        kernel,
        out_shape=jax.ShapeDtypeStruct((m, n), jnp.bfloat16),
        grid=(max(m, n) // tile,),
        in_specs=[left, right, left, right],
        out_specs=out,
        compiler_params=PARAMS,
        cost_estimate=pl.CostEstimate(
            flops=40 * m * n * tokens, bytes_accessed=5 << 20, transcendentals=0
        ),
    )(a0, b0, a1, b1)


def body(acts, w_enc, b_enc, w_dec, b_dec):
    tokens_all = acts.shape[1]
    half = tokens_all // 2
    scale = tokens_all ** (-0.5)
    core = lax.axis_index("core")
    rows = block_rows()

    local = acts[0].T
    bias = jnp.broadcast_to(b_dec[0][:, None], (local.shape[0], 128))
    mine = lax.dynamic_slice_in_dim(local, core * half, half, 1)
    theirs = lax.dynamic_slice_in_dim(local, (1 - core) * half, half, 1)
    swapped = other_core(jnp.concatenate([theirs, bias], axis=1))
    start = jnp.concatenate([mine, swapped[:, :half]], axis=0)
    bias_both = jnp.concatenate([bias[:, :1], swapped[:, half : half + 1]], axis=0)

    start, enc, dec = lax.optimization_barrier((start, w_enc[0], w_dec[0]))
    enc_other, dec_other = other_core(enc), other_core(dec)
    acts_p, weights = gathered(start, (enc, enc_other, dec, dec_other))
    enc_r = relative_enc(rows, *weights[:2])
    dec_r = relative_dec(rows, *weights[2:])
    dec_rt = turned(dec_r)

    part = gathered_dot(enc_r, acts_p)
    part, acts_p = lax.optimization_barrier((part, acts_p))
    part_b = other_layer(part)
    acts_own, acts_other = placed(rows, acts_p)
    acts_b = other_core(acts_other)
    part_b, acts_b = lax.optimization_barrier((part_b, acts_b))
    pre = part.astype(jnp.float32) + part_b.astype(jnp.float32) + b_enc[:, None]
    feat = (jax.nn.softplus(4.0 * pre) / 4.0).astype(jnp.bfloat16)

    recon = scattered(blocked_dot(dec_r, feat))
    err = (recon + bias_both.astype(jnp.float32) - start.astype(jnp.float32)).astype(jnp.bfloat16)

    err_p, _ = gathered(err)
    term = gathered_dot(dec_rt, err_p)
    term, err_p, feat, err = lax.optimization_barrier((term, err_p, feat, err))
    term_b = other_layer(term)
    err_own, err_other = placed(rows, err_p)
    err_b, feat_b = other_core(err_other), other_core(feat)
    sums = jnp.sum(err.astype(jnp.float32), axis=1)
    width = sums.shape[0] // 2
    grad_bdec = scale * (sums[:width] + other_core(sums[width:]))
    term_b, err_b, feat_b, grad_bdec = lax.optimization_barrier((term_b, err_b, feat_b, grad_bdec))
    grad_dec = outer(feat, err_own, feat_b, err_b, scale)

    grad_feat = scale * (term.astype(jnp.float32) + term_b.astype(jnp.float32))
    grad_pre = grad_feat * jax.nn.sigmoid(4.0 * pre)
    grad_pre_b = grad_pre.astype(jnp.bfloat16)
    grad_pre_o = other_core(grad_pre_b)
    part_benc = jnp.sum(grad_pre, axis=1)
    grad_benc = part_benc + other_core(part_benc)
    grad_enc = outer(acts_own, grad_pre_b, acts_b, grad_pre_o, 1.0)
    return (grad_enc[None], grad_dec[None], grad_benc, grad_bdec[None])


def solution(mesh):
    finer = Mesh(mesh.devices.reshape(2, 2, 4, 4, 4), AXES)
    layer = ("z_lo", "core")
    return jax.shard_map(
        body,
        mesh=finer,
        in_specs=(
            P(layer, None, LATENT),
            P(layer, None, LATENT),
            P(LATENT),
            P(layer, LATENT, None),
            P(layer, LATENT),
        ),
        out_specs=(
            P(layer, None, LATENT),
            P(layer, LATENT, None),
            P(LATENT),
            P(layer, LATENT),
        ),
        check_vma=False,
    )
```

time: 190 us -> 167 us (0.88)
  starting transfers between devices: 91.6 us -> 62.5 us
  local copies, waits for them, and re-layouts: 20.3 us -> 7.61 us
  waiting for transfers between devices: 58.4 us -> 70.7 us
  Pallas kernels: 14.3 us -> 21.7 us
    ppermute x10 -> x9, starting transfers between devices: 47.8 us -> 18.9 us  [other_core(): return lax.ppermute(x, 'core', [(0, 1), (1, 0)])]
    ppermute x18, waiting for transfers between devices: 36.7 us -> 48.7 us  [in_plane(): return lax.ppermute(x, PLANE, pairs)]
    pallas_call x3 -> x8, Pallas kernels: 7.19 us -> 15.7 us  [the longest x2 5.82 us: gathered_dot(): pl.pallas_call(gathered_dot_kernel, out_shape=jax.ShapeDtypeStruct((n, to...]
    unnamed x46 -> x26, local copies, waits for them, and re-layouts: 13.6 us -> 5.9 us
    ppermute x1 -> x0, local copies, waits for them, and re-layouts: 3.92 us -> none  [other_core(): return lax.ppermute(x, 'core', [(0, 1), (1, 0)])]
    optimization_barrier x1 -> x0, local copies, waits for them, and re-layouts: 2.49 us -> none  [body(): enc_t, dec, dec_t = lax.optimization_barrier((enc_t, dec, dec_t))]
    ppermute x2, waiting for transfers between devices: 6.74 us -> 9.18 us  [other_layer(): return lax.ppermute(x, 'z_lo', [(0, 1), (1, 0)])]
    ppermute x10 -> x9, waiting for transfers between devices: 4.02 us -> 1.84 us  [other_core(): return lax.ppermute(x, 'core', [(0, 1), (1, 0)])]
  transfers between devices with their start and end apart: 39 -> 38, of which waited for: 20 -> 26; matrix products, arithmetic and copies ran while one was open for 5% -> 1% of each run, Pallas kernels for 4% -> 5%
where the time goes in v2:
time: 167 us
  waiting for transfers between devices  70.7 us (42%)
  starting transfers between devices  62.5 us (37%)
  Pallas kernels  21.7 us (13%)
  local copies, waits for them, and re-layouts  7.61 us (5%)
  other arithmetic  3.23 us (2%)
    ppermute x18, waiting for transfers between devices, in_plane(): return lax.ppermute(x, PLANE, pairs)  48.7 us
    ppermute x18, starting transfers between devices, in_plane(): return lax.ppermute(x, PLANE, pairs)  23.2 us
    ppermute x9, starting transfers between devices, other_core(): return lax.ppermute(x, 'core', [(0, 1), (1, 0)])  18.9 us
    ppermute x9, starting transfers between devices, along_z(): return lax.ppermute(x, 'z_hi', [(i, i ^ k) for i in range(4)])  17.9 us
    ppermute x9, waiting for transfers between devices, along_z(): return lax.ppermute(x, 'z_hi', [(i, i ^ k) for i in range(4)])  10.9 us
    ppermute x2, waiting for transfers between devices, other_layer(): return lax.ppermute(x, 'z_lo', [(0, 1), (1, 0)])  9.18 us
    pallas_call x2, Pallas kernels, outer(): pl.pallas_call(kernel, out_shape=jax.ShapeDtypeStruct((m, n), jnp.bfloat1...  6.02 us
    unnamed x26, local copies, waits for them, and re-layouts  5.9 us
  transfers between devices with their start and end apart: 38, of which 26 were waited for; matrix products, arithmetic and copies ran while one was open for 1% of the time, Pallas kernels for 5%

profile of v2, /device:TPU:1, one launch (start us, length us, event | category | flops | bytes accessed | tf_op | source)
XLA Modules:
  0.0 166.6 jit_solution(15025316923009345426)
XLA Ops:
  2.1 3.3 %collective-permute-start = (bf16[32,384]{1,0:T(8,128)(2,1)S(1)}, bf16[32,384]{1,0:T(8,128)(2,1)S(1)}, u32[]{:S(2)}, u32[]{:S(2)}) collective-permute-start(bf16[32,384]{1,0:T(8,128)(2,1)S(1)} %pad_maximum_fusion.2), channel_id=1, source_target_pairs={{0,64},{64,0},{1,65},{65,1},{2,66},{66,2},{3,67},{67,3},{4,68},{68... | collective-permute-start | bytes 73736 | tf_op jit(solution)/shard_map/ppermute | solution.py:23
  8.0 5.1 %collective-permute-start.2 = (bf16[64,256]{1,0:T(8,128)(2,1)S(1)}, bf16[64,256]{1,0:T(8,128)(2,1)S(1)}, u32[]{:S(2)}, u32[]{:S(2)}) collective-permute-start(bf16[64,256]{1,0:T(8,128)(2,1)S(1)} %pad_maximum_fusion.1), channel_id=1, source_target_pairs={{0,8},{4,12},{8,0},{12,4},{1,9},{5,13},{9,1},{13,5},{2,10},{6,14},... | collective-permute-start | bytes 98312 | tf_op jit(solution)/shard_map/ppermute | solution.py:31
  14.8 3.2 %collective-permute-done.3 = bf16[64,256]{1,0:T(8,128)(2,1)S(1)} collective-permute-done((bf16[64,256]{1,0:T(8,128)(2,1)S(1)}, bf16[64,256]{1,0:T(8,128)(2,1)S(1)}, u32[]{:S(2)}, u32[]{:S(2)}) %collective-permute-start.3) | collective-permute-done | bytes 32800 | tf_op jit(solution)/shard_map/ppermute | solution.py:31
  19.3 2.6 %collective-permute-start.5 = (bf16[256,256]{1,0:T(8,128)(2,1)S(1)}, bf16[256,256]{1,0:T(8,128)(2,1)S(1)}, u32[]{:S(2)}, u32[]{:S(2)}) collective-permute-start(bf16[256,256]{1,0:T(8,128)(2,1)S(1)} %get-tuple-element.82), channel_id=1, source_target_pairs={{0,32},{1,33},{2,34},{3,35},{16,48},{17,49},{18,50},{19,51},{32,0}... | collective-permute-start | bytes 393224 | tf_op jit(solution)/shard_map/ppermute | solution.py:41
  21.9 3.7 %collective-permute-done.5 = bf16[256,256]{1,0:T(8,128)(2,1)S(1)} collective-permute-done((bf16[256,256]{1,0:T(8,128)(2,1)S(1)}, bf16[256,256]{1,0:T(8,128)(2,1)S(1)}, u32[]{:S(2)}, u32[]{:S(2)}) %collective-permute-start.5) | collective-permute-done | bytes 131104 | tf_op jit(solution)/shard_map/ppermute | solution.py:41
  30.0 2.6 %collective-permute-start.10 = (bf16[1024,256]{1,0:T(8,128)(2,1)S(1)}, bf16[1024,256]{1,0:T(8,128)(2,1)S(1)}, u32[]{:S(2)}, u32[]{:S(2)}) collective-permute-start(bf16[1024,256]{1,0:T(8,128)(2,1)S(1)} %constant_dynamic-update-slice_fusion.4.p0), channel_id=1, source_target_pairs={{0,2},{1,3},{2,0},{3,1},{16,18},{17,19},{18,16},{19,17},{32,34},{3... | collective-permute-start | bytes 1572872 | tf_op jit(solution)/shard_map/ppermute | solution.py:41
  37.2 2.0 %shard_map.111.w = bf16[4,512,1024]{2,1,0:T(8,128)(2,1)S(1)} custom-call(s32[64]{0:T(128)S(1)} %fusion.5.rows, bf16[2048,512]{1,0:T(8,128)(2,1)S(1)} %bitcast.15, bf16[2048,512]{1,0:T(8,128)(2,1)S(1)} %copy-done.5), custom_call_target="tpu_custom_call" | custom-call | flops 1048576 | bytes 16777216 | tf_op jit(solution)/shard_map/pallas_call | solution.py:94
  39.9 5.6 %collective-permute-done.11.p3 = bf16[1024,256]{1,0:T(8,128)(2,1)S(1)} collective-permute-done((bf16[1024,256]{1,0:T(8,128)(2,1)S(1)}, bf16[1024,256]{1,0:T(8,128)(2,1)S(1)}, u32[]{:S(2)}, u32[]{:S(2)}) %collective-permute-start.11) | collective-permute-done | bytes 524320 | tf_op jit(solution)/shard_map/ppermute | solution.py:41
  45.6 2.9 %shard_map.112 = bf16[512,256]{1,0:T(8,128)(2,1)S(1)} custom-call(bf16[4,512,1024]{2,1,0:T(8,128)(2,1)S(1)} %shard_map.111.w, bf16[1024,256]{1,0:T(8,128)(2,1)S(1)} %constant_dynamic-update-slice_fusion.4.p0, bf16[1024,256]{1,0:T(8,128)(2,1)S(1)} %collective-permute-done.9.p1, bf16[1024,256]{1,0:T(8,128)(2,1)S(1)} %collective-permute-done.10.p2, ...), custom_call_target="tpu_custom_call" | custom-call | flops 1073741824 | bytes 8388608 | tf_op jit(solution)/shard_map/pallas_call | solution.py:168
  49.3 4.3 %collective-permute-start.13 = (bf16[2048,256]{1,0:T(8,128)(2,1)S(1)}, bf16[2048,256]{1,0:T(8,128)(2,1)S(1)}, u32[]{:S(2)}, u32[]{:S(2)}) collective-permute-start(bf16[2048,256]{1,0:T(8,128)(2,1)S(1)} %get-tuple-element.52), channel_id=1, source_target_pairs={{0,64},{64,0},{1,65},{65,1},{2,66},{66,2},{3,67},{67,3},{4,68},{68... | collective-permute-start | bytes 3145736 | tf_op jit(solution)/shard_map/ppermute | solution.py:23
  54.3 2.0 %shard_map.114.x.w = bf16[4,1024,512]{2,1,0:T(8,128)(2,1)S(1)} custom-call(s32[64]{0:T(128)S(1)} %fusion.5.rows, bf16[512,2048]{1,0:T(8,128)(2,1)S(1)} %bitcast.17, bf16[512,2048]{1,0:T(8,128)(2,1)S(1)} %copy-done.3), custom_call_target="tpu_custom_call" | custom-call | flops 1048576 | bytes 16777216 | tf_op jit(solution)/shard_map/pallas_call | solution.py:124
  56.3 4.8 %collective-permute-done.12 = bf16[512,256]{1,0:T(8,128)(2,1)S(1)} collective-permute-done((bf16[512,256]{1,0:T(8,128)(2,1)S(1)}, bf16[512,256]{1,0:T(8,128)(2,1)S(1)}, u32[]{:S(2)}, u32[]{:S(2)}) %collective-permute-start.12) | collective-permute-done | bytes 262176 | tf_op jit(solution)/shard_map/ppermute | solution.py:27
  61.6 3.1 %shard_map.116 = (bf16[1024,256]{1,0:T(8,128)(2,1)S(1)}, bf16[1024,256]{1,0:T(8,128)(2,1)S(1)}, bf16[1024,256]{1,0:T(8,128)(2,1)S(1)}, bf16[1024,256]{1,0:T(8,128)(2,1)S(1)}) custom-call(bf16[4,1024,512]{2,1,0:T(8,128)(2,1)S(1)} %shard_map.114.x.w, bf16[512,256]{1,0:T(8,128)(2,1)S(1)} %fusion.1.feat.refs_0_), custom_call_target="tpu_custom_call" | custom-call | flops 1073741824 | bytes 7340032 | tf_op jit(solution)/shard_map/pallas_call | solution.py:197
  68.7 4.5 %collective-permute-done.14 = bf16[1024,256]{1,0:T(8,128)(2,1)S(1)} collective-permute-done((bf16[1024,256]{1,0:T(8,128)(2,1)S(1)}, bf16[1024,256]{1,0:T(8,128)(2,1)S(1)}, u32[]{:S(2)}, u32[]{:S(2)}) %collective-permute-start.14) | collective-permute-done | bytes 524320 | tf_op jit(solution)/shard_map/ppermute | solution.py:41
  73.1 6.2 %collective-permute-done.15 = bf16[1024,256]{1,0:T(8,128)(2,1)S(1)} collective-permute-done((bf16[1024,256]{1,0:T(8,128)(2,1)S(1)}, bf16[1024,256]{1,0:T(8,128)(2,1)S(1)}, u32[]{:S(2)}, u32[]{:S(2)}) %collective-permute-start.15) | collective-permute-done | bytes 524320 | tf_op jit(solution)/shard_map/ppermute | solution.py:41
  79.3 2.6 %collective-permute-done.16 = bf16[1024,256]{1,0:T(8,128)(2,1)S(1)} collective-permute-done((bf16[1024,256]{1,0:T(8,128)(2,1)S(1)}, bf16[1024,256]{1,0:T(8,128)(2,1)S(1)}, u32[]{:S(2)}, u32[]{:S(2)}) %collective-permute-start.16) | collective-permute-done | bytes 524320 | tf_op jit(solution)/shard_map/ppermute | solution.py:41
  83.1 2.8 %collective-permute-start.18 = (bf16[256,256]{1,0:T(8,128)(2,1)S(1)}, bf16[256,256]{1,0:T(8,128)(2,1)S(1)}, u32[]{:S(2)}, u32[]{:S(2)}) collective-permute-start(bf16[256,256]{1,0:T(8,128)(2,1)S(1)} %get-tuple-element.78), channel_id=1, source_target_pairs={{0,32},{1,33},{2,34},{3,35},{16,48},{17,49},{18,50},{19,51},{32,0}... | collective-permute-start | bytes 393224 | tf_op jit(solution)/shard_map/ppermute | solution.py:41
  86.3 3.3 %collective-permute-done.18 = bf16[256,256]{1,0:T(8,128)(2,1)S(1)} collective-permute-done((bf16[256,256]{1,0:T(8,128)(2,1)S(1)}, bf16[256,256]{1,0:T(8,128)(2,1)S(1)}, u32[]{:S(2)}, u32[]{:S(2)}) %collective-permute-start.18) | collective-permute-done | bytes 131104 | tf_op jit(solution)/shard_map/ppermute | solution.py:41
  94.2 2.7 %collective-permute-start.22 = (bf16[64,256]{1,0:T(8,128)(2,1)S(1)}, bf16[64,256]{1,0:T(8,128)(2,1)S(1)}, u32[]{:S(2)}, u32[]{:S(2)}) collective-permute-start(bf16[64,256]{1,0:T(8,128)(2,1)S(1)} %get-tuple-element.80), channel_id=1, source_target_pairs={{0,12},{4,8},{8,4},{12,0},{1,13},{5,9},{9,5},{13,1},{2,14},{6,10},... | collective-permute-start | bytes 98312 | tf_op jit(solution)/shard_map/ppermute | solution.py:31
  96.9 2.1 %collective-permute-done.21 = bf16[64,256]{1,0:T(8,128)(2,1)S(1)} collective-permute-done((bf16[64,256]{1,0:T(8,128)(2,1)S(1)}, bf16[64,256]{1,0:T(8,128)(2,1)S(1)}, u32[]{:S(2)}, u32[]{:S(2)}) %collective-permute-start.21) | collective-permute-done | bytes 32800 | tf_op jit(solution)/shard_map/ppermute | solution.py:31
  100.5 3.5 %collective-permute-start.24 = (bf16[64,256]{1,0:T(8,128)(2,1)S(1)}, bf16[64,256]{1,0:T(8,128)(2,1)S(1)}, u32[]{:S(2)}, u32[]{:S(2)}) collective-permute-start(bf16[64,256]{1,0:T(8,128)(2,1)S(1)} %get-tuple-element.65), channel_id=1, source_target_pairs={{0,8},{4,12},{8,0},{12,4},{1,9},{5,13},{9,1},{13,5},{2,10},{6,14},... | collective-permute-start | bytes 98312 | tf_op jit(solution)/shard_map/ppermute | solution.py:31
  105.3 2.0 %collective-permute-done.24 = bf16[64,256]{1,0:T(8,128)(2,1)S(1)} collective-permute-done((bf16[64,256]{1,0:T(8,128)(2,1)S(1)}, bf16[64,256]{1,0:T(8,128)(2,1)S(1)}, u32[]{:S(2)}, u32[]{:S(2)}) %collective-permute-start.24) | collective-permute-done | bytes 32800 | tf_op jit(solution)/shard_map/ppermute | solution.py:31
  110.6 2.2 %collective-permute-start.28 = (bf16[256,256]{1,0:T(8,128)(2,1)S(1)}, bf16[256,256]{1,0:T(8,128)(2,1)S(1)}, u32[]{:S(2)}, u32[]{:S(2)}) collective-permute-start(bf16[256,256]{1,0:T(8,128)(2,1)S(1)} %pad_maximum_fusion), channel_id=1, source_target_pairs={{0,48},{1,49},{2,50},{3,51},{16,32},{17,33},{18,34},{19,35},{32,16... | collective-permute-start | bytes 393224 | tf_op jit(solution)/shard_map/ppermute | solution.py:41
  116.3 3.1 %collective-permute-start.30 = (bf16[1024,256]{1,0:T(8,128)(2,1)S(1)}, bf16[1024,256]{1,0:T(8,128)(2,1)S(1)}, u32[]{:S(2)}, u32[]{:S(2)}) collective-permute-start(bf16[1024,256]{1,0:T(8,128)(2,1)S(1)} %constant_dynamic-update-slice_fusion.11.p0), channel_id=1, source_target_pairs={{0,2},{1,3},{2,0},{3,1},{16,18},{17,19},{18,16},{19,17},{32,34},{3... | collective-permute-start | bytes 1572872 | tf_op jit(solution)/shard_map/ppermute | solution.py:41
  121.6 5.9 %collective-permute-done.29.p1 = bf16[1024,256]{1,0:T(8,128)(2,1)S(1)} collective-permute-done((bf16[1024,256]{1,0:T(8,128)(2,1)S(1)}, bf16[1024,256]{1,0:T(8,128)(2,1)S(1)}, u32[]{:S(2)}, u32[]{:S(2)}) %collective-permute-start.29) | collective-permute-done | bytes 524320 | tf_op jit(solution)/shard_map/ppermute | solution.py:41
  127.4 7.0 %collective-permute-done.30.p2 = bf16[1024,256]{1,0:T(8,128)(2,1)S(1)} collective-permute-done((bf16[1024,256]{1,0:T(8,128)(2,1)S(1)}, bf16[1024,256]{1,0:T(8,128)(2,1)S(1)}, u32[]{:S(2)}, u32[]{:S(2)}) %collective-permute-start.30) | collective-permute-done | bytes 524320 | tf_op jit(solution)/shard_map/ppermute | solution.py:41
  134.5 2.9 %collective-permute-done.31.p3 = bf16[1024,256]{1,0:T(8,128)(2,1)S(1)} collective-permute-done((bf16[1024,256]{1,0:T(8,128)(2,1)S(1)}, bf16[1024,256]{1,0:T(8,128)(2,1)S(1)}, u32[]{:S(2)}, u32[]{:S(2)}) %collective-permute-start.31) | collective-permute-done | bytes 524320 | tf_op jit(solution)/shard_map/ppermute | solution.py:41
  137.3 2.9 %shard_map.117 = bf16[512,256]{1,0:T(8,128)(2,1)S(1)} custom-call(bf16[4,512,1024]{2,1,0:T(8,128)(2,1)S(1)} %shard_map.115.w, bf16[1024,256]{1,0:T(8,128)(2,1)S(1)} %constant_dynamic-update-slice_fusion.11.p0, bf16[1024,256]{1,0:T(8,128)(2,1)S(1)} %collective-permute-done.29.p1, bf16[1024,256]{1,0:T(8,128)(2,1)S(1)} %collective-permute-done.30.p2, ...), custom_call_target="tpu_custom_call" | custom-call | flops 1073741824 | bytes 8388608 | tf_op jit(solution)/shard_map/pallas_call | solution.py:168
  140.9 9.4 %collective-permute-start.33 = (bf16[2048,256]{1,0:T(8,128)(2,1)S(1)}, bf16[2048,256]{1,0:T(8,128)(2,1)S(1)}, u32[]{:S(2)}, u32[]{:S(2)}) collective-permute-start(bf16[2048,256]{1,0:T(8,128)(2,1)S(1)} %get-tuple-element.63), channel_id=1, source_target_pairs={{0,64},{64,0},{1,65},{65,1},{2,66},{66,2},{3,67},{67,3},{4,68},{68... | collective-permute-start | bytes 3145736 | tf_op jit(solution)/shard_map/ppermute | solution.py:23
  154.4 4.4 %collective-permute-done.32 = bf16[512,256]{1,0:T(8,128)(2,1)S(1)} collective-permute-done((bf16[512,256]{1,0:T(8,128)(2,1)S(1)}, bf16[512,256]{1,0:T(8,128)(2,1)S(1)}, u32[]{:S(2)}, u32[]{:S(2)}) %collective-permute-start.32) | collective-permute-done | bytes 262176 | tf_op jit(solution)/shard_map/ppermute | solution.py:27
  160.0 3.0 %shard_map.120 = bf16[512,2048]{1,0:T(8,128)(2,1)} custom-call(bf16[512,256]{1,0:T(8,128)(2,1)S(1)} %fusion.1.feat.refs_0_, bf16[2048,256]{1,0:T(8,128)(2,1)S(1)} %get-tuple-element.68.refs_1_, bf16[512,256]{1,0:T(8,128)(2,1)S(1)} %collective-permute-done.34.refs_2_, bf16[2048,256]{1,0:T(8,128)(2,1)S(1)} %collective-permute-done.33.refs_3_), custom_call_target="tpu_custom_call" | custom-call | flops 10737418240 | bytes 5242880 | tf_op jit(solution)/shard_map/pallas_call | solution.py:258
  163.6 3.0 %shard_map.119 = bf16[2048,512]{1,0:T(8,128)(2,1)} custom-call(bf16[2048,256]{1,0:T(8,128)(2,1)S(1)} %get-tuple-element.48.refs_0_, bf16[512,256]{1,0:T(8,128)(2,1)S(1)} %get-tuple-element.73.refs_1_, bf16[2048,256]{1,0:T(8,128)(2,1)S(1)} %collective-permute-done.13.refs_2_, bf16[512,256]{1,0:T(8,128)(2,1)S(1)} %collective-permute-done.36.refs_3_), custom_call_target="tpu_custom_call" | custom-call | flops 10737418240 | bytes 5242880 | tf_op jit(solution)/shard_map/pallas_call | solution.py:258
  (103 shorter events, 47.1 us)
Async XLA Ops:
  6.2 21.2 %collective-permute-start.7 = (bf16[2048,512]{1,0:T(8,128)(2,1)}, bf16[2048,512]{1,0:T(8,128)(2,1)S(1)}, u32[]{:S(2)}, u32[]{:S(2)}) collective-permute-start(bf16[2048,512]{1,0:T(8,128)(2,1)} %bitcast.14), channel_id=1, source_target_pairs={{0,64},{64,0},{1,65},{65,1},{2,66},{66,2},{3,67},{67,3},{4,68},{68... | collective-permute-start | bytes 6291464 | tf_op jit(solution)/shard_map/ppermute | solution.py:23
  6.6 22.1 %collective-permute-start.8 = (bf16[512,2048]{1,0:T(8,128)(2,1)}, bf16[512,2048]{1,0:T(8,128)(2,1)S(1)}, u32[]{:S(2)}, u32[]{:S(2)}) collective-permute-start(bf16[512,2048]{1,0:T(8,128)(2,1)} %bitcast.16), channel_id=1, source_target_pairs={{0,64},{64,0},{1,65},{65,1},{2,66},{66,2},{3,67},{67,3},{4,68},{68... | collective-permute-start | bytes 6291464 | tf_op jit(solution)/shard_map/ppermute | solution.py:23
  6.7 6.4 %collective-permute-start.1 = (bf16[64,256]{1,0:T(8,128)(2,1)S(1)}, bf16[64,256]{1,0:T(8,128)(2,1)S(1)}, u32[]{:S(2)}, u32[]{:S(2)}) collective-permute-start(bf16[64,256]{1,0:T(8,128)(2,1)S(1)} %pad_maximum_fusion.1), channel_id=1, source_target_pairs={{0,4},{4,0},{8,12},{12,8},{1,5},{5,1},{9,13},{13,9},{2,6},{6,2},{1... | collective-permute-start | bytes 98312 | tf_op jit(solution)/shard_map/ppermute | solution.py:31
  8.0 6.8 %collective-permute-start.2 = (bf16[64,256]{1,0:T(8,128)(2,1)S(1)}, bf16[64,256]{1,0:T(8,128)(2,1)S(1)}, u32[]{:S(2)}, u32[]{:S(2)}) collective-permute-start(bf16[64,256]{1,0:T(8,128)(2,1)S(1)} %pad_maximum_fusion.1), channel_id=1, source_target_pairs={{0,8},{4,12},{8,0},{12,4},{1,9},{5,13},{9,1},{13,5},{2,10},{6,14},... | collective-permute-start | bytes 98312 | tf_op jit(solution)/shard_map/ppermute | solution.py:31
  13.1 4.9 %collective-permute-start.3 = (bf16[64,256]{1,0:T(8,128)(2,1)S(1)}, bf16[64,256]{1,0:T(8,128)(2,1)S(1)}, u32[]{:S(2)}, u32[]{:S(2)}) collective-permute-start(bf16[64,256]{1,0:T(8,128)(2,1)S(1)} %pad_maximum_fusion.1), channel_id=1, source_target_pairs={{0,12},{4,8},{8,4},{12,0},{1,13},{5,9},{9,5},{13,1},{2,14},{6,10},... | collective-permute-start | bytes 98312 | tf_op jit(solution)/shard_map/ppermute | solution.py:31
  19.3 6.4 %collective-permute-start.5 = (bf16[256,256]{1,0:T(8,128)(2,1)S(1)}, bf16[256,256]{1,0:T(8,128)(2,1)S(1)}, u32[]{:S(2)}, u32[]{:S(2)}) collective-permute-start(bf16[256,256]{1,0:T(8,128)(2,1)S(1)} %get-tuple-element.82), channel_id=1, source_target_pairs={{0,32},{1,33},{2,34},{3,35},{16,48},{17,49},{18,50},{19,51},{32,0}... | collective-permute-start | bytes 393224 | tf_op jit(solution)/shard_map/ppermute | solution.py:41
  21.9 5.5 %collective-permute-start.6 = (bf16[256,256]{1,0:T(8,128)(2,1)S(1)}, bf16[256,256]{1,0:T(8,128)(2,1)S(1)}, u32[]{:S(2)}, u32[]{:S(2)}) collective-permute-start(bf16[256,256]{1,0:T(8,128)(2,1)S(1)} %get-tuple-element.82), channel_id=1, source_target_pairs={{0,48},{1,49},{2,50},{3,51},{16,32},{17,33},{18,34},{19,35},{32,16... | collective-permute-start | bytes 393224 | tf_op jit(solution)/shard_map/ppermute | solution.py:41
  30.0 9.9 %collective-permute-start.10 = (bf16[1024,256]{1,0:T(8,128)(2,1)S(1)}, bf16[1024,256]{1,0:T(8,128)(2,1)S(1)}, u32[]{:S(2)}, u32[]{:S(2)}) collective-permute-start(bf16[1024,256]{1,0:T(8,128)(2,1)S(1)} %constant_dynamic-update-slice_fusion.4.p0), channel_id=1, source_target_pairs={{0,2},{1,3},{2,0},{3,1},{16,18},{17,19},{18,16},{19,17},{32,34},{3... | collective-permute-start | bytes 1572872 | tf_op jit(solution)/shard_map/ppermute | solution.py:41
  32.6 12.9 %collective-permute-start.11 = (bf16[1024,256]{1,0:T(8,128)(2,1)S(1)}, bf16[1024,256]{1,0:T(8,128)(2,1)S(1)}, u32[]{:S(2)}, u32[]{:S(2)}) collective-permute-start(bf16[1024,256]{1,0:T(8,128)(2,1)S(1)} %constant_dynamic-update-slice_fusion.4.p0), channel_id=1, source_target_pairs={{0,3},{1,2},{2,1},{3,0},{16,19},{17,18},{18,17},{19,16},{32,35},{3... | collective-permute-start | bytes 1572872 | tf_op jit(solution)/shard_map/ppermute | solution.py:41
  33.4 12.3 %collective-permute-start.9 = (bf16[1024,256]{1,0:T(8,128)(2,1)S(1)}, bf16[1024,256]{1,0:T(8,128)(2,1)S(1)}, u32[]{:S(2)}, u32[]{:S(2)}) collective-permute-start(bf16[1024,256]{1,0:T(8,128)(2,1)S(1)} %constant_dynamic-update-slice_fusion.4.p0), channel_id=1, source_target_pairs={{0,1},{1,0},{2,3},{3,2},{16,17},{17,16},{18,19},{19,18},{32,33},{3... | collective-permute-start | bytes 1572872 | tf_op jit(solution)/shard_map/ppermute | solution.py:41
  49.3 11.9 %collective-permute-start.13 = (bf16[2048,256]{1,0:T(8,128)(2,1)S(1)}, bf16[2048,256]{1,0:T(8,128)(2,1)S(1)}, u32[]{:S(2)}, u32[]{:S(2)}) collective-permute-start(bf16[2048,256]{1,0:T(8,128)(2,1)S(1)} %get-tuple-element.52), channel_id=1, source_target_pairs={{0,64},{64,0},{1,65},{65,1},{2,66},{66,2},{3,67},{67,3},{4,68},{68... | collective-permute-start | bytes 3145736 | tf_op jit(solution)/shard_map/ppermute | solution.py:23
  53.5 7.6 %collective-permute-start.12 = (bf16[512,256]{1,0:T(8,128)(2,1)S(1)}, bf16[512,256]{1,0:T(8,128)(2,1)S(1)}, u32[]{:S(2)}, u32[]{:S(2)}) collective-permute-start(bf16[512,256]{1,0:T(8,128)(2,1)S(1)} %shard_map.112), channel_id=1, source_target_pairs={{0,128},{128,0},{1,129},{129,1},{2,130},{130,2},{3,131},{131,3},{4... | collective-permute-start | bytes 786440 | tf_op jit(solution)/shard_map/ppermute | solution.py:27
  64.7 8.4 %collective-permute-start.14 = (bf16[1024,256]{1,0:T(8,128)(2,1)S(1)}, bf16[1024,256]{1,0:T(8,128)(2,1)S(1)}, u32[]{:S(2)}, u32[]{:S(2)}) collective-permute-start(bf16[1024,256]{1,0:T(8,128)(2,1)S(1)} %get-tuple-element.55), channel_id=1, source_target_pairs={{0,1},{1,0},{2,3},{3,2},{16,17},{17,16},{18,19},{19,18},{32,33},{3... | collective-permute-start | bytes 1572872 | tf_op jit(solution)/shard_map/ppermute | solution.py:41
  64.8 14.5 %collective-permute-start.15 = (bf16[1024,256]{1,0:T(8,128)(2,1)S(1)}, bf16[1024,256]{1,0:T(8,128)(2,1)S(1)}, u32[]{:S(2)}, u32[]{:S(2)}) collective-permute-start(bf16[1024,256]{1,0:T(8,128)(2,1)S(1)} %get-tuple-element.56), channel_id=1, source_target_pairs={{0,2},{1,3},{2,0},{3,1},{16,18},{17,19},{18,16},{19,17},{32,34},{3... | collective-permute-start | bytes 1572872 | tf_op jit(solution)/shard_map/ppermute | solution.py:41
  66.8 15.2 %collective-permute-start.16 = (bf16[1024,256]{1,0:T(8,128)(2,1)S(1)}, bf16[1024,256]{1,0:T(8,128)(2,1)S(1)}, u32[]{:S(2)}, u32[]{:S(2)}) collective-permute-start(bf16[1024,256]{1,0:T(8,128)(2,1)S(1)} %get-tuple-element.57), channel_id=1, source_target_pairs={{0,3},{1,2},{2,1},{3,0},{16,19},{17,18},{18,17},{19,16},{32,35},{3... | collective-permute-start | bytes 1572872 | tf_op jit(solution)/shard_map/ppermute | solution.py:41
  83.1 6.5 %collective-permute-start.18 = (bf16[256,256]{1,0:T(8,128)(2,1)S(1)}, bf16[256,256]{1,0:T(8,128)(2,1)S(1)}, u32[]{:S(2)}, u32[]{:S(2)}) collective-permute-start(bf16[256,256]{1,0:T(8,128)(2,1)S(1)} %get-tuple-element.78), channel_id=1, source_target_pairs={{0,32},{1,33},{2,34},{3,35},{16,48},{17,49},{18,50},{19,51},{32,0}... | collective-permute-start | bytes 393224 | tf_op jit(solution)/shard_map/ppermute | solution.py:41
  85.8 5.2 %collective-permute-start.19 = (bf16[256,256]{1,0:T(8,128)(2,1)S(1)}, bf16[256,256]{1,0:T(8,128)(2,1)S(1)}, u32[]{:S(2)}, u32[]{:S(2)}) collective-permute-start(bf16[256,256]{1,0:T(8,128)(2,1)S(1)} %get-tuple-element.77), channel_id=1, source_target_pairs={{0,48},{1,49},{2,50},{3,51},{16,32},{17,33},{18,34},{19,35},{32,16... | collective-permute-start | bytes 393224 | tf_op jit(solution)/shard_map/ppermute | solution.py:41
  91.1 5.8 %collective-permute-start.20 = (bf16[64,256]{1,0:T(8,128)(2,1)S(1)}, bf16[64,256]{1,0:T(8,128)(2,1)S(1)}, u32[]{:S(2)}, u32[]{:S(2)}) collective-permute-start(bf16[64,256]{1,0:T(8,128)(2,1)S(1)} %get-tuple-element.79), channel_id=1, source_target_pairs={{0,4},{4,0},{8,12},{12,8},{1,5},{5,1},{9,13},{13,9},{2,6},{6,2},{1... | collective-permute-start | bytes 98312 | tf_op jit(solution)/shard_map/ppermute | solution.py:31
  92.4 6.7 %collective-permute-start.21 = (bf16[64,256]{1,0:T(8,128)(2,1)S(1)}, bf16[64,256]{1,0:T(8,128)(2,1)S(1)}, u32[]{:S(2)}, u32[]{:S(2)}) collective-permute-start(bf16[64,256]{1,0:T(8,128)(2,1)S(1)} %get-tuple-element.81), channel_id=1, source_target_pairs={{0,8},{4,12},{8,0},{12,4},{1,9},{5,13},{9,1},{13,5},{2,10},{6,14},... | collective-permute-start | bytes 98312 | tf_op jit(solution)/shard_map/ppermute | solution.py:31
  94.2 5.3 %collective-permute-start.22 = (bf16[64,256]{1,0:T(8,128)(2,1)S(1)}, bf16[64,256]{1,0:T(8,128)(2,1)S(1)}, u32[]{:S(2)}, u32[]{:S(2)}) collective-permute-start(bf16[64,256]{1,0:T(8,128)(2,1)S(1)} %get-tuple-element.80), channel_id=1, source_target_pairs={{0,12},{4,8},{8,4},{12,0},{1,13},{5,9},{9,5},{13,1},{2,14},{6,10},... | collective-permute-start | bytes 98312 | tf_op jit(solution)/shard_map/ppermute | solution.py:31
  99.6 5.7 %collective-permute-start.23 = (bf16[64,256]{1,0:T(8,128)(2,1)S(1)}, bf16[64,256]{1,0:T(8,128)(2,1)S(1)}, u32[]{:S(2)}, u32[]{:S(2)}) collective-permute-start(bf16[64,256]{1,0:T(8,128)(2,1)S(1)} %get-tuple-element.65), channel_id=1, source_target_pairs={{0,4},{4,0},{8,12},{12,8},{1,5},{5,1},{9,13},{13,9},{2,6},{6,2},{1... | collective-permute-start | bytes 98312 | tf_op jit(solution)/shard_map/ppermute | solution.py:31
  100.5 6.8 %collective-permute-start.24 = (bf16[64,256]{1,0:T(8,128)(2,1)S(1)}, bf16[64,256]{1,0:T(8,128)(2,1)S(1)}, u32[]{:S(2)}, u32[]{:S(2)}) collective-permute-start(bf16[64,256]{1,0:T(8,128)(2,1)S(1)} %get-tuple-element.65), channel_id=1, source_target_pairs={{0,8},{4,12},{8,0},{12,4},{1,9},{5,13},{9,1},{13,5},{2,10},{6,14},... | collective-permute-start | bytes 98312 | tf_op jit(solution)/shard_map/ppermute | solution.py:31
  104.0 4.9 %collective-permute-start.25 = (bf16[64,256]{1,0:T(8,128)(2,1)S(1)}, bf16[64,256]{1,0:T(8,128)(2,1)S(1)}, u32[]{:S(2)}, u32[]{:S(2)}) collective-permute-start(bf16[64,256]{1,0:T(8,128)(2,1)S(1)} %get-tuple-element.65), channel_id=1, source_target_pairs={{0,12},{4,8},{8,4},{12,0},{1,13},{5,9},{9,5},{13,1},{2,14},{6,10},... | collective-permute-start | bytes 98312 | tf_op jit(solution)/shard_map/ppermute | solution.py:31
  108.9 4.2 %collective-permute-start.26 = (bf16[256,256]{1,0:T(8,128)(2,1)S(1)}, bf16[256,256]{1,0:T(8,128)(2,1)S(1)}, u32[]{:S(2)}, u32[]{:S(2)}) collective-permute-start(bf16[256,256]{1,0:T(8,128)(2,1)S(1)} %pad_maximum_fusion), channel_id=1, source_target_pairs={{0,16},{1,17},{2,18},{3,19},{16,0},{17,1},{18,2},{19,3},{32,48},{3... | collective-permute-start | bytes 393224 | tf_op jit(solution)/shard_map/ppermute | solution.py:41
  109.0 5.4 %collective-permute-start.27 = (bf16[256,256]{1,0:T(8,128)(2,1)S(1)}, bf16[256,256]{1,0:T(8,128)(2,1)S(1)}, u32[]{:S(2)}, u32[]{:S(2)}) collective-permute-start(bf16[256,256]{1,0:T(8,128)(2,1)S(1)} %pad_maximum_fusion), channel_id=1, source_target_pairs={{0,32},{1,33},{2,34},{3,35},{16,48},{17,49},{18,50},{19,51},{32,0}... | collective-permute-start | bytes 393224 | tf_op jit(solution)/shard_map/ppermute | solution.py:41
  110.6 5.4 %collective-permute-start.28 = (bf16[256,256]{1,0:T(8,128)(2,1)S(1)}, bf16[256,256]{1,0:T(8,128)(2,1)S(1)}, u32[]{:S(2)}, u32[]{:S(2)}) collective-permute-start(bf16[256,256]{1,0:T(8,128)(2,1)S(1)} %pad_maximum_fusion), channel_id=1, source_target_pairs={{0,48},{1,49},{2,50},{3,51},{16,32},{17,33},{18,34},{19,35},{32,16... | collective-permute-start | bytes 393224 | tf_op jit(solution)/shard_map/ppermute | solution.py:41
  116.0 11.4 %collective-permute-start.29 = (bf16[1024,256]{1,0:T(8,128)(2,1)S(1)}, bf16[1024,256]{1,0:T(8,128)(2,1)S(1)}, u32[]{:S(2)}, u32[]{:S(2)}) collective-permute-start(bf16[1024,256]{1,0:T(8,128)(2,1)S(1)} %constant_dynamic-update-slice_fusion.11.p0), channel_id=1, source_target_pairs={{0,1},{1,0},{2,3},{3,2},{16,17},{17,16},{18,19},{19,18},{32,33},{3... | collective-permute-start | bytes 1572872 | tf_op jit(solution)/shard_map/ppermute | solution.py:41
  116.3 18.2 %collective-permute-start.30 = (bf16[1024,256]{1,0:T(8,128)(2,1)S(1)}, bf16[1024,256]{1,0:T(8,128)(2,1)S(1)}, u32[]{:S(2)}, u32[]{:S(2)}) collective-permute-start(bf16[1024,256]{1,0:T(8,128)(2,1)S(1)} %constant_dynamic-update-slice_fusion.11.p0), channel_id=1, source_target_pairs={{0,2},{1,3},{2,0},{3,1},{16,18},{17,19},{18,16},{19,17},{32,34},{3... | collective-permute-start | bytes 1572872 | tf_op jit(solution)/shard_map/ppermute | solution.py:41
  119.4 18.0 %collective-permute-start.31 = (bf16[1024,256]{1,0:T(8,128)(2,1)S(1)}, bf16[1024,256]{1,0:T(8,128)(2,1)S(1)}, u32[]{:S(2)}, u32[]{:S(2)}) collective-permute-start(bf16[1024,256]{1,0:T(8,128)(2,1)S(1)} %constant_dynamic-update-slice_fusion.11.p0), channel_id=1, source_target_pairs={{0,3},{1,2},{2,1},{3,0},{16,19},{17,18},{18,17},{19,16},{32,35},{3... | collective-permute-start | bytes 1572872 | tf_op jit(solution)/shard_map/ppermute | solution.py:41
  140.9 17.8 %collective-permute-start.33 = (bf16[2048,256]{1,0:T(8,128)(2,1)S(1)}, bf16[2048,256]{1,0:T(8,128)(2,1)S(1)}, u32[]{:S(2)}, u32[]{:S(2)}) collective-permute-start(bf16[2048,256]{1,0:T(8,128)(2,1)S(1)} %get-tuple-element.63), channel_id=1, source_target_pairs={{0,64},{64,0},{1,65},{65,1},{2,66},{66,2},{3,67},{67,3},{4,68},{68... | collective-permute-start | bytes 3145736 | tf_op jit(solution)/shard_map/ppermute | solution.py:23
  150.4 8.4 %collective-permute-start.32 = (bf16[512,256]{1,0:T(8,128)(2,1)S(1)}, bf16[512,256]{1,0:T(8,128)(2,1)S(1)}, u32[]{:S(2)}, u32[]{:S(2)}) collective-permute-start(bf16[512,256]{1,0:T(8,128)(2,1)S(1)} %shard_map.117), channel_id=1, source_target_pairs={{0,128},{128,0},{1,129},{129,1},{2,130},{130,2},{3,131},{131,3},{4... | collective-permute-start | bytes 786440 | tf_op jit(solution)/shard_map/ppermute | solution.py:27
  152.2 6.6 %collective-permute-start.34 = (bf16[512,256]{1,0:T(8,128)(2,1)S(1)}, bf16[512,256]{1,0:T(8,128)(2,1)S(1)}, u32[]{:S(2)}, u32[]{:S(2)}) collective-permute-start(bf16[512,256]{1,0:T(8,128)(2,1)S(1)} %fusion.1.feat.refs_0_), channel_id=1, source_target_pairs={{0,64},{64,0},{1,65},{65,1},{2,66},{66,2},{3,67},{67,3},{4,68},{68... | collective-permute-start | bytes 786440 | tf_op jit(solution)/shard_map/ppermute | solution.py:23
  (14 other events, 67.9 us)

commit v3 on v2

--- a/solution.py
+++ b/solution.py
@@ -1,3 +1,5 @@
+import functools
+
 import jax
 import jax.numpy as jnp
 import numpy as np
@@ -14,7 +16,6 @@
 BLOCK = 32
 
 VMEM = pl.BlockSpec(memory_space=pltpu.VMEM)
-FAR = pl.BlockSpec(memory_space=pltpu.HBM)
 SMEM = pl.BlockSpec(memory_space=pltpu.SMEM)
 PARAMS = pltpu.CompilerParams(vmem_limit_bytes=16 * 1024 * 1024)
 
@@ -54,19 +55,26 @@
     return [pieces[0], got[1], got[2], got[3]]
 
 
-def gathered(x, beside=()):
-    for send in (along_z, first):
-        x = jnp.concatenate(received([x] * 4, send), axis=0)
-    x, beside = lax.optimization_barrier((x, beside))
-    return received([x] * 4, second), beside
-
-
-def scattered(pieces):
-    total = sum(p.astype(jnp.float32) for p in received(pieces, second))
-    for send in (first, along_z):
-        pieces = jnp.split(total.astype(jnp.bfloat16), 4, axis=0)
-        total = sum(p.astype(jnp.float32) for p in received(pieces, send))
-    return total
+def gathered(x):
+    for k in (1, 2):
+        x = jnp.concatenate([x, along_z(x, k)], axis=0)
+    x = jnp.concatenate(received([x] * 4, first), axis=0)
+    return received([x] * 4, second)
+
+
+def summed(pieces):
+    return sum(p.astype(jnp.float32) for p in pieces)
+
+
+def scattered(pieces, beside):
+    pieces, beside = lax.optimization_barrier((pieces, beside))
+    total = summed(received(pieces, second))
+    total, swapped = lax.optimization_barrier((total, [other_core(b) for b in beside]))
+    total = summed(received(jnp.split(total.astype(jnp.bfloat16), 4, axis=0), first))
+    for k in (2, 1):
+        kept, sent = jnp.split(total.astype(jnp.bfloat16), 2, axis=0)
+        total = summed([kept, along_z(sent, k)])
+    return total, swapped
 
 
 def block_rows():
@@ -150,16 +158,12 @@
     )(x)
 
 
-def gathered_dot_kernel(w, p0, p1, p2, p3, out, held, sems):
-    copies = [pltpu.make_async_copy(w.at[k], held.at[k], sems.at[k]) for k in range(4)]
-    for copy in copies:
-        copy.start()
-    total = None
-    for k, piece in enumerate((p0, p1, p2, p3)):
-        copies[k].wait()
-        term = jnp.dot(held[k], piece[...], preferred_element_type=jnp.float32)
-        total = term if total is None else total + term
-    out[...] = total.astype(out.dtype)
+def gathered_dot_kernel(w, p0, p1, p2, p3, out):
+    terms = [
+        jnp.dot(w[k], p[...], preferred_element_type=jnp.float32)
+        for k, p in enumerate((p0, p1, p2, p3))
+    ]
+    out[...] = (terms[0] + terms[1] + terms[2] + terms[3]).astype(out.dtype)
 
 
 def gathered_dot(w, pieces):
@@ -168,9 +172,8 @@
     return pl.pallas_call(
         gathered_dot_kernel,
         out_shape=jax.ShapeDtypeStruct((n, tokens), jnp.bfloat16),
-        in_specs=[FAR] + [VMEM] * 4,
+        in_specs=[VMEM] * 5,
         out_specs=VMEM,
-        scratch_shapes=[pltpu.VMEM(w.shape, jnp.bfloat16), pltpu.SemaphoreType.DMA((4,))],
         compiler_params=PARAMS,
         cost_estimate=pl.CostEstimate(
             flops=8 * n * depth * tokens, bytes_accessed=8 << 20, transcendentals=0
@@ -178,14 +181,9 @@
     )(w, *pieces)
 
 
-def blocked_dot_kernel(w, feat, p0, p1, p2, p3, held, sems):
-    order = ((2, p2), (1, p1), (3, p3), (0, p0))
-    copies = {k: pltpu.make_async_copy(w.at[k], held.at[k], sems.at[k]) for k, _ in order}
-    for k, _ in order:
-        copies[k].start()
-    for k, piece in order:
-        copies[k].wait()
-        piece[...] = jnp.dot(held[k], feat[...], preferred_element_type=jnp.float32).astype(
+def blocked_dot_kernel(w, feat, *pieces):
+    for k, piece in enumerate(pieces):
+        piece[...] = jnp.dot(w[k], feat[...], preferred_element_type=jnp.float32).astype(
             piece.dtype
         )
 
@@ -197,9 +195,8 @@
     return pl.pallas_call(
         blocked_dot_kernel,
         out_shape=(piece,) * 4,
-        in_specs=[FAR, VMEM],
+        in_specs=[VMEM] * 2,
         out_specs=(VMEM,) * 4,
-        scratch_shapes=[pltpu.VMEM(w.shape, jnp.bfloat16), pltpu.SemaphoreType.DMA((4,))],
         compiler_params=PARAMS,
         cost_estimate=pl.CostEstimate(
             flops=8 * n * width * tokens, bytes_accessed=7 << 20, transcendentals=0
@@ -228,44 +225,61 @@
     )(rows, *pieces)
 
 
-def outer_kernel(scale, a0, b0, a1, b1, out):
-    dims = (((1,), (1,)), ((), ()))
-    out[...] = (
-        scale
-        * (
-            lax.dot_general(a0[...], b0[...], dims, preferred_element_type=jnp.float32)
-            + lax.dot_general(a1[...], b1[...], dims, preferred_element_type=jnp.float32)
-        )
-    ).astype(out.dtype)
-
-
-def outer(a0, b0, a1, b1, scale):
-    m, tokens = a0.shape
-    n = b0.shape[0]
-    tile = 512
-
-    def kernel(*refs):
-        outer_kernel(scale, *refs)
-
-    if m > n:
-        left = pl.BlockSpec((tile, tokens), lambda i: (i, 0))
-        right = pl.BlockSpec((n, tokens), lambda i: (0, 0))
-        out = pl.BlockSpec((tile, n), lambda i: (i, 0))
-    else:
-        left = pl.BlockSpec((m, tokens), lambda i: (0, 0))
-        right = pl.BlockSpec((tile, tokens), lambda i: (i, 0))
-        out = pl.BlockSpec((m, tile), lambda i: (0, i))
-    return pl.pallas_call(
-        kernel,
+def dot_nt(a, b):
+    return lax.dot_general(a, b, (((1,), (1,)), ((), ())), preferred_element_type=jnp.float32)
+
+
+def outer_dec_kernel(scale, feat, err, feat_b, err_b, out):
+    out[...] = (scale * (dot_nt(feat[...], err[...]) + dot_nt(feat_b[...], err_b[...]))).astype(
+        out.dtype
+    )
+
+
+def outer_dec(feat, err, feat_b, err_b, scale):
+    m, tokens = feat.shape
+    n = err.shape[0]
+    tile = n // 4
+    left = pl.BlockSpec((m, tokens), lambda i: (0, 0))
+    right = pl.BlockSpec((tile, tokens), lambda i: (i, 0))
+    return pl.pallas_call(
+        functools.partial(outer_dec_kernel, scale),
         out_shape=jax.ShapeDtypeStruct((m, n), jnp.bfloat16),
-        grid=(max(m, n) // tile,),
+        grid=(4,),
         in_specs=[left, right, left, right],
-        out_specs=out,
+        out_specs=pl.BlockSpec((m, tile), lambda i: (0, i)),
         compiler_params=PARAMS,
         cost_estimate=pl.CostEstimate(
             flops=40 * m * n * tokens, bytes_accessed=5 << 20, transcendentals=0
         ),
-    )(a0, b0, a1, b1)
+    )(feat, err, feat_b, err_b)
+
+
+def outer_enc_kernel(acts, grad, grad_b, *rest):
+    acts_b, out = rest[:-1], rest[-1]
+    own = dot_nt(acts[...], grad[...])
+    for j, part in enumerate(acts_b):
+
+        @pl.when(pl.program_id(0) == j)
+        def _():
+            out[...] = (own + dot_nt(part[...], grad_b[...])).astype(out.dtype)
+
+
+def outer_enc(acts, grad, acts_b, grad_b):
+    m, tokens = acts.shape
+    n = grad.shape[0]
+    tile = m // len(acts_b)
+    rows = pl.BlockSpec((tile, tokens), lambda i: (i, 0))
+    return pl.pallas_call(
+        outer_enc_kernel,
+        out_shape=jax.ShapeDtypeStruct((m, n), jnp.bfloat16),
+        grid=(len(acts_b),),
+        in_specs=[rows] + [VMEM] * (2 + len(acts_b)),
+        out_specs=pl.BlockSpec((tile, n), lambda i: (i, 0)),
+        compiler_params=PARAMS,
+        cost_estimate=pl.CostEstimate(
+            flops=40 * m * n * tokens, bytes_accessed=5 << 20, transcendentals=0
+        ),
+    )(acts, grad, grad_b, *acts_b)
 
 
 def body(acts, w_enc, b_enc, w_dec, b_dec):
@@ -285,34 +299,32 @@
 
     start, enc, dec = lax.optimization_barrier((start, w_enc[0], w_dec[0]))
     enc_other, dec_other = other_core(enc), other_core(dec)
-    acts_p, weights = gathered(start, (enc, enc_other, dec, dec_other))
-    enc_r = relative_enc(rows, *weights[:2])
-    dec_r = relative_dec(rows, *weights[2:])
+    enc_r = relative_enc(rows, enc, enc_other)
+    dec_r = relative_dec(rows, dec, dec_other)
+    acts_p = gathered(start)
     dec_rt = turned(dec_r)
 
     part = gathered_dot(enc_r, acts_p)
     part, acts_p = lax.optimization_barrier((part, acts_p))
     part_b = other_layer(part)
     acts_own, acts_other = placed(rows, acts_p)
-    acts_b = other_core(acts_other)
-    part_b, acts_b = lax.optimization_barrier((part_b, acts_b))
     pre = part.astype(jnp.float32) + part_b.astype(jnp.float32) + b_enc[:, None]
     feat = (jax.nn.softplus(4.0 * pre) / 4.0).astype(jnp.bfloat16)
 
-    recon = scattered(blocked_dot(dec_r, feat))
+    recon, (*acts_b, feat_b) = scattered(blocked_dot(dec_r, feat), [*jnp.split(acts_other, 4), feat])
     err = (recon + bias_both.astype(jnp.float32) - start.astype(jnp.float32)).astype(jnp.bfloat16)
 
-    err_p, _ = gathered(err)
+    err_p = gathered(err)
     term = gathered_dot(dec_rt, err_p)
-    term, err_p, feat, err = lax.optimization_barrier((term, err_p, feat, err))
+    term, err_p, err = lax.optimization_barrier((term, err_p, err))
     term_b = other_layer(term)
     err_own, err_other = placed(rows, err_p)
-    err_b, feat_b = other_core(err_other), other_core(feat)
+    term_b, err_own, err_other = lax.optimization_barrier((term_b, err_own, err_other))
+    err_b = other_core(err_other)
     sums = jnp.sum(err.astype(jnp.float32), axis=1)
     width = sums.shape[0] // 2
     grad_bdec = scale * (sums[:width] + other_core(sums[width:]))
-    term_b, err_b, feat_b, grad_bdec = lax.optimization_barrier((term_b, err_b, feat_b, grad_bdec))
-    grad_dec = outer(feat, err_own, feat_b, err_b, scale)
+    grad_dec = outer_dec(feat, err_own, feat_b, err_b, scale)
 
     grad_feat = scale * (term.astype(jnp.float32) + term_b.astype(jnp.float32))
     grad_pre = grad_feat * jax.nn.sigmoid(4.0 * pre)
@@ -320,7 +332,7 @@
     grad_pre_o = other_core(grad_pre_b)
     part_benc = jnp.sum(grad_pre, axis=1)
     grad_benc = part_benc + other_core(part_benc)
-    grad_enc = outer(acts_own, grad_pre_b, acts_b, grad_pre_o, 1.0)
+    grad_enc = outer_enc(acts_own, grad_pre_b, acts_b, grad_pre_o)
     return (grad_enc[None], grad_dec[None], grad_benc, grad_bdec[None])
 
 

time: 167 us -> 172 us (1.030)
  starting transfers between devices: 62.5 us -> 92.9 us
  waiting for transfers between devices: 70.7 us -> 51.3 us
  local copies, waits for them, and re-layouts: 7.61 us -> 3.69 us
  Pallas kernels: 21.7 us -> 19.3 us
    ppermute x9 -> x12, starting transfers between devices: 18.9 us -> 46.4 us  [other_core(): return lax.ppermute(x, 'core', [(0, 1), (1, 0)])]
    ppermute x18, waiting for transfers between devices: 48.7 us -> 32.1 us  [in_plane(): return lax.ppermute(x, PLANE, pairs)]
    ppermute x2, waiting for transfers between devices: 9.18 us -> 4.69 us  [other_layer(): return lax.ppermute(x, 'z_lo', [(0, 1), (1, 0)])]
    ppermute x9 -> x6, starting transfers between devices: 17.9 us -> 22.2 us  [along_z(): return lax.ppermute(x, 'z_hi', [(i, i ^ k) for i in range(4)])]
    unnamed x26 -> x16, local copies, waits for them, and re-layouts: 5.9 us -> 1.9 us
    pallas_call x2, Pallas kernels: 5.82 us -> 2.5 us  [gathered_dot(): pl.pallas_call(gathered_dot_kernel, out_shape=jax.ShapeDtypeStruct((n, to...]
    ppermute x9 -> x6, waiting for transfers between devices: 10.9 us -> 12.3 us  [along_z(): return lax.ppermute(x, 'z_hi', [(i, i ^ k) for i in range(4)])]
  transfers between devices with their start and end apart: 38 -> 38, of which waited for: 26 -> 21; matrix products, arithmetic and copies ran while one was open for 1% -> 1% of each run, Pallas kernels for 5% -> 8%
where the time goes in v3:
time: 172 us; the launch traced here: 171 us
  starting transfers between devices  92.9 us (54%)
  waiting for transfers between devices  51.3 us (30%)
  Pallas kernels  19.3 us (11%)
  local copies, waits for them, and re-layouts  3.69 us (2%)
  other arithmetic  3.25 us (2%)
    ppermute x12, starting transfers between devices, other_core(): return lax.ppermute(x, 'core', [(0, 1), (1, 0)])  46.4 us
    ppermute x18, waiting for transfers between devices, in_plane(): return lax.ppermute(x, PLANE, pairs)  32.1 us
    ppermute x18, starting transfers between devices, in_plane(): return lax.ppermute(x, PLANE, pairs)  22.4 us
    ppermute x6, starting transfers between devices, along_z(): return lax.ppermute(x, 'z_hi', [(i, i ^ k) for i in range(4)])  22.2 us
    ppermute x6, waiting for transfers between devices, along_z(): return lax.ppermute(x, 'z_hi', [(i, i ^ k) for i in range(4)])  12.3 us
    ppermute x2, waiting for transfers between devices, other_layer(): return lax.ppermute(x, 'z_lo', [(0, 1), (1, 0)])  4.69 us
    pallas_call x1, Pallas kernels, outer_enc(): pl.pallas_call(outer_enc_kernel, out_shape=jax.ShapeDtypeStruct((m, n), j...  3.6 us
  transfers between devices with their start and end apart: 38, of which 21 were waited for; matrix products, arithmetic and copies ran while one was open for 1% of the time, Pallas kernels for 8%

profile of v3, /device:TPU:1, one launch (start us, length us, event | category | flops | bytes accessed | tf_op | source)
XLA Modules:
  0.0 171.4 jit_solution(63593916744857518)
XLA Ops:
  2.1 3.3 %collective-permute-start = (bf16[32,384]{1,0:T(8,128)(2,1)S(1)}, bf16[32,384]{1,0:T(8,128)(2,1)S(1)}, u32[]{:S(2)}, u32[]{:S(2)}) collective-permute-start(bf16[32,384]{1,0:T(8,128)(2,1)S(1)} %pad_maximum_fusion.4), channel_id=1, source_target_pairs={{0,64},{64,0},{1,65},{65,1},{2,66},{66,2},{3,67},{67,3},{4,68},{68... | collective-permute-start | bytes 73736 | tf_op jit(solution)/shard_map/ppermute | solution.py:24
  8.0 2.8 %collective-permute-done.2 = bf16[64,256]{1,0:T(8,128)(2,1)S(1)} collective-permute-done((bf16[64,256]{1,0:T(8,128)(2,1)S(1)}, bf16[64,256]{1,0:T(8,128)(2,1)S(1)}, u32[]{:S(2)}, u32[]{:S(2)}) %collective-permute-start.2) | collective-permute-done | bytes 32800 | tf_op jit(solution)/shard_map/ppermute | solution.py:32
  10.8 4.8 %collective-permute-start.3 = (bf16[128,256]{1,0:T(8,128)(2,1)S(1)}, bf16[128,256]{1,0:T(8,128)(2,1)S(1)}, u32[]{:S(2)}, u32[]{:S(2)}) collective-permute-start(bf16[128,256]{1,0:T(8,128)(2,1)S(1)} %pad_maximum_fusion.1), channel_id=1, source_target_pairs={{0,8},{4,12},{8,0},{12,4},{1,9},{5,13},{9,1},{13,5},{2,10},{6,14},... | collective-permute-start | bytes 196616 | tf_op jit(solution)/shard_map/ppermute | solution.py:32
  15.6 2.2 %collective-permute-done.3 = bf16[128,256]{1,0:T(8,128)(2,1)S(1)} collective-permute-done((bf16[128,256]{1,0:T(8,128)(2,1)S(1)}, bf16[128,256]{1,0:T(8,128)(2,1)S(1)}, u32[]{:S(2)}, u32[]{:S(2)}) %collective-permute-start.3) | collective-permute-done | bytes 65568 | tf_op jit(solution)/shard_map/ppermute | solution.py:32
  18.7 2.6 %collective-permute-start.5 = (bf16[256,256]{1,0:T(8,128)(2,1)S(1)}, bf16[256,256]{1,0:T(8,128)(2,1)S(1)}, u32[]{:S(2)}, u32[]{:S(2)}) collective-permute-start(bf16[256,256]{1,0:T(8,128)(2,1)S(1)} %get-tuple-element.95), channel_id=1, source_target_pairs={{0,32},{1,33},{2,34},{3,35},{16,48},{17,49},{18,50},{19,51},{32,0}... | collective-permute-start | bytes 393224 | tf_op jit(solution)/shard_map/ppermute | solution.py:42
  21.8 3.3 %collective-permute-done.5 = bf16[256,256]{1,0:T(8,128)(2,1)S(1)} collective-permute-done((bf16[256,256]{1,0:T(8,128)(2,1)S(1)}, bf16[256,256]{1,0:T(8,128)(2,1)S(1)}, u32[]{:S(2)}, u32[]{:S(2)}) %collective-permute-start.5) | collective-permute-done | bytes 131104 | tf_op jit(solution)/shard_map/ppermute | solution.py:42
  25.1 1.7 collective-permute-done.6
  26.8 2.5 %collective-permute-start.9 = (bf16[1024,256]{1,0:T(8,128)(2,1)S(1)}, bf16[1024,256]{1,0:T(8,128)(2,1)S(1)}, u32[]{:S(2)}, u32[]{:S(2)}) collective-permute-start(bf16[1024,256]{1,0:T(8,128)(2,1)S(1)} %constant_dynamic-update-slice_fusion.3.p0), channel_id=1, source_target_pairs={{0,3},{1,2},{2,1},{3,0},{16,19},{17,18},{18,17},{19,16},{32,35},{3... | collective-permute-start | bytes 1572872 | tf_op jit(solution)/shard_map/ppermute | solution.py:42
  32.4 3.1 %shard_map.111.w = bf16[4,512,1024]{2,1,0:T(8,128)(2,1)S(1)} custom-call(s32[64]{0:T(128)S(1)} %fusion.5.rows, bf16[2048,512]{1,0:T(8,128)(2,1)S(1)} %bitcast.16, bf16[2048,512]{1,0:T(8,128)(2,1)} %collective-permute-done.1.other), custom_call_target="tpu_custom_call" | custom-call | flops 1048576 | bytes 16777216 | tf_op jit(solution)/shard_map/pallas_call | solution.py:102
  35.5 6.5 %collective-permute-done.9.p3 = bf16[1024,256]{1,0:T(8,128)(2,1)S(1)} collective-permute-done((bf16[1024,256]{1,0:T(8,128)(2,1)S(1)}, bf16[1024,256]{1,0:T(8,128)(2,1)S(1)}, u32[]{:S(2)}, u32[]{:S(2)}) %collective-permute-start.9) | collective-permute-done | bytes 524320 | tf_op jit(solution)/shard_map/ppermute | solution.py:42
  45.5 3.1 %shard_map.114.x.w = bf16[4,1024,512]{2,1,0:T(8,128)(2,1)S(1)} custom-call(s32[64]{0:T(128)S(1)} %fusion.5.rows, bf16[512,2048]{1,0:T(8,128)(2,1)S(1)} %bitcast.18, bf16[512,2048]{1,0:T(8,128)(2,1)} %collective-permute-done.10.other), custom_call_target="tpu_custom_call" | custom-call | flops 1048576 | bytes 16777216 | tf_op jit(solution)/shard_map/pallas_call | solution.py:132
  52.2 2.5 %collective-permute-start.13 = (bf16[1024,256]{1,0:T(8,128)(2,1)S(1)}, bf16[1024,256]{1,0:T(8,128)(2,1)S(1)}, u32[]{:S(2)}, u32[]{:S(2)}) collective-permute-start(bf16[1024,256]{1,0:T(8,128)(2,1)S(1)} %get-tuple-element.60), channel_id=1, source_target_pairs={{0,2},{1,3},{2,0},{3,1},{16,18},{17,19},{18,16},{19,17},{32,34},{3... | collective-permute-start | bytes 1572872 | tf_op jit(solution)/shard_map/ppermute | solution.py:42
  55.2 12.8 %collective-permute-start.15 = (bf16[512,256]{1,0:T(8,128)(2,1)S(1)}, bf16[512,256]{1,0:T(8,128)(2,1)S(1)}, u32[]{:S(2)}, u32[]{:S(2)}) collective-permute-start(bf16[512,256]{1,0:T(8,128)(2,1)S(1)} %get-tuple-element.62), channel_id=1, source_target_pairs={{0,64},{64,0},{1,65},{65,1},{2,66},{66,2},{3,67},{67,3},{4,68},{68... | collective-permute-start | bytes 786440 | tf_op jit(solution)/shard_map/ppermute | solution.py:24
  68.1 4.5 %collective-permute-start.17 = (bf16[512,256]{1,0:T(8,128)(2,1)S(1)}, bf16[512,256]{1,0:T(8,128)(2,1)S(1)}, u32[]{:S(2)}, u32[]{:S(2)}) collective-permute-start(bf16[512,256]{1,0:T(8,128)(2,1)S(1)} %get-tuple-element.64), channel_id=1, source_target_pairs={{0,64},{64,0},{1,65},{65,1},{2,66},{66,2},{3,67},{67,3},{4,68},{68... | collective-permute-start | bytes 786440 | tf_op jit(solution)/shard_map/ppermute | solution.py:24
  72.5 8.3 %collective-permute-start.18 = (bf16[512,256]{1,0:T(8,128)(2,1)S(1)}, bf16[512,256]{1,0:T(8,128)(2,1)S(1)}, u32[]{:S(2)}, u32[]{:S(2)}) collective-permute-start(bf16[512,256]{1,0:T(8,128)(2,1)S(1)} %get-tuple-element.65), channel_id=1, source_target_pairs={{0,64},{64,0},{1,65},{65,1},{2,66},{66,2},{3,67},{67,3},{4,68},{68... | collective-permute-start | bytes 786440 | tf_op jit(solution)/shard_map/ppermute | solution.py:24
  80.8 3.1 %collective-permute-start.19 = (bf16[512,256]{1,0:T(8,128)(2,1)S(1)}, bf16[512,256]{1,0:T(8,128)(2,1)S(1)}, u32[]{:S(2)}, u32[]{:S(2)}) collective-permute-start(bf16[512,256]{1,0:T(8,128)(2,1)S(1)} %fusion.1.feat), channel_id=1, source_target_pairs={{0,64},{64,0},{1,65},{65,1},{2,66},{66,2},{3,67},{67,3},{4,68},{68... | collective-permute-start | bytes 786440 | tf_op jit(solution)/shard_map/ppermute | solution.py:24
  86.2 2.9 %collective-permute-start.22 = (bf16[256,256]{1,0:T(8,128)(2,1)S(1)}, bf16[256,256]{1,0:T(8,128)(2,1)S(1)}, u32[]{:S(2)}, u32[]{:S(2)}) collective-permute-start(bf16[256,256]{1,0:T(8,128)(2,1)S(1)} %get-tuple-element.94), channel_id=1, source_target_pairs={{0,48},{1,49},{2,50},{3,51},{16,32},{17,33},{18,34},{19,35},{32,16... | collective-permute-start | bytes 393224 | tf_op jit(solution)/shard_map/ppermute | solution.py:42
  92.5 6.2 %collective-permute-start.23 = (bf16[128,256]{1,0:T(8,128)(2,1)S(1)}, bf16[128,256]{1,0:T(8,128)(2,1)S(1)}, u32[]{:S(2)}, u32[]{:S(2)}) collective-permute-start(bf16[128,256]{1,0:T(8,128)(2,1)S(1)} %split.53), channel_id=1, source_target_pairs={{0,8},{4,12},{8,0},{12,4},{1,9},{5,13},{9,1},{13,5},{2,10},{6,14},... | collective-permute-start | bytes 196616 | tf_op jit(solution)/shard_map/ppermute | solution.py:32
  98.8 1.6 collective-permute-done.23
  100.4 2.8 %collective-permute-start.24 = (bf16[64,256]{1,0:T(8,128)(2,1)S(1)}, bf16[64,256]{1,0:T(8,128)(2,1)S(1)}, u32[]{:S(2)}, u32[]{:S(2)}) collective-permute-start(bf16[64,256]{1,0:T(8,128)(2,1)S(1)} %split.55), channel_id=1, source_target_pairs={{0,4},{4,0},{8,12},{12,8},{1,5},{5,1},{9,13},{13,9},{2,6},{6,2},{1... | collective-permute-start | bytes 98312 | tf_op jit(solution)/shard_map/ppermute | solution.py:32
  104.9 2.1 %collective-permute-start.25 = (bf16[64,256]{1,0:T(8,128)(2,1)S(1)}, bf16[64,256]{1,0:T(8,128)(2,1)S(1)}, u32[]{:S(2)}, u32[]{:S(2)}) collective-permute-start(bf16[64,256]{1,0:T(8,128)(2,1)S(1)} %get-tuple-element.83), channel_id=1, source_target_pairs={{0,4},{4,0},{8,12},{12,8},{1,5},{5,1},{9,13},{13,9},{2,6},{6,2},{1... | collective-permute-start | bytes 98312 | tf_op jit(solution)/shard_map/ppermute | solution.py:32
  107.0 1.9 %collective-permute-done.25 = bf16[64,256]{1,0:T(8,128)(2,1)S(1)} collective-permute-done((bf16[64,256]{1,0:T(8,128)(2,1)S(1)}, bf16[64,256]{1,0:T(8,128)(2,1)S(1)}, u32[]{:S(2)}, u32[]{:S(2)}) %collective-permute-start.25) | collective-permute-done | bytes 32800 | tf_op jit(solution)/shard_map/ppermute | solution.py:32
  109.0 5.1 %collective-permute-start.26 = (bf16[128,256]{1,0:T(8,128)(2,1)S(1)}, bf16[128,256]{1,0:T(8,128)(2,1)S(1)}, u32[]{:S(2)}, u32[]{:S(2)}) collective-permute-start(bf16[128,256]{1,0:T(8,128)(2,1)S(1)} %pad_maximum_fusion.2), channel_id=1, source_target_pairs={{0,8},{4,12},{8,0},{12,4},{1,9},{5,13},{9,1},{13,5},{2,10},{6,14},... | collective-permute-start | bytes 196616 | tf_op jit(solution)/shard_map/ppermute | solution.py:32
  114.0 2.2 %collective-permute-done.26 = bf16[128,256]{1,0:T(8,128)(2,1)S(1)} collective-permute-done((bf16[128,256]{1,0:T(8,128)(2,1)S(1)}, bf16[128,256]{1,0:T(8,128)(2,1)S(1)}, u32[]{:S(2)}, u32[]{:S(2)}) %collective-permute-start.26) | collective-permute-done | bytes 65568 | tf_op jit(solution)/shard_map/ppermute | solution.py:32
  116.8 2.2 %collective-permute-start.29 = (bf16[256,256]{1,0:T(8,128)(2,1)S(1)}, bf16[256,256]{1,0:T(8,128)(2,1)S(1)}, u32[]{:S(2)}, u32[]{:S(2)}) collective-permute-start(bf16[256,256]{1,0:T(8,128)(2,1)S(1)} %pad_maximum_fusion), channel_id=1, source_target_pairs={{0,48},{1,49},{2,50},{3,51},{16,32},{17,33},{18,34},{19,35},{32,16... | collective-permute-start | bytes 393224 | tf_op jit(solution)/shard_map/ppermute | solution.py:42
  120.4 3.9 %collective-permute-done.28 = bf16[256,256]{1,0:T(8,128)(2,1)S(1)} collective-permute-done((bf16[256,256]{1,0:T(8,128)(2,1)S(1)}, bf16[256,256]{1,0:T(8,128)(2,1)S(1)}, u32[]{:S(2)}, u32[]{:S(2)}) %collective-permute-start.28) | collective-permute-done | bytes 131104 | tf_op jit(solution)/shard_map/ppermute | solution.py:42
  124.8 2.9 %collective-permute-start.30 = (bf16[1024,256]{1,0:T(8,128)(2,1)S(1)}, bf16[1024,256]{1,0:T(8,128)(2,1)S(1)}, u32[]{:S(2)}, u32[]{:S(2)}) collective-permute-start(bf16[1024,256]{1,0:T(8,128)(2,1)S(1)} %constant_dynamic-update-slice_fusion.9.p0), channel_id=1, source_target_pairs={{0,1},{1,0},{2,3},{3,2},{16,17},{17,16},{18,19},{19,18},{32,33},{3... | collective-permute-start | bytes 1572872 | tf_op jit(solution)/shard_map/ppermute | solution.py:42
  129.1 12.4 %collective-permute-done.32.p3 = bf16[1024,256]{1,0:T(8,128)(2,1)S(1)} collective-permute-done((bf16[1024,256]{1,0:T(8,128)(2,1)S(1)}, bf16[1024,256]{1,0:T(8,128)(2,1)S(1)}, u32[]{:S(2)}, u32[]{:S(2)}) %collective-permute-start.32) | collective-permute-done | bytes 524320 | tf_op jit(solution)/shard_map/ppermute | solution.py:42
  144.8 3.9 %collective-permute-done.33 = bf16[512,256]{1,0:T(8,128)(2,1)S(1)} collective-permute-done((bf16[512,256]{1,0:T(8,128)(2,1)S(1)}, bf16[512,256]{1,0:T(8,128)(2,1)S(1)}, u32[]{:S(2)}, u32[]{:S(2)}) %collective-permute-start.33) | collective-permute-done | bytes 262176 | tf_op jit(solution)/shard_map/ppermute | solution.py:28
  149.0 13.3 %collective-permute-start.34 = (bf16[512,256]{1,0:T(8,128)(2,1)S(1)}, bf16[512,256]{1,0:T(8,128)(2,1)S(1)}, u32[]{:S(2)}, u32[]{:S(2)}) collective-permute-start(bf16[512,256]{1,0:T(8,128)(2,1)S(1)} %get-tuple-element.85.grad), channel_id=1, source_target_pairs={{0,64},{64,0},{1,65},{65,1},{2,66},{66,2},{3,67},{67,3},{4,68},{68... | collective-permute-start | bytes 786440 | tf_op jit(solution)/shard_map/ppermute | solution.py:24
  164.8 3.6 %shard_map.119 = bf16[2048,512]{1,0:T(8,128)(2,1)} custom-call(bf16[2048,256]{1,0:T(8,128)(2,1)S(1)} %get-tuple-element.50.acts, bf16[512,256]{1,0:T(8,128)(2,1)S(1)} %get-tuple-element.85.grad, bf16[512,256]{1,0:T(8,128)(2,1)S(1)} %collective-permute-done.34.grad_b, bf16[512,256]{1,0:T(8,128)(2,1)S(1)} %collective-permute-done.15.rest_0_, ...), custom_call_target="tpu_custom_call" | custom-call | flops 10737418240 | bytes 5242880 | tf_op jit(solution)/shard_map/pallas_call | solution.py:272
  168.4 3.0 %shard_map.120 = bf16[512,2048]{1,0:T(8,128)(2,1)} custom-call(bf16[512,256]{1,0:T(8,128)(2,1)S(1)} %fusion.1.feat, bf16[2048,256]{1,0:T(8,128)(2,1)S(1)} %get-tuple-element.80.err, bf16[512,256]{1,0:T(8,128)(2,1)S(1)} %collective-permute-done.19.feat_b, bf16[2048,256]{1,0:T(8,128)(2,1)S(1)} %collective-permute-done.35.err_b), custom_call_target="tpu_custom_call" | custom-call | flops 10737418240 | bytes 5242880 | tf_op jit(solution)/shard_map/pallas_call | solution.py:244
  (98 shorter events, 33.4 us)
Async XLA Ops:
  6.2 24.6 %collective-permute-start.1 = (bf16[2048,512]{1,0:T(8,128)(2,1)}, bf16[2048,512]{1,0:T(8,128)(2,1)}, u32[]{:S(2)}, u32[]{:S(2)}) collective-permute-start(bf16[2048,512]{1,0:T(8,128)(2,1)} %bitcast.15), channel_id=1, source_target_pairs={{0,64},{64,0},{1,65},{65,1},{2,66},{66,2},{3,67},{67,3},{4,68},{68... | collective-permute-start | bytes 6291464 | tf_op jit(solution)/shard_map/ppermute | solution.py:24
  6.6 38.7 %collective-permute-start.10 = (bf16[512,2048]{1,0:T(8,128)(2,1)}, bf16[512,2048]{1,0:T(8,128)(2,1)}, u32[]{:S(2)}, u32[]{:S(2)}) collective-permute-start(bf16[512,2048]{1,0:T(8,128)(2,1)} %bitcast.17), channel_id=1, source_target_pairs={{0,64},{64,0},{1,65},{65,1},{2,66},{66,2},{3,67},{67,3},{4,68},{68... | collective-permute-start | bytes 6291464 | tf_op jit(solution)/shard_map/ppermute | solution.py:24
  10.8 7.0 %collective-permute-start.3 = (bf16[128,256]{1,0:T(8,128)(2,1)S(1)}, bf16[128,256]{1,0:T(8,128)(2,1)S(1)}, u32[]{:S(2)}, u32[]{:S(2)}) collective-permute-start(bf16[128,256]{1,0:T(8,128)(2,1)S(1)} %pad_maximum_fusion.1), channel_id=1, source_target_pairs={{0,8},{4,12},{8,0},{12,4},{1,9},{5,13},{9,1},{13,5},{2,10},{6,14},... | collective-permute-start | bytes 196616 | tf_op jit(solution)/shard_map/ppermute | solution.py:32
  18.7 6.4 %collective-permute-start.5 = (bf16[256,256]{1,0:T(8,128)(2,1)S(1)}, bf16[256,256]{1,0:T(8,128)(2,1)S(1)}, u32[]{:S(2)}, u32[]{:S(2)}) collective-permute-start(bf16[256,256]{1,0:T(8,128)(2,1)S(1)} %get-tuple-element.95), channel_id=1, source_target_pairs={{0,32},{1,33},{2,34},{3,35},{16,48},{17,49},{18,50},{19,51},{32,0}... | collective-permute-start | bytes 393224 | tf_op jit(solution)/shard_map/ppermute | solution.py:42
  21.3 5.5 %collective-permute-start.6 = (bf16[256,256]{1,0:T(8,128)(2,1)S(1)}, bf16[256,256]{1,0:T(8,128)(2,1)S(1)}, u32[]{:S(2)}, u32[]{:S(2)}) collective-permute-start(bf16[256,256]{1,0:T(8,128)(2,1)S(1)} %get-tuple-element.95), channel_id=1, source_target_pairs={{0,48},{1,49},{2,50},{3,51},{16,32},{17,33},{18,34},{19,35},{32,16... | collective-permute-start | bytes 393224 | tf_op jit(solution)/shard_map/ppermute | solution.py:42
  26.8 15.2 %collective-permute-start.9 = (bf16[1024,256]{1,0:T(8,128)(2,1)S(1)}, bf16[1024,256]{1,0:T(8,128)(2,1)S(1)}, u32[]{:S(2)}, u32[]{:S(2)}) collective-permute-start(bf16[1024,256]{1,0:T(8,128)(2,1)S(1)} %constant_dynamic-update-slice_fusion.3.p0), channel_id=1, source_target_pairs={{0,3},{1,2},{2,1},{3,0},{16,19},{17,18},{18,17},{19,16},{32,35},{3... | collective-permute-start | bytes 1572872 | tf_op jit(solution)/shard_map/ppermute | solution.py:42
  29.3 12.8 %collective-permute-start.8 = (bf16[1024,256]{1,0:T(8,128)(2,1)S(1)}, bf16[1024,256]{1,0:T(8,128)(2,1)S(1)}, u32[]{:S(2)}, u32[]{:S(2)}) collective-permute-start(bf16[1024,256]{1,0:T(8,128)(2,1)S(1)} %constant_dynamic-update-slice_fusion.3.p0), channel_id=1, source_target_pairs={{0,2},{1,3},{2,0},{3,1},{16,18},{17,19},{18,16},{19,17},{32,34},{3... | collective-permute-start | bytes 1572872 | tf_op jit(solution)/shard_map/ppermute | solution.py:42
  29.7 12.9 %collective-permute-start.7 = (bf16[1024,256]{1,0:T(8,128)(2,1)S(1)}, bf16[1024,256]{1,0:T(8,128)(2,1)S(1)}, u32[]{:S(2)}, u32[]{:S(2)}) collective-permute-start(bf16[1024,256]{1,0:T(8,128)(2,1)S(1)} %constant_dynamic-update-slice_fusion.3.p0), channel_id=1, source_target_pairs={{0,1},{1,0},{2,3},{3,2},{16,17},{17,16},{18,19},{19,18},{32,33},{3... | collective-permute-start | bytes 1572872 | tf_op jit(solution)/shard_map/ppermute | solution.py:42
  43.9 5.6 %collective-permute-start.11 = (bf16[512,256]{1,0:T(8,128)(2,1)S(1)}, bf16[512,256]{1,0:T(8,128)(2,1)S(1)}, u32[]{:S(2)}, u32[]{:S(2)}) collective-permute-start(bf16[512,256]{1,0:T(8,128)(2,1)S(1)} %shard_map.112), channel_id=1, source_target_pairs={{0,128},{128,0},{1,129},{129,1},{2,130},{130,2},{3,131},{131,3},{4... | collective-permute-start | bytes 786440 | tf_op jit(solution)/shard_map/ppermute | solution.py:28
  51.3 16.8 %collective-permute-start.12 = (bf16[1024,256]{1,0:T(8,128)(2,1)S(1)}, bf16[1024,256]{1,0:T(8,128)(2,1)S(1)}, u32[]{:S(2)}, u32[]{:S(2)}) collective-permute-start(bf16[1024,256]{1,0:T(8,128)(2,1)S(1)} %get-tuple-element.59), channel_id=1, source_target_pairs={{0,1},{1,0},{2,3},{3,2},{16,17},{17,16},{18,19},{19,18},{32,33},{3... | collective-permute-start | bytes 1572872 | tf_op jit(solution)/shard_map/ppermute | solution.py:42
  52.2 20.4 %collective-permute-start.13 = (bf16[1024,256]{1,0:T(8,128)(2,1)S(1)}, bf16[1024,256]{1,0:T(8,128)(2,1)S(1)}, u32[]{:S(2)}, u32[]{:S(2)}) collective-permute-start(bf16[1024,256]{1,0:T(8,128)(2,1)S(1)} %get-tuple-element.60), channel_id=1, source_target_pairs={{0,2},{1,3},{2,0},{3,1},{16,18},{17,19},{18,16},{19,17},{32,34},{3... | collective-permute-start | bytes 1572872 | tf_op jit(solution)/shard_map/ppermute | solution.py:42
  54.7 26.1 %collective-permute-start.14 = (bf16[1024,256]{1,0:T(8,128)(2,1)S(1)}, bf16[1024,256]{1,0:T(8,128)(2,1)S(1)}, u32[]{:S(2)}, u32[]{:S(2)}) collective-permute-start(bf16[1024,256]{1,0:T(8,128)(2,1)S(1)} %get-tuple-element.61), channel_id=1, source_target_pairs={{0,3},{1,2},{2,1},{3,0},{16,19},{17,18},{18,17},{19,16},{32,35},{3... | collective-permute-start | bytes 1572872 | tf_op jit(solution)/shard_map/ppermute | solution.py:42
  55.2 29.0 %collective-permute-start.15 = (bf16[512,256]{1,0:T(8,128)(2,1)S(1)}, bf16[512,256]{1,0:T(8,128)(2,1)S(1)}, u32[]{:S(2)}, u32[]{:S(2)}) collective-permute-start(bf16[512,256]{1,0:T(8,128)(2,1)S(1)} %get-tuple-element.62), channel_id=1, source_target_pairs={{0,64},{64,0},{1,65},{65,1},{2,66},{66,2},{3,67},{67,3},{4,68},{68... | collective-permute-start | bytes 786440 | tf_op jit(solution)/shard_map/ppermute | solution.py:24
  68.0 16.2 %collective-permute-start.16 = (bf16[512,256]{1,0:T(8,128)(2,1)S(1)}, bf16[512,256]{1,0:T(8,128)(2,1)S(1)}, u32[]{:S(2)}, u32[]{:S(2)}) collective-permute-start(bf16[512,256]{1,0:T(8,128)(2,1)S(1)} %get-tuple-element.63), channel_id=1, source_target_pairs={{0,64},{64,0},{1,65},{65,1},{2,66},{66,2},{3,67},{67,3},{4,68},{68... | collective-permute-start | bytes 786440 | tf_op jit(solution)/shard_map/ppermute | solution.py:24
  68.1 16.2 %collective-permute-start.17 = (bf16[512,256]{1,0:T(8,128)(2,1)S(1)}, bf16[512,256]{1,0:T(8,128)(2,1)S(1)}, u32[]{:S(2)}, u32[]{:S(2)}) collective-permute-start(bf16[512,256]{1,0:T(8,128)(2,1)S(1)} %get-tuple-element.64), channel_id=1, source_target_pairs={{0,64},{64,0},{1,65},{65,1},{2,66},{66,2},{3,67},{67,3},{4,68},{68... | collective-permute-start | bytes 786440 | tf_op jit(solution)/shard_map/ppermute | solution.py:24
  72.5 11.7 %collective-permute-start.18 = (bf16[512,256]{1,0:T(8,128)(2,1)S(1)}, bf16[512,256]{1,0:T(8,128)(2,1)S(1)}, u32[]{:S(2)}, u32[]{:S(2)}) collective-permute-start(bf16[512,256]{1,0:T(8,128)(2,1)S(1)} %get-tuple-element.65), channel_id=1, source_target_pairs={{0,64},{64,0},{1,65},{65,1},{2,66},{66,2},{3,67},{67,3},{4,68},{68... | collective-permute-start | bytes 786440 | tf_op jit(solution)/shard_map/ppermute | solution.py:24
  80.8 4.3 %collective-permute-start.19 = (bf16[512,256]{1,0:T(8,128)(2,1)S(1)}, bf16[512,256]{1,0:T(8,128)(2,1)S(1)}, u32[]{:S(2)}, u32[]{:S(2)}) collective-permute-start(bf16[512,256]{1,0:T(8,128)(2,1)S(1)} %fusion.1.feat), channel_id=1, source_target_pairs={{0,64},{64,0},{1,65},{65,1},{2,66},{66,2},{3,67},{67,3},{4,68},{68... | collective-permute-start | bytes 786440 | tf_op jit(solution)/shard_map/ppermute | solution.py:24
  85.2 4.2 %collective-permute-start.20 = (bf16[256,256]{1,0:T(8,128)(2,1)S(1)}, bf16[256,256]{1,0:T(8,128)(2,1)S(1)}, u32[]{:S(2)}, u32[]{:S(2)}) collective-permute-start(bf16[256,256]{1,0:T(8,128)(2,1)S(1)} %get-tuple-element.92), channel_id=1, source_target_pairs={{0,16},{1,17},{2,18},{3,19},{16,0},{17,1},{18,2},{19,3},{32,48},{3... | collective-permute-start | bytes 393224 | tf_op jit(solution)/shard_map/ppermute | solution.py:42
  85.3 5.7 %collective-permute-start.21 = (bf16[256,256]{1,0:T(8,128)(2,1)S(1)}, bf16[256,256]{1,0:T(8,128)(2,1)S(1)}, u32[]{:S(2)}, u32[]{:S(2)}) collective-permute-start(bf16[256,256]{1,0:T(8,128)(2,1)S(1)} %get-tuple-element.93), channel_id=1, source_target_pairs={{0,32},{1,33},{2,34},{3,35},{16,48},{17,49},{18,50},{19,51},{32,0}... | collective-permute-start | bytes 393224 | tf_op jit(solution)/shard_map/ppermute | solution.py:42
  86.2 6.1 %collective-permute-start.22 = (bf16[256,256]{1,0:T(8,128)(2,1)S(1)}, bf16[256,256]{1,0:T(8,128)(2,1)S(1)}, u32[]{:S(2)}, u32[]{:S(2)}) collective-permute-start(bf16[256,256]{1,0:T(8,128)(2,1)S(1)} %get-tuple-element.94), channel_id=1, source_target_pairs={{0,48},{1,49},{2,50},{3,51},{16,32},{17,33},{18,34},{19,35},{32,16... | collective-permute-start | bytes 393224 | tf_op jit(solution)/shard_map/ppermute | solution.py:42
  92.5 8.0 %collective-permute-start.23 = (bf16[128,256]{1,0:T(8,128)(2,1)S(1)}, bf16[128,256]{1,0:T(8,128)(2,1)S(1)}, u32[]{:S(2)}, u32[]{:S(2)}) collective-permute-start(bf16[128,256]{1,0:T(8,128)(2,1)S(1)} %split.53), channel_id=1, source_target_pairs={{0,8},{4,12},{8,0},{12,4},{1,9},{5,13},{9,1},{13,5},{2,10},{6,14},... | collective-permute-start | bytes 196616 | tf_op jit(solution)/shard_map/ppermute | solution.py:32
  100.4 4.4 %collective-permute-start.24 = (bf16[64,256]{1,0:T(8,128)(2,1)S(1)}, bf16[64,256]{1,0:T(8,128)(2,1)S(1)}, u32[]{:S(2)}, u32[]{:S(2)}) collective-permute-start(bf16[64,256]{1,0:T(8,128)(2,1)S(1)} %split.55), channel_id=1, source_target_pairs={{0,4},{4,0},{8,12},{12,8},{1,5},{5,1},{9,13},{13,9},{2,6},{6,2},{1... | collective-permute-start | bytes 98312 | tf_op jit(solution)/shard_map/ppermute | solution.py:32
  109.0 7.2 %collective-permute-start.26 = (bf16[128,256]{1,0:T(8,128)(2,1)S(1)}, bf16[128,256]{1,0:T(8,128)(2,1)S(1)}, u32[]{:S(2)}, u32[]{:S(2)}) collective-permute-start(bf16[128,256]{1,0:T(8,128)(2,1)S(1)} %pad_maximum_fusion.2), channel_id=1, source_target_pairs={{0,8},{4,12},{8,0},{12,4},{1,9},{5,13},{9,1},{13,5},{2,10},{6,14},... | collective-permute-start | bytes 196616 | tf_op jit(solution)/shard_map/ppermute | solution.py:32
  116.2 4.2 %collective-permute-start.27 = (bf16[256,256]{1,0:T(8,128)(2,1)S(1)}, bf16[256,256]{1,0:T(8,128)(2,1)S(1)}, u32[]{:S(2)}, u32[]{:S(2)}) collective-permute-start(bf16[256,256]{1,0:T(8,128)(2,1)S(1)} %pad_maximum_fusion), channel_id=1, source_target_pairs={{0,16},{1,17},{2,18},{3,19},{16,0},{17,1},{18,2},{19,3},{32,48},{3... | collective-permute-start | bytes 393224 | tf_op jit(solution)/shard_map/ppermute | solution.py:42
  116.8 7.6 %collective-permute-start.29 = (bf16[256,256]{1,0:T(8,128)(2,1)S(1)}, bf16[256,256]{1,0:T(8,128)(2,1)S(1)}, u32[]{:S(2)}, u32[]{:S(2)}) collective-permute-start(bf16[256,256]{1,0:T(8,128)(2,1)S(1)} %pad_maximum_fusion), channel_id=1, source_target_pairs={{0,48},{1,49},{2,50},{3,51},{16,32},{17,33},{18,34},{19,35},{32,16... | collective-permute-start | bytes 393224 | tf_op jit(solution)/shard_map/ppermute | solution.py:42
  119.0 5.3 %collective-permute-start.28 = (bf16[256,256]{1,0:T(8,128)(2,1)S(1)}, bf16[256,256]{1,0:T(8,128)(2,1)S(1)}, u32[]{:S(2)}, u32[]{:S(2)}) collective-permute-start(bf16[256,256]{1,0:T(8,128)(2,1)S(1)} %pad_maximum_fusion), channel_id=1, source_target_pairs={{0,32},{1,33},{2,34},{3,35},{16,48},{17,49},{18,50},{19,51},{32,0}... | collective-permute-start | bytes 393224 | tf_op jit(solution)/shard_map/ppermute | solution.py:42
  124.4 17.2 %collective-permute-start.32 = (bf16[1024,256]{1,0:T(8,128)(2,1)S(1)}, bf16[1024,256]{1,0:T(8,128)(2,1)S(1)}, u32[]{:S(2)}, u32[]{:S(2)}) collective-permute-start(bf16[1024,256]{1,0:T(8,128)(2,1)S(1)} %constant_dynamic-update-slice_fusion.9.p0), channel_id=1, source_target_pairs={{0,3},{1,2},{2,1},{3,0},{16,19},{17,18},{18,17},{19,16},{32,35},{3... | collective-permute-start | bytes 1572872 | tf_op jit(solution)/shard_map/ppermute | solution.py:42
  124.5 17.1 %collective-permute-start.31 = (bf16[1024,256]{1,0:T(8,128)(2,1)S(1)}, bf16[1024,256]{1,0:T(8,128)(2,1)S(1)}, u32[]{:S(2)}, u32[]{:S(2)}) collective-permute-start(bf16[1024,256]{1,0:T(8,128)(2,1)S(1)} %constant_dynamic-update-slice_fusion.9.p0), channel_id=1, source_target_pairs={{0,2},{1,3},{2,0},{3,1},{16,18},{17,19},{18,16},{19,17},{32,34},{3... | collective-permute-start | bytes 1572872 | tf_op jit(solution)/shard_map/ppermute | solution.py:42
  124.8 16.7 %collective-permute-start.30 = (bf16[1024,256]{1,0:T(8,128)(2,1)S(1)}, bf16[1024,256]{1,0:T(8,128)(2,1)S(1)}, u32[]{:S(2)}, u32[]{:S(2)}) collective-permute-start(bf16[1024,256]{1,0:T(8,128)(2,1)S(1)} %constant_dynamic-update-slice_fusion.9.p0), channel_id=1, source_target_pairs={{0,1},{1,0},{2,3},{3,2},{16,17},{17,16},{18,19},{19,18},{32,33},{3... | collective-permute-start | bytes 1572872 | tf_op jit(solution)/shard_map/ppermute | solution.py:42
  142.8 5.8 %collective-permute-start.33 = (bf16[512,256]{1,0:T(8,128)(2,1)S(1)}, bf16[512,256]{1,0:T(8,128)(2,1)S(1)}, u32[]{:S(2)}, u32[]{:S(2)}) collective-permute-start(bf16[512,256]{1,0:T(8,128)(2,1)S(1)} %shard_map.117), channel_id=1, source_target_pairs={{0,128},{128,0},{1,129},{129,1},{2,130},{130,2},{3,131},{131,3},{4... | collective-permute-start | bytes 786440 | tf_op jit(solution)/shard_map/ppermute | solution.py:28
  149.0 15.7 %collective-permute-start.34 = (bf16[512,256]{1,0:T(8,128)(2,1)S(1)}, bf16[512,256]{1,0:T(8,128)(2,1)S(1)}, u32[]{:S(2)}, u32[]{:S(2)}) collective-permute-start(bf16[512,256]{1,0:T(8,128)(2,1)S(1)} %get-tuple-element.85.grad), channel_id=1, source_target_pairs={{0,64},{64,0},{1,65},{65,1},{2,66},{66,2},{3,67},{67,3},{4,68},{68... | collective-permute-start | bytes 786440 | tf_op jit(solution)/shard_map/ppermute | solution.py:24
  163.0 5.3 %collective-permute-start.35 = (bf16[2048,256]{1,0:T(8,128)(2,1)S(1)}, bf16[2048,256]{1,0:T(8,128)(2,1)S(1)}, u32[]{:S(2)}, u32[]{:S(2)}) collective-permute-start(bf16[2048,256]{1,0:T(8,128)(2,1)S(1)} %get-tuple-element.82), channel_id=1, source_target_pairs={{0,64},{64,0},{1,65},{65,1},{2,66},{66,2},{3,67},{67,3},{4,68},{68... | collective-permute-start | bytes 3145736 | tf_op jit(solution)/shard_map/ppermute | solution.py:24
  (10 other events, 74.9 us)

commit v4 on v3

--- a/solution.py
+++ b/solution.py
@@ -12,6 +12,12 @@
 AXES = ("z_lo", "core", "x", "z_hi", "y")
 LATENT = ("x", "z_hi", "y")
 PLANE = ("core", "x", "y")
+SPACE = ("core", "x", "z_hi", "y")
+GROUPS = [
+    [((c * 4 + (i if c == 0 else j)) * 4 + z) * 4 + (j if c == 0 else i) for i in range(4) for z in range(4)]
+    for c in range(2)
+    for j in range(4)
+]
 ORDER = (2, 1, 3)
 BLOCK = 32
 
@@ -28,63 +34,48 @@
     return lax.ppermute(x, "z_lo", [(0, 1), (1, 0)])
 
 
-def along_z(x, k):
-    return lax.ppermute(x, "z_hi", [(i, i ^ k) for i in range(4)])
-
-
-def in_plane(x, k, x_core):
+def among_sixteen(x):
+    return lax.all_to_all(x, SPACE, 0, 0, axis_index_groups=GROUPS, tiled=True)
+
+
+def along_last(x, k):
     pairs = []
     for c in range(2):
         for i in range(4):
             for j in range(4):
-                a, b = (i ^ k, j) if c == x_core else (i, j ^ k)
+                a, b = (i, j ^ k) if c == 0 else (i ^ k, j)
                 pairs.append((c * 16 + i * 4 + j, c * 16 + a * 4 + b))
     return lax.ppermute(x, PLANE, pairs)
 
 
-def first(x, k):
-    return in_plane(x, k, 0)
-
-
-def second(x, k):
-    return in_plane(x, k, 1)
-
-
-def received(pieces, send):
-    got = {k: send(pieces[k], k) for k in ORDER}
+def received(pieces):
+    got = {k: along_last(pieces[k], k) for k in ORDER}
     return [pieces[0], got[1], got[2], got[3]]
 
 
 def gathered(x):
-    for k in (1, 2):
-        x = jnp.concatenate([x, along_z(x, k)], axis=0)
-    x = jnp.concatenate(received([x] * 4, first), axis=0)
-    return received([x] * 4, second)
+    x = among_sixteen(jnp.broadcast_to(x[None], (16, *x.shape)))
+    return received([x.reshape(-1, x.shape[-1])] * 4)
 
 
 def summed(pieces):
     return sum(p.astype(jnp.float32) for p in pieces)
 
 
-def scattered(pieces, beside):
-    pieces, beside = lax.optimization_barrier((pieces, beside))
-    total = summed(received(pieces, second))
-    total, swapped = lax.optimization_barrier((total, [other_core(b) for b in beside]))
-    total = summed(received(jnp.split(total.astype(jnp.bfloat16), 4, axis=0), first))
-    for k in (2, 1):
-        kept, sent = jnp.split(total.astype(jnp.bfloat16), 2, axis=0)
-        total = summed([kept, along_z(sent, k)])
-    return total, swapped
+def scattered(pieces):
+    total = summed(received(pieces)).astype(jnp.bfloat16)
+    blocks = among_sixteen(total.reshape(16, -1, total.shape[-1]))
+    return jnp.sum(blocks.astype(jnp.float32), axis=0)
 
 
 def block_rows():
     c = lax.axis_index("core")
-    x, z, y = (lax.axis_index(a) for a in LATENT)
+    x, y = lax.axis_index("x"), lax.axis_index("y")
     k = np.arange(64)
-    far, near, up = k // 16, (k // 4) % 4, k % 4
-    bx = jnp.where(c == 0, near ^ x, far ^ x)
-    by = jnp.where(c == 0, far ^ y, near ^ y)
-    return (BLOCK * (bx * 16 + (up ^ z) * 4 + by)).astype(jnp.int32)
+    last, near, up = k // 16, (k // 4) % 4, k % 4
+    bx = jnp.where(c == 0, near, last ^ x)
+    by = jnp.where(c == 0, last ^ y, near)
+    return (BLOCK * (bx * 16 + up * 4 + by)).astype(jnp.int32)
 
 
 def relative_enc_kernel(rows, own, other, out, blocks):
@@ -254,32 +245,38 @@
     )(feat, err, feat_b, err_b)
 
 
-def outer_enc_kernel(acts, grad, grad_b, *rest):
-    acts_b, out = rest[:-1], rest[-1]
-    own = dot_nt(acts[...], grad[...])
-    for j, part in enumerate(acts_b):
-
-        @pl.when(pl.program_id(0) == j)
-        def _():
-            out[...] = (own + dot_nt(part[...], grad_b[...])).astype(out.dtype)
+def outer_enc_kernel(acts, grad, acts_b, grad_b, out, sums):
+    out[...] = (dot_nt(acts[...], grad[...]) + dot_nt(acts_b[...], grad_b[...])).astype(out.dtype)
+
+    @pl.when(pl.program_id(0) == 0)
+    def _():
+        ones = jnp.ones((8, grad.shape[1]), grad.dtype)
+        sums[...] = (dot_nt(ones, grad[...]) + dot_nt(ones, grad_b[...]))[:1]
 
 
 def outer_enc(acts, grad, acts_b, grad_b):
     m, tokens = acts.shape
     n = grad.shape[0]
-    tile = m // len(acts_b)
+    tile = m // 4
     rows = pl.BlockSpec((tile, tokens), lambda i: (i, 0))
+    whole = pl.BlockSpec((n, tokens), lambda i: (0, 0))
     return pl.pallas_call(
         outer_enc_kernel,
-        out_shape=jax.ShapeDtypeStruct((m, n), jnp.bfloat16),
-        grid=(len(acts_b),),
-        in_specs=[rows] + [VMEM] * (2 + len(acts_b)),
-        out_specs=pl.BlockSpec((tile, n), lambda i: (i, 0)),
+        out_shape=(
+            jax.ShapeDtypeStruct((m, n), jnp.bfloat16),
+            jax.ShapeDtypeStruct((1, n), jnp.float32),
+        ),
+        grid=(4,),
+        in_specs=[rows, whole, rows, whole],
+        out_specs=(
+            pl.BlockSpec((tile, n), lambda i: (i, 0)),
+            pl.BlockSpec((1, n), lambda i: (0, 0)),
+        ),
         compiler_params=PARAMS,
         cost_estimate=pl.CostEstimate(
             flops=40 * m * n * tokens, bytes_accessed=5 << 20, transcendentals=0
         ),
-    )(acts, grad, grad_b, *acts_b)
+    )(acts, grad, acts_b, grad_b)
 
 
 def body(acts, w_enc, b_enc, w_dec, b_dec):
@@ -290,15 +287,13 @@
     rows = block_rows()
 
     local = acts[0].T
-    bias = jnp.broadcast_to(b_dec[0][:, None], (local.shape[0], 128))
-    mine = lax.dynamic_slice_in_dim(local, core * half, half, 1)
-    theirs = lax.dynamic_slice_in_dim(local, (1 - core) * half, half, 1)
-    swapped = other_core(jnp.concatenate([theirs, bias], axis=1))
-    start = jnp.concatenate([mine, swapped[:, :half]], axis=0)
-    bias_both = jnp.concatenate([bias[:, :1], swapped[:, half : half + 1]], axis=0)
-
-    start, enc, dec = lax.optimization_barrier((start, w_enc[0], w_dec[0]))
-    enc_other, dec_other = other_core(enc), other_core(dec)
+    swapped = other_core(local)
+    start = jnp.concatenate(
+        [lax.dynamic_slice_in_dim(a, core * half, half, 1) for a in (local, swapped)], axis=0
+    )
+
+    start, enc, dec, bias = lax.optimization_barrier((start, w_enc[0], w_dec[0], b_dec))
+    enc_other, dec_other, bias_other = other_core(enc), other_core(dec), other_core(bias)
     enc_r = relative_enc(rows, enc, enc_other)
     dec_r = relative_dec(rows, dec, dec_other)
     acts_p = gathered(start)
@@ -308,31 +303,31 @@
     part, acts_p = lax.optimization_barrier((part, acts_p))
     part_b = other_layer(part)
     acts_own, acts_other = placed(rows, acts_p)
+    acts_b = other_core(acts_other)
+    part_b, acts_b = lax.optimization_barrier((part_b, acts_b))
     pre = part.astype(jnp.float32) + part_b.astype(jnp.float32) + b_enc[:, None]
     feat = (jax.nn.softplus(4.0 * pre) / 4.0).astype(jnp.bfloat16)
 
-    recon, (*acts_b, feat_b) = scattered(blocked_dot(dec_r, feat), [*jnp.split(acts_other, 4), feat])
+    recon = scattered(blocked_dot(dec_r, feat))
+    bias_both = jnp.concatenate([bias[0], bias_other[0]])[:, None]
     err = (recon + bias_both.astype(jnp.float32) - start.astype(jnp.float32)).astype(jnp.bfloat16)
 
     err_p = gathered(err)
     term = gathered_dot(dec_rt, err_p)
-    term, err_p, err = lax.optimization_barrier((term, err_p, err))
+    term, err_p, feat, err = lax.optimization_barrier((term, err_p, feat, err))
     term_b = other_layer(term)
     err_own, err_other = placed(rows, err_p)
-    term_b, err_own, err_other = lax.optimization_barrier((term_b, err_own, err_other))
-    err_b = other_core(err_other)
+    err_b, feat_b = other_core(err_other), other_core(feat)
     sums = jnp.sum(err.astype(jnp.float32), axis=1)
     width = sums.shape[0] // 2
     grad_bdec = scale * (sums[:width] + other_core(sums[width:]))
     grad_dec = outer_dec(feat, err_own, feat_b, err_b, scale)
+    term_b, grad_dec, grad_bdec = lax.optimization_barrier((term_b, grad_dec, grad_bdec))
 
     grad_feat = scale * (term.astype(jnp.float32) + term_b.astype(jnp.float32))
-    grad_pre = grad_feat * jax.nn.sigmoid(4.0 * pre)
-    grad_pre_b = grad_pre.astype(jnp.bfloat16)
-    grad_pre_o = other_core(grad_pre_b)
-    part_benc = jnp.sum(grad_pre, axis=1)
-    grad_benc = part_benc + other_core(part_benc)
-    grad_enc = outer_enc(acts_own, grad_pre_b, acts_b, grad_pre_o)
+    grad_pre = (grad_feat * jax.nn.sigmoid(4.0 * pre)).astype(jnp.bfloat16)
+    grad_enc, grad_benc = outer_enc(acts_own, grad_pre, acts_b, other_core(grad_pre))
+    grad_benc = grad_benc[0]
     return (grad_enc[None], grad_dec[None], grad_benc, grad_bdec[None])
 
 

time: 172 us -> 163 us (0.948)
  starting transfers between devices: 92.9 us -> 37.7 us
  waiting for transfers between devices: 51.3 us -> 74.5 us
  blocking collectives: 0 us -> 21.3 us
  local copies, waits for them, and re-layouts: 3.69 us -> 5.49 us
    ppermute x12 -> x9, starting transfers between devices: 46.4 us -> 13.2 us  [other_core(): return lax.ppermute(x, 'core', [(0, 1), (1, 0)])]
    ppermute x24 -> x9, starting transfers between devices: 44.6 us -> 11.6 us  [along_last(): return lax.ppermute(x, PLANE, pairs)]
    all_to_all x0 -> x2, waiting for transfers between devices: none -> 32.1 us  [among_sixteen(): return lax.all_to_all(x, SPACE, 0, 0, axis_index_groups=GROUPS, tiled=True)]
    all_to_all x0 -> x1, blocking collectives: none -> 21.3 us  [among_sixteen(): return lax.all_to_all(x, SPACE, 0, 0, axis_index_groups=GROUPS, tiled=True)]
    ppermute x24 -> x9, waiting for transfers between devices: 44.4 us -> 31.1 us  [along_last(): return lax.ppermute(x, PLANE, pairs)]
    all_to_all x0 -> x2, starting transfers between devices: none -> 12.8 us  [among_sixteen(): return lax.all_to_all(x, SPACE, 0, 0, axis_index_groups=GROUPS, tiled=True)]
    ppermute x2, waiting for transfers between devices: 4.69 us -> 7.07 us  [other_layer(): return lax.ppermute(x, 'z_lo', [(0, 1), (1, 0)])]
    ppermute x12 -> x9, waiting for transfers between devices: 2.24 us -> 4.24 us  [other_core(): return lax.ppermute(x, 'core', [(0, 1), (1, 0)])]
  transfers between devices with their start and end apart: 38 -> 22, of which waited for: 21 -> 15; matrix products, arithmetic and copies ran while one was open for 1% -> 2% of each run, Pallas kernels for 8% -> 8%
where the time goes in v4:
time: 163 us; the launch traced here: 162 us
  waiting for transfers between devices  74.5 us (46%)
  starting transfers between devices  37.7 us (23%)
  blocking collectives  21.3 us (13%)
  Pallas kernels  19 us (12%)
  local copies, waits for them, and re-layouts  5.49 us (3%)
  other arithmetic  3.33 us (2%)
    all_to_all x2, waiting for transfers between devices, among_sixteen(): return lax.all_to_all(x, SPACE, 0, 0, axis_index_groups=GROUPS, tiled=True)  32.1 us
    ppermute x9, waiting for transfers between devices, along_last(): return lax.ppermute(x, PLANE, pairs)  31.1 us
    all_to_all x1, blocking collectives, among_sixteen(): return lax.all_to_all(x, SPACE, 0, 0, axis_index_groups=GROUPS, tiled=True)  21.3 us
    ppermute x9, starting transfers between devices, other_core(): return lax.ppermute(x, 'core', [(0, 1), (1, 0)])  13.2 us
    all_to_all x2, starting transfers between devices, among_sixteen(): return lax.all_to_all(x, SPACE, 0, 0, axis_index_groups=GROUPS, tiled=True)  12.8 us
    ppermute x9, starting transfers between devices, along_last(): return lax.ppermute(x, PLANE, pairs)  11.6 us
    ppermute x2, waiting for transfers between devices, other_layer(): return lax.ppermute(x, 'z_lo', [(0, 1), (1, 0)])  7.07 us
    ppermute x9, waiting for transfers between devices, other_core(): return lax.ppermute(x, 'core', [(0, 1), (1, 0)])  4.24 us
  transfers between devices with their start and end apart: 22, of which 15 were waited for; matrix products, arithmetic and copies ran while one was open for 2% of the time, Pallas kernels for 8%

profile of v4, /device:TPU:1, one launch (start us, length us, event | category | flops | bytes accessed | tf_op | source)
XLA Modules:
  0.0 162.1 jit_solution(5623130330230801535)
XLA Ops:
  0.6 3.3 %collective-permute-start = (bf16[32,512]{1,0:T(8,128)(2,1)}, bf16[32,512]{1,0:T(8,128)(2,1)S(1)}, u32[]{:S(2)}, u32[]{:S(2)}) collective-permute-start(bf16[32,512]{1,0:T(8,128)(2,1)} %bitcast.32), channel_id=1, source_target_pairs={{0,64},{64,0},{1,65},{65,1},{2,66},{66,2},{3,67},{67,3},{4,68},{68... | collective-permute-start | bytes 98312 | tf_op jit(solution)/shard_map/ppermute | solution.py:30
  6.2 9.2 %all-to-all-start = ((bf16[16,64,256]{2,1,0:T(8,128)(2,1)}), bf16[16,64,256]{2,1,0:T(8,128)(2,1)S(1)}, u32[]{:S(2)}, u32[]{:S(2)}) async-start(bf16[16,64,256]{2,1,0:T(8,128)(2,1)} %broadcast_in_dim.10), calls=%async_computation | async-start | bytes 1048576 | tf_op jit(solution)/shard_map/all_to_all | solution.py:38
  15.8 16.6 %all-to-all-done = bf16[16,64,256]{2,1,0:T(8,128)(2,1)S(1)} async-done(((bf16[16,64,256]{2,1,0:T(8,128)(2,1)}), bf16[16,64,256]{2,1,0:T(8,128)(2,1)S(1)}, u32[]{:S(2)}, u32[]{:S(2)}) %all-to-all-start) | async-done | bytes 524320 | tf_op jit(solution)/shard_map/all_to_all | solution.py:38
  32.4 1.2 collective-permute-start.2
  33.6 2.6 %collective-permute-start.3 = (bf16[1024,256]{1,0:T(8,128)(2,1)S(1)}, bf16[1024,256]{1,0:T(8,128)(2,1)S(1)}, u32[]{:S(2)}, u32[]{:S(2)}) collective-permute-start(bf16[1024,256]{1,0:T(8,128)(2,1)S(1)} %bitcast.19), channel_id=1, source_target_pairs={{0,2},{1,3},{2,0},{3,1},{16,18},{17,19},{18,16},{19,17},{32,34},{3... | collective-permute-start | bytes 1572872 | tf_op jit(solution)/shard_map/ppermute | solution.py:48
  37.0 1.6 copy-done.2
  38.5 3.1 %shard_map.111.w = bf16[4,512,1024]{2,1,0:T(8,128)(2,1)S(1)} custom-call(s32[64]{0:T(128)S(1)} %fusion.5.rows, bf16[2048,512]{1,0:T(8,128)(2,1)S(1)} %bitcast.29, bf16[2048,512]{1,0:T(8,128)(2,1)} %collective-permute-done.1.other), custom_call_target="tpu_custom_call" | custom-call | flops 1048576 | bytes 16777216 | tf_op jit(solution)/shard_map/pallas_call | solution.py:93
  41.6 7.1 %collective-permute-done.3.p2 = bf16[1024,256]{1,0:T(8,128)(2,1)S(1)} collective-permute-done((bf16[1024,256]{1,0:T(8,128)(2,1)S(1)}, bf16[1024,256]{1,0:T(8,128)(2,1)S(1)}, u32[]{:S(2)}, u32[]{:S(2)}) %collective-permute-start.3) | collective-permute-done | bytes 524320 | tf_op jit(solution)/shard_map/ppermute | solution.py:48
  48.7 2.6 %collective-permute-done.4.p3 = bf16[1024,256]{1,0:T(8,128)(2,1)S(1)} collective-permute-done((bf16[1024,256]{1,0:T(8,128)(2,1)S(1)}, bf16[1024,256]{1,0:T(8,128)(2,1)S(1)}, u32[]{:S(2)}, u32[]{:S(2)}) %collective-permute-start.4) | collective-permute-done | bytes 524320 | tf_op jit(solution)/shard_map/ppermute | solution.py:48
  51.3 1.2 shard_map.112
  53.3 4.5 %collective-permute-start.7 = (bf16[2048,256]{1,0:T(8,128)(2,1)S(1)}, bf16[2048,256]{1,0:T(8,128)(2,1)S(1)}, u32[]{:S(2)}, u32[]{:S(2)}) collective-permute-start(bf16[2048,256]{1,0:T(8,128)(2,1)S(1)} %get-tuple-element.44), channel_id=1, source_target_pairs={{0,64},{64,0},{1,65},{65,1},{2,66},{66,2},{3,67},{67,3},{4,68},{68... | collective-permute-start | bytes 3145736 | tf_op jit(solution)/shard_map/ppermute | solution.py:30
  57.8 3.1 %shard_map.114.x.w = bf16[4,1024,512]{2,1,0:T(8,128)(2,1)S(1)} custom-call(s32[64]{0:T(128)S(1)} %fusion.5.rows, bf16[512,2048]{1,0:T(8,128)(2,1)S(1)} %bitcast.31, bf16[512,2048]{1,0:T(8,128)(2,1)} %collective-permute-done.5.other), custom_call_target="tpu_custom_call" | custom-call | flops 1048576 | bytes 16777216 | tf_op jit(solution)/shard_map/pallas_call | solution.py:123
  60.9 4.7 %collective-permute-done.6 = bf16[512,256]{1,0:T(8,128)(2,1)S(1)} collective-permute-done((bf16[512,256]{1,0:T(8,128)(2,1)S(1)}, bf16[512,256]{1,0:T(8,128)(2,1)S(1)}, u32[]{:S(2)}, u32[]{:S(2)}) %collective-permute-start.6) | collective-permute-done | bytes 262176 | tf_op jit(solution)/shard_map/ppermute | solution.py:34
  66.1 1.2 shard_map.116
  67.6 3.7 %collective-permute-start.9 = (bf16[1024,256]{1,0:T(8,128)(2,1)S(1)}, bf16[1024,256]{1,0:T(8,128)(2,1)S(1)}, u32[]{:S(2)}, u32[]{:S(2)}) collective-permute-start(bf16[1024,256]{1,0:T(8,128)(2,1)S(1)} %get-tuple-element.48), channel_id=1, source_target_pairs={{0,2},{1,3},{2,0},{3,1},{16,18},{17,19},{18,16},{19,17},{32,34},{3... | collective-permute-start | bytes 1572872 | tf_op jit(solution)/shard_map/ppermute | solution.py:48
  71.3 5.7 %collective-permute-done.10 = bf16[1024,256]{1,0:T(8,128)(2,1)S(1)} collective-permute-done((bf16[1024,256]{1,0:T(8,128)(2,1)S(1)}, bf16[1024,256]{1,0:T(8,128)(2,1)S(1)}, u32[]{:S(2)}, u32[]{:S(2)}) %collective-permute-start.10) | collective-permute-done | bytes 524320 | tf_op jit(solution)/shard_map/ppermute | solution.py:48
  77.0 6.8 %collective-permute-done.9 = bf16[1024,256]{1,0:T(8,128)(2,1)S(1)} collective-permute-done((bf16[1024,256]{1,0:T(8,128)(2,1)S(1)}, bf16[1024,256]{1,0:T(8,128)(2,1)S(1)}, u32[]{:S(2)}, u32[]{:S(2)}) %collective-permute-start.9) | collective-permute-done | bytes 524320 | tf_op jit(solution)/shard_map/ppermute | solution.py:48
  84.9 3.6 %all-to-all-start.1 = ((bf16[16,64,256]{2,1,0:T(8,128)(2,1)}), bf16[16,64,256]{2,1,0:T(8,128)(2,1)S(1)}, u32[]{:S(2)}, u32[]{:S(2)}) async-start(bf16[16,64,256]{2,1,0:T(8,128)(2,1)} %bitcast.7), calls=%async_computation.1 | async-start | bytes 1048576 | tf_op jit(solution)/shard_map/all_to_all | solution.py:38
  88.5 2.1 %collective-permute-start.11 = (bf16[1,32]{1,0:T(2,128)(2,1)S(1)}, bf16[1,32]{1,0:T(2,128)(2,1)S(1)}, u32[]{:S(2)}, u32[]{:S(2)}) collective-permute-start(bf16[1,32]{1,0:T(2,128)(2,1)S(1)} %copy-done.7), channel_id=1, source_target_pairs={{0,64},{64,0},{1,65},{65,1},{2,66},{66,2},{3,67},{67,3},{4,68},{68... | collective-permute-start | bytes 200 | tf_op jit(solution)/shard_map/ppermute | solution.py:30
  91.5 15.5 %all-to-all-done.1 = bf16[16,64,256]{2,1,0:T(8,128)(2,1)S(1)} async-done(((bf16[16,64,256]{2,1,0:T(8,128)(2,1)}), bf16[16,64,256]{2,1,0:T(8,128)(2,1)S(1)}, u32[]{:S(2)}, u32[]{:S(2)}) %all-to-all-start.1) | async-done | bytes 524320 | tf_op jit(solution)/shard_map/all_to_all | solution.py:38
  107.1 21.3 %all_to_all.15 = bf16[16,64,256]{2,1,0:T(8,128)(2,1)S(1)} all-to-all(bf16[16,64,256]{2,1,0:T(8,128)(2,1)S(1)} %broadcast_in_dim.11), channel_id=1, replica_groups={{0,4,8,12,16,20,24,28,32,36,40,44,48,52,56,60},{1,5,9,13,17,21,25,29,33..., dimensions={0} | all-to-all | bytes 1048576 | tf_op jit(solution)/shard_map/all_to_all | solution.py:38
  128.5 3.9 %collective-permute-start.14 = (bf16[1024,256]{1,0:T(8,128)(2,1)S(1)}, bf16[1024,256]{1,0:T(8,128)(2,1)S(1)}, u32[]{:S(2)}, u32[]{:S(2)}) collective-permute-start(bf16[1024,256]{1,0:T(8,128)(2,1)S(1)} %bitcast.25), channel_id=1, source_target_pairs={{0,3},{1,2},{2,1},{3,0},{16,19},{17,18},{18,17},{19,16},{32,35},{3... | collective-permute-start | bytes 1572872 | tf_op jit(solution)/shard_map/ppermute | solution.py:48
  132.3 2.2 %copy-done.1 = bf16[4,1024,512]{2,1,0:T(8,128)(2,1)S(1)} copy-done((bf16[4,1024,512]{2,1,0:T(8,128)(2,1)S(1)}, bf16[4,1024,512]{2,1,0:T(8,128)(2,1)}, u32[]{:S(2)}) %copy-start.1) | copy-done | bytes 4194328
  134.5 1.4 shard_map.115.w
  136.8 3.5 %collective-permute-done.13.p2 = bf16[1024,256]{1,0:T(8,128)(2,1)S(1)} collective-permute-done((bf16[1024,256]{1,0:T(8,128)(2,1)S(1)}, bf16[1024,256]{1,0:T(8,128)(2,1)S(1)}, u32[]{:S(2)}, u32[]{:S(2)}) %collective-permute-start.13) | collective-permute-done | bytes 524320 | tf_op jit(solution)/shard_map/ppermute | solution.py:48
  140.2 4.5 %collective-permute-done.14.p3 = bf16[1024,256]{1,0:T(8,128)(2,1)S(1)} collective-permute-done((bf16[1024,256]{1,0:T(8,128)(2,1)S(1)}, bf16[1024,256]{1,0:T(8,128)(2,1)S(1)}, u32[]{:S(2)}, u32[]{:S(2)}) %collective-permute-start.14) | collective-permute-done | bytes 524320 | tf_op jit(solution)/shard_map/ppermute | solution.py:48
  144.8 1.3 shard_map.117
  148.6 1.9 %collective-permute-done.18 = f32[32]{0:T(128)S(1)} collective-permute-done((f32[32]{0:T(128)S(1)}, f32[32]{0:T(128)S(1)}, u32[]{:S(2)}, u32[]{:S(2)}) %collective-permute-start.18) | collective-permute-done | bytes 160 | tf_op jit(solution)/shard_map/ppermute | solution.py:30
  151.0 3.0 %shard_map.119 = bf16[512,2048]{1,0:T(8,128)(2,1)} custom-call(bf16[512,256]{1,0:T(8,128)(2,1)S(1)} %fusion.1.feat, bf16[2048,256]{1,0:T(8,128)(2,1)S(1)} %get-tuple-element.57.err, bf16[512,256]{1,0:T(8,128)(2,1)S(1)} %collective-permute-done.16.feat_b, bf16[2048,256]{1,0:T(8,128)(2,1)S(1)} %collective-permute-done.17.err_b), custom_call_target="tpu_custom_call" | custom-call | flops 10737418240 | bytes 5242880 | tf_op jit(solution)/shard_map/pallas_call | solution.py:235
  154.1 2.4 %collective-permute-done.15 = bf16[512,256]{1,0:T(8,128)(2,1)S(1)} collective-permute-done((bf16[512,256]{1,0:T(8,128)(2,1)S(1)}, bf16[512,256]{1,0:T(8,128)(2,1)S(1)}, u32[]{:S(2)}, u32[]{:S(2)}) %collective-permute-start.15) | collective-permute-done | bytes 262176 | tf_op jit(solution)/shard_map/ppermute | solution.py:34
  157.7 1.2 collective-permute-done.19.grad_b
  158.9 3.2 %shard_map.120 = (bf16[2048,512]{1,0:T(8,128)(2,1)}, f32[1,512]{1,0:T(1,128)}) custom-call(bf16[2048,256]{1,0:T(8,128)(2,1)S(1)} %get-tuple-element.41.acts, bf16[512,256]{1,0:T(8,128)(2,1)S(1)} %multiply_convert_fusion.grad, bf16[2048,256]{1,0:T(8,128)(2,1)S(1)} %collective-permute-done.7.acts_b, bf16[512,256]{1,0:T(8,128)(2,1)S(1)} %collective-permute-done.19.grad_b), custom_call_target="tpu_custom_call" | custom-call | flops 10737418240 | bytes 5242880 | tf_op jit(solution)/shard_map/pallas_call | solution.py:263
  (54 shorter events, 12.1 us)
Async XLA Ops:
  0.6 4.4 %collective-permute-start = (bf16[32,512]{1,0:T(8,128)(2,1)}, bf16[32,512]{1,0:T(8,128)(2,1)S(1)}, u32[]{:S(2)}, u32[]{:S(2)}) collective-permute-start(bf16[32,512]{1,0:T(8,128)(2,1)} %bitcast.32), channel_id=1, source_target_pairs={{0,64},{64,0},{1,65},{65,1},{2,66},{66,2},{3,67},{67,3},{4,68},{68... | collective-permute-start | bytes 98312 | tf_op jit(solution)/shard_map/ppermute | solution.py:30
  5.0 31.9 %collective-permute-start.1 = (bf16[2048,512]{1,0:T(8,128)(2,1)}, bf16[2048,512]{1,0:T(8,128)(2,1)}, u32[]{:S(2)}, u32[]{:S(2)}) collective-permute-start(bf16[2048,512]{1,0:T(8,128)(2,1)} %bitcast.28), channel_id=1, source_target_pairs={{0,64},{64,0},{1,65},{65,1},{2,66},{66,2},{3,67},{67,3},{4,68},{68... | collective-permute-start | bytes 6291464 | tf_op jit(solution)/shard_map/ppermute | solution.py:30
  6.2 26.2 %all-to-all-start = ((bf16[16,64,256]{2,1,0:T(8,128)(2,1)}), bf16[16,64,256]{2,1,0:T(8,128)(2,1)S(1)}, u32[]{:S(2)}, u32[]{:S(2)}) async-start(bf16[16,64,256]{2,1,0:T(8,128)(2,1)} %broadcast_in_dim.10), calls=%async_computation | async-start | bytes 1048576 | tf_op jit(solution)/shard_map/all_to_all | solution.py:38
  15.4 42.4 %collective-permute-start.5 = (bf16[512,2048]{1,0:T(8,128)(2,1)}, bf16[512,2048]{1,0:T(8,128)(2,1)}, u32[]{:S(2)}, u32[]{:S(2)}) collective-permute-start(bf16[512,2048]{1,0:T(8,128)(2,1)} %bitcast.30), channel_id=1, source_target_pairs={{0,64},{64,0},{1,65},{65,1},{2,66},{66,2},{3,67},{67,3},{4,68},{68... | collective-permute-start | bytes 6291464 | tf_op jit(solution)/shard_map/ppermute | solution.py:30
  32.4 9.2 %collective-permute-start.2 = (bf16[1024,256]{1,0:T(8,128)(2,1)S(1)}, bf16[1024,256]{1,0:T(8,128)(2,1)S(1)}, u32[]{:S(2)}, u32[]{:S(2)}) collective-permute-start(bf16[1024,256]{1,0:T(8,128)(2,1)S(1)} %bitcast.18), channel_id=1, source_target_pairs={{0,1},{1,0},{2,3},{3,2},{16,17},{17,16},{18,19},{19,18},{32,33},{3... | collective-permute-start | bytes 1572872 | tf_op jit(solution)/shard_map/ppermute | solution.py:48
  33.6 15.1 %collective-permute-start.3 = (bf16[1024,256]{1,0:T(8,128)(2,1)S(1)}, bf16[1024,256]{1,0:T(8,128)(2,1)S(1)}, u32[]{:S(2)}, u32[]{:S(2)}) collective-permute-start(bf16[1024,256]{1,0:T(8,128)(2,1)S(1)} %bitcast.19), channel_id=1, source_target_pairs={{0,2},{1,3},{2,0},{3,1},{16,18},{17,19},{18,16},{19,17},{32,34},{3... | collective-permute-start | bytes 1572872 | tf_op jit(solution)/shard_map/ppermute | solution.py:48
  36.2 15.2 %collective-permute-start.4 = (bf16[1024,256]{1,0:T(8,128)(2,1)S(1)}, bf16[1024,256]{1,0:T(8,128)(2,1)S(1)}, u32[]{:S(2)}, u32[]{:S(2)}) collective-permute-start(bf16[1024,256]{1,0:T(8,128)(2,1)S(1)} %bitcast.20), channel_id=1, source_target_pairs={{0,3},{1,2},{2,1},{3,0},{16,19},{17,18},{18,17},{19,16},{32,35},{3... | collective-permute-start | bytes 1572872 | tf_op jit(solution)/shard_map/ppermute | solution.py:48
  36.9 1.6 copy-start.2
  52.6 5.2 %copy-start.3 = (bf16[1,512,2048]{2,1,0:T(8,128)(2,1)S(1)}, bf16[1,512,2048]{2,1,0:T(8,128)(2,1)}, u32[]{:S(2)}) copy-start(bf16[1,512,2048]{2,1,0:T(8,128)(2,1)} %param.11) | copy-start | bytes 6291460
  53.3 12.4 %copy-start.6 = (f32[512]{0:T(512)S(1)}, f32[512]{0:T(512)}, u32[]{:S(2)}) copy-start(f32[512]{0:T(512)} %param.10) | copy-start | bytes 6148
  53.3 12.4 %collective-permute-start.7 = (bf16[2048,256]{1,0:T(8,128)(2,1)S(1)}, bf16[2048,256]{1,0:T(8,128)(2,1)S(1)}, u32[]{:S(2)}, u32[]{:S(2)}) collective-permute-start(bf16[2048,256]{1,0:T(8,128)(2,1)S(1)} %get-tuple-element.44), channel_id=1, source_target_pairs={{0,64},{64,0},{1,65},{65,1},{2,66},{66,2},{3,67},{67,3},{4,68},{68... | collective-permute-start | bytes 3145736 | tf_op jit(solution)/shard_map/ppermute | solution.py:30
  57.8 7.9 %collective-permute-start.6 = (bf16[512,256]{1,0:T(8,128)(2,1)S(1)}, bf16[512,256]{1,0:T(8,128)(2,1)S(1)}, u32[]{:S(2)}, u32[]{:S(2)}) collective-permute-start(bf16[512,256]{1,0:T(8,128)(2,1)S(1)} %shard_map.112), channel_id=1, source_target_pairs={{0,128},{128,0},{1,129},{129,1},{2,130},{130,2},{3,131},{131,3},{4... | collective-permute-start | bytes 786440 | tf_op jit(solution)/shard_map/ppermute | solution.py:34
  60.9 6.4 %copy-start = (bf16[4,1024,512]{2,1,0:T(8,128)(2,1)}, bf16[4,1024,512]{2,1,0:T(8,128)(2,1)S(1)}, u32[]{:S(2)}) copy-start(bf16[4,1024,512]{2,1,0:T(8,128)(2,1)S(1)} %shard_map.114.x.w) | copy-start | bytes 12582916
  65.6 1.7 %copy-start.4 = (bf16[512,256]{1,0:T(8,128)(2,1)}, bf16[512,256]{1,0:T(8,128)(2,1)S(1)}, u32[]{:S(2)}) copy-start(bf16[512,256]{1,0:T(8,128)(2,1)S(1)} %collective-permute-done.6) | copy-start | bytes 786436
  67.4 21.1 %copy-start.7 = (bf16[1,32]{1,0:T(2,128)(2,1)S(1)}, bf16[1,32]{1,0:T(2,128)(2,1)}, u32[]{:S(2)}) copy-start(bf16[1,32]{1,0:T(2,128)(2,1)} %param.12) | copy-start | bytes 196
  67.4 9.6 %collective-permute-start.10 = (bf16[1024,256]{1,0:T(8,128)(2,1)S(1)}, bf16[1024,256]{1,0:T(8,128)(2,1)S(1)}, u32[]{:S(2)}, u32[]{:S(2)}) collective-permute-start(bf16[1024,256]{1,0:T(8,128)(2,1)S(1)} %get-tuple-element.49), channel_id=1, source_target_pairs={{0,3},{1,2},{2,1},{3,0},{16,19},{17,18},{18,17},{19,16},{32,35},{3... | collective-permute-start | bytes 1572872 | tf_op jit(solution)/shard_map/ppermute | solution.py:48
  67.5 9.5 %collective-permute-start.8 = (bf16[1024,256]{1,0:T(8,128)(2,1)S(1)}, bf16[1024,256]{1,0:T(8,128)(2,1)S(1)}, u32[]{:S(2)}, u32[]{:S(2)}) collective-permute-start(bf16[1024,256]{1,0:T(8,128)(2,1)S(1)} %get-tuple-element.47), channel_id=1, source_target_pairs={{0,1},{1,0},{2,3},{3,2},{16,17},{17,16},{18,19},{19,18},{32,33},{3... | collective-permute-start | bytes 1572872 | tf_op jit(solution)/shard_map/ppermute | solution.py:48
  67.6 16.2 %collective-permute-start.9 = (bf16[1024,256]{1,0:T(8,128)(2,1)S(1)}, bf16[1024,256]{1,0:T(8,128)(2,1)S(1)}, u32[]{:S(2)}, u32[]{:S(2)}) collective-permute-start(bf16[1024,256]{1,0:T(8,128)(2,1)S(1)} %get-tuple-element.48), channel_id=1, source_target_pairs={{0,2},{1,3},{2,0},{3,1},{16,18},{17,19},{18,16},{19,17},{32,34},{3... | collective-permute-start | bytes 1572872 | tf_op jit(solution)/shard_map/ppermute | solution.py:48
  84.9 22.1 %all-to-all-start.1 = ((bf16[16,64,256]{2,1,0:T(8,128)(2,1)}), bf16[16,64,256]{2,1,0:T(8,128)(2,1)S(1)}, u32[]{:S(2)}, u32[]{:S(2)}) async-start(bf16[16,64,256]{2,1,0:T(8,128)(2,1)} %bitcast.7), calls=%async_computation.1 | async-start | bytes 1048576 | tf_op jit(solution)/shard_map/all_to_all | solution.py:38
  88.5 2.9 %collective-permute-start.11 = (bf16[1,32]{1,0:T(2,128)(2,1)S(1)}, bf16[1,32]{1,0:T(2,128)(2,1)S(1)}, u32[]{:S(2)}, u32[]{:S(2)}) collective-permute-start(bf16[1,32]{1,0:T(2,128)(2,1)S(1)} %copy-done.7), channel_id=1, source_target_pairs={{0,64},{64,0},{1,65},{65,1},{2,66},{66,2},{3,67},{67,3},{4,68},{68... | collective-permute-start | bytes 200 | tf_op jit(solution)/shard_map/ppermute | solution.py:30
  128.4 8.3 %collective-permute-start.12 = (bf16[1024,256]{1,0:T(8,128)(2,1)S(1)}, bf16[1024,256]{1,0:T(8,128)(2,1)S(1)}, u32[]{:S(2)}, u32[]{:S(2)}) collective-permute-start(bf16[1024,256]{1,0:T(8,128)(2,1)S(1)} %bitcast.23), channel_id=1, source_target_pairs={{0,1},{1,0},{2,3},{3,2},{16,17},{17,16},{18,19},{19,18},{32,33},{3... | collective-permute-start | bytes 1572872 | tf_op jit(solution)/shard_map/ppermute | solution.py:48
  128.5 11.8 %collective-permute-start.13 = (bf16[1024,256]{1,0:T(8,128)(2,1)S(1)}, bf16[1024,256]{1,0:T(8,128)(2,1)S(1)}, u32[]{:S(2)}, u32[]{:S(2)}) collective-permute-start(bf16[1024,256]{1,0:T(8,128)(2,1)S(1)} %bitcast.24), channel_id=1, source_target_pairs={{0,2},{1,3},{2,0},{3,1},{16,18},{17,19},{18,16},{19,17},{32,34},{3... | collective-permute-start | bytes 1572872 | tf_op jit(solution)/shard_map/ppermute | solution.py:48
  128.5 16.3 %collective-permute-start.14 = (bf16[1024,256]{1,0:T(8,128)(2,1)S(1)}, bf16[1024,256]{1,0:T(8,128)(2,1)S(1)}, u32[]{:S(2)}, u32[]{:S(2)}) collective-permute-start(bf16[1024,256]{1,0:T(8,128)(2,1)S(1)} %bitcast.25), channel_id=1, source_target_pairs={{0,3},{1,2},{2,1},{3,0},{16,19},{17,18},{18,17},{19,16},{32,35},{3... | collective-permute-start | bytes 1572872 | tf_op jit(solution)/shard_map/ppermute | solution.py:48
  132.3 2.2 %copy-start.1 = (bf16[4,1024,512]{2,1,0:T(8,128)(2,1)S(1)}, bf16[4,1024,512]{2,1,0:T(8,128)(2,1)}, u32[]{:S(2)}) copy-start(bf16[4,1024,512]{2,1,0:T(8,128)(2,1)} %copy-done) | copy-start | bytes 12582916
  146.7 4.3 %collective-permute-start.17 = (bf16[2048,256]{1,0:T(8,128)(2,1)S(1)}, bf16[2048,256]{1,0:T(8,128)(2,1)S(1)}, u32[]{:S(2)}, u32[]{:S(2)}) collective-permute-start(bf16[2048,256]{1,0:T(8,128)(2,1)S(1)} %get-tuple-element.58), channel_id=1, source_target_pairs={{0,64},{64,0},{1,65},{65,1},{2,66},{66,2},{3,67},{67,3},{4,68},{68... | collective-permute-start | bytes 3145736 | tf_op jit(solution)/shard_map/ppermute | solution.py:30
  147.9 3.2 %collective-permute-start.16 = (bf16[512,256]{1,0:T(8,128)(2,1)S(1)}, bf16[512,256]{1,0:T(8,128)(2,1)S(1)}, u32[]{:S(2)}, u32[]{:S(2)}) collective-permute-start(bf16[512,256]{1,0:T(8,128)(2,1)S(1)} %fusion.1.feat), channel_id=1, source_target_pairs={{0,64},{64,0},{1,65},{65,1},{2,66},{66,2},{3,67},{67,3},{4,68},{68... | collective-permute-start | bytes 786440 | tf_op jit(solution)/shard_map/ppermute | solution.py:30
  148.1 2.4 %collective-permute-start.18 = (f32[32]{0:T(128)S(1)}, f32[32]{0:T(128)S(1)}, u32[]{:S(2)}, u32[]{:S(2)}) collective-permute-start(f32[32]{0:T(128)S(1)} %slice.7), channel_id=1, source_target_pairs={{0,64},{64,0},{1,65},{65,1},{2,66},{66,2},{3,67},{67,3},{4,68},{68... | collective-permute-start | bytes 392 | tf_op jit(solution)/shard_map/ppermute | solution.py:30
  148.6 7.9 %collective-permute-start.15 = (bf16[512,256]{1,0:T(8,128)(2,1)S(1)}, bf16[512,256]{1,0:T(8,128)(2,1)S(1)}, u32[]{:S(2)}, u32[]{:S(2)}) collective-permute-start(bf16[512,256]{1,0:T(8,128)(2,1)S(1)} %shard_map.117), channel_id=1, source_target_pairs={{0,128},{128,0},{1,129},{129,1},{2,130},{130,2},{3,131},{131,3},{4... | collective-permute-start | bytes 786440 | tf_op jit(solution)/shard_map/ppermute | solution.py:34
  151.0 5.4 %copy-start.5 = (bf16[512,256]{1,0:T(8,128)(2,1)S(1)}, bf16[512,256]{1,0:T(8,128)(2,1)}, u32[]{:S(2)}) copy-start(bf16[512,256]{1,0:T(8,128)(2,1)} %copy-done.4) | copy-start | bytes 786436
  156.7 2.1 %collective-permute-start.19 = (bf16[512,256]{1,0:T(8,128)(2,1)S(1)}, bf16[512,256]{1,0:T(8,128)(2,1)S(1)}, u32[]{:S(2)}, u32[]{:S(2)}) collective-permute-start(bf16[512,256]{1,0:T(8,128)(2,1)S(1)} %multiply_convert_fusion.grad), channel_id=1, source_target_pairs={{0,64},{64,0},{1,65},{65,1},{2,66},{66,2},{3,67},{67,3},{4,68},{68... | collective-permute-start | bytes 786440 | tf_op jit(solution)/shard_map/ppermute | solution.py:30

commit v5 on v4

--- a/solution.py
+++ b/solution.py
@@ -24,6 +24,7 @@
 VMEM = pl.BlockSpec(memory_space=pltpu.VMEM)
 SMEM = pl.BlockSpec(memory_space=pltpu.SMEM)
 PARAMS = pltpu.CompilerParams(vmem_limit_bytes=16 * 1024 * 1024)
+SMALL = pltpu.CompilerParams(vmem_limit_bytes=6 * 1024 * 1024)
 
 
 def other_core(x):
@@ -38,14 +39,18 @@
     return lax.all_to_all(x, SPACE, 0, 0, axis_index_groups=GROUPS, tiled=True)
 
 
-def along_last(x, k):
+def in_plane(x, k, x_core):
     pairs = []
     for c in range(2):
         for i in range(4):
             for j in range(4):
-                a, b = (i, j ^ k) if c == 0 else (i ^ k, j)
+                a, b = (i ^ k, j) if c == x_core else (i, j ^ k)
                 pairs.append((c * 16 + i * 4 + j, c * 16 + a * 4 + b))
     return lax.ppermute(x, PLANE, pairs)
+
+
+def along_last(x, k):
+    return in_plane(x, k, 1)
 
 
 def received(pieces):
@@ -53,29 +58,55 @@
     return [pieces[0], got[1], got[2], got[3]]
 
 
+def along_z(x, k):
+    return lax.ppermute(x, "z_hi", [(i, i ^ k) for i in range(4)])
+
+
+def along_first(x, k):
+    return in_plane(x, k, 0)
+
+
+def in_two(x):
+    return [received([g] * 4) for g in jnp.split(x, 2, axis=1)]
+
+
 def gathered(x):
     x = among_sixteen(jnp.broadcast_to(x[None], (16, *x.shape)))
-    return received([x.reshape(-1, x.shape[-1])] * 4)
+    return in_two(x.reshape(-1, x.shape[-1]))
+
+
+def gathered_by_permutes(x):
+    for send in (along_z, along_first):
+        got = {k: send(x, k) for k in ORDER}
+        x = jnp.concatenate([x, got[1], got[2], got[3]], axis=0)
+    return in_two(x)
 
 
 def summed(pieces):
     return sum(p.astype(jnp.float32) for p in pieces)
 
 
-def scattered(pieces):
-    total = summed(received(pieces)).astype(jnp.bfloat16)
+def scattered(parts):
+    total = [summed(received(pieces)).astype(jnp.bfloat16) for pieces in parts]
+    total = jnp.concatenate(total, axis=1)
     blocks = among_sixteen(total.reshape(16, -1, total.shape[-1]))
     return jnp.sum(blocks.astype(jnp.float32), axis=0)
 
 
-def block_rows():
+def block_rows(relative):
     c = lax.axis_index("core")
-    x, y = lax.axis_index("x"), lax.axis_index("y")
+    x, z, y = (lax.axis_index(a) for a in LATENT)
     k = np.arange(64)
     last, near, up = k // 16, (k // 4) % 4, k % 4
-    bx = jnp.where(c == 0, near, last ^ x)
-    by = jnp.where(c == 0, last ^ y, near)
-    return (BLOCK * (bx * 16 + up * 4 + by)).astype(jnp.int32)
+    if relative:
+        bx = jnp.where(c == 0, near ^ x, last ^ x)
+        by = jnp.where(c == 0, last ^ y, near ^ y)
+        bz = up ^ z
+    else:
+        bx = jnp.where(c == 0, near, last ^ x)
+        by = jnp.where(c == 0, last ^ y, near)
+        bz = up
+    return (BLOCK * (bx * 16 + bz * 4 + by)).astype(jnp.int32)
 
 
 def relative_enc_kernel(rows, own, other, out, blocks):
@@ -165,55 +196,62 @@
         out_shape=jax.ShapeDtypeStruct((n, tokens), jnp.bfloat16),
         in_specs=[VMEM] * 5,
         out_specs=VMEM,
-        compiler_params=PARAMS,
+        compiler_params=SMALL,
         cost_estimate=pl.CostEstimate(
             flops=8 * n * depth * tokens, bytes_accessed=8 << 20, transcendentals=0
         ),
     )(w, *pieces)
 
 
-def blocked_dot_kernel(w, feat, *pieces):
-    for k, piece in enumerate(pieces):
-        piece[...] = jnp.dot(w[k], feat[...], preferred_element_type=jnp.float32).astype(
-            piece.dtype
+def blocked_dot_kernel(w, part, part_b, bias, feat, *pieces):
+    pre = part[...].astype(jnp.float32) + part_b[...].astype(jnp.float32) + bias[...]
+    feat[...] = (jax.nn.softplus(4.0 * pre) / 4.0).astype(feat.dtype)
+    for k in ORDER + (0,):
+        pieces[k][...] = jnp.dot(w[k], feat[...], preferred_element_type=jnp.float32).astype(
+            feat.dtype
         )
 
 
-def blocked_dot(w, feat):
+def blocked_dot(w, part, part_b, bias):
     _, width, n = w.shape
-    tokens = feat.shape[1]
+    tokens = part.shape[1]
     piece = jax.ShapeDtypeStruct((width, tokens), jnp.bfloat16)
-    return pl.pallas_call(
+    feat, *pieces = pl.pallas_call(
         blocked_dot_kernel,
-        out_shape=(piece,) * 4,
-        in_specs=[VMEM] * 2,
-        out_specs=(VMEM,) * 4,
-        compiler_params=PARAMS,
+        out_shape=(jax.ShapeDtypeStruct((n, tokens), jnp.bfloat16),) + (piece,) * 4,
+        in_specs=[VMEM] * 4,
+        out_specs=(VMEM,) * 5,
+        compiler_params=SMALL,
         cost_estimate=pl.CostEstimate(
-            flops=8 * n * width * tokens, bytes_accessed=7 << 20, transcendentals=0
-        ),
-    )(w, feat)
-
-
-def placed_kernel(rows, p0, p1, p2, p3, own, other):
+            flops=1 << 20, bytes_accessed=1 << 20, transcendentals=0
+        ),
+    )(w, part, part_b, bias)
+    return feat, pieces
+
+
+def placed_kernel(rows, *refs):
+    pieces, (own, other) = refs[:-2], refs[-2:]
+    tokens = pieces[0].shape[1]
     for k in range(64):
         at = pl.ds(pl.multiple_of(rows[k], BLOCK), BLOCK)
-        piece, src = (p0, p1, p2, p3)[k // 16], (k % 16) * 2 * BLOCK
-        own[at, :] = piece[src : src + BLOCK, :]
-        other[at, :] = piece[src + BLOCK : src + 2 * BLOCK, :]
-
-
-def placed(rows, pieces):
-    depth, tokens = pieces[0].shape
-    whole = jax.ShapeDtypeStruct((2 * depth, tokens), jnp.bfloat16)
+        src = (k % 16) * 2 * BLOCK
+        for half in range(2):
+            piece, to = pieces[half * 4 + k // 16], slice(half * tokens, (half + 1) * tokens)
+            own[at, to] = piece[src : src + BLOCK, :]
+            other[at, to] = piece[src + BLOCK : src + 2 * BLOCK, :]
+
+
+def placed(rows, parts):
+    depth, tokens = parts[0][0].shape
+    whole = jax.ShapeDtypeStruct((2 * depth, 2 * tokens), jnp.bfloat16)
     return pl.pallas_call(
         placed_kernel,
         out_shape=(whole, whole),
-        in_specs=[SMEM] + [VMEM] * 4,
+        in_specs=[SMEM] + [VMEM] * 8,
         out_specs=(VMEM,) * 2,
-        compiler_params=PARAMS,
+        compiler_params=SMALL,
         cost_estimate=pl.CostEstimate(flops=1 << 20, bytes_accessed=4 << 20, transcendentals=0),
-    )(rows, *pieces)
+    )(rows, *parts[0], *parts[1])
 
 
 def dot_nt(a, b):
@@ -240,7 +278,7 @@
         out_specs=pl.BlockSpec((m, tile), lambda i: (0, i)),
         compiler_params=PARAMS,
         cost_estimate=pl.CostEstimate(
-            flops=40 * m * n * tokens, bytes_accessed=5 << 20, transcendentals=0
+            flops=4 * m * n * tokens, bytes_accessed=5 << 20, transcendentals=0
         ),
     )(feat, err, feat_b, err_b)
 
@@ -284,7 +322,7 @@
     half = tokens_all // 2
     scale = tokens_all ** (-0.5)
     core = lax.axis_index("core")
-    rows = block_rows()
+    rows, acts_rows = block_rows(False), block_rows(True)
 
     local = acts[0].T
     swapped = other_core(local)
@@ -294,38 +332,51 @@
 
     start, enc, dec, bias = lax.optimization_barrier((start, w_enc[0], w_dec[0], b_dec))
     enc_other, dec_other, bias_other = other_core(enc), other_core(dec), other_core(bias)
-    enc_r = relative_enc(rows, enc, enc_other)
+    enc_r = relative_enc(acts_rows, enc, enc_other)
     dec_r = relative_dec(rows, dec, dec_other)
-    acts_p = gathered(start)
+    acts_p = gathered_by_permutes(start)
     dec_rt = turned(dec_r)
 
-    part = gathered_dot(enc_r, acts_p)
-    part, acts_p = lax.optimization_barrier((part, acts_p))
-    part_b = other_layer(part)
-    acts_own, acts_other = placed(rows, acts_p)
+    enc_r, dec_r = lax.optimization_barrier((enc_r, dec_r))
+    part = [gathered_dot(enc_r, pieces) for pieces in acts_p]
+    part_b = [other_layer(part[0]), None]
+    part_b[0], part[1], acts_p = lax.optimization_barrier((part_b[0], part[1], acts_p))
+    part_b[1] = other_layer(part[1])
+    acts_own, acts_other = placed(acts_rows, acts_p)
     acts_b = other_core(acts_other)
-    part_b, acts_b = lax.optimization_barrier((part_b, acts_b))
-    pre = part.astype(jnp.float32) + part_b.astype(jnp.float32) + b_enc[:, None]
-    feat = (jax.nn.softplus(4.0 * pre) / 4.0).astype(jnp.bfloat16)
-
-    recon = scattered(blocked_dot(dec_r, feat))
+    part_b[1], acts_b = lax.optimization_barrier((part_b[1], acts_b))
+    b_lanes = jnp.broadcast_to(b_enc[:, None], part[0].shape)
+    feats, recon = zip(*(blocked_dot(dec_r, p, q, b_lanes) for p, q in zip(part, part_b)))
+    recon = scattered(recon)
+    feat = jnp.concatenate(feats, axis=1)
     bias_both = jnp.concatenate([bias[0], bias_other[0]])[:, None]
     err = (recon + bias_both.astype(jnp.float32) - start.astype(jnp.float32)).astype(jnp.bfloat16)
 
     err_p = gathered(err)
-    term = gathered_dot(dec_rt, err_p)
-    term, err_p, feat, err = lax.optimization_barrier((term, err_p, feat, err))
-    term_b = other_layer(term)
+    term = [gathered_dot(dec_rt, pieces) for pieces in err_p]
+    term_b = [other_layer(term[0]), None]
+    term_b[0], term[1], err_p, feat, err = lax.optimization_barrier(
+        (term_b[0], term[1], err_p, feat, err)
+    )
+    term_b[1] = other_layer(term[1])
     err_own, err_other = placed(rows, err_p)
     err_b, feat_b = other_core(err_other), other_core(feat)
     sums = jnp.sum(err.astype(jnp.float32), axis=1)
     width = sums.shape[0] // 2
     grad_bdec = scale * (sums[:width] + other_core(sums[width:]))
     grad_dec = outer_dec(feat, err_own, feat_b, err_b, scale)
-    term_b, grad_dec, grad_bdec = lax.optimization_barrier((term_b, grad_dec, grad_bdec))
-
-    grad_feat = scale * (term.astype(jnp.float32) + term_b.astype(jnp.float32))
-    grad_pre = (grad_feat * jax.nn.sigmoid(4.0 * pre)).astype(jnp.bfloat16)
+    term_b[1], grad_dec, grad_bdec = lax.optimization_barrier((term_b[1], grad_dec, grad_bdec))
+
+    pre = [
+        p.astype(jnp.float32) + q.astype(jnp.float32) + b_enc[:, None] for p, q in zip(part, part_b)
+    ]
+    grad_pre = [
+        (scale * (t.astype(jnp.float32) + u.astype(jnp.float32)) * jax.nn.sigmoid(4.0 * p)).astype(
+            jnp.bfloat16
+        )
+        for t, u, p in zip(term, term_b, pre)
+    ]
+    grad_pre = jnp.concatenate(grad_pre, axis=1)
     grad_enc, grad_benc = outer_enc(acts_own, grad_pre, acts_b, other_core(grad_pre))
     grad_benc = grad_benc[0]
     return (grad_enc[None], grad_dec[None], grad_benc, grad_bdec[None])

time: 163 us -> 167 us (1.025)
  waiting for transfers between devices: 74.5 us -> 44.1 us
  starting transfers between devices: 37.7 us -> 67.3 us
  Pallas kernels: 19 us -> 25.1 us
    ppermute x9 -> x24, starting transfers between devices: 11.6 us -> 33.2 us  [the longest x21 26.9 us: in_plane(): return lax.ppermute(x, PLANE, pairs)]
    all_to_all x2 -> x1, waiting for transfers between devices: 32.1 us -> 13 us  [among_sixteen(): return lax.all_to_all(x, SPACE, 0, 0, axis_index_groups=GROUPS, tiled=True)]
    ppermute x9 -> x24, waiting for transfers between devices: 31.1 us -> 22 us  [the longest x21 17.1 us: in_plane(): return lax.ppermute(x, PLANE, pairs)]
    ppermute x2 -> x4, starting transfers between devices: 0.05 us -> 8.25 us  [other_layer(): return lax.ppermute(x, 'z_lo', [(0, 1), (1, 0)])]
    all_to_all x2 -> x1, starting transfers between devices: 12.8 us -> 5.77 us  [among_sixteen(): return lax.all_to_all(x, SPACE, 0, 0, axis_index_groups=GROUPS, tiled=True)]
    ppermute x9, starting transfers between devices: 13.2 us -> 20.1 us  [other_core(): return lax.ppermute(x, 'core', [(0, 1), (1, 0)])]
    pallas_call x2 -> x4, Pallas kernels: 2.51 us -> 4.99 us  [gathered_dot(): pl.pallas_call(gathered_dot_kernel, out_shape=jax.ShapeDtypeStruct((n, to...]
    ppermute x9, waiting for transfers between devices: 4.24 us -> 2.35 us  [other_core(): return lax.ppermute(x, 'core', [(0, 1), (1, 0)])]
  transfers between devices with their start and end apart: 22 -> 38, of which waited for: 15 -> 17; matrix products, arithmetic and copies ran while one was open for 2% -> 1% of each run, Pallas kernels for 8% -> 12%
where the time goes in v5:
time: 167 us
  starting transfers between devices  67.3 us (40%)
  waiting for transfers between devices  44.1 us (26%)
  Pallas kernels  25.1 us (15%)
  blocking collectives  21.2 us (13%)
  local copies, waits for them, and re-layouts  5.96 us (4%)
  other arithmetic  2.37 us (1%)
    ppermute x21, starting transfers between devices, in_plane(): return lax.ppermute(x, PLANE, pairs)  26.9 us
    all_to_all x1, blocking collectives, among_sixteen(): return lax.all_to_all(x, SPACE, 0, 0, axis_index_groups=GROUPS, tiled=True)  21.2 us
    ppermute x9, starting transfers between devices, other_core(): return lax.ppermute(x, 'core', [(0, 1), (1, 0)])  20.1 us
    ppermute x21, waiting for transfers between devices, in_plane(): return lax.ppermute(x, PLANE, pairs)  17.1 us
    all_to_all x1, waiting for transfers between devices, among_sixteen(): return lax.all_to_all(x, SPACE, 0, 0, axis_index_groups=GROUPS, tiled=True)  13 us
    ppermute x4, starting transfers between devices, other_layer(): return lax.ppermute(x, 'z_lo', [(0, 1), (1, 0)])  8.25 us
    ppermute x4, waiting for transfers between devices, other_layer(): return lax.ppermute(x, 'z_lo', [(0, 1), (1, 0)])  6.74 us
    ppermute x3, starting transfers between devices, along_z(): return lax.ppermute(x, 'z_hi', [(i, i ^ k) for i in range(4)])  6.37 us
  transfers between devices with their start and end apart: 38, of which 17 were waited for; matrix products, arithmetic and copies ran while one was open for 1% of the time, Pallas kernels for 12%

profile of v5, /device:TPU:1, one launch (start us, length us, event | category | flops | bytes accessed | tf_op | source)
XLA Modules:
  0.0 167.0 jit_solution(1395028434149430663)
XLA Ops:
  0.7 3.3 %collective-permute-start = (bf16[32,512]{1,0:T(8,128)(2,1)}, bf16[32,512]{1,0:T(8,128)(2,1)S(1)}, u32[]{:S(2)}, u32[]{:S(2)}) collective-permute-start(bf16[32,512]{1,0:T(8,128)(2,1)} %bitcast.23), channel_id=1, source_target_pairs={{0,64},{64,0},{1,65},{65,1},{2,66},{66,2},{3,67},{67,3},{4,68},{68... | collective-permute-start | bytes 98312 | tf_op jit(solution)/shard_map/ppermute | solution.py:31
  7.0 5.1 %collective-permute-start.4 = (bf16[64,256]{1,0:T(8,128)(2,1)S(1)}, bf16[64,256]{1,0:T(8,128)(2,1)S(1)}, u32[]{:S(2)}, u32[]{:S(2)}) collective-permute-start(bf16[64,256]{1,0:T(8,128)(2,1)S(1)} %pad_maximum_fusion.3), channel_id=1, source_target_pairs={{0,8},{4,12},{8,0},{12,4},{1,9},{5,13},{9,1},{13,5},{2,10},{6,14},... | collective-permute-start | bytes 98312 | tf_op jit(solution)/shard_map/ppermute | solution.py:62
  12.1 1.7 %collective-permute-done.4 = bf16[64,256]{1,0:T(8,128)(2,1)S(1)} collective-permute-done((bf16[64,256]{1,0:T(8,128)(2,1)S(1)}, bf16[64,256]{1,0:T(8,128)(2,1)S(1)}, u32[]{:S(2)}, u32[]{:S(2)}) %collective-permute-start.4) | collective-permute-done | bytes 32800 | tf_op jit(solution)/shard_map/ppermute | solution.py:62
  13.8 3.2 %collective-permute-done.5 = bf16[64,256]{1,0:T(8,128)(2,1)S(1)} collective-permute-done((bf16[64,256]{1,0:T(8,128)(2,1)S(1)}, bf16[64,256]{1,0:T(8,128)(2,1)S(1)}, u32[]{:S(2)}, u32[]{:S(2)}) %collective-permute-start.5) | collective-permute-done | bytes 32800 | tf_op jit(solution)/shard_map/ppermute | solution.py:62
  18.2 2.6 %collective-permute-start.7 = (bf16[256,256]{1,0:T(8,128)(2,1)S(1)}, bf16[256,256]{1,0:T(8,128)(2,1)S(1)}, u32[]{:S(2)}, u32[]{:S(2)}) collective-permute-start(bf16[256,256]{1,0:T(8,128)(2,1)S(1)} %get-tuple-element.106), channel_id=1, source_target_pairs={{0,32},{1,33},{2,34},{3,35},{16,48},{17,49},{18,50},{19,51},{32,0}... | collective-permute-start | bytes 393224 | tf_op jit(solution)/shard_map/ppermute | solution.py:49
  20.9 3.7 %collective-permute-done.7 = bf16[256,256]{1,0:T(8,128)(2,1)S(1)} collective-permute-done((bf16[256,256]{1,0:T(8,128)(2,1)S(1)}, bf16[256,256]{1,0:T(8,128)(2,1)S(1)}, u32[]{:S(2)}, u32[]{:S(2)}) %collective-permute-start.7) | collective-permute-done | bytes 131104 | tf_op jit(solution)/shard_map/ppermute | solution.py:49
  24.6 1.7 %collective-permute-done.8 = bf16[256,256]{1,0:T(8,128)(2,1)S(1)} collective-permute-done((bf16[256,256]{1,0:T(8,128)(2,1)S(1)}, bf16[256,256]{1,0:T(8,128)(2,1)S(1)}, u32[]{:S(2)}, u32[]{:S(2)}) %collective-permute-start.8) | collective-permute-done | bytes 131104 | tf_op jit(solution)/shard_map/ppermute | solution.py:49
  26.4 2.7 %collective-permute-start.10 = (bf16[1024,128]{1,0:T(8,128)(2,1)S(1)}, bf16[1024,128]{1,0:T(8,128)(2,1)S(1)}, u32[]{:S(2)}, u32[]{:S(2)}) collective-permute-start(bf16[1024,128]{1,0:T(8,128)(2,1)S(1)} %get-tuple-element.57.p0.refs_0_), channel_id=1, source_target_pairs={{0,2},{1,3},{2,0},{3,1},{16,18},{17,19},{18,16},{19,17},{32,34},{3... | collective-permute-start | bytes 786440 | tf_op jit(solution)/shard_map/ppermute | solution.py:49
  29.8 3.5 %collective-permute-done.10.p2.refs_2_ = bf16[1024,128]{1,0:T(8,128)(2,1)S(1)} collective-permute-done((bf16[1024,128]{1,0:T(8,128)(2,1)S(1)}, bf16[1024,128]{1,0:T(8,128)(2,1)S(1)}, u32[]{:S(2)}, u32[]{:S(2)}) %collective-permute-start.10) | collective-permute-done | bytes 262176 | tf_op jit(solution)/shard_map/ppermute | solution.py:49
  34.5 2.5 %collective-permute-start.14 = (bf16[1024,128]{1,0:T(8,128)(2,1)S(1)}, bf16[1024,128]{1,0:T(8,128)(2,1)S(1)}, u32[]{:S(2)}, u32[]{:S(2)}) collective-permute-start(bf16[1024,128]{1,0:T(8,128)(2,1)S(1)} %get-tuple-element.61.p0.refs_4_), channel_id=1, source_target_pairs={{0,2},{1,3},{2,0},{3,1},{16,18},{17,19},{18,16},{19,17},{32,34},{3... | collective-permute-start | bytes 786440 | tf_op jit(solution)/shard_map/ppermute | solution.py:49
  37.2 3.3 %shard_map.139.x.w = bf16[4,1024,512]{2,1,0:T(8,128)(2,1)S(1)} custom-call(s32[64]{0:T(128)S(1)} %get-tuple-element.116.rows, bf16[512,2048]{1,0:T(8,128)(2,1)S(1)} %bitcast.18, bf16[512,2048]{1,0:T(8,128)(2,1)} %collective-permute-done.2.other), custom_call_target="tpu_custom_call" | custom-call | flops 1048576 | bytes 16777216 | tf_op jit(solution)/shard_map/pallas_call | solution.py:154
  40.5 4.6 %shard_map.138.w = bf16[4,512,1024]{2,1,0:T(8,128)(2,1)S(1)} custom-call(s32[64]{0:T(128)S(1)} %get-tuple-element.117.rows, bf16[2048,512]{1,0:T(8,128)(2,1)S(1)} %bitcast.20, bf16[2048,512]{1,0:T(8,128)(2,1)} %collective-permute-done.1.other), custom_call_target="tpu_custom_call" | custom-call | flops 1048576 | bytes 16777216 | tf_op jit(solution)/shard_map/pallas_call | solution.py:124
  50.3 2.1 %collective-permute-done.12.part_b = bf16[512,128]{1,0:T(8,128)(2,1)S(1)} collective-permute-done((bf16[512,128]{1,0:T(8,128)(2,1)S(1)}, bf16[512,128]{1,0:T(8,128)(2,1)S(1)}, u32[]{:S(2)}, u32[]{:S(2)}) %collective-permute-start.12) | collective-permute-done | bytes 131104 | tf_op jit(solution)/shard_map/ppermute | solution.py:35
  54.3 9.3 %collective-permute-start.20 = (bf16[2048,256]{1,0:T(8,128)(2,1)S(1)}, bf16[2048,256]{1,0:T(8,128)(2,1)S(1)}, u32[]{:S(2)}, u32[]{:S(2)}) collective-permute-start(bf16[2048,256]{1,0:T(8,128)(2,1)S(1)} %get-tuple-element.73), channel_id=1, source_target_pairs={{0,64},{64,0},{1,65},{65,1},{2,66},{66,2},{3,67},{67,3},{4,68},{68... | collective-permute-start | bytes 3145736 | tf_op jit(solution)/shard_map/ppermute | solution.py:31
  65.6 3.4 %collective-permute-start.18 = (bf16[1024,128]{1,0:T(8,128)(2,1)S(1)}, bf16[1024,128]{1,0:T(8,128)(2,1)S(1)}, u32[]{:S(2)}, u32[]{:S(2)}) collective-permute-start(bf16[1024,128]{1,0:T(8,128)(2,1)S(1)} %get-tuple-element.71), channel_id=1, source_target_pairs={{0,3},{1,2},{2,1},{3,0},{16,19},{17,18},{18,17},{19,16},{32,35},{3... | collective-permute-start | bytes 786440 | tf_op jit(solution)/shard_map/ppermute | solution.py:49
  69.7 3.4 %collective-permute-done.19.part_b = bf16[512,128]{1,0:T(8,128)(2,1)S(1)} collective-permute-done((bf16[512,128]{1,0:T(8,128)(2,1)S(1)}, bf16[512,128]{1,0:T(8,128)(2,1)S(1)}, u32[]{:S(2)}, u32[]{:S(2)}) %collective-permute-start.19) | collective-permute-done | bytes 131104 | tf_op jit(solution)/shard_map/ppermute | solution.py:35
  74.7 2.1 %collective-permute-start.22 = (bf16[1024,128]{1,0:T(8,128)(2,1)S(1)}, bf16[1024,128]{1,0:T(8,128)(2,1)S(1)}, u32[]{:S(2)}, u32[]{:S(2)}) collective-permute-start(bf16[1024,128]{1,0:T(8,128)(2,1)S(1)} %get-tuple-element.77), channel_id=1, source_target_pairs={{0,2},{1,3},{2,0},{3,1},{16,18},{17,19},{18,16},{19,17},{32,34},{3... | collective-permute-start | bytes 786440 | tf_op jit(solution)/shard_map/ppermute | solution.py:49
  76.7 1.8 %collective-permute-start.23 = (bf16[1024,128]{1,0:T(8,128)(2,1)S(1)}, bf16[1024,128]{1,0:T(8,128)(2,1)S(1)}, u32[]{:S(2)}, u32[]{:S(2)}) collective-permute-start(bf16[1024,128]{1,0:T(8,128)(2,1)S(1)} %get-tuple-element.78), channel_id=1, source_target_pairs={{0,3},{1,2},{2,1},{3,0},{16,19},{17,18},{18,17},{19,16},{32,35},{3... | collective-permute-start | bytes 786440 | tf_op jit(solution)/shard_map/ppermute | solution.py:49
  80.2 3.2 %collective-permute-done.22 = bf16[1024,128]{1,0:T(8,128)(2,1)S(1)} collective-permute-done((bf16[1024,128]{1,0:T(8,128)(2,1)S(1)}, bf16[1024,128]{1,0:T(8,128)(2,1)S(1)}, u32[]{:S(2)}, u32[]{:S(2)}) %collective-permute-start.22) | collective-permute-done | bytes 262176 | tf_op jit(solution)/shard_map/ppermute | solution.py:49
  83.4 2.9 %collective-permute-done.23 = bf16[1024,128]{1,0:T(8,128)(2,1)S(1)} collective-permute-done((bf16[1024,128]{1,0:T(8,128)(2,1)S(1)}, bf16[1024,128]{1,0:T(8,128)(2,1)S(1)}, u32[]{:S(2)}, u32[]{:S(2)}) %collective-permute-start.23) | collective-permute-done | bytes 262176 | tf_op jit(solution)/shard_map/ppermute | solution.py:49
  87.3 5.8 %all-to-all-start = ((bf16[16,64,256]{2,1,0:T(8,128)(2,1)}), bf16[16,64,256]{2,1,0:T(8,128)(2,1)S(1)}, u32[]{:S(2)}, u32[]{:S(2)}) async-start(bf16[16,64,256]{2,1,0:T(8,128)(2,1)} %bitcast.6), calls=%async_computation | async-start | bytes 1048576 | tf_op jit(solution)/shard_map/all_to_all | solution.py:39
  93.1 2.3 %collective-permute-start.24 = (bf16[1,32]{1,0:T(2,128)(2,1)S(1)}, bf16[1,32]{1,0:T(2,128)(2,1)S(1)}, u32[]{:S(2)}, u32[]{:S(2)}) collective-permute-start(bf16[1,32]{1,0:T(2,128)(2,1)S(1)} %copy-done.18), channel_id=1, source_target_pairs={{0,64},{64,0},{1,65},{65,1},{2,66},{66,2},{3,67},{67,3},{4,68},{68... | collective-permute-start | bytes 200 | tf_op jit(solution)/shard_map/ppermute | solution.py:31
  96.3 13.0 %all-to-all-done = bf16[16,64,256]{2,1,0:T(8,128)(2,1)S(1)} async-done(((bf16[16,64,256]{2,1,0:T(8,128)(2,1)}), bf16[16,64,256]{2,1,0:T(8,128)(2,1)S(1)}, u32[]{:S(2)}, u32[]{:S(2)}) %all-to-all-start) | async-done | bytes 524320 | tf_op jit(solution)/shard_map/all_to_all | solution.py:39
  109.5 21.2 %all_to_all.10 = bf16[16,64,256]{2,1,0:T(8,128)(2,1)S(1)} all-to-all(bf16[16,64,256]{2,1,0:T(8,128)(2,1)S(1)} %broadcast_in_dim.11), channel_id=1, replica_groups={{0,4,8,12,16,20,24,28,32,36,40,44,48,52,56,60},{1,5,9,13,17,21,25,29,33..., dimensions={0} | all-to-all | bytes 1048576 | tf_op jit(solution)/shard_map/all_to_all | solution.py:39
  130.9 2.4 %collective-permute-start.26 = (bf16[1024,128]{1,0:T(8,128)(2,1)S(1)}, bf16[1024,128]{1,0:T(8,128)(2,1)S(1)}, u32[]{:S(2)}, u32[]{:S(2)}) collective-permute-start(bf16[1024,128]{1,0:T(8,128)(2,1)S(1)} %get-tuple-element.85.p0.refs_0_), channel_id=1, source_target_pairs={{0,2},{1,3},{2,0},{3,1},{16,18},{17,19},{18,16},{19,17},{32,34},{3... | collective-permute-start | bytes 786440 | tf_op jit(solution)/shard_map/ppermute | solution.py:49
  134.7 2.4 %collective-permute-start.30 = (bf16[1024,128]{1,0:T(8,128)(2,1)S(1)}, bf16[1024,128]{1,0:T(8,128)(2,1)S(1)}, u32[]{:S(2)}, u32[]{:S(2)}) collective-permute-start(bf16[1024,128]{1,0:T(8,128)(2,1)S(1)} %get-tuple-element.89.p0.refs_4_), channel_id=1, source_target_pairs={{0,2},{1,3},{2,0},{3,1},{16,18},{17,19},{18,16},{19,17},{32,34},{3... | collective-permute-start | bytes 786440 | tf_op jit(solution)/shard_map/ppermute | solution.py:49
  138.6 2.2 %copy-done.1 = bf16[4,1024,512]{2,1,0:T(8,128)(2,1)S(1)} copy-done((bf16[4,1024,512]{2,1,0:T(8,128)(2,1)S(1)}, bf16[4,1024,512]{2,1,0:T(8,128)(2,1)}, u32[]{:S(2)}) %copy-start.1) | copy-done | bytes 4194328
  144.0 4.5 %collective-permute-start.28 = (bf16[512,128]{1,0:T(8,128)(2,1)S(1)}, bf16[512,128]{1,0:T(8,128)(2,1)S(1)}, u32[]{:S(2)}, u32[]{:S(2)}) collective-permute-start(bf16[512,128]{1,0:T(8,128)(2,1)S(1)} %shard_map.146), channel_id=1, source_target_pairs={{0,128},{128,0},{1,129},{129,1},{2,130},{130,2},{3,131},{131,3},{4... | collective-permute-start | bytes 393224 | tf_op jit(solution)/shard_map/ppermute | solution.py:35
  151.9 3.2 %collective-permute-start.34 = (bf16[2048,256]{1,0:T(8,128)(2,1)S(1)}, bf16[2048,256]{1,0:T(8,128)(2,1)S(1)}, u32[]{:S(2)}, u32[]{:S(2)}) collective-permute-start(bf16[2048,256]{1,0:T(8,128)(2,1)S(1)} %get-tuple-element.94), channel_id=1, source_target_pairs={{0,64},{64,0},{1,65},{65,1},{2,66},{66,2},{3,67},{67,3},{4,68},{68... | collective-permute-start | bytes 3145736 | tf_op jit(solution)/shard_map/ppermute | solution.py:31
  155.8 2.0 %collective-permute-start.32 = (bf16[512,128]{1,0:T(8,128)(2,1)S(1)}, bf16[512,128]{1,0:T(8,128)(2,1)S(1)}, u32[]{:S(2)}, u32[]{:S(2)}) collective-permute-start(bf16[512,128]{1,0:T(8,128)(2,1)S(1)} %shard_map.147), channel_id=1, source_target_pairs={{0,128},{128,0},{1,129},{129,1},{2,130},{130,2},{3,131},{131,3},{4... | collective-permute-start | bytes 393224 | tf_op jit(solution)/shard_map/ppermute | solution.py:35
  158.3 3.0 %shard_map.149 = bf16[512,2048]{1,0:T(8,128)(2,1)} custom-call(bf16[512,256]{1,0:T(8,128)(2,1)S(1)} %pad_maximum_fusion.1.feat, bf16[2048,256]{1,0:T(8,128)(2,1)S(1)} %get-tuple-element.93.err, bf16[512,256]{1,0:T(8,128)(2,1)S(1)} %collective-permute-done.33.feat_b, bf16[2048,256]{1,0:T(8,128)(2,1)S(1)} %collective-permute-done.34.err_b), custom_call_target="tpu_custom_call" | custom-call | flops 1073741824 | bytes 5242880 | tf_op jit(solution)/shard_map/pallas_call | solution.py:273
  163.8 3.2 %shard_map.150 = (bf16[2048,512]{1,0:T(8,128)(2,1)}, f32[1,512]{1,0:T(1,128)}) custom-call(bf16[2048,256]{1,0:T(8,128)(2,1)S(1)} %copy-done.8, bf16[512,256]{1,0:T(8,128)(2,1)S(1)} %pad_maximum_fusion.2.grad, bf16[2048,256]{1,0:T(8,128)(2,1)S(1)} %copy-done.10, bf16[512,256]{1,0:T(8,128)(2,1)S(1)} %collective-permute-done.36.grad_b), custom_call_target="tpu_custom_call" | custom-call | flops 10737418240 | bytes 5242880 | tf_op jit(solution)/shard_map/pallas_call | solution.py:301
  (123 shorter events, 34.7 us)
Async XLA Ops:
  0.7 4.4 %collective-permute-start = (bf16[32,512]{1,0:T(8,128)(2,1)}, bf16[32,512]{1,0:T(8,128)(2,1)S(1)}, u32[]{:S(2)}, u32[]{:S(2)}) collective-permute-start(bf16[32,512]{1,0:T(8,128)(2,1)} %bitcast.23), channel_id=1, source_target_pairs={{0,64},{64,0},{1,65},{65,1},{2,66},{66,2},{3,67},{67,3},{4,68},{68... | collective-permute-start | bytes 98312 | tf_op jit(solution)/shard_map/ppermute | solution.py:31
  5.1 29.4 %collective-permute-start.2 = (bf16[512,2048]{1,0:T(8,128)(2,1)}, bf16[512,2048]{1,0:T(8,128)(2,1)}, u32[]{:S(2)}, u32[]{:S(2)}) collective-permute-start(bf16[512,2048]{1,0:T(8,128)(2,1)} %bitcast.17), channel_id=1, source_target_pairs={{0,64},{64,0},{1,65},{65,1},{2,66},{66,2},{3,67},{67,3},{4,68},{68... | collective-permute-start | bytes 6291464 | tf_op jit(solution)/shard_map/ppermute | solution.py:31
  5.5 31.4 %collective-permute-start.1 = (bf16[2048,512]{1,0:T(8,128)(2,1)}, bf16[2048,512]{1,0:T(8,128)(2,1)}, u32[]{:S(2)}, u32[]{:S(2)}) collective-permute-start(bf16[2048,512]{1,0:T(8,128)(2,1)} %bitcast.19), channel_id=1, source_target_pairs={{0,64},{64,0},{1,65},{65,1},{2,66},{66,2},{3,67},{67,3},{4,68},{68... | collective-permute-start | bytes 6291464 | tf_op jit(solution)/shard_map/ppermute | solution.py:31
  5.7 6.4 %collective-permute-start.3 = (bf16[64,256]{1,0:T(8,128)(2,1)S(1)}, bf16[64,256]{1,0:T(8,128)(2,1)S(1)}, u32[]{:S(2)}, u32[]{:S(2)}) collective-permute-start(bf16[64,256]{1,0:T(8,128)(2,1)S(1)} %pad_maximum_fusion.3), channel_id=1, source_target_pairs={{0,4},{4,0},{8,12},{12,8},{1,5},{5,1},{9,13},{13,9},{2,6},{6,2},{1... | collective-permute-start | bytes 98312 | tf_op jit(solution)/shard_map/ppermute | solution.py:62
  7.0 6.8 %collective-permute-start.4 = (bf16[64,256]{1,0:T(8,128)(2,1)S(1)}, bf16[64,256]{1,0:T(8,128)(2,1)S(1)}, u32[]{:S(2)}, u32[]{:S(2)}) collective-permute-start(bf16[64,256]{1,0:T(8,128)(2,1)S(1)} %pad_maximum_fusion.3), channel_id=1, source_target_pairs={{0,8},{4,12},{8,0},{12,4},{1,9},{5,13},{9,1},{13,5},{2,10},{6,14},... | collective-permute-start | bytes 98312 | tf_op jit(solution)/shard_map/ppermute | solution.py:62
  12.1 4.9 %collective-permute-start.5 = (bf16[64,256]{1,0:T(8,128)(2,1)S(1)}, bf16[64,256]{1,0:T(8,128)(2,1)S(1)}, u32[]{:S(2)}, u32[]{:S(2)}) collective-permute-start(bf16[64,256]{1,0:T(8,128)(2,1)S(1)} %pad_maximum_fusion.3), channel_id=1, source_target_pairs={{0,12},{4,8},{8,4},{12,0},{1,13},{5,9},{9,5},{13,1},{2,14},{6,10},... | collective-permute-start | bytes 98312 | tf_op jit(solution)/shard_map/ppermute | solution.py:62
  18.2 6.4 %collective-permute-start.7 = (bf16[256,256]{1,0:T(8,128)(2,1)S(1)}, bf16[256,256]{1,0:T(8,128)(2,1)S(1)}, u32[]{:S(2)}, u32[]{:S(2)}) collective-permute-start(bf16[256,256]{1,0:T(8,128)(2,1)S(1)} %get-tuple-element.106), channel_id=1, source_target_pairs={{0,32},{1,33},{2,34},{3,35},{16,48},{17,49},{18,50},{19,51},{32,0}... | collective-permute-start | bytes 393224 | tf_op jit(solution)/shard_map/ppermute | solution.py:49
  20.9 5.5 %collective-permute-start.8 = (bf16[256,256]{1,0:T(8,128)(2,1)S(1)}, bf16[256,256]{1,0:T(8,128)(2,1)S(1)}, u32[]{:S(2)}, u32[]{:S(2)}) collective-permute-start(bf16[256,256]{1,0:T(8,128)(2,1)S(1)} %get-tuple-element.106), channel_id=1, source_target_pairs={{0,48},{1,49},{2,50},{3,51},{16,32},{17,33},{18,34},{19,35},{32,16... | collective-permute-start | bytes 393224 | tf_op jit(solution)/shard_map/ppermute | solution.py:49
  26.4 6.9 %collective-permute-start.10 = (bf16[1024,128]{1,0:T(8,128)(2,1)S(1)}, bf16[1024,128]{1,0:T(8,128)(2,1)S(1)}, u32[]{:S(2)}, u32[]{:S(2)}) collective-permute-start(bf16[1024,128]{1,0:T(8,128)(2,1)S(1)} %get-tuple-element.57.p0.refs_0_), channel_id=1, source_target_pairs={{0,2},{1,3},{2,0},{3,1},{16,18},{17,19},{18,16},{19,17},{32,34},{3... | collective-permute-start | bytes 786440 | tf_op jit(solution)/shard_map/ppermute | solution.py:49
  29.1 16.0 %collective-permute-start.11 = (bf16[1024,128]{1,0:T(8,128)(2,1)S(1)}, bf16[1024,128]{1,0:T(8,128)(2,1)S(1)}, u32[]{:S(2)}, u32[]{:S(2)}) collective-permute-start(bf16[1024,128]{1,0:T(8,128)(2,1)S(1)} %get-tuple-element.57.p0.refs_0_), channel_id=1, source_target_pairs={{0,3},{1,2},{2,1},{3,0},{16,19},{17,18},{18,17},{19,16},{32,35},{3... | collective-permute-start | bytes 786440 | tf_op jit(solution)/shard_map/ppermute | solution.py:49
  29.8 15.3 %collective-permute-start.9 = (bf16[1024,128]{1,0:T(8,128)(2,1)S(1)}, bf16[1024,128]{1,0:T(8,128)(2,1)S(1)}, u32[]{:S(2)}, u32[]{:S(2)}) collective-permute-start(bf16[1024,128]{1,0:T(8,128)(2,1)S(1)} %get-tuple-element.57.p0.refs_0_), channel_id=1, source_target_pairs={{0,1},{1,0},{2,3},{3,2},{16,17},{17,16},{18,19},{19,18},{32,33},{3... | collective-permute-start | bytes 786440 | tf_op jit(solution)/shard_map/ppermute | solution.py:49
  33.3 15.7 %collective-permute-start.13 = (bf16[1024,128]{1,0:T(8,128)(2,1)S(1)}, bf16[1024,128]{1,0:T(8,128)(2,1)S(1)}, u32[]{:S(2)}, u32[]{:S(2)}) collective-permute-start(bf16[1024,128]{1,0:T(8,128)(2,1)S(1)} %get-tuple-element.61.p0.refs_4_), channel_id=1, source_target_pairs={{0,1},{1,0},{2,3},{3,2},{16,17},{17,16},{18,19},{19,18},{32,33},{3... | collective-permute-start | bytes 786440 | tf_op jit(solution)/shard_map/ppermute | solution.py:49
  34.5 14.5 %collective-permute-start.14 = (bf16[1024,128]{1,0:T(8,128)(2,1)S(1)}, bf16[1024,128]{1,0:T(8,128)(2,1)S(1)}, u32[]{:S(2)}, u32[]{:S(2)}) collective-permute-start(bf16[1024,128]{1,0:T(8,128)(2,1)S(1)} %get-tuple-element.61.p0.refs_4_), channel_id=1, source_target_pairs={{0,2},{1,3},{2,0},{3,1},{16,18},{17,19},{18,16},{19,17},{32,34},{3... | collective-permute-start | bytes 786440 | tf_op jit(solution)/shard_map/ppermute | solution.py:49
  37.0 12.0 %collective-permute-start.15 = (bf16[1024,128]{1,0:T(8,128)(2,1)S(1)}, bf16[1024,128]{1,0:T(8,128)(2,1)S(1)}, u32[]{:S(2)}, u32[]{:S(2)}) collective-permute-start(bf16[1024,128]{1,0:T(8,128)(2,1)S(1)} %get-tuple-element.61.p0.refs_4_), channel_id=1, source_target_pairs={{0,3},{1,2},{2,1},{3,0},{16,19},{17,18},{18,17},{19,16},{32,35},{3... | collective-permute-start | bytes 786440 | tf_op jit(solution)/shard_map/ppermute | solution.py:49
  48.0 4.4 %collective-permute-start.12 = (bf16[512,128]{1,0:T(8,128)(2,1)S(1)}, bf16[512,128]{1,0:T(8,128)(2,1)S(1)}, u32[]{:S(2)}, u32[]{:S(2)}) collective-permute-start(bf16[512,128]{1,0:T(8,128)(2,1)S(1)} %shard_map.140.part), channel_id=1, source_target_pairs={{0,128},{128,0},{1,129},{129,1},{2,130},{130,2},{3,131},{131,3},{4... | collective-permute-start | bytes 393224 | tf_op jit(solution)/shard_map/ppermute | solution.py:35
  54.3 18.9 %collective-permute-start.20 = (bf16[2048,256]{1,0:T(8,128)(2,1)S(1)}, bf16[2048,256]{1,0:T(8,128)(2,1)S(1)}, u32[]{:S(2)}, u32[]{:S(2)}) collective-permute-start(bf16[2048,256]{1,0:T(8,128)(2,1)S(1)} %get-tuple-element.73), channel_id=1, source_target_pairs={{0,64},{64,0},{1,65},{65,1},{2,66},{66,2},{3,67},{67,3},{4,68},{68... | collective-permute-start | bytes 3145736 | tf_op jit(solution)/shard_map/ppermute | solution.py:31
  65.0 11.7 %collective-permute-start.16 = (bf16[1024,128]{1,0:T(8,128)(2,1)S(1)}, bf16[1024,128]{1,0:T(8,128)(2,1)S(1)}, u32[]{:S(2)}, u32[]{:S(2)}) collective-permute-start(bf16[1024,128]{1,0:T(8,128)(2,1)S(1)} %get-tuple-element.69), channel_id=1, source_target_pairs={{0,1},{1,0},{2,3},{3,2},{16,17},{17,16},{18,19},{19,18},{32,33},{3... | collective-permute-start | bytes 786440 | tf_op jit(solution)/shard_map/ppermute | solution.py:49
  65.1 13.4 %collective-permute-start.17 = (bf16[1024,128]{1,0:T(8,128)(2,1)S(1)}, bf16[1024,128]{1,0:T(8,128)(2,1)S(1)}, u32[]{:S(2)}, u32[]{:S(2)}) collective-permute-start(bf16[1024,128]{1,0:T(8,128)(2,1)S(1)} %get-tuple-element.70), channel_id=1, source_target_pairs={{0,2},{1,3},{2,0},{3,1},{16,18},{17,19},{18,16},{19,17},{32,34},{3... | collective-permute-start | bytes 786440 | tf_op jit(solution)/shard_map/ppermute | solution.py:49
  65.6 12.9 %collective-permute-start.18 = (bf16[1024,128]{1,0:T(8,128)(2,1)S(1)}, bf16[1024,128]{1,0:T(8,128)(2,1)S(1)}, u32[]{:S(2)}, u32[]{:S(2)}) collective-permute-start(bf16[1024,128]{1,0:T(8,128)(2,1)S(1)} %get-tuple-element.71), channel_id=1, source_target_pairs={{0,3},{1,2},{2,1},{3,0},{16,19},{17,18},{18,17},{19,16},{32,35},{3... | collective-permute-start | bytes 786440 | tf_op jit(solution)/shard_map/ppermute | solution.py:49
  74.6 5.6 %collective-permute-start.21 = (bf16[1024,128]{1,0:T(8,128)(2,1)S(1)}, bf16[1024,128]{1,0:T(8,128)(2,1)S(1)}, u32[]{:S(2)}, u32[]{:S(2)}) collective-permute-start(bf16[1024,128]{1,0:T(8,128)(2,1)S(1)} %get-tuple-element.76), channel_id=1, source_target_pairs={{0,1},{1,0},{2,3},{3,2},{16,17},{17,16},{18,19},{19,18},{32,33},{3... | collective-permute-start | bytes 786440 | tf_op jit(solution)/shard_map/ppermute | solution.py:49
  74.7 8.7 %collective-permute-start.22 = (bf16[1024,128]{1,0:T(8,128)(2,1)S(1)}, bf16[1024,128]{1,0:T(8,128)(2,1)S(1)}, u32[]{:S(2)}, u32[]{:S(2)}) collective-permute-start(bf16[1024,128]{1,0:T(8,128)(2,1)S(1)} %get-tuple-element.77), channel_id=1, source_target_pairs={{0,2},{1,3},{2,0},{3,1},{16,18},{17,19},{18,16},{19,17},{32,34},{3... | collective-permute-start | bytes 786440 | tf_op jit(solution)/shard_map/ppermute | solution.py:49
  76.7 9.5 %collective-permute-start.23 = (bf16[1024,128]{1,0:T(8,128)(2,1)S(1)}, bf16[1024,128]{1,0:T(8,128)(2,1)S(1)}, u32[]{:S(2)}, u32[]{:S(2)}) collective-permute-start(bf16[1024,128]{1,0:T(8,128)(2,1)S(1)} %get-tuple-element.78), channel_id=1, source_target_pairs={{0,3},{1,2},{2,1},{3,0},{16,19},{17,18},{18,17},{19,16},{32,35},{3... | collective-permute-start | bytes 786440 | tf_op jit(solution)/shard_map/ppermute | solution.py:49
  87.3 22.0 %all-to-all-start = ((bf16[16,64,256]{2,1,0:T(8,128)(2,1)}), bf16[16,64,256]{2,1,0:T(8,128)(2,1)S(1)}, u32[]{:S(2)}, u32[]{:S(2)}) async-start(bf16[16,64,256]{2,1,0:T(8,128)(2,1)} %bitcast.6), calls=%async_computation | async-start | bytes 1048576 | tf_op jit(solution)/shard_map/all_to_all | solution.py:39
  130.8 6.4 %collective-permute-start.25 = (bf16[1024,128]{1,0:T(8,128)(2,1)S(1)}, bf16[1024,128]{1,0:T(8,128)(2,1)S(1)}, u32[]{:S(2)}, u32[]{:S(2)}) collective-permute-start(bf16[1024,128]{1,0:T(8,128)(2,1)S(1)} %get-tuple-element.85.p0.refs_0_), channel_id=1, source_target_pairs={{0,1},{1,0},{2,3},{3,2},{16,17},{17,16},{18,19},{19,18},{32,33},{3... | collective-permute-start | bytes 786440 | tf_op jit(solution)/shard_map/ppermute | solution.py:49
  130.9 11.3 %collective-permute-start.26 = (bf16[1024,128]{1,0:T(8,128)(2,1)S(1)}, bf16[1024,128]{1,0:T(8,128)(2,1)S(1)}, u32[]{:S(2)}, u32[]{:S(2)}) collective-permute-start(bf16[1024,128]{1,0:T(8,128)(2,1)S(1)} %get-tuple-element.85.p0.refs_0_), channel_id=1, source_target_pairs={{0,2},{1,3},{2,0},{3,1},{16,18},{17,19},{18,16},{19,17},{32,34},{3... | collective-permute-start | bytes 786440 | tf_op jit(solution)/shard_map/ppermute | solution.py:49
  133.3 9.5 %collective-permute-start.27 = (bf16[1024,128]{1,0:T(8,128)(2,1)S(1)}, bf16[1024,128]{1,0:T(8,128)(2,1)S(1)}, u32[]{:S(2)}, u32[]{:S(2)}) collective-permute-start(bf16[1024,128]{1,0:T(8,128)(2,1)S(1)} %get-tuple-element.85.p0.refs_0_), channel_id=1, source_target_pairs={{0,3},{1,2},{2,1},{3,0},{16,19},{17,18},{18,17},{19,16},{32,35},{3... | collective-permute-start | bytes 786440 | tf_op jit(solution)/shard_map/ppermute | solution.py:49
  134.7 13.9 %collective-permute-start.29 = (bf16[1024,128]{1,0:T(8,128)(2,1)S(1)}, bf16[1024,128]{1,0:T(8,128)(2,1)S(1)}, u32[]{:S(2)}, u32[]{:S(2)}) collective-permute-start(bf16[1024,128]{1,0:T(8,128)(2,1)S(1)} %get-tuple-element.89.p0.refs_4_), channel_id=1, source_target_pairs={{0,1},{1,0},{2,3},{3,2},{16,17},{17,16},{18,19},{19,18},{32,33},{3... | collective-permute-start | bytes 786440 | tf_op jit(solution)/shard_map/ppermute | solution.py:49
  134.7 13.9 %collective-permute-start.30 = (bf16[1024,128]{1,0:T(8,128)(2,1)S(1)}, bf16[1024,128]{1,0:T(8,128)(2,1)S(1)}, u32[]{:S(2)}, u32[]{:S(2)}) collective-permute-start(bf16[1024,128]{1,0:T(8,128)(2,1)S(1)} %get-tuple-element.89.p0.refs_4_), channel_id=1, source_target_pairs={{0,2},{1,3},{2,0},{3,1},{16,18},{17,19},{18,16},{19,17},{32,34},{3... | collective-permute-start | bytes 786440 | tf_op jit(solution)/shard_map/ppermute | solution.py:49
  137.1 11.5 %collective-permute-start.31 = (bf16[1024,128]{1,0:T(8,128)(2,1)S(1)}, bf16[1024,128]{1,0:T(8,128)(2,1)S(1)}, u32[]{:S(2)}, u32[]{:S(2)}) collective-permute-start(bf16[1024,128]{1,0:T(8,128)(2,1)S(1)} %get-tuple-element.89.p0.refs_4_), channel_id=1, source_target_pairs={{0,3},{1,2},{2,1},{3,0},{16,19},{17,18},{18,17},{19,16},{32,35},{3... | collective-permute-start | bytes 786440 | tf_op jit(solution)/shard_map/ppermute | solution.py:49
  144.0 6.9 %collective-permute-start.28 = (bf16[512,128]{1,0:T(8,128)(2,1)S(1)}, bf16[512,128]{1,0:T(8,128)(2,1)S(1)}, u32[]{:S(2)}, u32[]{:S(2)}) collective-permute-start(bf16[512,128]{1,0:T(8,128)(2,1)S(1)} %shard_map.146), channel_id=1, source_target_pairs={{0,128},{128,0},{1,129},{129,1},{2,130},{130,2},{3,131},{131,3},{4... | collective-permute-start | bytes 393224 | tf_op jit(solution)/shard_map/ppermute | solution.py:35
  151.9 6.4 %collective-permute-start.34 = (bf16[2048,256]{1,0:T(8,128)(2,1)S(1)}, bf16[2048,256]{1,0:T(8,128)(2,1)S(1)}, u32[]{:S(2)}, u32[]{:S(2)}) collective-permute-start(bf16[2048,256]{1,0:T(8,128)(2,1)S(1)} %get-tuple-element.94), channel_id=1, source_target_pairs={{0,64},{64,0},{1,65},{65,1},{2,66},{66,2},{3,67},{67,3},{4,68},{68... | collective-permute-start | bytes 3145736 | tf_op jit(solution)/shard_map/ppermute | solution.py:31
  155.8 5.7 %collective-permute-start.32 = (bf16[512,128]{1,0:T(8,128)(2,1)S(1)}, bf16[512,128]{1,0:T(8,128)(2,1)S(1)}, u32[]{:S(2)}, u32[]{:S(2)}) collective-permute-start(bf16[512,128]{1,0:T(8,128)(2,1)S(1)} %shard_map.147), channel_id=1, source_target_pairs={{0,128},{128,0},{1,129},{129,1},{2,130},{130,2},{3,131},{131,3},{4... | collective-permute-start | bytes 393224 | tf_op jit(solution)/shard_map/ppermute | solution.py:35
  (25 other events, 338.5 us)

commit v6 on v5

--- a/solution.py
+++ b/solution.py
@@ -79,16 +79,15 @@
     for send in (along_z, along_first):
         got = {k: send(x, k) for k in ORDER}
         x = jnp.concatenate([x, got[1], got[2], got[3]], axis=0)
-    return in_two(x)
+    return received([x] * 4)
 
 
 def summed(pieces):
     return sum(p.astype(jnp.float32) for p in pieces)
 
 
-def scattered(parts):
-    total = [summed(received(pieces)).astype(jnp.bfloat16) for pieces in parts]
-    total = jnp.concatenate(total, axis=1)
+def scattered(pieces):
+    total = summed(received(pieces)).astype(jnp.bfloat16)
     blocks = among_sixteen(total.reshape(16, -1, total.shape[-1]))
     return jnp.sum(blocks.astype(jnp.float32), axis=0)
 
@@ -235,23 +234,23 @@
     for k in range(64):
         at = pl.ds(pl.multiple_of(rows[k], BLOCK), BLOCK)
         src = (k % 16) * 2 * BLOCK
-        for half in range(2):
-            piece, to = pieces[half * 4 + k // 16], slice(half * tokens, (half + 1) * tokens)
+        for part in range(len(pieces) // 4):
+            piece, to = pieces[part * 4 + k // 16], slice(part * tokens, (part + 1) * tokens)
             own[at, to] = piece[src : src + BLOCK, :]
             other[at, to] = piece[src + BLOCK : src + 2 * BLOCK, :]
 
 
 def placed(rows, parts):
     depth, tokens = parts[0][0].shape
-    whole = jax.ShapeDtypeStruct((2 * depth, 2 * tokens), jnp.bfloat16)
+    whole = jax.ShapeDtypeStruct((2 * depth, len(parts) * tokens), jnp.bfloat16)
     return pl.pallas_call(
         placed_kernel,
         out_shape=(whole, whole),
-        in_specs=[SMEM] + [VMEM] * 8,
+        in_specs=[SMEM] + [VMEM] * (4 * len(parts)),
         out_specs=(VMEM,) * 2,
         compiler_params=SMALL,
         cost_estimate=pl.CostEstimate(flops=1 << 20, bytes_accessed=4 << 20, transcendentals=0),
-    )(rows, *parts[0], *parts[1])
+    )(rows, *(p for part in parts for p in part))
 
 
 def dot_nt(a, b):
@@ -335,48 +334,38 @@
     enc_r = relative_enc(acts_rows, enc, enc_other)
     dec_r = relative_dec(rows, dec, dec_other)
     acts_p = gathered_by_permutes(start)
-    dec_rt = turned(dec_r)
-
-    enc_r, dec_r = lax.optimization_barrier((enc_r, dec_r))
-    part = [gathered_dot(enc_r, pieces) for pieces in acts_p]
-    part_b = [other_layer(part[0]), None]
-    part_b[0], part[1], acts_p = lax.optimization_barrier((part_b[0], part[1], acts_p))
-    part_b[1] = other_layer(part[1])
-    acts_own, acts_other = placed(acts_rows, acts_p)
+
+    part = gathered_dot(enc_r, acts_p)
+    part, acts_p = lax.optimization_barrier((part, acts_p))
+    part_b = other_layer(part)
+    acts_own, acts_other = placed(acts_rows, [acts_p])
     acts_b = other_core(acts_other)
-    part_b[1], acts_b = lax.optimization_barrier((part_b[1], acts_b))
-    b_lanes = jnp.broadcast_to(b_enc[:, None], part[0].shape)
-    feats, recon = zip(*(blocked_dot(dec_r, p, q, b_lanes) for p, q in zip(part, part_b)))
+    part_b, acts_b = lax.optimization_barrier((part_b, acts_b))
+    b_lanes = jnp.broadcast_to(b_enc[:, None], part.shape)
+    feat, recon = blocked_dot(dec_r, part, part_b, b_lanes)
     recon = scattered(recon)
-    feat = jnp.concatenate(feats, axis=1)
     bias_both = jnp.concatenate([bias[0], bias_other[0]])[:, None]
     err = (recon + bias_both.astype(jnp.float32) - start.astype(jnp.float32)).astype(jnp.bfloat16)
 
+    sums = jnp.sum(err.astype(jnp.float32), axis=1)
+    width = sums.shape[0] // 2
+    grad_bdec = scale * (sums[:width] + other_core(sums[width:]))
     err_p = gathered(err)
+    err_p[0][2], dec_r = lax.optimization_barrier((err_p[0][2], dec_r))
+    dec_rt = turned(dec_r)
+    err_p[1], grad_bdec = lax.optimization_barrier((err_p[1], grad_bdec))
     term = [gathered_dot(dec_rt, pieces) for pieces in err_p]
     term_b = [other_layer(term[0]), None]
-    term_b[0], term[1], err_p, feat, err = lax.optimization_barrier(
-        (term_b[0], term[1], err_p, feat, err)
-    )
+    term_b[0], term[1], err_p, feat = lax.optimization_barrier((term_b[0], term[1], err_p, feat))
     term_b[1] = other_layer(term[1])
     err_own, err_other = placed(rows, err_p)
     err_b, feat_b = other_core(err_other), other_core(feat)
-    sums = jnp.sum(err.astype(jnp.float32), axis=1)
-    width = sums.shape[0] // 2
-    grad_bdec = scale * (sums[:width] + other_core(sums[width:]))
     grad_dec = outer_dec(feat, err_own, feat_b, err_b, scale)
-    term_b[1], grad_dec, grad_bdec = lax.optimization_barrier((term_b[1], grad_dec, grad_bdec))
-
-    pre = [
-        p.astype(jnp.float32) + q.astype(jnp.float32) + b_enc[:, None] for p, q in zip(part, part_b)
-    ]
-    grad_pre = [
-        (scale * (t.astype(jnp.float32) + u.astype(jnp.float32)) * jax.nn.sigmoid(4.0 * p)).astype(
-            jnp.bfloat16
-        )
-        for t, u, p in zip(term, term_b, pre)
-    ]
-    grad_pre = jnp.concatenate(grad_pre, axis=1)
+    term_b[1], grad_dec = lax.optimization_barrier((term_b[1], grad_dec))
+
+    term, term_b = (jnp.concatenate(t, axis=1).astype(jnp.float32) for t in (term, term_b))
+    pre = part.astype(jnp.float32) + part_b.astype(jnp.float32) + b_enc[:, None]
+    grad_pre = (scale * (term + term_b) * jax.nn.sigmoid(4.0 * pre)).astype(jnp.bfloat16)
     grad_enc, grad_benc = outer_enc(acts_own, grad_pre, acts_b, other_core(grad_pre))
     grad_benc = grad_benc[0]
     return (grad_enc[None], grad_dec[None], grad_benc, grad_bdec[None])

time: 167 us -> 157 us (0.940); the launches traced: 167 us -> 155 us
  starting transfers between devices: 67.3 us -> 41.8 us
  waiting for transfers between devices: 44.1 us -> 59.5 us
  Pallas kernels: 25.1 us -> 20.7 us
  blocking collectives: 21.2 us -> 24.4 us
    ppermute x21 -> x15, waiting for transfers between devices: 17.1 us -> 33.6 us  [in_plane(): return lax.ppermute(x, PLANE, pairs)]
    ppermute x21 -> x15, starting transfers between devices: 26.9 us -> 17 us  [in_plane(): return lax.ppermute(x, PLANE, pairs)]
    ppermute x9, starting transfers between devices: 20.1 us -> 12.6 us  [other_core(): return lax.ppermute(x, 'core', [(0, 1), (1, 0)])]
    ppermute x4 -> x3, starting transfers between devices: 8.25 us -> 2.18 us  [other_layer(): return lax.ppermute(x, 'z_lo', [(0, 1), (1, 0)])]
    all_to_all x1, blocking collectives: 21.2 us -> 24.4 us  [among_sixteen(): return lax.all_to_all(x, SPACE, 0, 0, axis_index_groups=GROUPS, tiled=True)]
    ppermute x4 -> x3, waiting for transfers between devices: 6.74 us -> 3.97 us  [other_layer(): return lax.ppermute(x, 'z_lo', [(0, 1), (1, 0)])]
    all_to_all x1, starting transfers between devices: 5.77 us -> 3.57 us  [among_sixteen(): return lax.all_to_all(x, SPACE, 0, 0, axis_index_groups=GROUPS, tiled=True)]
    pallas_call x4 -> x3, Pallas kernels: 4.99 us -> 3.75 us  [gathered_dot(): pl.pallas_call(gathered_dot_kernel, out_shape=jax.ShapeDtypeStruct((n, to...]
  transfers between devices with their start and end apart: 38 -> 31, of which waited for: 17 -> 17; matrix products, arithmetic and copies ran while one was open for 1% -> 1% of each run, Pallas kernels for 12% -> 10%
where the time goes in v6:
time: 157 us; the launch traced here: 155 us
  waiting for transfers between devices  59.5 us (38%)
  starting transfers between devices  41.8 us (27%)
  blocking collectives  24.4 us (16%)
  Pallas kernels  20.7 us (13%)
  local copies, waits for them, and re-layouts  4.85 us (3%)
  other arithmetic  2.89 us (2%)
    ppermute x15, waiting for transfers between devices, in_plane(): return lax.ppermute(x, PLANE, pairs)  33.6 us
    all_to_all x1, blocking collectives, among_sixteen(): return lax.all_to_all(x, SPACE, 0, 0, axis_index_groups=GROUPS, tiled=True)  24.4 us
    ppermute x15, starting transfers between devices, in_plane(): return lax.ppermute(x, PLANE, pairs)  17 us
    all_to_all x1, waiting for transfers between devices, among_sixteen(): return lax.all_to_all(x, SPACE, 0, 0, axis_index_groups=GROUPS, tiled=True)  13.5 us
    ppermute x9, starting transfers between devices, other_core(): return lax.ppermute(x, 'core', [(0, 1), (1, 0)])  12.6 us
    ppermute x3, starting transfers between devices, along_z(): return lax.ppermute(x, 'z_hi', [(i, i ^ k) for i in range(4)])  6.37 us
    ppermute x3, waiting for transfers between devices, along_z(): return lax.ppermute(x, 'z_hi', [(i, i ^ k) for i in range(4)])  4.86 us
    ppermute x3, waiting for transfers between devices, other_layer(): return lax.ppermute(x, 'z_lo', [(0, 1), (1, 0)])  3.97 us
  transfers between devices with their start and end apart: 31, of which 17 were waited for; matrix products, arithmetic and copies ran while one was open for 1% of the time, Pallas kernels for 10%

profile of v6, /device:TPU:1, one launch (start us, length us, event | category | flops | bytes accessed | tf_op | source)
XLA Modules:
  0.0 155.0 jit_solution(16861610383437443831)
XLA Ops:
  0.6 3.3 %collective-permute-start = (bf16[32,512]{1,0:T(8,128)(2,1)}, bf16[32,512]{1,0:T(8,128)(2,1)S(1)}, u32[]{:S(2)}, u32[]{:S(2)}) collective-permute-start(bf16[32,512]{1,0:T(8,128)(2,1)} %bitcast.23), channel_id=1, source_target_pairs={{0,64},{64,0},{1,65},{65,1},{2,66},{66,2},{3,67},{67,3},{4,68},{68... | collective-permute-start | bytes 98312 | tf_op jit(solution)/shard_map/ppermute | solution.py:31
  6.6 5.1 %collective-permute-start.3 = (bf16[64,256]{1,0:T(8,128)(2,1)S(1)}, bf16[64,256]{1,0:T(8,128)(2,1)S(1)}, u32[]{:S(2)}, u32[]{:S(2)}) collective-permute-start(bf16[64,256]{1,0:T(8,128)(2,1)S(1)} %pad_maximum_fusion), channel_id=1, source_target_pairs={{0,8},{4,12},{8,0},{12,4},{1,9},{5,13},{9,1},{13,5},{2,10},{6,14},... | collective-permute-start | bytes 98312 | tf_op jit(solution)/shard_map/ppermute | solution.py:62
  11.8 1.8 %collective-permute-done.3 = bf16[64,256]{1,0:T(8,128)(2,1)S(1)} collective-permute-done((bf16[64,256]{1,0:T(8,128)(2,1)S(1)}, bf16[64,256]{1,0:T(8,128)(2,1)S(1)}, u32[]{:S(2)}, u32[]{:S(2)}) %collective-permute-start.3) | collective-permute-done | bytes 32800 | tf_op jit(solution)/shard_map/ppermute | solution.py:62
  13.6 3.0 %collective-permute-done.4 = bf16[64,256]{1,0:T(8,128)(2,1)S(1)} collective-permute-done((bf16[64,256]{1,0:T(8,128)(2,1)S(1)}, bf16[64,256]{1,0:T(8,128)(2,1)S(1)}, u32[]{:S(2)}, u32[]{:S(2)}) %collective-permute-start.4) | collective-permute-done | bytes 32800 | tf_op jit(solution)/shard_map/ppermute | solution.py:62
  17.9 2.1 %collective-permute-start.11 = (bf16[512,2048]{1,0:T(8,128)(2,1)}, bf16[512,2048]{1,0:T(8,128)(2,1)}, u32[]{:S(2)}, u32[]{:S(2)}) collective-permute-start(bf16[512,2048]{1,0:T(8,128)(2,1)} %bitcast.19), channel_id=1, source_target_pairs={{0,64},{64,0},{1,65},{65,1},{2,66},{66,2},{3,67},{67,3},{4,68},{68... | collective-permute-start | bytes 6291464 | tf_op jit(solution)/shard_map/ppermute | solution.py:31
  20.0 2.9 %collective-permute-start.6 = (bf16[256,256]{1,0:T(8,128)(2,1)S(1)}, bf16[256,256]{1,0:T(8,128)(2,1)S(1)}, u32[]{:S(2)}, u32[]{:S(2)}) collective-permute-start(bf16[256,256]{1,0:T(8,128)(2,1)S(1)} %get-tuple-element.92), channel_id=1, source_target_pairs={{0,32},{1,33},{2,34},{3,35},{16,48},{17,49},{18,50},{19,51},{32,0}... | collective-permute-start | bytes 393224 | tf_op jit(solution)/shard_map/ppermute | solution.py:49
  23.7 1.9 %collective-permute-done.6 = bf16[256,256]{1,0:T(8,128)(2,1)S(1)} collective-permute-done((bf16[256,256]{1,0:T(8,128)(2,1)S(1)}, bf16[256,256]{1,0:T(8,128)(2,1)S(1)}, u32[]{:S(2)}, u32[]{:S(2)}) %collective-permute-start.6) | collective-permute-done | bytes 131104 | tf_op jit(solution)/shard_map/ppermute | solution.py:49
  25.6 2.6 %collective-permute-done.7 = bf16[256,256]{1,0:T(8,128)(2,1)S(1)} collective-permute-done((bf16[256,256]{1,0:T(8,128)(2,1)S(1)}, bf16[256,256]{1,0:T(8,128)(2,1)S(1)}, u32[]{:S(2)}, u32[]{:S(2)}) %collective-permute-start.7) | collective-permute-done | bytes 131104 | tf_op jit(solution)/shard_map/ppermute | solution.py:49
  28.4 2.7 %collective-permute-start.9 = (bf16[1024,256]{1,0:T(8,128)(2,1)S(1)}, bf16[1024,256]{1,0:T(8,128)(2,1)S(1)}, u32[]{:S(2)}, u32[]{:S(2)}) collective-permute-start(bf16[1024,256]{1,0:T(8,128)(2,1)S(1)} %constant_dynamic-update-slice_fusion.4.p0.refs_0_), channel_id=1, source_target_pairs={{0,2},{1,3},{2,0},{3,1},{16,18},{17,19},{18,16},{19,17},{32,34},{3... | collective-permute-start | bytes 1572872 | tf_op jit(solution)/shard_map/ppermute | solution.py:49
  32.9 1.6 %copy-done.2 = bf16[1,2048,512]{2,1,0:T(8,128)(2,1)S(1)} copy-done((bf16[1,2048,512]{2,1,0:T(8,128)(2,1)S(1)}, bf16[1,2048,512]{2,1,0:T(8,128)(2,1)}, u32[]{:S(2)}) %copy-start.2) | copy-done | bytes 2097176
  34.5 3.1 %shard_map.138.w = bf16[4,512,1024]{2,1,0:T(8,128)(2,1)S(1)} custom-call(s32[64]{0:T(128)S(1)} %get-tuple-element.101.rows, bf16[2048,512]{1,0:T(8,128)(2,1)S(1)} %bitcast.18, bf16[2048,512]{1,0:T(8,128)(2,1)} %collective-permute-done.1.other), custom_call_target="tpu_custom_call" | custom-call | flops 1048576 | bytes 16777216 | tf_op jit(solution)/shard_map/pallas_call | solution.py:123
  37.6 6.0 %collective-permute-done.9.p2.refs_2_ = bf16[1024,256]{1,0:T(8,128)(2,1)S(1)} collective-permute-done((bf16[1024,256]{1,0:T(8,128)(2,1)S(1)}, bf16[1024,256]{1,0:T(8,128)(2,1)S(1)}, u32[]{:S(2)}, u32[]{:S(2)}) %collective-permute-start.9) | collective-permute-done | bytes 524320 | tf_op jit(solution)/shard_map/ppermute | solution.py:49
  43.6 2.6 %collective-permute-done.10.p3.refs_3_ = bf16[1024,256]{1,0:T(8,128)(2,1)S(1)} collective-permute-done((bf16[1024,256]{1,0:T(8,128)(2,1)S(1)}, bf16[1024,256]{1,0:T(8,128)(2,1)S(1)}, u32[]{:S(2)}, u32[]{:S(2)}) %collective-permute-start.10) | collective-permute-done | bytes 524320 | tf_op jit(solution)/shard_map/ppermute | solution.py:49
  48.2 3.4 %collective-permute-start.13 = (bf16[2048,256]{1,0:T(8,128)(2,1)S(1)}, bf16[2048,256]{1,0:T(8,128)(2,1)S(1)}, u32[]{:S(2)}, u32[]{:S(2)}) collective-permute-start(bf16[2048,256]{1,0:T(8,128)(2,1)S(1)} %get-tuple-element.55), channel_id=1, source_target_pairs={{0,64},{64,0},{1,65},{65,1},{2,66},{66,2},{3,67},{67,3},{4,68},{68... | collective-permute-start | bytes 3145736 | tf_op jit(solution)/shard_map/ppermute | solution.py:31
  52.3 3.1 %shard_map.141.w.x = bf16[4,1024,512]{2,1,0:T(8,128)(2,1)S(1)} custom-call(s32[64]{0:T(128)S(1)} %get-tuple-element.100.rows, bf16[512,2048]{1,0:T(8,128)(2,1)S(1)} %bitcast.20, bf16[512,2048]{1,0:T(8,128)(2,1)} %collective-permute-done.11.other), custom_call_target="tpu_custom_call" | custom-call | flops 1048576 | bytes 16777216 | tf_op jit(solution)/shard_map/pallas_call | solution.py:153
  55.5 4.0 %collective-permute-done.12.part_b = bf16[512,256]{1,0:T(8,128)(2,1)S(1)} collective-permute-done((bf16[512,256]{1,0:T(8,128)(2,1)S(1)}, bf16[512,256]{1,0:T(8,128)(2,1)S(1)}, u32[]{:S(2)}, u32[]{:S(2)}) %collective-permute-start.12) | collective-permute-done | bytes 262176 | tf_op jit(solution)/shard_map/ppermute | solution.py:35
  59.6 1.5 shard_map.142
  62.6 1.9 %collective-permute-start.14 = (bf16[1024,256]{1,0:T(8,128)(2,1)S(1)}, bf16[1024,256]{1,0:T(8,128)(2,1)S(1)}, u32[]{:S(2)}, u32[]{:S(2)}) collective-permute-start(bf16[1024,256]{1,0:T(8,128)(2,1)S(1)} %get-tuple-element.58), channel_id=1, source_target_pairs={{0,1},{1,0},{2,3},{3,2},{16,17},{17,16},{18,19},{19,18},{32,33},{3... | collective-permute-start | bytes 1572872 | tf_op jit(solution)/shard_map/ppermute | solution.py:49
  64.6 11.9 %collective-permute-done.16 = bf16[1024,256]{1,0:T(8,128)(2,1)S(1)} collective-permute-done((bf16[1024,256]{1,0:T(8,128)(2,1)S(1)}, bf16[1024,256]{1,0:T(8,128)(2,1)S(1)}, u32[]{:S(2)}, u32[]{:S(2)}) %collective-permute-start.16) | collective-permute-done | bytes 524320 | tf_op jit(solution)/shard_map/ppermute | solution.py:49
  78.2 3.6 %all-to-all-start = ((bf16[16,64,256]{2,1,0:T(8,128)(2,1)}), bf16[16,64,256]{2,1,0:T(8,128)(2,1)S(1)}, u32[]{:S(2)}, u32[]{:S(2)}) async-start(bf16[16,64,256]{2,1,0:T(8,128)(2,1)} %bitcast.6), calls=%async_computation | async-start | bytes 1048576 | tf_op jit(solution)/shard_map/all_to_all | solution.py:39
  81.8 2.4 %collective-permute-start.17 = (bf16[1,32]{1,0:T(2,128)(2,1)S(1)}, bf16[1,32]{1,0:T(2,128)(2,1)S(1)}, u32[]{:S(2)}, u32[]{:S(2)}) collective-permute-start(bf16[1,32]{1,0:T(2,128)(2,1)S(1)} %copy-done.5), channel_id=1, source_target_pairs={{0,64},{64,0},{1,65},{65,1},{2,66},{66,2},{3,67},{67,3},{4,68},{68... | collective-permute-start | bytes 200 | tf_op jit(solution)/shard_map/ppermute | solution.py:31
  85.1 13.5 %all-to-all-done = bf16[16,64,256]{2,1,0:T(8,128)(2,1)S(1)} async-done(((bf16[16,64,256]{2,1,0:T(8,128)(2,1)}), bf16[16,64,256]{2,1,0:T(8,128)(2,1)S(1)}, u32[]{:S(2)}, u32[]{:S(2)}) %all-to-all-start) | async-done | bytes 524320 | tf_op jit(solution)/shard_map/all_to_all | solution.py:39
  98.9 24.4 %all_to_all.10 = bf16[16,64,256]{2,1,0:T(8,128)(2,1)S(1)} all-to-all(bf16[16,64,256]{2,1,0:T(8,128)(2,1)S(1)} %broadcast_in_dim.11), channel_id=1, replica_groups={{0,4,8,12,16,20,24,28,32,36,40,44,48,52,56,60},{1,5,9,13,17,21,25,29,33..., dimensions={0} | all-to-all | bytes 1048576 | tf_op jit(solution)/shard_map/all_to_all | solution.py:39
  123.6 3.1 %collective-permute-start.20 = (bf16[1024,128]{1,0:T(8,128)(2,1)S(1)}, bf16[1024,128]{1,0:T(8,128)(2,1)S(1)}, u32[]{:S(2)}, u32[]{:S(2)}) collective-permute-start(bf16[1024,128]{1,0:T(8,128)(2,1)S(1)} %get-tuple-element.72.p0.refs_0_), channel_id=1, source_target_pairs={{0,3},{1,2},{2,1},{3,0},{16,19},{17,18},{18,17},{19,16},{32,35},{3... | collective-permute-start | bytes 786440 | tf_op jit(solution)/shard_map/ppermute | solution.py:49
  127.6 2.7 %collective-permute-done.18.p2.refs_2_ = bf16[1024,128]{1,0:T(8,128)(2,1)S(1)} collective-permute-done((bf16[1024,128]{1,0:T(8,128)(2,1)S(1)}, bf16[1024,128]{1,0:T(8,128)(2,1)S(1)}, u32[]{:S(2)}, u32[]{:S(2)}) %collective-permute-start.18) | collective-permute-done | bytes 262176 | tf_op jit(solution)/shard_map/ppermute | solution.py:49
  130.5 2.2 %copy-done.1 = bf16[4,1024,512]{2,1,0:T(8,128)(2,1)S(1)} copy-done((bf16[4,1024,512]{2,1,0:T(8,128)(2,1)S(1)}, bf16[4,1024,512]{2,1,0:T(8,128)(2,1)}, u32[]{:S(2)}) %copy-start.1) | copy-done | bytes 4194328
  132.7 1.4 shard_map.143.w
  136.3 2.5 %collective-permute-done.23.p2.refs_6_ = bf16[1024,128]{1,0:T(8,128)(2,1)S(1)} collective-permute-done((bf16[1024,128]{1,0:T(8,128)(2,1)S(1)}, bf16[1024,128]{1,0:T(8,128)(2,1)S(1)}, u32[]{:S(2)}, u32[]{:S(2)}) %collective-permute-start.23) | collective-permute-done | bytes 262176 | tf_op jit(solution)/shard_map/ppermute | solution.py:49
  138.8 2.7 %collective-permute-done.24.p3.refs_7_ = bf16[1024,128]{1,0:T(8,128)(2,1)S(1)} collective-permute-done((bf16[1024,128]{1,0:T(8,128)(2,1)S(1)}, bf16[1024,128]{1,0:T(8,128)(2,1)S(1)}, u32[]{:S(2)}, u32[]{:S(2)}) %collective-permute-start.24) | collective-permute-done | bytes 262176 | tf_op jit(solution)/shard_map/ppermute | solution.py:49
  144.3 1.3 collective-permute-start.26
  146.8 3.0 %shard_map.147 = bf16[512,2048]{1,0:T(8,128)(2,1)} custom-call(bf16[512,256]{1,0:T(8,128)(2,1)S(1)} %get-tuple-element.71.feat, bf16[2048,256]{1,0:T(8,128)(2,1)S(1)} %get-tuple-element.80.err, bf16[512,256]{1,0:T(8,128)(2,1)S(1)} %collective-permute-done.27.feat_b, bf16[2048,256]{1,0:T(8,128)(2,1)S(1)} %collective-permute-done.28.err_b), custom_call_target="tpu_custom_call" | custom-call | flops 1073741824 | bytes 5242880 | tf_op jit(solution)/shard_map/pallas_call | solution.py:272
  151.7 3.2 %shard_map.148 = (bf16[2048,512]{1,0:T(8,128)(2,1)}, f32[1,512]{1,0:T(1,128)}) custom-call(bf16[2048,256]{1,0:T(8,128)(2,1)S(1)} %get-tuple-element.52.acts, bf16[512,256]{1,0:T(8,128)(2,1)S(1)} %multiply_convert_fusion.grad, bf16[2048,256]{1,0:T(8,128)(2,1)S(1)} %collective-permute-done.13.acts_b, bf16[512,256]{1,0:T(8,128)(2,1)S(1)} %collective-permute-done.29.grad_b), custom_call_target="tpu_custom_call" | custom-call | flops 10737418240 | bytes 5242880 | tf_op jit(solution)/shard_map/pallas_call | solution.py:300
  (75 shorter events, 23.4 us)
Async XLA Ops:
  0.6 4.4 %collective-permute-start = (bf16[32,512]{1,0:T(8,128)(2,1)}, bf16[32,512]{1,0:T(8,128)(2,1)S(1)}, u32[]{:S(2)}, u32[]{:S(2)}) collective-permute-start(bf16[32,512]{1,0:T(8,128)(2,1)} %bitcast.23), channel_id=1, source_target_pairs={{0,64},{64,0},{1,65},{65,1},{2,66},{66,2},{3,67},{67,3},{4,68},{68... | collective-permute-start | bytes 98312 | tf_op jit(solution)/shard_map/ppermute | solution.py:31
  5.0 27.9 %collective-permute-start.1 = (bf16[2048,512]{1,0:T(8,128)(2,1)}, bf16[2048,512]{1,0:T(8,128)(2,1)}, u32[]{:S(2)}, u32[]{:S(2)}) collective-permute-start(bf16[2048,512]{1,0:T(8,128)(2,1)} %bitcast.17), channel_id=1, source_target_pairs={{0,64},{64,0},{1,65},{65,1},{2,66},{66,2},{3,67},{67,3},{4,68},{68... | collective-permute-start | bytes 6291464 | tf_op jit(solution)/shard_map/ppermute | solution.py:31
  5.4 6.4 %collective-permute-start.2 = (bf16[64,256]{1,0:T(8,128)(2,1)S(1)}, bf16[64,256]{1,0:T(8,128)(2,1)S(1)}, u32[]{:S(2)}, u32[]{:S(2)}) collective-permute-start(bf16[64,256]{1,0:T(8,128)(2,1)S(1)} %pad_maximum_fusion), channel_id=1, source_target_pairs={{0,4},{4,0},{8,12},{12,8},{1,5},{5,1},{9,13},{13,9},{2,6},{6,2},{1... | collective-permute-start | bytes 98312 | tf_op jit(solution)/shard_map/ppermute | solution.py:62
  6.6 7.0 %collective-permute-start.3 = (bf16[64,256]{1,0:T(8,128)(2,1)S(1)}, bf16[64,256]{1,0:T(8,128)(2,1)S(1)}, u32[]{:S(2)}, u32[]{:S(2)}) collective-permute-start(bf16[64,256]{1,0:T(8,128)(2,1)S(1)} %pad_maximum_fusion), channel_id=1, source_target_pairs={{0,8},{4,12},{8,0},{12,4},{1,9},{5,13},{9,1},{13,5},{2,10},{6,14},... | collective-permute-start | bytes 98312 | tf_op jit(solution)/shard_map/ppermute | solution.py:62
  11.8 4.9 %collective-permute-start.4 = (bf16[64,256]{1,0:T(8,128)(2,1)S(1)}, bf16[64,256]{1,0:T(8,128)(2,1)S(1)}, u32[]{:S(2)}, u32[]{:S(2)}) collective-permute-start(bf16[64,256]{1,0:T(8,128)(2,1)S(1)} %pad_maximum_fusion), channel_id=1, source_target_pairs={{0,12},{4,8},{8,4},{12,0},{1,13},{5,9},{9,5},{13,1},{2,14},{6,10},... | collective-permute-start | bytes 98312 | tf_op jit(solution)/shard_map/ppermute | solution.py:62
  16.6 7.1 %collective-permute-start.5 = (bf16[256,256]{1,0:T(8,128)(2,1)S(1)}, bf16[256,256]{1,0:T(8,128)(2,1)S(1)}, u32[]{:S(2)}, u32[]{:S(2)}) collective-permute-start(bf16[256,256]{1,0:T(8,128)(2,1)S(1)} %get-tuple-element.92), channel_id=1, source_target_pairs={{0,16},{1,17},{2,18},{3,19},{16,0},{17,1},{18,2},{19,3},{32,48},{3... | collective-permute-start | bytes 393224 | tf_op jit(solution)/shard_map/ppermute | solution.py:49
  17.9 34.4 %collective-permute-start.11 = (bf16[512,2048]{1,0:T(8,128)(2,1)}, bf16[512,2048]{1,0:T(8,128)(2,1)}, u32[]{:S(2)}, u32[]{:S(2)}) collective-permute-start(bf16[512,2048]{1,0:T(8,128)(2,1)} %bitcast.19), channel_id=1, source_target_pairs={{0,64},{64,0},{1,65},{65,1},{2,66},{66,2},{3,67},{67,3},{4,68},{68... | collective-permute-start | bytes 6291464 | tf_op jit(solution)/shard_map/ppermute | solution.py:31
  20.0 5.6 %collective-permute-start.6 = (bf16[256,256]{1,0:T(8,128)(2,1)S(1)}, bf16[256,256]{1,0:T(8,128)(2,1)S(1)}, u32[]{:S(2)}, u32[]{:S(2)}) collective-permute-start(bf16[256,256]{1,0:T(8,128)(2,1)S(1)} %get-tuple-element.92), channel_id=1, source_target_pairs={{0,32},{1,33},{2,34},{3,35},{16,48},{17,49},{18,50},{19,51},{32,0}... | collective-permute-start | bytes 393224 | tf_op jit(solution)/shard_map/ppermute | solution.py:49
  22.9 5.3 %collective-permute-start.7 = (bf16[256,256]{1,0:T(8,128)(2,1)S(1)}, bf16[256,256]{1,0:T(8,128)(2,1)S(1)}, u32[]{:S(2)}, u32[]{:S(2)}) collective-permute-start(bf16[256,256]{1,0:T(8,128)(2,1)S(1)} %get-tuple-element.92), channel_id=1, source_target_pairs={{0,48},{1,49},{2,50},{3,51},{16,32},{17,33},{18,34},{19,35},{32,16... | collective-permute-start | bytes 393224 | tf_op jit(solution)/shard_map/ppermute | solution.py:49
  28.3 9.3 %collective-permute-start.8 = (bf16[1024,256]{1,0:T(8,128)(2,1)S(1)}, bf16[1024,256]{1,0:T(8,128)(2,1)S(1)}, u32[]{:S(2)}, u32[]{:S(2)}) collective-permute-start(bf16[1024,256]{1,0:T(8,128)(2,1)S(1)} %constant_dynamic-update-slice_fusion.4.p0.refs_0_), channel_id=1, source_target_pairs={{0,1},{1,0},{2,3},{3,2},{16,17},{17,16},{18,19},{19,18},{32,33},{3... | collective-permute-start | bytes 1572872 | tf_op jit(solution)/shard_map/ppermute | solution.py:49
  28.4 15.2 %collective-permute-start.9 = (bf16[1024,256]{1,0:T(8,128)(2,1)S(1)}, bf16[1024,256]{1,0:T(8,128)(2,1)S(1)}, u32[]{:S(2)}, u32[]{:S(2)}) collective-permute-start(bf16[1024,256]{1,0:T(8,128)(2,1)S(1)} %constant_dynamic-update-slice_fusion.4.p0.refs_0_), channel_id=1, source_target_pairs={{0,2},{1,3},{2,0},{3,1},{16,18},{17,19},{18,16},{19,17},{32,34},{3... | collective-permute-start | bytes 1572872 | tf_op jit(solution)/shard_map/ppermute | solution.py:49
  31.0 15.2 %collective-permute-start.10 = (bf16[1024,256]{1,0:T(8,128)(2,1)S(1)}, bf16[1024,256]{1,0:T(8,128)(2,1)S(1)}, u32[]{:S(2)}, u32[]{:S(2)}) collective-permute-start(bf16[1024,256]{1,0:T(8,128)(2,1)S(1)} %constant_dynamic-update-slice_fusion.4.p0.refs_0_), channel_id=1, source_target_pairs={{0,3},{1,2},{2,1},{3,0},{16,19},{17,18},{18,17},{19,16},{32,35},{3... | collective-permute-start | bytes 1572872 | tf_op jit(solution)/shard_map/ppermute | solution.py:49
  48.2 11.3 %collective-permute-start.13 = (bf16[2048,256]{1,0:T(8,128)(2,1)S(1)}, bf16[2048,256]{1,0:T(8,128)(2,1)S(1)}, u32[]{:S(2)}, u32[]{:S(2)}) collective-permute-start(bf16[2048,256]{1,0:T(8,128)(2,1)S(1)} %get-tuple-element.55), channel_id=1, source_target_pairs={{0,64},{64,0},{1,65},{65,1},{2,66},{66,2},{3,67},{67,3},{4,68},{68... | collective-permute-start | bytes 3145736 | tf_op jit(solution)/shard_map/ppermute | solution.py:31
  51.6 7.9 %collective-permute-start.12 = (bf16[512,256]{1,0:T(8,128)(2,1)S(1)}, bf16[512,256]{1,0:T(8,128)(2,1)S(1)}, u32[]{:S(2)}, u32[]{:S(2)}) collective-permute-start(bf16[512,256]{1,0:T(8,128)(2,1)S(1)} %shard_map.139.part), channel_id=1, source_target_pairs={{0,128},{128,0},{1,129},{129,1},{2,130},{130,2},{3,131},{131,3},{4... | collective-permute-start | bytes 786440 | tf_op jit(solution)/shard_map/ppermute | solution.py:35
  61.1 20.7 %copy-start.5 = (bf16[1,32]{1,0:T(2,128)(2,1)S(1)}, bf16[1,32]{1,0:T(2,128)(2,1)}, u32[]{:S(2)}) copy-start(bf16[1,32]{1,0:T(2,128)(2,1)} %param.15) | copy-start | bytes 196
  61.1 15.4 %collective-permute-start.16 = (bf16[1024,256]{1,0:T(8,128)(2,1)S(1)}, bf16[1024,256]{1,0:T(8,128)(2,1)S(1)}, u32[]{:S(2)}, u32[]{:S(2)}) collective-permute-start(bf16[1024,256]{1,0:T(8,128)(2,1)S(1)} %get-tuple-element.60), channel_id=1, source_target_pairs={{0,3},{1,2},{2,1},{3,0},{16,19},{17,18},{18,17},{19,16},{32,35},{3... | collective-permute-start | bytes 1572872 | tf_op jit(solution)/shard_map/ppermute | solution.py:49
  62.1 14.4 %collective-permute-start.15 = (bf16[1024,256]{1,0:T(8,128)(2,1)S(1)}, bf16[1024,256]{1,0:T(8,128)(2,1)S(1)}, u32[]{:S(2)}, u32[]{:S(2)}) collective-permute-start(bf16[1024,256]{1,0:T(8,128)(2,1)S(1)} %get-tuple-element.59), channel_id=1, source_target_pairs={{0,2},{1,3},{2,0},{3,1},{16,18},{17,19},{18,16},{19,17},{32,34},{3... | collective-permute-start | bytes 1572872 | tf_op jit(solution)/shard_map/ppermute | solution.py:49
  62.6 14.5 %collective-permute-start.14 = (bf16[1024,256]{1,0:T(8,128)(2,1)S(1)}, bf16[1024,256]{1,0:T(8,128)(2,1)S(1)}, u32[]{:S(2)}, u32[]{:S(2)}) collective-permute-start(bf16[1024,256]{1,0:T(8,128)(2,1)S(1)} %get-tuple-element.58), channel_id=1, source_target_pairs={{0,1},{1,0},{2,3},{3,2},{16,17},{17,16},{18,19},{19,18},{32,33},{3... | collective-permute-start | bytes 1572872 | tf_op jit(solution)/shard_map/ppermute | solution.py:49
  78.2 20.4 %all-to-all-start = ((bf16[16,64,256]{2,1,0:T(8,128)(2,1)}), bf16[16,64,256]{2,1,0:T(8,128)(2,1)S(1)}, u32[]{:S(2)}, u32[]{:S(2)}) async-start(bf16[16,64,256]{2,1,0:T(8,128)(2,1)} %bitcast.6), calls=%async_computation | async-start | bytes 1048576 | tf_op jit(solution)/shard_map/all_to_all | solution.py:39
  81.8 3.2 %collective-permute-start.17 = (bf16[1,32]{1,0:T(2,128)(2,1)S(1)}, bf16[1,32]{1,0:T(2,128)(2,1)S(1)}, u32[]{:S(2)}, u32[]{:S(2)}) collective-permute-start(bf16[1,32]{1,0:T(2,128)(2,1)S(1)} %copy-done.5), channel_id=1, source_target_pairs={{0,64},{64,0},{1,65},{65,1},{2,66},{66,2},{3,67},{67,3},{4,68},{68... | collective-permute-start | bytes 200 | tf_op jit(solution)/shard_map/ppermute | solution.py:31
  123.4 6.9 %collective-permute-start.18 = (bf16[1024,128]{1,0:T(8,128)(2,1)S(1)}, bf16[1024,128]{1,0:T(8,128)(2,1)S(1)}, u32[]{:S(2)}, u32[]{:S(2)}) collective-permute-start(bf16[1024,128]{1,0:T(8,128)(2,1)S(1)} %get-tuple-element.72.p0.refs_0_), channel_id=1, source_target_pairs={{0,2},{1,3},{2,0},{3,1},{16,18},{17,19},{18,16},{19,17},{32,34},{3... | collective-permute-start | bytes 786440 | tf_op jit(solution)/shard_map/ppermute | solution.py:49
  123.5 10.6 %collective-permute-start.19 = (bf16[1024,128]{1,0:T(8,128)(2,1)S(1)}, bf16[1024,128]{1,0:T(8,128)(2,1)S(1)}, u32[]{:S(2)}, u32[]{:S(2)}) collective-permute-start(bf16[1024,128]{1,0:T(8,128)(2,1)S(1)} %get-tuple-element.72.p0.refs_0_), channel_id=1, source_target_pairs={{0,1},{1,0},{2,3},{3,2},{16,17},{17,16},{18,19},{19,18},{32,33},{3... | collective-permute-start | bytes 786440 | tf_op jit(solution)/shard_map/ppermute | solution.py:49
  123.6 10.8 %collective-permute-start.20 = (bf16[1024,128]{1,0:T(8,128)(2,1)S(1)}, bf16[1024,128]{1,0:T(8,128)(2,1)S(1)}, u32[]{:S(2)}, u32[]{:S(2)}) collective-permute-start(bf16[1024,128]{1,0:T(8,128)(2,1)S(1)} %get-tuple-element.72.p0.refs_0_), channel_id=1, source_target_pairs={{0,3},{1,2},{2,1},{3,0},{16,19},{17,18},{18,17},{19,16},{32,35},{3... | collective-permute-start | bytes 786440 | tf_op jit(solution)/shard_map/ppermute | solution.py:49
  126.8 8.9 %collective-permute-start.25 = (f32[32]{0:T(128)S(1)}, f32[32]{0:T(128)S(1)}, u32[]{:S(2)}, u32[]{:S(2)}) collective-permute-start(f32[32]{0:T(128)S(1)} %slice.7), channel_id=1, source_target_pairs={{0,64},{64,0},{1,65},{65,1},{2,66},{66,2},{3,67},{67,3},{4,68},{68... | collective-permute-start | bytes 392 | tf_op jit(solution)/shard_map/ppermute | solution.py:31
  126.8 9.5 %collective-permute-start.22 = (bf16[1024,128]{1,0:T(8,128)(2,1)S(1)}, bf16[1024,128]{1,0:T(8,128)(2,1)S(1)}, u32[]{:S(2)}, u32[]{:S(2)}) collective-permute-start(bf16[1024,128]{1,0:T(8,128)(2,1)S(1)} %get-tuple-element.76.p0.refs_4_), channel_id=1, source_target_pairs={{0,1},{1,0},{2,3},{3,2},{16,17},{17,16},{18,19},{19,18},{32,33},{3... | collective-permute-start | bytes 786440 | tf_op jit(solution)/shard_map/ppermute | solution.py:49
  130.3 8.5 %collective-permute-start.23 = (bf16[1024,128]{1,0:T(8,128)(2,1)S(1)}, bf16[1024,128]{1,0:T(8,128)(2,1)S(1)}, u32[]{:S(2)}, u32[]{:S(2)}) collective-permute-start(bf16[1024,128]{1,0:T(8,128)(2,1)S(1)} %get-tuple-element.76.p0.refs_4_), channel_id=1, source_target_pairs={{0,2},{1,3},{2,0},{3,1},{16,18},{17,19},{18,16},{19,17},{32,34},{3... | collective-permute-start | bytes 786440 | tf_op jit(solution)/shard_map/ppermute | solution.py:49
  134.1 7.4 %collective-permute-start.24 = (bf16[1024,128]{1,0:T(8,128)(2,1)S(1)}, bf16[1024,128]{1,0:T(8,128)(2,1)S(1)}, u32[]{:S(2)}, u32[]{:S(2)}) collective-permute-start(bf16[1024,128]{1,0:T(8,128)(2,1)S(1)} %get-tuple-element.76.p0.refs_4_), channel_id=1, source_target_pairs={{0,3},{1,2},{2,1},{3,0},{16,19},{17,18},{18,17},{19,16},{32,35},{3... | collective-permute-start | bytes 786440 | tf_op jit(solution)/shard_map/ppermute | solution.py:49
  135.6 7.1 %collective-permute-start.21 = (bf16[512,128]{1,0:T(8,128)(2,1)S(1)}, bf16[512,128]{1,0:T(8,128)(2,1)S(1)}, u32[]{:S(2)}, u32[]{:S(2)}) collective-permute-start(bf16[512,128]{1,0:T(8,128)(2,1)S(1)} %shard_map.144), channel_id=1, source_target_pairs={{0,128},{128,0},{1,129},{129,1},{2,130},{130,2},{3,131},{131,3},{4... | collective-permute-start | bytes 393224 | tf_op jit(solution)/shard_map/ppermute | solution.py:35
  143.7 3.1 %collective-permute-start.28 = (bf16[2048,256]{1,0:T(8,128)(2,1)S(1)}, bf16[2048,256]{1,0:T(8,128)(2,1)S(1)}, u32[]{:S(2)}, u32[]{:S(2)}) collective-permute-start(bf16[2048,256]{1,0:T(8,128)(2,1)S(1)} %get-tuple-element.81), channel_id=1, source_target_pairs={{0,64},{64,0},{1,65},{65,1},{2,66},{66,2},{3,67},{67,3},{4,68},{68... | collective-permute-start | bytes 3145736 | tf_op jit(solution)/shard_map/ppermute | solution.py:31
  143.9 2.8 %collective-permute-start.27 = (bf16[512,256]{1,0:T(8,128)(2,1)S(1)}, bf16[512,256]{1,0:T(8,128)(2,1)S(1)}, u32[]{:S(2)}, u32[]{:S(2)}) collective-permute-start(bf16[512,256]{1,0:T(8,128)(2,1)S(1)} %get-tuple-element.71.feat), channel_id=1, source_target_pairs={{0,64},{64,0},{1,65},{65,1},{2,66},{66,2},{3,67},{67,3},{4,68},{68... | collective-permute-start | bytes 786440 | tf_op jit(solution)/shard_map/ppermute | solution.py:31
  144.3 5.5 %collective-permute-start.26 = (bf16[512,128]{1,0:T(8,128)(2,1)S(1)}, bf16[512,128]{1,0:T(8,128)(2,1)S(1)}, u32[]{:S(2)}, u32[]{:S(2)}) collective-permute-start(bf16[512,128]{1,0:T(8,128)(2,1)S(1)} %shard_map.145), channel_id=1, source_target_pairs={{0,128},{128,0},{1,129},{129,1},{2,130},{130,2},{3,131},{131,3},{4... | collective-permute-start | bytes 393224 | tf_op jit(solution)/shard_map/ppermute | solution.py:35
  150.1 1.6 %collective-permute-start.29 = (bf16[512,256]{1,0:T(8,128)(2,1)S(1)}, bf16[512,256]{1,0:T(8,128)(2,1)S(1)}, u32[]{:S(2)}, u32[]{:S(2)}) collective-permute-start(bf16[512,256]{1,0:T(8,128)(2,1)S(1)} %multiply_convert_fusion.grad), channel_id=1, source_target_pairs={{0,64},{64,0},{1,65},{65,1},{2,66},{66,2},{3,67},{67,3},{4,68},{68... | collective-permute-start | bytes 786440 | tf_op jit(solution)/shard_map/ppermute | solution.py:31
  (5 other events, 21.3 us)

commit v7 on v6

--- a/solution.py
+++ b/solution.py
@@ -258,9 +258,9 @@
 
 
 def outer_dec_kernel(scale, feat, err, feat_b, err_b, out):
-    out[...] = (scale * (dot_nt(feat[...], err[...]) + dot_nt(feat_b[...], err_b[...]))).astype(
-        out.dtype
-    )
+    left = jnp.concatenate([feat[...], feat_b[...]], axis=1)
+    right = jnp.concatenate([err[...], err_b[...]], axis=1)
+    out[...] = (scale * dot_nt(left, right)).astype(out.dtype)
 
 
 def outer_dec(feat, err, feat_b, err_b, scale):
@@ -283,7 +283,9 @@
 
 
 def outer_enc_kernel(acts, grad, acts_b, grad_b, out, sums):
-    out[...] = (dot_nt(acts[...], grad[...]) + dot_nt(acts_b[...], grad_b[...])).astype(out.dtype)
+    left = jnp.concatenate([acts[...], acts_b[...]], axis=1)
+    right = jnp.concatenate([grad[...], grad_b[...]], axis=1)
+    out[...] = dot_nt(left, right).astype(out.dtype)
 
     @pl.when(pl.program_id(0) == 0)
     def _():
@@ -339,11 +341,13 @@
     part, acts_p = lax.optimization_barrier((part, acts_p))
     part_b = other_layer(part)
     acts_own, acts_other = placed(acts_rows, [acts_p])
-    acts_b = other_core(acts_other)
-    part_b, acts_b = lax.optimization_barrier((part_b, acts_b))
+    part_b, acts_own, acts_other = lax.optimization_barrier((part_b, acts_own, acts_other))
     b_lanes = jnp.broadcast_to(b_enc[:, None], part.shape)
     feat, recon = blocked_dot(dec_r, part, part_b, b_lanes)
     recon = scattered(recon)
+    recon, acts_b, feat_b = lax.optimization_barrier(
+        (recon, other_core(acts_other), other_core(feat))
+    )
     bias_both = jnp.concatenate([bias[0], bias_other[0]])[:, None]
     err = (recon + bias_both.astype(jnp.float32) - start.astype(jnp.float32)).astype(jnp.bfloat16)
 
@@ -359,7 +363,7 @@
     term_b[0], term[1], err_p, feat = lax.optimization_barrier((term_b[0], term[1], err_p, feat))
     term_b[1] = other_layer(term[1])
     err_own, err_other = placed(rows, err_p)
-    err_b, feat_b = other_core(err_other), other_core(feat)
+    err_b = other_core(err_other)
     grad_dec = outer_dec(feat, err_own, feat_b, err_b, scale)
     term_b[1], grad_dec = lax.optimization_barrier((term_b[1], grad_dec))
 

time: 157 us -> 149 us (0.949); the launches traced: 155 us -> 149 us
  waiting for transfers between devices: 59.5 us -> 42.5 us
  starting transfers between devices: 41.8 us -> 56.5 us
  blocking collectives: 24.4 us -> 17.2 us
  local copies, waits for them, and re-layouts: 4.85 us -> 7.13 us
    ppermute x9, starting transfers between devices: 12.6 us -> 24.4 us  [other_core(): return lax.ppermute(x, 'core', [(0, 1), (1, 0)])]
    all_to_all x1, waiting for transfers between devices: 13.5 us -> 3.96 us  [among_sixteen(): return lax.all_to_all(x, SPACE, 0, 0, axis_index_groups=GROUPS, tiled=True)]
    all_to_all x1, blocking collectives: 24.4 us -> 17.2 us  [among_sixteen(): return lax.all_to_all(x, SPACE, 0, 0, axis_index_groups=GROUPS, tiled=True)]
    ppermute x15, waiting for transfers between devices: 33.6 us -> 29.1 us  [in_plane(): return lax.ppermute(x, PLANE, pairs)]
    ppermute x3, waiting for transfers between devices: 3.97 us -> 0.01 us  [other_layer(): return lax.ppermute(x, 'z_lo', [(0, 1), (1, 0)])]
    unnamed x17 -> x29, local copies, waits for them, and re-layouts: 3.83 us -> 6.1 us
  transfers between devices with their start and end apart: 31 -> 31, of which waited for: 17 -> 14; matrix products, arithmetic and copies ran while one was open for 1% -> 2% of each run, Pallas kernels for 10% -> 10%
where the time goes in v7:
time: 149 us
  starting transfers between devices  56.5 us (38%)
  waiting for transfers between devices  42.5 us (29%)
  Pallas kernels  20.6 us (14%)
  blocking collectives  17.2 us (12%)
  local copies, waits for them, and re-layouts  7.13 us (5%)
  other arithmetic  4.01 us (3%)
    ppermute x15, waiting for transfers between devices, in_plane(): return lax.ppermute(x, PLANE, pairs)  29.1 us
    ppermute x9, starting transfers between devices, other_core(): return lax.ppermute(x, 'core', [(0, 1), (1, 0)])  24.4 us
    ppermute x15, starting transfers between devices, in_plane(): return lax.ppermute(x, PLANE, pairs)  18.4 us
    all_to_all x1, blocking collectives, among_sixteen(): return lax.all_to_all(x, SPACE, 0, 0, axis_index_groups=GROUPS, tiled=True)  17.2 us
    ppermute x3, starting transfers between devices, along_z(): return lax.ppermute(x, 'z_hi', [(i, i ^ k) for i in range(4)])  6.37 us
    unnamed x29, local copies, waits for them, and re-layouts  6.1 us
    ppermute x3, waiting for transfers between devices, along_z(): return lax.ppermute(x, 'z_hi', [(i, i ^ k) for i in range(4)])  4.86 us
    ppermute x9, waiting for transfers between devices, other_core(): return lax.ppermute(x, 'core', [(0, 1), (1, 0)])  4.54 us
  transfers between devices with their start and end apart: 31, of which 14 were waited for; matrix products, arithmetic and copies ran while one was open for 2% of the time, Pallas kernels for 10%

profile of v7, /device:TPU:1, one launch (start us, length us, event | category | flops | bytes accessed | tf_op | source)
XLA Modules:
  0.0 148.8 jit_solution(305105013932360608)
XLA Ops:
  0.6 3.3 %collective-permute-start = (bf16[32,512]{1,0:T(8,128)(2,1)}, bf16[32,512]{1,0:T(8,128)(2,1)S(1)}, u32[]{:S(2)}, u32[]{:S(2)}) collective-permute-start(bf16[32,512]{1,0:T(8,128)(2,1)} %bitcast.23), channel_id=1, source_target_pairs={{0,64},{64,0},{1,65},{65,1},{2,66},{66,2},{3,67},{67,3},{4,68},{68... | collective-permute-start | bytes 98312 | tf_op jit(solution)/shard_map/ppermute | solution.py:31
  6.8 5.1 %collective-permute-start.3 = (bf16[64,256]{1,0:T(8,128)(2,1)S(1)}, bf16[64,256]{1,0:T(8,128)(2,1)S(1)}, u32[]{:S(2)}, u32[]{:S(2)}) collective-permute-start(bf16[64,256]{1,0:T(8,128)(2,1)S(1)} %pad_maximum_fusion), channel_id=1, source_target_pairs={{0,8},{4,12},{8,0},{12,4},{1,9},{5,13},{9,1},{13,5},{2,10},{6,14},... | collective-permute-start | bytes 98312 | tf_op jit(solution)/shard_map/ppermute | solution.py:62
  11.9 1.7 %collective-permute-done.3 = bf16[64,256]{1,0:T(8,128)(2,1)S(1)} collective-permute-done((bf16[64,256]{1,0:T(8,128)(2,1)S(1)}, bf16[64,256]{1,0:T(8,128)(2,1)S(1)}, u32[]{:S(2)}, u32[]{:S(2)}) %collective-permute-start.3) | collective-permute-done | bytes 32800 | tf_op jit(solution)/shard_map/ppermute | solution.py:62
  13.6 3.2 %collective-permute-done.4 = bf16[64,256]{1,0:T(8,128)(2,1)S(1)} collective-permute-done((bf16[64,256]{1,0:T(8,128)(2,1)S(1)}, bf16[64,256]{1,0:T(8,128)(2,1)S(1)}, u32[]{:S(2)}, u32[]{:S(2)}) %collective-permute-start.4) | collective-permute-done | bytes 32800 | tf_op jit(solution)/shard_map/ppermute | solution.py:62
  18.1 2.6 %collective-permute-start.6 = (bf16[256,256]{1,0:T(8,128)(2,1)S(1)}, bf16[256,256]{1,0:T(8,128)(2,1)S(1)}, u32[]{:S(2)}, u32[]{:S(2)}) collective-permute-start(bf16[256,256]{1,0:T(8,128)(2,1)S(1)} %get-tuple-element.100), channel_id=1, source_target_pairs={{0,32},{1,33},{2,34},{3,35},{16,48},{17,49},{18,50},{19,51},{32,0}... | collective-permute-start | bytes 393224 | tf_op jit(solution)/shard_map/ppermute | solution.py:49
  20.7 3.7 %collective-permute-done.6 = bf16[256,256]{1,0:T(8,128)(2,1)S(1)} collective-permute-done((bf16[256,256]{1,0:T(8,128)(2,1)S(1)}, bf16[256,256]{1,0:T(8,128)(2,1)S(1)}, u32[]{:S(2)}, u32[]{:S(2)}) %collective-permute-start.6) | collective-permute-done | bytes 131104 | tf_op jit(solution)/shard_map/ppermute | solution.py:49
  24.5 1.7 %collective-permute-done.7 = bf16[256,256]{1,0:T(8,128)(2,1)S(1)} collective-permute-done((bf16[256,256]{1,0:T(8,128)(2,1)S(1)}, bf16[256,256]{1,0:T(8,128)(2,1)S(1)}, u32[]{:S(2)}, u32[]{:S(2)}) %collective-permute-start.7) | collective-permute-done | bytes 131104 | tf_op jit(solution)/shard_map/ppermute | solution.py:49
  27.2 2.7 %collective-permute-start.9 = (bf16[1024,256]{1,0:T(8,128)(2,1)S(1)}, bf16[1024,256]{1,0:T(8,128)(2,1)S(1)}, u32[]{:S(2)}, u32[]{:S(2)}) collective-permute-start(bf16[1024,256]{1,0:T(8,128)(2,1)S(1)} %constant_dynamic-update-slice_fusion.4.p0.refs_0_), channel_id=1, source_target_pairs={{0,2},{1,3},{2,0},{3,1},{16,18},{17,19},{18,16},{19,17},{32,34},{3... | collective-permute-start | bytes 1572872 | tf_op jit(solution)/shard_map/ppermute | solution.py:49
  30.9 1.6 %copy-done.2 = bf16[1,2048,512]{2,1,0:T(8,128)(2,1)S(1)} copy-done((bf16[1,2048,512]{2,1,0:T(8,128)(2,1)S(1)}, bf16[1,2048,512]{2,1,0:T(8,128)(2,1)}, u32[]{:S(2)}) %copy-start.2) | copy-done | bytes 2097176
  32.5 3.1 %shard_map.138.w = bf16[4,512,1024]{2,1,0:T(8,128)(2,1)S(1)} custom-call(s32[64]{0:T(128)S(1)} %get-tuple-element.109.rows, bf16[2048,512]{1,0:T(8,128)(2,1)S(1)} %bitcast.18, bf16[2048,512]{1,0:T(8,128)(2,1)} %collective-permute-done.1.other), custom_call_target="tpu_custom_call" | custom-call | flops 1048576 | bytes 16777216 | tf_op jit(solution)/shard_map/pallas_call | solution.py:123
  35.5 6.9 %collective-permute-done.9.p2.refs_2_ = bf16[1024,256]{1,0:T(8,128)(2,1)S(1)} collective-permute-done((bf16[1024,256]{1,0:T(8,128)(2,1)S(1)}, bf16[1024,256]{1,0:T(8,128)(2,1)S(1)}, u32[]{:S(2)}, u32[]{:S(2)}) %collective-permute-start.9) | collective-permute-done | bytes 524320 | tf_op jit(solution)/shard_map/ppermute | solution.py:49
  42.5 2.6 %collective-permute-done.10.p3.refs_3_ = bf16[1024,256]{1,0:T(8,128)(2,1)S(1)} collective-permute-done((bf16[1024,256]{1,0:T(8,128)(2,1)S(1)}, bf16[1024,256]{1,0:T(8,128)(2,1)S(1)}, u32[]{:S(2)}, u32[]{:S(2)}) %collective-permute-start.10) | collective-permute-done | bytes 524320 | tf_op jit(solution)/shard_map/ppermute | solution.py:49
  49.8 3.1 %shard_map.141.w.x = bf16[4,1024,512]{2,1,0:T(8,128)(2,1)S(1)} custom-call(s32[64]{0:T(128)S(1)} %get-tuple-element.108.rows, bf16[512,2048]{1,0:T(8,128)(2,1)S(1)} %bitcast.20, bf16[512,2048]{1,0:T(8,128)(2,1)} %collective-permute-done.12.other), custom_call_target="tpu_custom_call" | custom-call | flops 1048576 | bytes 16777216 | tf_op jit(solution)/shard_map/pallas_call | solution.py:153
  53.1 1.5 shard_map.142
  55.3 2.9 %collective-permute-start.13 = (bf16[1024,256]{1,0:T(8,128)(2,1)S(1)}, bf16[1024,256]{1,0:T(8,128)(2,1)S(1)}, u32[]{:S(2)}, u32[]{:S(2)}) collective-permute-start(bf16[1024,256]{1,0:T(8,128)(2,1)S(1)} %get-tuple-element.63), channel_id=1, source_target_pairs={{0,1},{1,0},{2,3},{3,2},{16,17},{17,16},{18,19},{19,18},{32,33},{3... | collective-permute-start | bytes 1572872 | tf_op jit(solution)/shard_map/ppermute | solution.py:49
  58.2 11.9 %collective-permute-done.15 = bf16[1024,256]{1,0:T(8,128)(2,1)S(1)} collective-permute-done((bf16[1024,256]{1,0:T(8,128)(2,1)S(1)}, bf16[1024,256]{1,0:T(8,128)(2,1)S(1)}, u32[]{:S(2)}, u32[]{:S(2)}) %collective-permute-start.15) | collective-permute-done | bytes 524320 | tf_op jit(solution)/shard_map/ppermute | solution.py:49
  71.8 4.2 %all-to-all-start = ((bf16[16,64,256]{2,1,0:T(8,128)(2,1)}), bf16[16,64,256]{2,1,0:T(8,128)(2,1)}, u32[]{:S(2)}, u32[]{:S(2)}) async-start(bf16[16,64,256]{2,1,0:T(8,128)(2,1)} %bitcast.6), calls=%async_computation | async-start | bytes 1048576 | tf_op jit(solution)/shard_map/all_to_all | solution.py:39
  76.1 6.5 %collective-permute-start.16 = (bf16[2048,256]{1,0:T(8,128)(2,1)S(1)}, bf16[2048,256]{1,0:T(8,128)(2,1)S(1)}, u32[]{:S(2)}, u32[]{:S(2)}) collective-permute-start(bf16[2048,256]{1,0:T(8,128)(2,1)S(1)} %copy-done.9), channel_id=1, source_target_pairs={{0,64},{64,0},{1,65},{65,1},{2,66},{66,2},{3,67},{67,3},{4,68},{68... | collective-permute-start | bytes 3145736 | tf_op jit(solution)/shard_map/ppermute | solution.py:31
  83.1 2.1 %collective-permute-done.18 = bf16[1,32]{1,0:T(2,128)(2,1)S(1)} collective-permute-done((bf16[1,32]{1,0:T(2,128)(2,1)S(1)}, bf16[1,32]{1,0:T(2,128)(2,1)S(1)}, u32[]{:S(2)}, u32[]{:S(2)}) %collective-permute-start.18) | collective-permute-done | bytes 96 | tf_op jit(solution)/shard_map/ppermute | solution.py:31
  85.3 4.0 %all-to-all-done = bf16[16,64,256]{2,1,0:T(8,128)(2,1)} async-done(((bf16[16,64,256]{2,1,0:T(8,128)(2,1)}), bf16[16,64,256]{2,1,0:T(8,128)(2,1)}, u32[]{:S(2)}, u32[]{:S(2)}) %all-to-all-start) | async-done | bytes 524320 | tf_op jit(solution)/shard_map/all_to_all | solution.py:39
  90.7 17.2 %all_to_all.10 = bf16[16,64,256]{2,1,0:T(8,128)(2,1)S(1)} all-to-all(bf16[16,64,256]{2,1,0:T(8,128)(2,1)S(1)} %broadcast_in_dim.11), channel_id=1, replica_groups={{0,4,8,12,16,20,24,28,32,36,40,44,48,52,56,60},{1,5,9,13,17,21,25,29,33..., dimensions={0} | all-to-all | bytes 1048576 | tf_op jit(solution)/shard_map/all_to_all | solution.py:39
  107.9 1.9 %collective-permute-start.19 = (bf16[1024,128]{1,0:T(8,128)(2,1)S(1)}, bf16[1024,128]{1,0:T(8,128)(2,1)S(1)}, u32[]{:S(2)}, u32[]{:S(2)}) collective-permute-start(bf16[1024,128]{1,0:T(8,128)(2,1)S(1)} %get-tuple-element.79.p0.refs_0_), channel_id=1, source_target_pairs={{0,2},{1,3},{2,0},{3,1},{16,18},{17,19},{18,16},{19,17},{32,34},{3... | collective-permute-start | bytes 786440 | tf_op jit(solution)/shard_map/ppermute | solution.py:49
  111.3 9.4 %collective-permute-start.26 = (f32[32]{0:T(128)S(1)}, f32[32]{0:T(128)S(1)}, u32[]{:S(2)}, u32[]{:S(2)}) collective-permute-start(f32[32]{0:T(128)S(1)} %slice.7), channel_id=1, source_target_pairs={{0,64},{64,0},{1,65},{65,1},{2,66},{66,2},{3,67},{67,3},{4,68},{68... | collective-permute-start | bytes 392 | tf_op jit(solution)/shard_map/ppermute | solution.py:31
  120.7 1.4 collective-permute-start.24
  122.1 2.2 %copy-done.1 = bf16[4,1024,512]{2,1,0:T(8,128)(2,1)S(1)} copy-done((bf16[4,1024,512]{2,1,0:T(8,128)(2,1)S(1)}, bf16[4,1024,512]{2,1,0:T(8,128)(2,1)}, u32[]{:S(2)}) %copy-start.1) | copy-done | bytes 4194328
  124.3 1.4 shard_map.143.w
  125.7 2.5 %collective-permute-start.25 = (bf16[1024,128]{1,0:T(8,128)(2,1)S(1)}, bf16[1024,128]{1,0:T(8,128)(2,1)S(1)}, u32[]{:S(2)}, u32[]{:S(2)}) collective-permute-start(bf16[1024,128]{1,0:T(8,128)(2,1)S(1)} %get-tuple-element.83.p0.refs_4_), channel_id=1, source_target_pairs={{0,3},{1,2},{2,1},{3,0},{16,19},{17,18},{18,17},{19,16},{32,35},{3... | collective-permute-start | bytes 786440 | tf_op jit(solution)/shard_map/ppermute | solution.py:49
  130.9 1.6 %collective-permute-done.25.p3.refs_7_ = bf16[1024,128]{1,0:T(8,128)(2,1)S(1)} collective-permute-done((bf16[1024,128]{1,0:T(8,128)(2,1)S(1)}, bf16[1024,128]{1,0:T(8,128)(2,1)S(1)}, u32[]{:S(2)}, u32[]{:S(2)}) %collective-permute-start.25) | collective-permute-done | bytes 262176 | tf_op jit(solution)/shard_map/ppermute | solution.py:49
  134.7 3.4 %collective-permute-start.28 = (bf16[2048,256]{1,0:T(8,128)(2,1)S(1)}, bf16[2048,256]{1,0:T(8,128)(2,1)S(1)}, u32[]{:S(2)}, u32[]{:S(2)}) collective-permute-start(bf16[2048,256]{1,0:T(8,128)(2,1)S(1)} %get-tuple-element.89), channel_id=1, source_target_pairs={{0,64},{64,0},{1,65},{65,1},{2,66},{66,2},{3,67},{67,3},{4,68},{68... | collective-permute-start | bytes 3145736 | tf_op jit(solution)/shard_map/ppermute | solution.py:31
  138.1 1.4 collective-permute-start.27
  140.3 3.0 %shard_map.147 = bf16[512,2048]{1,0:T(8,128)(2,1)} custom-call(bf16[512,256]{1,0:T(8,128)(2,1)S(1)} %get-tuple-element.78.feat, bf16[2048,256]{1,0:T(8,128)(2,1)S(1)} %get-tuple-element.87.err, bf16[512,256]{1,0:T(8,128)(2,1)S(1)} %collective-permute-done.17.feat_b, bf16[2048,256]{1,0:T(8,128)(2,1)S(1)} %collective-permute-done.28.err_b), custom_call_target="tpu_custom_call" | custom-call | flops 1073741824 | bytes 5242880 | tf_op jit(solution)/shard_map/pallas_call | solution.py:272
  145.5 3.2 %shard_map.148 = (bf16[2048,512]{1,0:T(8,128)(2,1)}, f32[1,512]{1,0:T(1,128)}) custom-call(bf16[2048,256]{1,0:T(8,128)(2,1)S(1)} %copy-done.5, bf16[512,256]{1,0:T(8,128)(2,1)S(1)} %multiply_convert_fusion.grad, bf16[2048,256]{1,0:T(8,128)(2,1)S(1)} %copy-done.7, bf16[512,256]{1,0:T(8,128)(2,1)S(1)} %collective-permute-done.29.grad_b), custom_call_target="tpu_custom_call" | custom-call | flops 10737418240 | bytes 5242880 | tf_op jit(solution)/shard_map/pallas_call | solution.py:302
  (87 shorter events, 24.7 us)
Async XLA Ops:
  0.6 4.4 %collective-permute-start = (bf16[32,512]{1,0:T(8,128)(2,1)}, bf16[32,512]{1,0:T(8,128)(2,1)S(1)}, u32[]{:S(2)}, u32[]{:S(2)}) collective-permute-start(bf16[32,512]{1,0:T(8,128)(2,1)} %bitcast.23), channel_id=1, source_target_pairs={{0,64},{64,0},{1,65},{65,1},{2,66},{66,2},{3,67},{67,3},{4,68},{68... | collective-permute-start | bytes 98312 | tf_op jit(solution)/shard_map/ppermute | solution.py:31
  5.0 25.8 %collective-permute-start.1 = (bf16[2048,512]{1,0:T(8,128)(2,1)}, bf16[2048,512]{1,0:T(8,128)(2,1)}, u32[]{:S(2)}, u32[]{:S(2)}) collective-permute-start(bf16[2048,512]{1,0:T(8,128)(2,1)} %bitcast.17), channel_id=1, source_target_pairs={{0,64},{64,0},{1,65},{65,1},{2,66},{66,2},{3,67},{67,3},{4,68},{68... | collective-permute-start | bytes 6291464 | tf_op jit(solution)/shard_map/ppermute | solution.py:31
  5.4 44.4 %collective-permute-start.12 = (bf16[512,2048]{1,0:T(8,128)(2,1)}, bf16[512,2048]{1,0:T(8,128)(2,1)}, u32[]{:S(2)}, u32[]{:S(2)}) collective-permute-start(bf16[512,2048]{1,0:T(8,128)(2,1)} %bitcast.19), channel_id=1, source_target_pairs={{0,64},{64,0},{1,65},{65,1},{2,66},{66,2},{3,67},{67,3},{4,68},{68... | collective-permute-start | bytes 6291464 | tf_op jit(solution)/shard_map/ppermute | solution.py:31
  5.5 6.4 %collective-permute-start.2 = (bf16[64,256]{1,0:T(8,128)(2,1)S(1)}, bf16[64,256]{1,0:T(8,128)(2,1)S(1)}, u32[]{:S(2)}, u32[]{:S(2)}) collective-permute-start(bf16[64,256]{1,0:T(8,128)(2,1)S(1)} %pad_maximum_fusion), channel_id=1, source_target_pairs={{0,4},{4,0},{8,12},{12,8},{1,5},{5,1},{9,13},{13,9},{2,6},{6,2},{1... | collective-permute-start | bytes 98312 | tf_op jit(solution)/shard_map/ppermute | solution.py:62
  6.8 6.8 %collective-permute-start.3 = (bf16[64,256]{1,0:T(8,128)(2,1)S(1)}, bf16[64,256]{1,0:T(8,128)(2,1)S(1)}, u32[]{:S(2)}, u32[]{:S(2)}) collective-permute-start(bf16[64,256]{1,0:T(8,128)(2,1)S(1)} %pad_maximum_fusion), channel_id=1, source_target_pairs={{0,8},{4,12},{8,0},{12,4},{1,9},{5,13},{9,1},{13,5},{2,10},{6,14},... | collective-permute-start | bytes 98312 | tf_op jit(solution)/shard_map/ppermute | solution.py:62
  11.9 4.9 %collective-permute-start.4 = (bf16[64,256]{1,0:T(8,128)(2,1)S(1)}, bf16[64,256]{1,0:T(8,128)(2,1)S(1)}, u32[]{:S(2)}, u32[]{:S(2)}) collective-permute-start(bf16[64,256]{1,0:T(8,128)(2,1)S(1)} %pad_maximum_fusion), channel_id=1, source_target_pairs={{0,12},{4,8},{8,4},{12,0},{1,13},{5,9},{9,5},{13,1},{2,14},{6,10},... | collective-permute-start | bytes 98312 | tf_op jit(solution)/shard_map/ppermute | solution.py:62
  16.8 3.9 %collective-permute-start.5 = (bf16[256,256]{1,0:T(8,128)(2,1)S(1)}, bf16[256,256]{1,0:T(8,128)(2,1)S(1)}, u32[]{:S(2)}, u32[]{:S(2)}) collective-permute-start(bf16[256,256]{1,0:T(8,128)(2,1)S(1)} %get-tuple-element.100), channel_id=1, source_target_pairs={{0,16},{1,17},{2,18},{3,19},{16,0},{17,1},{18,2},{19,3},{32,48},{3... | collective-permute-start | bytes 393224 | tf_op jit(solution)/shard_map/ppermute | solution.py:49
  18.1 6.4 %collective-permute-start.6 = (bf16[256,256]{1,0:T(8,128)(2,1)S(1)}, bf16[256,256]{1,0:T(8,128)(2,1)S(1)}, u32[]{:S(2)}, u32[]{:S(2)}) collective-permute-start(bf16[256,256]{1,0:T(8,128)(2,1)S(1)} %get-tuple-element.100), channel_id=1, source_target_pairs={{0,32},{1,33},{2,34},{3,35},{16,48},{17,49},{18,50},{19,51},{32,0}... | collective-permute-start | bytes 393224 | tf_op jit(solution)/shard_map/ppermute | solution.py:49
  20.7 5.5 %collective-permute-start.7 = (bf16[256,256]{1,0:T(8,128)(2,1)S(1)}, bf16[256,256]{1,0:T(8,128)(2,1)S(1)}, u32[]{:S(2)}, u32[]{:S(2)}) collective-permute-start(bf16[256,256]{1,0:T(8,128)(2,1)S(1)} %get-tuple-element.100), channel_id=1, source_target_pairs={{0,48},{1,49},{2,50},{3,51},{16,32},{17,33},{18,34},{19,35},{32,16... | collective-permute-start | bytes 393224 | tf_op jit(solution)/shard_map/ppermute | solution.py:49
  26.2 9.3 %collective-permute-start.8 = (bf16[1024,256]{1,0:T(8,128)(2,1)S(1)}, bf16[1024,256]{1,0:T(8,128)(2,1)S(1)}, u32[]{:S(2)}, u32[]{:S(2)}) collective-permute-start(bf16[1024,256]{1,0:T(8,128)(2,1)S(1)} %constant_dynamic-update-slice_fusion.4.p0.refs_0_), channel_id=1, source_target_pairs={{0,1},{1,0},{2,3},{3,2},{16,17},{17,16},{18,19},{19,18},{32,33},{3... | collective-permute-start | bytes 1572872 | tf_op jit(solution)/shard_map/ppermute | solution.py:49
  27.2 15.3 %collective-permute-start.9 = (bf16[1024,256]{1,0:T(8,128)(2,1)S(1)}, bf16[1024,256]{1,0:T(8,128)(2,1)S(1)}, u32[]{:S(2)}, u32[]{:S(2)}) collective-permute-start(bf16[1024,256]{1,0:T(8,128)(2,1)S(1)} %constant_dynamic-update-slice_fusion.4.p0.refs_0_), channel_id=1, source_target_pairs={{0,2},{1,3},{2,0},{3,1},{16,18},{17,19},{18,16},{19,17},{32,34},{3... | collective-permute-start | bytes 1572872 | tf_op jit(solution)/shard_map/ppermute | solution.py:49
  29.9 15.2 %collective-permute-start.10 = (bf16[1024,256]{1,0:T(8,128)(2,1)S(1)}, bf16[1024,256]{1,0:T(8,128)(2,1)S(1)}, u32[]{:S(2)}, u32[]{:S(2)}) collective-permute-start(bf16[1024,256]{1,0:T(8,128)(2,1)S(1)} %constant_dynamic-update-slice_fusion.4.p0.refs_0_), channel_id=1, source_target_pairs={{0,3},{1,2},{2,1},{3,0},{16,19},{17,18},{18,17},{19,16},{32,35},{3... | collective-permute-start | bytes 1572872 | tf_op jit(solution)/shard_map/ppermute | solution.py:49
  46.4 6.6 %collective-permute-start.11 = (bf16[512,256]{1,0:T(8,128)(2,1)S(1)}, bf16[512,256]{1,0:T(8,128)(2,1)S(1)}, u32[]{:S(2)}, u32[]{:S(2)}) collective-permute-start(bf16[512,256]{1,0:T(8,128)(2,1)S(1)} %shard_map.139.part), channel_id=1, source_target_pairs={{0,128},{128,0},{1,129},{129,1},{2,130},{130,2},{3,131},{131,3},{4... | collective-permute-start | bytes 786440 | tf_op jit(solution)/shard_map/ppermute | solution.py:35
  54.9 27.8 %copy-start.11 = (bf16[1,32]{1,0:T(2,128)(2,1)S(1)}, bf16[1,32]{1,0:T(2,128)(2,1)}, u32[]{:S(2)}) copy-start(bf16[1,32]{1,0:T(2,128)(2,1)} %param.15) | copy-start | bytes 196
  54.9 15.2 %collective-permute-start.15 = (bf16[1024,256]{1,0:T(8,128)(2,1)S(1)}, bf16[1024,256]{1,0:T(8,128)(2,1)S(1)}, u32[]{:S(2)}, u32[]{:S(2)}) collective-permute-start(bf16[1024,256]{1,0:T(8,128)(2,1)S(1)} %get-tuple-element.65), channel_id=1, source_target_pairs={{0,3},{1,2},{2,1},{3,0},{16,19},{17,18},{18,17},{19,16},{32,35},{3... | collective-permute-start | bytes 1572872 | tf_op jit(solution)/shard_map/ppermute | solution.py:49
  55.1 15.0 %collective-permute-start.14 = (bf16[1024,256]{1,0:T(8,128)(2,1)S(1)}, bf16[1024,256]{1,0:T(8,128)(2,1)S(1)}, u32[]{:S(2)}, u32[]{:S(2)}) collective-permute-start(bf16[1024,256]{1,0:T(8,128)(2,1)S(1)} %get-tuple-element.64), channel_id=1, source_target_pairs={{0,2},{1,3},{2,0},{3,1},{16,18},{17,19},{18,16},{19,17},{32,34},{3... | collective-permute-start | bytes 1572872 | tf_op jit(solution)/shard_map/ppermute | solution.py:49
  55.3 15.4 %collective-permute-start.13 = (bf16[1024,256]{1,0:T(8,128)(2,1)S(1)}, bf16[1024,256]{1,0:T(8,128)(2,1)S(1)}, u32[]{:S(2)}, u32[]{:S(2)}) collective-permute-start(bf16[1024,256]{1,0:T(8,128)(2,1)S(1)} %get-tuple-element.63), channel_id=1, source_target_pairs={{0,1},{1,0},{2,3},{3,2},{16,17},{17,16},{18,19},{19,18},{32,33},{3... | collective-permute-start | bytes 1572872 | tf_op jit(solution)/shard_map/ppermute | solution.py:49
  71.8 17.5 %all-to-all-start = ((bf16[16,64,256]{2,1,0:T(8,128)(2,1)}), bf16[16,64,256]{2,1,0:T(8,128)(2,1)}, u32[]{:S(2)}, u32[]{:S(2)}) async-start(bf16[16,64,256]{2,1,0:T(8,128)(2,1)} %bitcast.6), calls=%async_computation | async-start | bytes 1048576 | tf_op jit(solution)/shard_map/all_to_all | solution.py:39
  76.1 14.3 %collective-permute-start.16 = (bf16[2048,256]{1,0:T(8,128)(2,1)S(1)}, bf16[2048,256]{1,0:T(8,128)(2,1)S(1)}, u32[]{:S(2)}, u32[]{:S(2)}) collective-permute-start(bf16[2048,256]{1,0:T(8,128)(2,1)S(1)} %copy-done.9), channel_id=1, source_target_pairs={{0,64},{64,0},{1,65},{65,1},{2,66},{66,2},{3,67},{67,3},{4,68},{68... | collective-permute-start | bytes 3145736 | tf_op jit(solution)/shard_map/ppermute | solution.py:31
  82.6 7.8 %collective-permute-start.17 = (bf16[512,256]{1,0:T(8,128)(2,1)S(1)}, bf16[512,256]{1,0:T(8,128)(2,1)S(1)}, u32[]{:S(2)}, u32[]{:S(2)}) collective-permute-start(bf16[512,256]{1,0:T(8,128)(2,1)S(1)} %get-tuple-element.78.feat), channel_id=1, source_target_pairs={{0,64},{64,0},{1,65},{65,1},{2,66},{66,2},{3,67},{67,3},{4,68},{68... | collective-permute-start | bytes 786440 | tf_op jit(solution)/shard_map/ppermute | solution.py:31
  82.7 2.6 %collective-permute-start.18 = (bf16[1,32]{1,0:T(2,128)(2,1)S(1)}, bf16[1,32]{1,0:T(2,128)(2,1)S(1)}, u32[]{:S(2)}, u32[]{:S(2)}) collective-permute-start(bf16[1,32]{1,0:T(2,128)(2,1)S(1)} %copy-done.11), channel_id=1, source_target_pairs={{0,64},{64,0},{1,65},{65,1},{2,66},{66,2},{3,67},{67,3},{4,68},{68... | collective-permute-start | bytes 200 | tf_op jit(solution)/shard_map/ppermute | solution.py:31
  107.9 12.8 %collective-permute-start.19 = (bf16[1024,128]{1,0:T(8,128)(2,1)S(1)}, bf16[1024,128]{1,0:T(8,128)(2,1)S(1)}, u32[]{:S(2)}, u32[]{:S(2)}) collective-permute-start(bf16[1024,128]{1,0:T(8,128)(2,1)S(1)} %get-tuple-element.79.p0.refs_0_), channel_id=1, source_target_pairs={{0,2},{1,3},{2,0},{3,1},{16,18},{17,19},{18,16},{19,17},{32,34},{3... | collective-permute-start | bytes 786440 | tf_op jit(solution)/shard_map/ppermute | solution.py:49
  109.8 15.9 %collective-permute-start.20 = (bf16[1024,128]{1,0:T(8,128)(2,1)S(1)}, bf16[1024,128]{1,0:T(8,128)(2,1)S(1)}, u32[]{:S(2)}, u32[]{:S(2)}) collective-permute-start(bf16[1024,128]{1,0:T(8,128)(2,1)S(1)} %get-tuple-element.79.p0.refs_0_), channel_id=1, source_target_pairs={{0,1},{1,0},{2,3},{3,2},{16,17},{17,16},{18,19},{19,18},{32,33},{3... | collective-permute-start | bytes 786440 | tf_op jit(solution)/shard_map/ppermute | solution.py:49
  110.1 18.2 %collective-permute-start.21 = (bf16[1024,128]{1,0:T(8,128)(2,1)S(1)}, bf16[1024,128]{1,0:T(8,128)(2,1)S(1)}, u32[]{:S(2)}, u32[]{:S(2)}) collective-permute-start(bf16[1024,128]{1,0:T(8,128)(2,1)S(1)} %get-tuple-element.79.p0.refs_0_), channel_id=1, source_target_pairs={{0,3},{1,2},{2,1},{3,0},{16,19},{17,18},{18,17},{19,16},{32,35},{3... | collective-permute-start | bytes 786440 | tf_op jit(solution)/shard_map/ppermute | solution.py:49
  111.3 19.1 %collective-permute-start.26 = (f32[32]{0:T(128)S(1)}, f32[32]{0:T(128)S(1)}, u32[]{:S(2)}, u32[]{:S(2)}) collective-permute-start(f32[32]{0:T(128)S(1)} %slice.7), channel_id=1, source_target_pairs={{0,64},{64,0},{1,65},{65,1},{2,66},{66,2},{3,67},{67,3},{4,68},{68... | collective-permute-start | bytes 392 | tf_op jit(solution)/shard_map/ppermute | solution.py:31
  120.7 10.2 %collective-permute-start.23 = (bf16[1024,128]{1,0:T(8,128)(2,1)S(1)}, bf16[1024,128]{1,0:T(8,128)(2,1)S(1)}, u32[]{:S(2)}, u32[]{:S(2)}) collective-permute-start(bf16[1024,128]{1,0:T(8,128)(2,1)S(1)} %get-tuple-element.83.p0.refs_4_), channel_id=1, source_target_pairs={{0,1},{1,0},{2,3},{3,2},{16,17},{17,16},{18,19},{19,18},{32,33},{3... | collective-permute-start | bytes 786440 | tf_op jit(solution)/shard_map/ppermute | solution.py:49
  120.7 10.2 %collective-permute-start.24 = (bf16[1024,128]{1,0:T(8,128)(2,1)S(1)}, bf16[1024,128]{1,0:T(8,128)(2,1)S(1)}, u32[]{:S(2)}, u32[]{:S(2)}) collective-permute-start(bf16[1024,128]{1,0:T(8,128)(2,1)S(1)} %get-tuple-element.83.p0.refs_4_), channel_id=1, source_target_pairs={{0,2},{1,3},{2,0},{3,1},{16,18},{17,19},{18,16},{19,17},{32,34},{3... | collective-permute-start | bytes 786440 | tf_op jit(solution)/shard_map/ppermute | solution.py:49
  125.7 6.8 %collective-permute-start.25 = (bf16[1024,128]{1,0:T(8,128)(2,1)S(1)}, bf16[1024,128]{1,0:T(8,128)(2,1)S(1)}, u32[]{:S(2)}, u32[]{:S(2)}) collective-permute-start(bf16[1024,128]{1,0:T(8,128)(2,1)S(1)} %get-tuple-element.83.p0.refs_4_), channel_id=1, source_target_pairs={{0,3},{1,2},{2,1},{3,0},{16,19},{17,18},{18,17},{19,16},{32,35},{3... | collective-permute-start | bytes 786440 | tf_op jit(solution)/shard_map/ppermute | solution.py:49
  129.5 4.2 %collective-permute-start.22 = (bf16[512,128]{1,0:T(8,128)(2,1)S(1)}, bf16[512,128]{1,0:T(8,128)(2,1)S(1)}, u32[]{:S(2)}, u32[]{:S(2)}) collective-permute-start(bf16[512,128]{1,0:T(8,128)(2,1)S(1)} %shard_map.144), channel_id=1, source_target_pairs={{0,128},{128,0},{1,129},{129,1},{2,130},{130,2},{3,131},{131,3},{4... | collective-permute-start | bytes 393224 | tf_op jit(solution)/shard_map/ppermute | solution.py:35
  134.7 5.7 %collective-permute-start.28 = (bf16[2048,256]{1,0:T(8,128)(2,1)S(1)}, bf16[2048,256]{1,0:T(8,128)(2,1)S(1)}, u32[]{:S(2)}, u32[]{:S(2)}) collective-permute-start(bf16[2048,256]{1,0:T(8,128)(2,1)S(1)} %get-tuple-element.89), channel_id=1, source_target_pairs={{0,64},{64,0},{1,65},{65,1},{2,66},{66,2},{3,67},{67,3},{4,68},{68... | collective-permute-start | bytes 3145736 | tf_op jit(solution)/shard_map/ppermute | solution.py:31
  138.1 5.3 %collective-permute-start.27 = (bf16[512,128]{1,0:T(8,128)(2,1)S(1)}, bf16[512,128]{1,0:T(8,128)(2,1)S(1)}, u32[]{:S(2)}, u32[]{:S(2)}) collective-permute-start(bf16[512,128]{1,0:T(8,128)(2,1)S(1)} %shard_map.145), channel_id=1, source_target_pairs={{0,128},{128,0},{1,129},{129,1},{2,130},{130,2},{3,131},{131,3},{4... | collective-permute-start | bytes 393224 | tf_op jit(solution)/shard_map/ppermute | solution.py:35
  143.7 1.9 %collective-permute-start.29 = (bf16[512,256]{1,0:T(8,128)(2,1)S(1)}, bf16[512,256]{1,0:T(8,128)(2,1)S(1)}, u32[]{:S(2)}, u32[]{:S(2)}) collective-permute-start(bf16[512,256]{1,0:T(8,128)(2,1)S(1)} %multiply_convert_fusion.grad), channel_id=1, source_target_pairs={{0,64},{64,0},{1,65},{65,1},{2,66},{66,2},{3,67},{67,3},{4,68},{68... | collective-permute-start | bytes 786440 | tf_op jit(solution)/shard_map/ppermute | solution.py:31
  (11 other events, 63.3 us)

commit v8 on v7

--- a/solution.py
+++ b/solution.py
@@ -1,5 +1,3 @@
-import functools
-
 import jax
 import jax.numpy as jnp
 import numpy as np
@@ -86,10 +84,11 @@
     return sum(p.astype(jnp.float32) for p in pieces)
 
 
-def scattered(pieces):
+def scattered(pieces, beside):
     total = summed(received(pieces)).astype(jnp.bfloat16)
+    total, beside = lax.optimization_barrier((total, beside))
     blocks = among_sixteen(total.reshape(16, -1, total.shape[-1]))
-    return jnp.sum(blocks.astype(jnp.float32), axis=0)
+    return jnp.sum(blocks.astype(jnp.float32), axis=0), beside
 
 
 def block_rows(relative):
@@ -257,29 +256,9 @@
     return lax.dot_general(a, b, (((1,), (1,)), ((), ())), preferred_element_type=jnp.float32)
 
 
-def outer_dec_kernel(scale, feat, err, feat_b, err_b, out):
-    left = jnp.concatenate([feat[...], feat_b[...]], axis=1)
-    right = jnp.concatenate([err[...], err_b[...]], axis=1)
-    out[...] = (scale * dot_nt(left, right)).astype(out.dtype)
-
-
 def outer_dec(feat, err, feat_b, err_b, scale):
-    m, tokens = feat.shape
-    n = err.shape[0]
-    tile = n // 4
-    left = pl.BlockSpec((m, tokens), lambda i: (0, 0))
-    right = pl.BlockSpec((tile, tokens), lambda i: (i, 0))
-    return pl.pallas_call(
-        functools.partial(outer_dec_kernel, scale),
-        out_shape=jax.ShapeDtypeStruct((m, n), jnp.bfloat16),
-        grid=(4,),
-        in_specs=[left, right, left, right],
-        out_specs=pl.BlockSpec((m, tile), lambda i: (0, i)),
-        compiler_params=PARAMS,
-        cost_estimate=pl.CostEstimate(
-            flops=4 * m * n * tokens, bytes_accessed=5 << 20, transcendentals=0
-        ),
-    )(feat, err, feat_b, err_b)
+    left, right = jnp.concatenate([feat, feat_b], axis=1), jnp.concatenate([err, err_b], axis=1)
+    return (scale * dot_nt(left, right)).astype(jnp.bfloat16)
 
 
 def outer_enc_kernel(acts, grad, acts_b, grad_b, out, sums):
@@ -296,7 +275,7 @@
 def outer_enc(acts, grad, acts_b, grad_b):
     m, tokens = acts.shape
     n = grad.shape[0]
-    tile = m // 4
+    tile = m // 2
     rows = pl.BlockSpec((tile, tokens), lambda i: (i, 0))
     whole = pl.BlockSpec((n, tokens), lambda i: (0, 0))
     return pl.pallas_call(
@@ -305,7 +284,7 @@
             jax.ShapeDtypeStruct((m, n), jnp.bfloat16),
             jax.ShapeDtypeStruct((1, n), jnp.float32),
         ),
-        grid=(4,),
+        grid=(2,),
         in_specs=[rows, whole, rows, whole],
         out_specs=(
             pl.BlockSpec((tile, n), lambda i: (i, 0)),
@@ -344,7 +323,7 @@
     part_b, acts_own, acts_other = lax.optimization_barrier((part_b, acts_own, acts_other))
     b_lanes = jnp.broadcast_to(b_enc[:, None], part.shape)
     feat, recon = blocked_dot(dec_r, part, part_b, b_lanes)
-    recon = scattered(recon)
+    recon, dec_rt = scattered(recon, turned(dec_r))
     recon, acts_b, feat_b = lax.optimization_barrier(
         (recon, other_core(acts_other), other_core(feat))
     )
@@ -355,8 +334,6 @@
     width = sums.shape[0] // 2
     grad_bdec = scale * (sums[:width] + other_core(sums[width:]))
     err_p = gathered(err)
-    err_p[0][2], dec_r = lax.optimization_barrier((err_p[0][2], dec_r))
-    dec_rt = turned(dec_r)
     err_p[1], grad_bdec = lax.optimization_barrier((err_p[1], grad_bdec))
     term = [gathered_dot(dec_rt, pieces) for pieces in err_p]
     term_b = [other_layer(term[0]), None]

time: 149 us -> 149 us (level)
  matrix products: 0 us -> 3.71 us
  Pallas kernels: 20.6 us -> 17.1 us
  waiting for transfers between devices: 42.5 us -> 39.8 us
  local copies, waits for them, and re-layouts: 7.13 us -> 8.74 us
    dot_general x0 -> x1, matrix products: none -> 3.71 us  [dot_nt(): lax.dot_general(a, b, (((1,), (1,)), ((), ())), preferred_element_type=jn...]
    pallas_call x1 -> x0, Pallas kernels: 3.01 us -> none  [outer_dec(): pl.pallas_call(functools.partial(outer_dec_kernel, scale), out_shape=jax....]
    ppermute x9, starting transfers between devices: 24.4 us -> 26.3 us  [other_core(): return lax.ppermute(x, 'core', [(0, 1), (1, 0)])]
    ppermute x15, waiting for transfers between devices: 29.1 us -> 27.2 us  [in_plane(): return lax.ppermute(x, PLANE, pairs)]
    ppermute x15, starting transfers between devices: 18.4 us -> 20.2 us  [in_plane(): return lax.ppermute(x, PLANE, pairs)]
    all_to_all x1, waiting for transfers between devices: 3.96 us -> 2.24 us  [among_sixteen(): return lax.all_to_all(x, SPACE, 0, 0, axis_index_groups=GROUPS, tiled=True)]
    ppermute x3, starting transfers between devices: 3.11 us -> 1.46 us  [other_layer(): return lax.ppermute(x, 'z_lo', [(0, 1), (1, 0)])]
    unnamed x29 -> x31, local copies, waits for them, and re-layouts: 6.1 us -> 7.72 us
  transfers between devices with their start and end apart: 31 -> 31, of which waited for: 14 -> 17; matrix products, arithmetic and copies ran while one was open for 2% -> 4% of each run, Pallas kernels for 10% -> 8%
where the time goes in v8:
time: 149 us; the launch traced here: 148 us
  starting transfers between devices  57.9 us (39%)
  waiting for transfers between devices  39.8 us (27%)
  Pallas kernels  17.1 us (11%)
  blocking collectives  17 us (11%)
  local copies, waits for them, and re-layouts  8.74 us (6%)
  matrix products  3.71 us (2%)
  other arithmetic  2.91 us (2%)
    ppermute x15, waiting for transfers between devices, in_plane(): return lax.ppermute(x, PLANE, pairs)  27.2 us
    ppermute x9, starting transfers between devices, other_core(): return lax.ppermute(x, 'core', [(0, 1), (1, 0)])  26.3 us
    ppermute x15, starting transfers between devices, in_plane(): return lax.ppermute(x, PLANE, pairs)  20.2 us
    all_to_all x1, blocking collectives, among_sixteen(): return lax.all_to_all(x, SPACE, 0, 0, axis_index_groups=GROUPS, tiled=True)  17 us
    unnamed x31, local copies, waits for them, and re-layouts  7.72 us
    ppermute x3, starting transfers between devices, along_z(): return lax.ppermute(x, 'z_hi', [(i, i ^ k) for i in range(4)])  6.37 us
    ppermute x9, waiting for transfers between devices, other_core(): return lax.ppermute(x, 'core', [(0, 1), (1, 0)])  5.51 us
    ppermute x3, waiting for transfers between devices, along_z(): return lax.ppermute(x, 'z_hi', [(i, i ^ k) for i in range(4)])  4.86 us
  transfers between devices with their start and end apart: 31, of which 17 were waited for; matrix products, arithmetic and copies ran while one was open for 4% of the time, Pallas kernels for 8%

profile of v8, /device:TPU:1, one launch (start us, length us, event | category | flops | bytes accessed | tf_op | source)
XLA Modules:
  0.0 148.1 jit_solution(10564727778625024560)
XLA Ops:
  0.6 3.3 %collective-permute-start = (bf16[32,512]{1,0:T(8,128)(2,1)}, bf16[32,512]{1,0:T(8,128)(2,1)S(1)}, u32[]{:S(2)}, u32[]{:S(2)}) collective-permute-start(bf16[32,512]{1,0:T(8,128)(2,1)} %bitcast.22), channel_id=1, source_target_pairs={{0,64},{64,0},{1,65},{65,1},{2,66},{66,2},{3,67},{67,3},{4,68},{68... | collective-permute-start | bytes 98312 | tf_op jit(solution)/shard_map/ppermute | solution.py:29
  6.8 5.1 %collective-permute-start.3 = (bf16[64,256]{1,0:T(8,128)(2,1)S(1)}, bf16[64,256]{1,0:T(8,128)(2,1)S(1)}, u32[]{:S(2)}, u32[]{:S(2)}) collective-permute-start(bf16[64,256]{1,0:T(8,128)(2,1)S(1)} %pad_maximum_fusion), channel_id=1, source_target_pairs={{0,8},{4,12},{8,0},{12,4},{1,9},{5,13},{9,1},{13,5},{2,10},{6,14},... | collective-permute-start | bytes 98312 | tf_op jit(solution)/shard_map/ppermute | solution.py:60
  11.9 1.7 %collective-permute-done.3 = bf16[64,256]{1,0:T(8,128)(2,1)S(1)} collective-permute-done((bf16[64,256]{1,0:T(8,128)(2,1)S(1)}, bf16[64,256]{1,0:T(8,128)(2,1)S(1)}, u32[]{:S(2)}, u32[]{:S(2)}) %collective-permute-start.3) | collective-permute-done | bytes 32800 | tf_op jit(solution)/shard_map/ppermute | solution.py:60
  13.6 3.2 %collective-permute-done.4 = bf16[64,256]{1,0:T(8,128)(2,1)S(1)} collective-permute-done((bf16[64,256]{1,0:T(8,128)(2,1)S(1)}, bf16[64,256]{1,0:T(8,128)(2,1)S(1)}, u32[]{:S(2)}, u32[]{:S(2)}) %collective-permute-start.4) | collective-permute-done | bytes 32800 | tf_op jit(solution)/shard_map/ppermute | solution.py:60
  18.1 2.6 %collective-permute-start.6 = (bf16[256,256]{1,0:T(8,128)(2,1)S(1)}, bf16[256,256]{1,0:T(8,128)(2,1)S(1)}, u32[]{:S(2)}, u32[]{:S(2)}) collective-permute-start(bf16[256,256]{1,0:T(8,128)(2,1)S(1)} %get-tuple-element.100), channel_id=1, source_target_pairs={{0,32},{1,33},{2,34},{3,35},{16,48},{17,49},{18,50},{19,51},{32,0}... | collective-permute-start | bytes 393224 | tf_op jit(solution)/shard_map/ppermute | solution.py:47
  20.7 3.7 %collective-permute-done.6 = bf16[256,256]{1,0:T(8,128)(2,1)S(1)} collective-permute-done((bf16[256,256]{1,0:T(8,128)(2,1)S(1)}, bf16[256,256]{1,0:T(8,128)(2,1)S(1)}, u32[]{:S(2)}, u32[]{:S(2)}) %collective-permute-start.6) | collective-permute-done | bytes 131104 | tf_op jit(solution)/shard_map/ppermute | solution.py:47
  24.5 1.7 %collective-permute-done.7 = bf16[256,256]{1,0:T(8,128)(2,1)S(1)} collective-permute-done((bf16[256,256]{1,0:T(8,128)(2,1)S(1)}, bf16[256,256]{1,0:T(8,128)(2,1)S(1)}, u32[]{:S(2)}, u32[]{:S(2)}) %collective-permute-start.7) | collective-permute-done | bytes 131104 | tf_op jit(solution)/shard_map/ppermute | solution.py:47
  26.2 2.6 %collective-permute-start.10 = (bf16[1024,256]{1,0:T(8,128)(2,1)S(1)}, bf16[1024,256]{1,0:T(8,128)(2,1)S(1)}, u32[]{:S(2)}, u32[]{:S(2)}) collective-permute-start(bf16[1024,256]{1,0:T(8,128)(2,1)S(1)} %constant_dynamic-update-slice_fusion.4.p0.refs_0_), channel_id=1, source_target_pairs={{0,3},{1,2},{2,1},{3,0},{16,19},{17,18},{18,17},{19,16},{32,35},{3... | collective-permute-start | bytes 1572872 | tf_op jit(solution)/shard_map/ppermute | solution.py:47
  30.9 1.6 %copy-done.3 = bf16[1,2048,512]{2,1,0:T(8,128)(2,1)S(1)} copy-done((bf16[1,2048,512]{2,1,0:T(8,128)(2,1)S(1)}, bf16[1,2048,512]{2,1,0:T(8,128)(2,1)}, u32[]{:S(2)}) %copy-start.3) | copy-done | bytes 2097176
  32.5 3.1 %shard_map.138.w = bf16[4,512,1024]{2,1,0:T(8,128)(2,1)S(1)} custom-call(s32[64]{0:T(128)S(1)} %get-tuple-element.109.rows, bf16[2048,512]{1,0:T(8,128)(2,1)S(1)} %bitcast.18, bf16[2048,512]{1,0:T(8,128)(2,1)} %collective-permute-done.1.other), custom_call_target="tpu_custom_call" | custom-call | flops 1048576 | bytes 16777216 | tf_op jit(solution)/shard_map/pallas_call | solution.py:122
  37.1 5.5 %collective-permute-done.9.p2.refs_2_ = bf16[1024,256]{1,0:T(8,128)(2,1)S(1)} collective-permute-done((bf16[1024,256]{1,0:T(8,128)(2,1)S(1)}, bf16[1024,256]{1,0:T(8,128)(2,1)S(1)}, u32[]{:S(2)}, u32[]{:S(2)}) %collective-permute-start.9) | collective-permute-done | bytes 524320 | tf_op jit(solution)/shard_map/ppermute | solution.py:47
  47.4 3.1 %shard_map.141.w.x = bf16[4,1024,512]{2,1,0:T(8,128)(2,1)S(1)} custom-call(s32[64]{0:T(128)S(1)} %get-tuple-element.108.rows, bf16[512,2048]{1,0:T(8,128)(2,1)S(1)} %bitcast.20, bf16[512,2048]{1,0:T(8,128)(2,1)} %collective-permute-done.12.other), custom_call_target="tpu_custom_call" | custom-call | flops 1048576 | bytes 16777216 | tf_op jit(solution)/shard_map/pallas_call | solution.py:152
  52.2 3.6 %collective-permute-start.14 = (bf16[1024,256]{1,0:T(8,128)(2,1)S(1)}, bf16[1024,256]{1,0:T(8,128)(2,1)S(1)}, u32[]{:S(2)}, u32[]{:S(2)}) collective-permute-start(bf16[1024,256]{1,0:T(8,128)(2,1)S(1)} %get-tuple-element.64), channel_id=1, source_target_pairs={{0,2},{1,3},{2,0},{3,1},{16,18},{17,19},{18,16},{19,17},{32,34},{3... | collective-permute-start | bytes 1572872 | tf_op jit(solution)/shard_map/ppermute | solution.py:47
  57.5 1.9 %copy-done = bf16[4,512,1024]{2,1,0:T(8,128)(2,1)} copy-done((bf16[4,512,1024]{2,1,0:T(8,128)(2,1)}, bf16[4,512,1024]{2,1,0:T(8,128)(2,1)S(1)}, u32[]{:S(2)}) %copy-start) | copy-done | bytes 4194328
  60.2 7.9 %collective-permute-done.14 = bf16[1024,256]{1,0:T(8,128)(2,1)S(1)} collective-permute-done((bf16[1024,256]{1,0:T(8,128)(2,1)S(1)}, bf16[1024,256]{1,0:T(8,128)(2,1)S(1)}, u32[]{:S(2)}, u32[]{:S(2)}) %collective-permute-start.14) | collective-permute-done | bytes 524320 | tf_op jit(solution)/shard_map/ppermute | solution.py:47
  68.1 2.9 %collective-permute-done.15 = bf16[1024,256]{1,0:T(8,128)(2,1)S(1)} collective-permute-done((bf16[1024,256]{1,0:T(8,128)(2,1)S(1)}, bf16[1024,256]{1,0:T(8,128)(2,1)S(1)}, u32[]{:S(2)}, u32[]{:S(2)}) %collective-permute-start.15) | collective-permute-done | bytes 524320 | tf_op jit(solution)/shard_map/ppermute | solution.py:47
  72.1 3.6 %all-to-all-start = ((bf16[16,64,256]{2,1,0:T(8,128)(2,1)}), bf16[16,64,256]{2,1,0:T(8,128)(2,1)S(1)}, u32[]{:S(2)}, u32[]{:S(2)}) async-start(bf16[16,64,256]{2,1,0:T(8,128)(2,1)} %bitcast.6), calls=%async_computation | async-start | bytes 1048576 | tf_op jit(solution)/shard_map/all_to_all | solution.py:37
  75.7 7.8 %collective-permute-start.16 = (bf16[2048,256]{1,0:T(8,128)(2,1)S(1)}, bf16[2048,256]{1,0:T(8,128)(2,1)S(1)}, u32[]{:S(2)}, u32[]{:S(2)}) collective-permute-start(bf16[2048,256]{1,0:T(8,128)(2,1)S(1)} %copy-done.10), channel_id=1, source_target_pairs={{0,64},{64,0},{1,65},{65,1},{2,66},{66,2},{3,67},{67,3},{4,68},{68... | collective-permute-start | bytes 3145736 | tf_op jit(solution)/shard_map/ppermute | solution.py:29
  84.0 2.1 %collective-permute-done.18 = bf16[1,32]{1,0:T(2,128)(2,1)S(1)} collective-permute-done((bf16[1,32]{1,0:T(2,128)(2,1)S(1)}, bf16[1,32]{1,0:T(2,128)(2,1)S(1)}, u32[]{:S(2)}, u32[]{:S(2)}) %collective-permute-start.18) | collective-permute-done | bytes 96 | tf_op jit(solution)/shard_map/ppermute | solution.py:29
  86.2 2.2 %all-to-all-done = bf16[16,64,256]{2,1,0:T(8,128)(2,1)S(1)} async-done(((bf16[16,64,256]{2,1,0:T(8,128)(2,1)}), bf16[16,64,256]{2,1,0:T(8,128)(2,1)S(1)}, u32[]{:S(2)}, u32[]{:S(2)}) %all-to-all-start) | async-done | bytes 524320 | tf_op jit(solution)/shard_map/all_to_all | solution.py:37
  88.8 17.0 %all_to_all.10 = bf16[16,64,256]{2,1,0:T(8,128)(2,1)S(1)} all-to-all(bf16[16,64,256]{2,1,0:T(8,128)(2,1)S(1)} %broadcast_in_dim.11), channel_id=1, replica_groups={{0,4,8,12,16,20,24,28,32,36,40,44,48,52,56,60},{1,5,9,13,17,21,25,29,33..., dimensions={0} | all-to-all | bytes 1048576 | tf_op jit(solution)/shard_map/all_to_all | solution.py:37
  105.9 2.0 %collective-permute-start.19 = (bf16[1024,128]{1,0:T(8,128)(2,1)S(1)}, bf16[1024,128]{1,0:T(8,128)(2,1)S(1)}, u32[]{:S(2)}, u32[]{:S(2)}) collective-permute-start(bf16[1024,128]{1,0:T(8,128)(2,1)S(1)} %get-tuple-element.80.p0.refs_0_), channel_id=1, source_target_pairs={{0,1},{1,0},{2,3},{3,2},{16,17},{17,16},{18,19},{19,18},{32,33},{3... | collective-permute-start | bytes 786440 | tf_op jit(solution)/shard_map/ppermute | solution.py:47
  107.9 2.4 %collective-permute-start.20 = (bf16[1024,128]{1,0:T(8,128)(2,1)S(1)}, bf16[1024,128]{1,0:T(8,128)(2,1)S(1)}, u32[]{:S(2)}, u32[]{:S(2)}) collective-permute-start(bf16[1024,128]{1,0:T(8,128)(2,1)S(1)} %get-tuple-element.80.p0.refs_0_), channel_id=1, source_target_pairs={{0,2},{1,3},{2,0},{3,1},{16,18},{17,19},{18,16},{19,17},{32,34},{3... | collective-permute-start | bytes 786440 | tf_op jit(solution)/shard_map/ppermute | solution.py:47
  110.5 10.3 %collective-permute-start.26 = (f32[32]{0:T(128)S(1)}, f32[32]{0:T(128)S(1)}, u32[]{:S(2)}, u32[]{:S(2)}) collective-permute-start(f32[32]{0:T(128)S(1)} %slice.7), channel_id=1, source_target_pairs={{0,64},{64,0},{1,65},{65,1},{2,66},{66,2},{3,67},{67,3},{4,68},{68... | collective-permute-start | bytes 392 | tf_op jit(solution)/shard_map/ppermute | solution.py:29
  120.8 1.6 %collective-permute-start.24 = (bf16[1024,128]{1,0:T(8,128)(2,1)S(1)}, bf16[1024,128]{1,0:T(8,128)(2,1)S(1)}, u32[]{:S(2)}, u32[]{:S(2)}) collective-permute-start(bf16[1024,128]{1,0:T(8,128)(2,1)S(1)} %get-tuple-element.84.p0.refs_4_), channel_id=1, source_target_pairs={{0,2},{1,3},{2,0},{3,1},{16,18},{17,19},{18,16},{19,17},{32,34},{3... | collective-permute-start | bytes 786440 | tf_op jit(solution)/shard_map/ppermute | solution.py:47
  122.4 2.3 %collective-permute-start.25 = (bf16[1024,128]{1,0:T(8,128)(2,1)S(1)}, bf16[1024,128]{1,0:T(8,128)(2,1)S(1)}, u32[]{:S(2)}, u32[]{:S(2)}) collective-permute-start(bf16[1024,128]{1,0:T(8,128)(2,1)S(1)} %get-tuple-element.84.p0.refs_4_), channel_id=1, source_target_pairs={{0,3},{1,2},{2,1},{3,0},{16,19},{17,18},{18,17},{19,16},{32,35},{3... | collective-permute-start | bytes 786440 | tf_op jit(solution)/shard_map/ppermute | solution.py:47
  124.7 2.2 %copy-done.1 = bf16[4,512,1024]{2,1,0:T(8,128)(2,1)S(1)} copy-done((bf16[4,512,1024]{2,1,0:T(8,128)(2,1)S(1)}, bf16[4,512,1024]{2,1,0:T(8,128)(2,1)}, u32[]{:S(2)}) %copy-start.1) | copy-done | bytes 4194328
  129.3 2.6 %collective-permute-done.25.p3.refs_7_ = bf16[1024,128]{1,0:T(8,128)(2,1)S(1)} collective-permute-done((bf16[1024,128]{1,0:T(8,128)(2,1)S(1)}, bf16[1024,128]{1,0:T(8,128)(2,1)S(1)}, u32[]{:S(2)}, u32[]{:S(2)}) %collective-permute-start.25) | collective-permute-done | bytes 262176 | tf_op jit(solution)/shard_map/ppermute | solution.py:47
  134.1 3.4 %collective-permute-start.28 = (bf16[2048,256]{1,0:T(8,128)(2,1)S(1)}, bf16[2048,256]{1,0:T(8,128)(2,1)S(1)}, u32[]{:S(2)}, u32[]{:S(2)}) collective-permute-start(bf16[2048,256]{1,0:T(8,128)(2,1)S(1)} %get-tuple-element.89), channel_id=1, source_target_pairs={{0,64},{64,0},{1,65},{65,1},{2,66},{66,2},{3,67},{67,3},{4,68},{68... | collective-permute-start | bytes 3145736 | tf_op jit(solution)/shard_map/ppermute | solution.py:29
  138.0 1.8 %collective-permute-done.28 = bf16[2048,256]{1,0:T(8,128)(2,1)S(1)} collective-permute-done((bf16[2048,256]{1,0:T(8,128)(2,1)S(1)}, bf16[2048,256]{1,0:T(8,128)(2,1)S(1)}, u32[]{:S(2)}, u32[]{:S(2)}) %collective-permute-start.28) | collective-permute-done | bytes 1048608 | tf_op jit(solution)/shard_map/ppermute | solution.py:29
  139.8 3.7 %multiply_convert_fusion = bf16[512,2048]{1,0:T(8,128)(2,1)} fusion(bf16[2048,256]{1,0:T(8,128)(2,1)S(1)} %collective-permute-done.28, bf16[2048,256]{1,0:T(8,128)(2,1)S(1)} %get-tuple-element.88, bf16[512,256]{1,0:T(8,128)(2,1)} %collective-permute-done.17, bf16[512,256]{1,0:T(8,128)(2,1)S(1)} %get-tuple-element.78), kind=kOutput, calls=%fused_computation | convolution fusion | flops 1081081856 | bytes 4718592 | tf_op jit(solution)/shard_map/dot_general | solution.py:256
  145.4 2.7 %shard_map.147 = (bf16[2048,512]{1,0:T(8,128)(2,1)}, f32[1,512]{1,0:T(1,128)}) custom-call(bf16[2048,256]{1,0:T(8,128)(2,1)S(1)} %copy-done.6, bf16[512,256]{1,0:T(8,128)(2,1)S(1)} %multiply_convert_fusion.1.grad, bf16[2048,256]{1,0:T(8,128)(2,1)S(1)} %copy-done.8, bf16[512,256]{1,0:T(8,128)(2,1)S(1)} %collective-permute-done.29.grad_b), custom_call_target="tpu_custom_call" | custom-call | flops 10737418240 | bytes 5242880 | tf_op jit(solution)/shard_map/pallas_call | solution.py:281
  (89 shorter events, 25.8 us)
Async XLA Ops:
  0.6 4.4 %collective-permute-start = (bf16[32,512]{1,0:T(8,128)(2,1)}, bf16[32,512]{1,0:T(8,128)(2,1)S(1)}, u32[]{:S(2)}, u32[]{:S(2)}) collective-permute-start(bf16[32,512]{1,0:T(8,128)(2,1)} %bitcast.22), channel_id=1, source_target_pairs={{0,64},{64,0},{1,65},{65,1},{2,66},{66,2},{3,67},{67,3},{4,68},{68... | collective-permute-start | bytes 98312 | tf_op jit(solution)/shard_map/ppermute | solution.py:29
  5.0 25.8 %collective-permute-start.1 = (bf16[2048,512]{1,0:T(8,128)(2,1)}, bf16[2048,512]{1,0:T(8,128)(2,1)}, u32[]{:S(2)}, u32[]{:S(2)}) collective-permute-start(bf16[2048,512]{1,0:T(8,128)(2,1)} %bitcast.17), channel_id=1, source_target_pairs={{0,64},{64,0},{1,65},{65,1},{2,66},{66,2},{3,67},{67,3},{4,68},{68... | collective-permute-start | bytes 6291464 | tf_op jit(solution)/shard_map/ppermute | solution.py:29
  5.4 42.0 %collective-permute-start.12 = (bf16[512,2048]{1,0:T(8,128)(2,1)}, bf16[512,2048]{1,0:T(8,128)(2,1)}, u32[]{:S(2)}, u32[]{:S(2)}) collective-permute-start(bf16[512,2048]{1,0:T(8,128)(2,1)} %bitcast.19), channel_id=1, source_target_pairs={{0,64},{64,0},{1,65},{65,1},{2,66},{66,2},{3,67},{67,3},{4,68},{68... | collective-permute-start | bytes 6291464 | tf_op jit(solution)/shard_map/ppermute | solution.py:29
  5.5 6.4 %collective-permute-start.2 = (bf16[64,256]{1,0:T(8,128)(2,1)S(1)}, bf16[64,256]{1,0:T(8,128)(2,1)S(1)}, u32[]{:S(2)}, u32[]{:S(2)}) collective-permute-start(bf16[64,256]{1,0:T(8,128)(2,1)S(1)} %pad_maximum_fusion), channel_id=1, source_target_pairs={{0,4},{4,0},{8,12},{12,8},{1,5},{5,1},{9,13},{13,9},{2,6},{6,2},{1... | collective-permute-start | bytes 98312 | tf_op jit(solution)/shard_map/ppermute | solution.py:60
  6.8 6.8 %collective-permute-start.3 = (bf16[64,256]{1,0:T(8,128)(2,1)S(1)}, bf16[64,256]{1,0:T(8,128)(2,1)S(1)}, u32[]{:S(2)}, u32[]{:S(2)}) collective-permute-start(bf16[64,256]{1,0:T(8,128)(2,1)S(1)} %pad_maximum_fusion), channel_id=1, source_target_pairs={{0,8},{4,12},{8,0},{12,4},{1,9},{5,13},{9,1},{13,5},{2,10},{6,14},... | collective-permute-start | bytes 98312 | tf_op jit(solution)/shard_map/ppermute | solution.py:60
  11.9 4.9 %collective-permute-start.4 = (bf16[64,256]{1,0:T(8,128)(2,1)S(1)}, bf16[64,256]{1,0:T(8,128)(2,1)S(1)}, u32[]{:S(2)}, u32[]{:S(2)}) collective-permute-start(bf16[64,256]{1,0:T(8,128)(2,1)S(1)} %pad_maximum_fusion), channel_id=1, source_target_pairs={{0,12},{4,8},{8,4},{12,0},{1,13},{5,9},{9,5},{13,1},{2,14},{6,10},... | collective-permute-start | bytes 98312 | tf_op jit(solution)/shard_map/ppermute | solution.py:60
  16.8 3.9 %collective-permute-start.5 = (bf16[256,256]{1,0:T(8,128)(2,1)S(1)}, bf16[256,256]{1,0:T(8,128)(2,1)S(1)}, u32[]{:S(2)}, u32[]{:S(2)}) collective-permute-start(bf16[256,256]{1,0:T(8,128)(2,1)S(1)} %get-tuple-element.100), channel_id=1, source_target_pairs={{0,16},{1,17},{2,18},{3,19},{16,0},{17,1},{18,2},{19,3},{32,48},{3... | collective-permute-start | bytes 393224 | tf_op jit(solution)/shard_map/ppermute | solution.py:47
  18.1 6.4 %collective-permute-start.6 = (bf16[256,256]{1,0:T(8,128)(2,1)S(1)}, bf16[256,256]{1,0:T(8,128)(2,1)S(1)}, u32[]{:S(2)}, u32[]{:S(2)}) collective-permute-start(bf16[256,256]{1,0:T(8,128)(2,1)S(1)} %get-tuple-element.100), channel_id=1, source_target_pairs={{0,32},{1,33},{2,34},{3,35},{16,48},{17,49},{18,50},{19,51},{32,0}... | collective-permute-start | bytes 393224 | tf_op jit(solution)/shard_map/ppermute | solution.py:47
  20.7 5.5 %collective-permute-start.7 = (bf16[256,256]{1,0:T(8,128)(2,1)S(1)}, bf16[256,256]{1,0:T(8,128)(2,1)S(1)}, u32[]{:S(2)}, u32[]{:S(2)}) collective-permute-start(bf16[256,256]{1,0:T(8,128)(2,1)S(1)} %get-tuple-element.100), channel_id=1, source_target_pairs={{0,48},{1,49},{2,50},{3,51},{16,32},{17,33},{18,34},{19,35},{32,16... | collective-permute-start | bytes 393224 | tf_op jit(solution)/shard_map/ppermute | solution.py:47
  26.2 9.6 %collective-permute-start.10 = (bf16[1024,256]{1,0:T(8,128)(2,1)S(1)}, bf16[1024,256]{1,0:T(8,128)(2,1)S(1)}, u32[]{:S(2)}, u32[]{:S(2)}) collective-permute-start(bf16[1024,256]{1,0:T(8,128)(2,1)S(1)} %constant_dynamic-update-slice_fusion.4.p0.refs_0_), channel_id=1, source_target_pairs={{0,3},{1,2},{2,1},{3,0},{16,19},{17,18},{18,17},{19,16},{32,35},{3... | collective-permute-start | bytes 1572872 | tf_op jit(solution)/shard_map/ppermute | solution.py:47
  28.8 8.3 %collective-permute-start.8 = (bf16[1024,256]{1,0:T(8,128)(2,1)S(1)}, bf16[1024,256]{1,0:T(8,128)(2,1)S(1)}, u32[]{:S(2)}, u32[]{:S(2)}) collective-permute-start(bf16[1024,256]{1,0:T(8,128)(2,1)S(1)} %constant_dynamic-update-slice_fusion.4.p0.refs_0_), channel_id=1, source_target_pairs={{0,1},{1,0},{2,3},{3,2},{16,17},{17,16},{18,19},{19,18},{32,33},{3... | collective-permute-start | bytes 1572872 | tf_op jit(solution)/shard_map/ppermute | solution.py:47
  28.8 13.9 %collective-permute-start.9 = (bf16[1024,256]{1,0:T(8,128)(2,1)S(1)}, bf16[1024,256]{1,0:T(8,128)(2,1)S(1)}, u32[]{:S(2)}, u32[]{:S(2)}) collective-permute-start(bf16[1024,256]{1,0:T(8,128)(2,1)S(1)} %constant_dynamic-update-slice_fusion.4.p0.refs_0_), channel_id=1, source_target_pairs={{0,2},{1,3},{2,0},{3,1},{16,18},{17,19},{18,16},{19,17},{32,34},{3... | collective-permute-start | bytes 1572872 | tf_op jit(solution)/shard_map/ppermute | solution.py:47
  43.9 6.6 %collective-permute-start.11 = (bf16[512,256]{1,0:T(8,128)(2,1)S(1)}, bf16[512,256]{1,0:T(8,128)(2,1)S(1)}, u32[]{:S(2)}, u32[]{:S(2)}) collective-permute-start(bf16[512,256]{1,0:T(8,128)(2,1)S(1)} %shard_map.139.part), channel_id=1, source_target_pairs={{0,128},{128,0},{1,129},{129,1},{2,130},{130,2},{3,131},{131,3},{4... | collective-permute-start | bytes 786440 | tf_op jit(solution)/shard_map/ppermute | solution.py:33
  52.1 8.1 %collective-permute-start.13 = (bf16[1024,256]{1,0:T(8,128)(2,1)S(1)}, bf16[1024,256]{1,0:T(8,128)(2,1)S(1)}, u32[]{:S(2)}, u32[]{:S(2)}) collective-permute-start(bf16[1024,256]{1,0:T(8,128)(2,1)S(1)} %get-tuple-element.63), channel_id=1, source_target_pairs={{0,1},{1,0},{2,3},{3,2},{16,17},{17,16},{18,19},{19,18},{32,33},{3... | collective-permute-start | bytes 1572872 | tf_op jit(solution)/shard_map/ppermute | solution.py:47
  52.2 15.9 %collective-permute-start.14 = (bf16[1024,256]{1,0:T(8,128)(2,1)S(1)}, bf16[1024,256]{1,0:T(8,128)(2,1)S(1)}, u32[]{:S(2)}, u32[]{:S(2)}) collective-permute-start(bf16[1024,256]{1,0:T(8,128)(2,1)S(1)} %get-tuple-element.64), channel_id=1, source_target_pairs={{0,2},{1,3},{2,0},{3,1},{16,18},{17,19},{18,16},{19,17},{32,34},{3... | collective-permute-start | bytes 1572872 | tf_op jit(solution)/shard_map/ppermute | solution.py:47
  55.9 15.2 %collective-permute-start.15 = (bf16[1024,256]{1,0:T(8,128)(2,1)S(1)}, bf16[1024,256]{1,0:T(8,128)(2,1)S(1)}, u32[]{:S(2)}, u32[]{:S(2)}) collective-permute-start(bf16[1024,256]{1,0:T(8,128)(2,1)S(1)} %get-tuple-element.65), channel_id=1, source_target_pairs={{0,3},{1,2},{2,1},{3,0},{16,19},{17,18},{18,17},{19,16},{32,35},{3... | collective-permute-start | bytes 1572872 | tf_op jit(solution)/shard_map/ppermute | solution.py:47
  59.4 24.2 %copy-start.12 = (bf16[1,32]{1,0:T(2,128)(2,1)S(1)}, bf16[1,32]{1,0:T(2,128)(2,1)}, u32[]{:S(2)}) copy-start(bf16[1,32]{1,0:T(2,128)(2,1)} %param.15) | copy-start | bytes 196
  72.1 16.4 %all-to-all-start = ((bf16[16,64,256]{2,1,0:T(8,128)(2,1)}), bf16[16,64,256]{2,1,0:T(8,128)(2,1)S(1)}, u32[]{:S(2)}, u32[]{:S(2)}) async-start(bf16[16,64,256]{2,1,0:T(8,128)(2,1)} %bitcast.6), calls=%async_computation | async-start | bytes 1048576 | tf_op jit(solution)/shard_map/all_to_all | solution.py:37
  75.7 12.9 %collective-permute-start.16 = (bf16[2048,256]{1,0:T(8,128)(2,1)S(1)}, bf16[2048,256]{1,0:T(8,128)(2,1)S(1)}, u32[]{:S(2)}, u32[]{:S(2)}) collective-permute-start(bf16[2048,256]{1,0:T(8,128)(2,1)S(1)} %copy-done.10), channel_id=1, source_target_pairs={{0,64},{64,0},{1,65},{65,1},{2,66},{66,2},{3,67},{67,3},{4,68},{68... | collective-permute-start | bytes 3145736 | tf_op jit(solution)/shard_map/ppermute | solution.py:29
  83.5 5.1 %collective-permute-start.17 = (bf16[512,256]{1,0:T(8,128)(2,1)S(1)}, bf16[512,256]{1,0:T(8,128)(2,1)}, u32[]{:S(2)}, u32[]{:S(2)}) collective-permute-start(bf16[512,256]{1,0:T(8,128)(2,1)S(1)} %get-tuple-element.78), channel_id=1, source_target_pairs={{0,64},{64,0},{1,65},{65,1},{2,66},{66,2},{3,67},{67,3},{4,68},{68... | collective-permute-start | bytes 786440 | tf_op jit(solution)/shard_map/ppermute | solution.py:29
  83.6 2.6 %collective-permute-start.18 = (bf16[1,32]{1,0:T(2,128)(2,1)S(1)}, bf16[1,32]{1,0:T(2,128)(2,1)S(1)}, u32[]{:S(2)}, u32[]{:S(2)}) collective-permute-start(bf16[1,32]{1,0:T(2,128)(2,1)S(1)} %copy-done.12), channel_id=1, source_target_pairs={{0,64},{64,0},{1,65},{65,1},{2,66},{66,2},{3,67},{67,3},{4,68},{68... | collective-permute-start | bytes 200 | tf_op jit(solution)/shard_map/ppermute | solution.py:29
  105.9 14.9 %collective-permute-start.19 = (bf16[1024,128]{1,0:T(8,128)(2,1)S(1)}, bf16[1024,128]{1,0:T(8,128)(2,1)S(1)}, u32[]{:S(2)}, u32[]{:S(2)}) collective-permute-start(bf16[1024,128]{1,0:T(8,128)(2,1)S(1)} %get-tuple-element.80.p0.refs_0_), channel_id=1, source_target_pairs={{0,1},{1,0},{2,3},{3,2},{16,17},{17,16},{18,19},{19,18},{32,33},{3... | collective-permute-start | bytes 786440 | tf_op jit(solution)/shard_map/ppermute | solution.py:47
  107.9 14.5 %collective-permute-start.20 = (bf16[1024,128]{1,0:T(8,128)(2,1)S(1)}, bf16[1024,128]{1,0:T(8,128)(2,1)S(1)}, u32[]{:S(2)}, u32[]{:S(2)}) collective-permute-start(bf16[1024,128]{1,0:T(8,128)(2,1)S(1)} %get-tuple-element.80.p0.refs_0_), channel_id=1, source_target_pairs={{0,2},{1,3},{2,0},{3,1},{16,18},{17,19},{18,16},{19,17},{32,34},{3... | collective-permute-start | bytes 786440 | tf_op jit(solution)/shard_map/ppermute | solution.py:47
  110.3 14.4 %collective-permute-start.21 = (bf16[1024,128]{1,0:T(8,128)(2,1)S(1)}, bf16[1024,128]{1,0:T(8,128)(2,1)S(1)}, u32[]{:S(2)}, u32[]{:S(2)}) collective-permute-start(bf16[1024,128]{1,0:T(8,128)(2,1)S(1)} %get-tuple-element.80.p0.refs_0_), channel_id=1, source_target_pairs={{0,3},{1,2},{2,1},{3,0},{16,19},{17,18},{18,17},{19,16},{32,35},{3... | collective-permute-start | bytes 786440 | tf_op jit(solution)/shard_map/ppermute | solution.py:47
  110.5 17.8 %collective-permute-start.26 = (f32[32]{0:T(128)S(1)}, f32[32]{0:T(128)S(1)}, u32[]{:S(2)}, u32[]{:S(2)}) collective-permute-start(f32[32]{0:T(128)S(1)} %slice.7), channel_id=1, source_target_pairs={{0,64},{64,0},{1,65},{65,1},{2,66},{66,2},{3,67},{67,3},{4,68},{68... | collective-permute-start | bytes 392 | tf_op jit(solution)/shard_map/ppermute | solution.py:29
  120.8 8.0 %collective-permute-start.23 = (bf16[1024,128]{1,0:T(8,128)(2,1)S(1)}, bf16[1024,128]{1,0:T(8,128)(2,1)S(1)}, u32[]{:S(2)}, u32[]{:S(2)}) collective-permute-start(bf16[1024,128]{1,0:T(8,128)(2,1)S(1)} %get-tuple-element.84.p0.refs_4_), channel_id=1, source_target_pairs={{0,1},{1,0},{2,3},{3,2},{16,17},{17,16},{18,19},{19,18},{32,33},{3... | collective-permute-start | bytes 786440 | tf_op jit(solution)/shard_map/ppermute | solution.py:47
  120.8 8.5 %collective-permute-start.24 = (bf16[1024,128]{1,0:T(8,128)(2,1)S(1)}, bf16[1024,128]{1,0:T(8,128)(2,1)S(1)}, u32[]{:S(2)}, u32[]{:S(2)}) collective-permute-start(bf16[1024,128]{1,0:T(8,128)(2,1)S(1)} %get-tuple-element.84.p0.refs_4_), channel_id=1, source_target_pairs={{0,2},{1,3},{2,0},{3,1},{16,18},{17,19},{18,16},{19,17},{32,34},{3... | collective-permute-start | bytes 786440 | tf_op jit(solution)/shard_map/ppermute | solution.py:47
  122.4 9.5 %collective-permute-start.25 = (bf16[1024,128]{1,0:T(8,128)(2,1)S(1)}, bf16[1024,128]{1,0:T(8,128)(2,1)S(1)}, u32[]{:S(2)}, u32[]{:S(2)}) collective-permute-start(bf16[1024,128]{1,0:T(8,128)(2,1)S(1)} %get-tuple-element.84.p0.refs_4_), channel_id=1, source_target_pairs={{0,3},{1,2},{2,1},{3,0},{16,19},{17,18},{18,17},{19,16},{32,35},{3... | collective-permute-start | bytes 786440 | tf_op jit(solution)/shard_map/ppermute | solution.py:47
  128.1 5.1 %collective-permute-start.22 = (bf16[512,128]{1,0:T(8,128)(2,1)S(1)}, bf16[512,128]{1,0:T(8,128)(2,1)S(1)}, u32[]{:S(2)}, u32[]{:S(2)}) collective-permute-start(bf16[512,128]{1,0:T(8,128)(2,1)S(1)} %shard_map.144), channel_id=1, source_target_pairs={{0,128},{128,0},{1,129},{129,1},{2,130},{130,2},{3,131},{131,3},{4... | collective-permute-start | bytes 393224 | tf_op jit(solution)/shard_map/ppermute | solution.py:33
  134.1 5.7 %collective-permute-start.28 = (bf16[2048,256]{1,0:T(8,128)(2,1)S(1)}, bf16[2048,256]{1,0:T(8,128)(2,1)S(1)}, u32[]{:S(2)}, u32[]{:S(2)}) collective-permute-start(bf16[2048,256]{1,0:T(8,128)(2,1)S(1)} %get-tuple-element.89), channel_id=1, source_target_pairs={{0,64},{64,0},{1,65},{65,1},{2,66},{66,2},{3,67},{67,3},{4,68},{68... | collective-permute-start | bytes 3145736 | tf_op jit(solution)/shard_map/ppermute | solution.py:29
  137.5 6.0 %collective-permute-start.27 = (bf16[512,128]{1,0:T(8,128)(2,1)S(1)}, bf16[512,128]{1,0:T(8,128)(2,1)S(1)}, u32[]{:S(2)}, u32[]{:S(2)}) collective-permute-start(bf16[512,128]{1,0:T(8,128)(2,1)S(1)} %shard_map.145), channel_id=1, source_target_pairs={{0,128},{128,0},{1,129},{129,1},{2,130},{130,2},{3,131},{131,3},{4... | collective-permute-start | bytes 393224 | tf_op jit(solution)/shard_map/ppermute | solution.py:33
  143.8 1.6 %collective-permute-start.29 = (bf16[512,256]{1,0:T(8,128)(2,1)S(1)}, bf16[512,256]{1,0:T(8,128)(2,1)S(1)}, u32[]{:S(2)}, u32[]{:S(2)}) collective-permute-start(bf16[512,256]{1,0:T(8,128)(2,1)S(1)} %multiply_convert_fusion.1.grad), channel_id=1, source_target_pairs={{0,64},{64,0},{1,65},{65,1},{2,66},{66,2},{3,67},{67,3},{4,68},{68... | collective-permute-start | bytes 786440 | tf_op jit(solution)/shard_map/ppermute | solution.py:29
  (12 other events, 64.2 us)

commit v9 on v7

--- a/solution.py
+++ b/solution.py
@@ -86,10 +86,11 @@
     return sum(p.astype(jnp.float32) for p in pieces)
 
 
-def scattered(pieces):
+def scattered(pieces, beside):
     total = summed(received(pieces)).astype(jnp.bfloat16)
+    total, beside = lax.optimization_barrier((total, beside))
     blocks = among_sixteen(total.reshape(16, -1, total.shape[-1]))
-    return jnp.sum(blocks.astype(jnp.float32), axis=0)
+    return jnp.sum(blocks.astype(jnp.float32), axis=0), beside
 
 
 def block_rows(relative):
@@ -266,13 +267,13 @@
 def outer_dec(feat, err, feat_b, err_b, scale):
     m, tokens = feat.shape
     n = err.shape[0]
-    tile = n // 4
+    tile = n // 2
     left = pl.BlockSpec((m, tokens), lambda i: (0, 0))
     right = pl.BlockSpec((tile, tokens), lambda i: (i, 0))
     return pl.pallas_call(
         functools.partial(outer_dec_kernel, scale),
         out_shape=jax.ShapeDtypeStruct((m, n), jnp.bfloat16),
-        grid=(4,),
+        grid=(2,),
         in_specs=[left, right, left, right],
         out_specs=pl.BlockSpec((m, tile), lambda i: (0, i)),
         compiler_params=PARAMS,
@@ -296,7 +297,7 @@
 def outer_enc(acts, grad, acts_b, grad_b):
     m, tokens = acts.shape
     n = grad.shape[0]
-    tile = m // 4
+    tile = m // 2
     rows = pl.BlockSpec((tile, tokens), lambda i: (i, 0))
     whole = pl.BlockSpec((n, tokens), lambda i: (0, 0))
     return pl.pallas_call(
@@ -305,7 +306,7 @@
             jax.ShapeDtypeStruct((m, n), jnp.bfloat16),
             jax.ShapeDtypeStruct((1, n), jnp.float32),
         ),
-        grid=(4,),
+        grid=(2,),
         in_specs=[rows, whole, rows, whole],
         out_specs=(
             pl.BlockSpec((tile, n), lambda i: (i, 0)),
@@ -344,7 +345,7 @@
     part_b, acts_own, acts_other = lax.optimization_barrier((part_b, acts_own, acts_other))
     b_lanes = jnp.broadcast_to(b_enc[:, None], part.shape)
     feat, recon = blocked_dot(dec_r, part, part_b, b_lanes)
-    recon = scattered(recon)
+    recon, dec_rt = scattered(recon, turned(dec_r))
     recon, acts_b, feat_b = lax.optimization_barrier(
         (recon, other_core(acts_other), other_core(feat))
     )
@@ -355,17 +356,14 @@
     width = sums.shape[0] // 2
     grad_bdec = scale * (sums[:width] + other_core(sums[width:]))
     err_p = gathered(err)
-    err_p[0][2], dec_r = lax.optimization_barrier((err_p[0][2], dec_r))
-    dec_rt = turned(dec_r)
     err_p[1], grad_bdec = lax.optimization_barrier((err_p[1], grad_bdec))
     term = [gathered_dot(dec_rt, pieces) for pieces in err_p]
-    term_b = [other_layer(term[0]), None]
-    term_b[0], term[1], err_p, feat = lax.optimization_barrier((term_b[0], term[1], err_p, feat))
-    term_b[1] = other_layer(term[1])
+    term_b = [other_layer(t) for t in term]
+    term[1], err_p = lax.optimization_barrier((term[1], err_p))
     err_own, err_other = placed(rows, err_p)
+    term_b[1], err_own, err_other = lax.optimization_barrier((term_b[1], err_own, err_other))
     err_b = other_core(err_other)
     grad_dec = outer_dec(feat, err_own, feat_b, err_b, scale)
-    term_b[1], grad_dec = lax.optimization_barrier((term_b[1], grad_dec))
 
     term, term_b = (jnp.concatenate(t, axis=1).astype(jnp.float32) for t in (term, term_b))
     pre = part.astype(jnp.float32) + part_b.astype(jnp.float32) + b_enc[:, None]

time: 149 us -> 146 us (0.980)
  starting transfers between devices: 56.5 us -> 53.8 us
  local copies, waits for them, and re-layouts: 7.13 us -> 8.75 us
    ppermute x15, waiting for transfers between devices: 29.1 us -> 26.4 us  [in_plane(): return lax.ppermute(x, PLANE, pairs)]
    ppermute x9, starting transfers between devices: 24.4 us -> 21.8 us  [other_core(): return lax.ppermute(x, 'core', [(0, 1), (1, 0)])]
    ppermute x3, waiting for transfers between devices: 0.01 us -> 2.24 us  [other_layer(): return lax.ppermute(x, 'z_lo', [(0, 1), (1, 0)])]
    unnamed x29, local copies, waits for them, and re-layouts: 6.1 us -> 7.73 us
  transfers between devices with their start and end apart: 31 -> 31, of which waited for: 14 -> 15; matrix products, arithmetic and copies ran while one was open for 2% -> 2% of each run, Pallas kernels for 10% -> 11%
where the time goes in v9:
time: 146 us
  starting transfers between devices  53.8 us (37%)
  waiting for transfers between devices  41.8 us (29%)
  Pallas kernels  19.5 us (13%)
  blocking collectives  17.2 us (12%)
  local copies, waits for them, and re-layouts  8.75 us (6%)
  other arithmetic  3.97 us (3%)
    ppermute x15, waiting for transfers between devices, in_plane(): return lax.ppermute(x, PLANE, pairs)  26.4 us
    ppermute x9, starting transfers between devices, other_core(): return lax.ppermute(x, 'core', [(0, 1), (1, 0)])  21.8 us
    ppermute x15, starting transfers between devices, in_plane(): return lax.ppermute(x, PLANE, pairs)  18.2 us
    all_to_all x1, blocking collectives, among_sixteen(): return lax.all_to_all(x, SPACE, 0, 0, axis_index_groups=GROUPS, tiled=True)  17.2 us
    unnamed x29, local copies, waits for them, and re-layouts  7.73 us
    ppermute x3, starting transfers between devices, along_z(): return lax.ppermute(x, 'z_hi', [(i, i ^ k) for i in range(4)])  6.37 us
    ppermute x3, waiting for transfers between devices, along_z(): return lax.ppermute(x, 'z_hi', [(i, i ^ k) for i in range(4)])  4.86 us
    ppermute x9, waiting for transfers between devices, other_core(): return lax.ppermute(x, 'core', [(0, 1), (1, 0)])  4.39 us
  transfers between devices with their start and end apart: 31, of which 15 were waited for; matrix products, arithmetic and copies ran while one was open for 2% of the time, Pallas kernels for 11%

profile of v9, /device:TPU:1, one launch (start us, length us, event | category | flops | bytes accessed | tf_op | source)
XLA Modules:
  0.0 145.9 jit_solution(17378979224537375663)
XLA Ops:
  0.6 3.3 %collective-permute-start = (bf16[32,512]{1,0:T(8,128)(2,1)}, bf16[32,512]{1,0:T(8,128)(2,1)S(1)}, u32[]{:S(2)}, u32[]{:S(2)}) collective-permute-start(bf16[32,512]{1,0:T(8,128)(2,1)} %bitcast.23), channel_id=1, source_target_pairs={{0,64},{64,0},{1,65},{65,1},{2,66},{66,2},{3,67},{67,3},{4,68},{68... | collective-permute-start | bytes 98312 | tf_op jit(solution)/shard_map/ppermute | solution.py:31
  6.8 5.1 %collective-permute-start.3 = (bf16[64,256]{1,0:T(8,128)(2,1)S(1)}, bf16[64,256]{1,0:T(8,128)(2,1)S(1)}, u32[]{:S(2)}, u32[]{:S(2)}) collective-permute-start(bf16[64,256]{1,0:T(8,128)(2,1)S(1)} %pad_maximum_fusion), channel_id=1, source_target_pairs={{0,8},{4,12},{8,0},{12,4},{1,9},{5,13},{9,1},{13,5},{2,10},{6,14},... | collective-permute-start | bytes 98312 | tf_op jit(solution)/shard_map/ppermute | solution.py:62
  11.9 1.7 %collective-permute-done.3 = bf16[64,256]{1,0:T(8,128)(2,1)S(1)} collective-permute-done((bf16[64,256]{1,0:T(8,128)(2,1)S(1)}, bf16[64,256]{1,0:T(8,128)(2,1)S(1)}, u32[]{:S(2)}, u32[]{:S(2)}) %collective-permute-start.3) | collective-permute-done | bytes 32800 | tf_op jit(solution)/shard_map/ppermute | solution.py:62
  13.6 3.2 %collective-permute-done.4 = bf16[64,256]{1,0:T(8,128)(2,1)S(1)} collective-permute-done((bf16[64,256]{1,0:T(8,128)(2,1)S(1)}, bf16[64,256]{1,0:T(8,128)(2,1)S(1)}, u32[]{:S(2)}, u32[]{:S(2)}) %collective-permute-start.4) | collective-permute-done | bytes 32800 | tf_op jit(solution)/shard_map/ppermute | solution.py:62
  18.1 2.6 %collective-permute-start.6 = (bf16[256,256]{1,0:T(8,128)(2,1)S(1)}, bf16[256,256]{1,0:T(8,128)(2,1)S(1)}, u32[]{:S(2)}, u32[]{:S(2)}) collective-permute-start(bf16[256,256]{1,0:T(8,128)(2,1)S(1)} %get-tuple-element.98), channel_id=1, source_target_pairs={{0,32},{1,33},{2,34},{3,35},{16,48},{17,49},{18,50},{19,51},{32,0}... | collective-permute-start | bytes 393224 | tf_op jit(solution)/shard_map/ppermute | solution.py:49
  20.7 3.7 %collective-permute-done.6 = bf16[256,256]{1,0:T(8,128)(2,1)S(1)} collective-permute-done((bf16[256,256]{1,0:T(8,128)(2,1)S(1)}, bf16[256,256]{1,0:T(8,128)(2,1)S(1)}, u32[]{:S(2)}, u32[]{:S(2)}) %collective-permute-start.6) | collective-permute-done | bytes 131104 | tf_op jit(solution)/shard_map/ppermute | solution.py:49
  24.5 1.7 %collective-permute-done.7 = bf16[256,256]{1,0:T(8,128)(2,1)S(1)} collective-permute-done((bf16[256,256]{1,0:T(8,128)(2,1)S(1)}, bf16[256,256]{1,0:T(8,128)(2,1)S(1)}, u32[]{:S(2)}, u32[]{:S(2)}) %collective-permute-start.7) | collective-permute-done | bytes 131104 | tf_op jit(solution)/shard_map/ppermute | solution.py:49
  27.2 2.7 %collective-permute-start.9 = (bf16[1024,256]{1,0:T(8,128)(2,1)S(1)}, bf16[1024,256]{1,0:T(8,128)(2,1)S(1)}, u32[]{:S(2)}, u32[]{:S(2)}) collective-permute-start(bf16[1024,256]{1,0:T(8,128)(2,1)S(1)} %constant_dynamic-update-slice_fusion.4.p0.refs_0_), channel_id=1, source_target_pairs={{0,2},{1,3},{2,0},{3,1},{16,18},{17,19},{18,16},{19,17},{32,34},{3... | collective-permute-start | bytes 1572872 | tf_op jit(solution)/shard_map/ppermute | solution.py:49
  30.9 1.6 %copy-done.2 = bf16[1,2048,512]{2,1,0:T(8,128)(2,1)S(1)} copy-done((bf16[1,2048,512]{2,1,0:T(8,128)(2,1)S(1)}, bf16[1,2048,512]{2,1,0:T(8,128)(2,1)}, u32[]{:S(2)}) %copy-start.2) | copy-done | bytes 2097176
  32.5 3.1 %shard_map.138.w = bf16[4,512,1024]{2,1,0:T(8,128)(2,1)S(1)} custom-call(s32[64]{0:T(128)S(1)} %get-tuple-element.107.rows, bf16[2048,512]{1,0:T(8,128)(2,1)S(1)} %bitcast.18, bf16[2048,512]{1,0:T(8,128)(2,1)} %collective-permute-done.1.other), custom_call_target="tpu_custom_call" | custom-call | flops 1048576 | bytes 16777216 | tf_op jit(solution)/shard_map/pallas_call | solution.py:124
  35.5 6.9 %collective-permute-done.9.p2.refs_2_ = bf16[1024,256]{1,0:T(8,128)(2,1)S(1)} collective-permute-done((bf16[1024,256]{1,0:T(8,128)(2,1)S(1)}, bf16[1024,256]{1,0:T(8,128)(2,1)S(1)}, u32[]{:S(2)}, u32[]{:S(2)}) %collective-permute-start.9) | collective-permute-done | bytes 524320 | tf_op jit(solution)/shard_map/ppermute | solution.py:49
  42.5 2.6 %collective-permute-done.10.p3.refs_3_ = bf16[1024,256]{1,0:T(8,128)(2,1)S(1)} collective-permute-done((bf16[1024,256]{1,0:T(8,128)(2,1)S(1)}, bf16[1024,256]{1,0:T(8,128)(2,1)S(1)}, u32[]{:S(2)}, u32[]{:S(2)}) %collective-permute-start.10) | collective-permute-done | bytes 524320 | tf_op jit(solution)/shard_map/ppermute | solution.py:49
  49.8 3.1 %shard_map.141.w.x = bf16[4,1024,512]{2,1,0:T(8,128)(2,1)S(1)} custom-call(s32[64]{0:T(128)S(1)} %get-tuple-element.106.rows, bf16[512,2048]{1,0:T(8,128)(2,1)S(1)} %bitcast.20, bf16[512,2048]{1,0:T(8,128)(2,1)} %collective-permute-done.12.other), custom_call_target="tpu_custom_call" | custom-call | flops 1048576 | bytes 16777216 | tf_op jit(solution)/shard_map/pallas_call | solution.py:154
  53.1 1.5 shard_map.142
  55.0 2.9 %collective-permute-start.13 = (bf16[1024,256]{1,0:T(8,128)(2,1)S(1)}, bf16[1024,256]{1,0:T(8,128)(2,1)S(1)}, u32[]{:S(2)}, u32[]{:S(2)}) collective-permute-start(bf16[1024,256]{1,0:T(8,128)(2,1)S(1)} %get-tuple-element.62), channel_id=1, source_target_pairs={{0,1},{1,0},{2,3},{3,2},{16,17},{17,16},{18,19},{19,18},{32,33},{3... | collective-permute-start | bytes 1572872 | tf_op jit(solution)/shard_map/ppermute | solution.py:49
  57.9 1.4 shard_map.143.w
  59.3 1.9 %copy-done = bf16[4,512,1024]{2,1,0:T(8,128)(2,1)} copy-done((bf16[4,512,1024]{2,1,0:T(8,128)(2,1)}, bf16[4,512,1024]{2,1,0:T(8,128)(2,1)S(1)}, u32[]{:S(2)}) %copy-start) | copy-done | bytes 4194328
  61.3 8.5 %collective-permute-done.15 = bf16[1024,256]{1,0:T(8,128)(2,1)S(1)} collective-permute-done((bf16[1024,256]{1,0:T(8,128)(2,1)S(1)}, bf16[1024,256]{1,0:T(8,128)(2,1)S(1)}, u32[]{:S(2)}, u32[]{:S(2)}) %collective-permute-start.15) | collective-permute-done | bytes 524320 | tf_op jit(solution)/shard_map/ppermute | solution.py:49
  71.5 4.2 %all-to-all-start = ((bf16[16,64,256]{2,1,0:T(8,128)(2,1)}), bf16[16,64,256]{2,1,0:T(8,128)(2,1)}, u32[]{:S(2)}, u32[]{:S(2)}) async-start(bf16[16,64,256]{2,1,0:T(8,128)(2,1)} %bitcast.6), calls=%async_computation | async-start | bytes 1048576 | tf_op jit(solution)/shard_map/all_to_all | solution.py:39
  75.8 6.5 %collective-permute-start.16 = (bf16[2048,256]{1,0:T(8,128)(2,1)S(1)}, bf16[2048,256]{1,0:T(8,128)(2,1)S(1)}, u32[]{:S(2)}, u32[]{:S(2)}) collective-permute-start(bf16[2048,256]{1,0:T(8,128)(2,1)S(1)} %copy-done.9), channel_id=1, source_target_pairs={{0,64},{64,0},{1,65},{65,1},{2,66},{66,2},{3,67},{67,3},{4,68},{68... | collective-permute-start | bytes 3145736 | tf_op jit(solution)/shard_map/ppermute | solution.py:31
  82.8 2.1 %collective-permute-done.18 = bf16[1,32]{1,0:T(2,128)(2,1)S(1)} collective-permute-done((bf16[1,32]{1,0:T(2,128)(2,1)S(1)}, bf16[1,32]{1,0:T(2,128)(2,1)S(1)}, u32[]{:S(2)}, u32[]{:S(2)}) %collective-permute-start.18) | collective-permute-done | bytes 96 | tf_op jit(solution)/shard_map/ppermute | solution.py:31
  85.0 4.0 %all-to-all-done = bf16[16,64,256]{2,1,0:T(8,128)(2,1)} async-done(((bf16[16,64,256]{2,1,0:T(8,128)(2,1)}), bf16[16,64,256]{2,1,0:T(8,128)(2,1)}, u32[]{:S(2)}, u32[]{:S(2)}) %all-to-all-start) | async-done | bytes 524320 | tf_op jit(solution)/shard_map/all_to_all | solution.py:39
  90.4 17.2 %all_to_all.10 = bf16[16,64,256]{2,1,0:T(8,128)(2,1)S(1)} all-to-all(bf16[16,64,256]{2,1,0:T(8,128)(2,1)S(1)} %broadcast_in_dim.11), channel_id=1, replica_groups={{0,4,8,12,16,20,24,28,32,36,40,44,48,52,56,60},{1,5,9,13,17,21,25,29,33..., dimensions={0} | all-to-all | bytes 1048576 | tf_op jit(solution)/shard_map/all_to_all | solution.py:39
  108.0 2.4 %collective-permute-start.23 = (bf16[1024,128]{1,0:T(8,128)(2,1)S(1)}, bf16[1024,128]{1,0:T(8,128)(2,1)S(1)}, u32[]{:S(2)}, u32[]{:S(2)}) collective-permute-start(bf16[1024,128]{1,0:T(8,128)(2,1)S(1)} %get-tuple-element.80.p0.refs_4_), channel_id=1, source_target_pairs={{0,2},{1,3},{2,0},{3,1},{16,18},{17,19},{18,16},{19,17},{32,34},{3... | collective-permute-start | bytes 786440 | tf_op jit(solution)/shard_map/ppermute | solution.py:49
  111.6 9.2 %collective-permute-start.25 = (f32[32]{0:T(128)S(1)}, f32[32]{0:T(128)S(1)}, u32[]{:S(2)}, u32[]{:S(2)}) collective-permute-start(f32[32]{0:T(128)S(1)} %slice.7), channel_id=1, source_target_pairs={{0,64},{64,0},{1,65},{65,1},{2,66},{66,2},{3,67},{67,3},{4,68},{68... | collective-permute-start | bytes 392 | tf_op jit(solution)/shard_map/ppermute | solution.py:31
  122.4 2.2 %collective-permute-start.21 = (bf16[1024,128]{1,0:T(8,128)(2,1)S(1)}, bf16[1024,128]{1,0:T(8,128)(2,1)S(1)}, u32[]{:S(2)}, u32[]{:S(2)}) collective-permute-start(bf16[1024,128]{1,0:T(8,128)(2,1)S(1)} %get-tuple-element.76.p0.refs_0_), channel_id=1, source_target_pairs={{0,3},{1,2},{2,1},{3,0},{16,19},{17,18},{18,17},{19,16},{32,35},{3... | collective-permute-start | bytes 786440 | tf_op jit(solution)/shard_map/ppermute | solution.py:49
  125.2 2.2 %copy-done.1 = bf16[4,512,1024]{2,1,0:T(8,128)(2,1)S(1)} copy-done((bf16[4,512,1024]{2,1,0:T(8,128)(2,1)S(1)}, bf16[4,512,1024]{2,1,0:T(8,128)(2,1)}, u32[]{:S(2)}) %copy-start.1) | copy-done | bytes 4194328
  129.7 2.2 %collective-permute-done.21.p3.refs_3_ = bf16[1024,128]{1,0:T(8,128)(2,1)S(1)} collective-permute-done((bf16[1024,128]{1,0:T(8,128)(2,1)S(1)}, bf16[1024,128]{1,0:T(8,128)(2,1)S(1)}, u32[]{:S(2)}, u32[]{:S(2)}) %collective-permute-start.21) | collective-permute-done | bytes 262176 | tf_op jit(solution)/shard_map/ppermute | solution.py:49
  135.4 2.2 %collective-permute-done.26 = bf16[512,128]{1,0:T(8,128)(2,1)S(1)} collective-permute-done((bf16[512,128]{1,0:T(8,128)(2,1)S(1)}, bf16[512,128]{1,0:T(8,128)(2,1)S(1)}, u32[]{:S(2)}, u32[]{:S(2)}) %collective-permute-start.26) | collective-permute-done | bytes 131104 | tf_op jit(solution)/shard_map/ppermute | solution.py:35
  137.9 1.7 %collective-permute-start.28 = (bf16[512,256]{1,0:T(8,128)(2,1)S(1)}, bf16[512,256]{1,0:T(8,128)(2,1)S(1)}, u32[]{:S(2)}, u32[]{:S(2)}) collective-permute-start(bf16[512,256]{1,0:T(8,128)(2,1)S(1)} %multiply_convert_fusion.grad), channel_id=1, source_target_pairs={{0,64},{64,0},{1,65},{65,1},{2,66},{66,2},{3,67},{67,3},{4,68},{68... | collective-permute-start | bytes 786440 | tf_op jit(solution)/shard_map/ppermute | solution.py:31
  140.8 2.7 %shard_map.147 = (bf16[2048,512]{1,0:T(8,128)(2,1)}, f32[1,512]{1,0:T(1,128)}) custom-call(bf16[2048,256]{1,0:T(8,128)(2,1)S(1)} %copy-done.5, bf16[512,256]{1,0:T(8,128)(2,1)S(1)} %multiply_convert_fusion.grad, bf16[2048,256]{1,0:T(8,128)(2,1)S(1)} %copy-done.7, bf16[512,256]{1,0:T(8,128)(2,1)S(1)} %collective-permute-done.28.grad_b), custom_call_target="tpu_custom_call" | custom-call | flops 10737418240 | bytes 5242880 | tf_op jit(solution)/shard_map/pallas_call | solution.py:303
  143.5 2.5 %shard_map.148 = bf16[512,2048]{1,0:T(8,128)(2,1)} custom-call(bf16[512,256]{1,0:T(8,128)(2,1)S(1)} %get-tuple-element.68.feat, bf16[2048,256]{1,0:T(8,128)(2,1)S(1)} %get-tuple-element.89.err, bf16[512,256]{1,0:T(8,128)(2,1)S(1)} %collective-permute-done.17.feat_b, bf16[2048,256]{1,0:T(8,128)(2,1)S(1)} %collective-permute-done.29.err_b), custom_call_target="tpu_custom_call" | custom-call | flops 1073741824 | bytes 5242880 | tf_op jit(solution)/shard_map/pallas_call | solution.py:273
  (87 shorter events, 26.0 us)
Async XLA Ops:
  0.6 4.4 %collective-permute-start = (bf16[32,512]{1,0:T(8,128)(2,1)}, bf16[32,512]{1,0:T(8,128)(2,1)S(1)}, u32[]{:S(2)}, u32[]{:S(2)}) collective-permute-start(bf16[32,512]{1,0:T(8,128)(2,1)} %bitcast.23), channel_id=1, source_target_pairs={{0,64},{64,0},{1,65},{65,1},{2,66},{66,2},{3,67},{67,3},{4,68},{68... | collective-permute-start | bytes 98312 | tf_op jit(solution)/shard_map/ppermute | solution.py:31
  5.0 25.8 %collective-permute-start.1 = (bf16[2048,512]{1,0:T(8,128)(2,1)}, bf16[2048,512]{1,0:T(8,128)(2,1)}, u32[]{:S(2)}, u32[]{:S(2)}) collective-permute-start(bf16[2048,512]{1,0:T(8,128)(2,1)} %bitcast.17), channel_id=1, source_target_pairs={{0,64},{64,0},{1,65},{65,1},{2,66},{66,2},{3,67},{67,3},{4,68},{68... | collective-permute-start | bytes 6291464 | tf_op jit(solution)/shard_map/ppermute | solution.py:31
  5.4 44.4 %collective-permute-start.12 = (bf16[512,2048]{1,0:T(8,128)(2,1)}, bf16[512,2048]{1,0:T(8,128)(2,1)}, u32[]{:S(2)}, u32[]{:S(2)}) collective-permute-start(bf16[512,2048]{1,0:T(8,128)(2,1)} %bitcast.19), channel_id=1, source_target_pairs={{0,64},{64,0},{1,65},{65,1},{2,66},{66,2},{3,67},{67,3},{4,68},{68... | collective-permute-start | bytes 6291464 | tf_op jit(solution)/shard_map/ppermute | solution.py:31
  5.5 6.4 %collective-permute-start.2 = (bf16[64,256]{1,0:T(8,128)(2,1)S(1)}, bf16[64,256]{1,0:T(8,128)(2,1)S(1)}, u32[]{:S(2)}, u32[]{:S(2)}) collective-permute-start(bf16[64,256]{1,0:T(8,128)(2,1)S(1)} %pad_maximum_fusion), channel_id=1, source_target_pairs={{0,4},{4,0},{8,12},{12,8},{1,5},{5,1},{9,13},{13,9},{2,6},{6,2},{1... | collective-permute-start | bytes 98312 | tf_op jit(solution)/shard_map/ppermute | solution.py:62
  6.8 6.8 %collective-permute-start.3 = (bf16[64,256]{1,0:T(8,128)(2,1)S(1)}, bf16[64,256]{1,0:T(8,128)(2,1)S(1)}, u32[]{:S(2)}, u32[]{:S(2)}) collective-permute-start(bf16[64,256]{1,0:T(8,128)(2,1)S(1)} %pad_maximum_fusion), channel_id=1, source_target_pairs={{0,8},{4,12},{8,0},{12,4},{1,9},{5,13},{9,1},{13,5},{2,10},{6,14},... | collective-permute-start | bytes 98312 | tf_op jit(solution)/shard_map/ppermute | solution.py:62
  11.9 4.9 %collective-permute-start.4 = (bf16[64,256]{1,0:T(8,128)(2,1)S(1)}, bf16[64,256]{1,0:T(8,128)(2,1)S(1)}, u32[]{:S(2)}, u32[]{:S(2)}) collective-permute-start(bf16[64,256]{1,0:T(8,128)(2,1)S(1)} %pad_maximum_fusion), channel_id=1, source_target_pairs={{0,12},{4,8},{8,4},{12,0},{1,13},{5,9},{9,5},{13,1},{2,14},{6,10},... | collective-permute-start | bytes 98312 | tf_op jit(solution)/shard_map/ppermute | solution.py:62
  16.8 3.9 %collective-permute-start.5 = (bf16[256,256]{1,0:T(8,128)(2,1)S(1)}, bf16[256,256]{1,0:T(8,128)(2,1)S(1)}, u32[]{:S(2)}, u32[]{:S(2)}) collective-permute-start(bf16[256,256]{1,0:T(8,128)(2,1)S(1)} %get-tuple-element.98), channel_id=1, source_target_pairs={{0,16},{1,17},{2,18},{3,19},{16,0},{17,1},{18,2},{19,3},{32,48},{3... | collective-permute-start | bytes 393224 | tf_op jit(solution)/shard_map/ppermute | solution.py:49
  18.1 6.4 %collective-permute-start.6 = (bf16[256,256]{1,0:T(8,128)(2,1)S(1)}, bf16[256,256]{1,0:T(8,128)(2,1)S(1)}, u32[]{:S(2)}, u32[]{:S(2)}) collective-permute-start(bf16[256,256]{1,0:T(8,128)(2,1)S(1)} %get-tuple-element.98), channel_id=1, source_target_pairs={{0,32},{1,33},{2,34},{3,35},{16,48},{17,49},{18,50},{19,51},{32,0}... | collective-permute-start | bytes 393224 | tf_op jit(solution)/shard_map/ppermute | solution.py:49
  20.7 5.5 %collective-permute-start.7 = (bf16[256,256]{1,0:T(8,128)(2,1)S(1)}, bf16[256,256]{1,0:T(8,128)(2,1)S(1)}, u32[]{:S(2)}, u32[]{:S(2)}) collective-permute-start(bf16[256,256]{1,0:T(8,128)(2,1)S(1)} %get-tuple-element.98), channel_id=1, source_target_pairs={{0,48},{1,49},{2,50},{3,51},{16,32},{17,33},{18,34},{19,35},{32,16... | collective-permute-start | bytes 393224 | tf_op jit(solution)/shard_map/ppermute | solution.py:49
  26.2 9.3 %collective-permute-start.8 = (bf16[1024,256]{1,0:T(8,128)(2,1)S(1)}, bf16[1024,256]{1,0:T(8,128)(2,1)S(1)}, u32[]{:S(2)}, u32[]{:S(2)}) collective-permute-start(bf16[1024,256]{1,0:T(8,128)(2,1)S(1)} %constant_dynamic-update-slice_fusion.4.p0.refs_0_), channel_id=1, source_target_pairs={{0,1},{1,0},{2,3},{3,2},{16,17},{17,16},{18,19},{19,18},{32,33},{3... | collective-permute-start | bytes 1572872 | tf_op jit(solution)/shard_map/ppermute | solution.py:49
  27.2 15.3 %collective-permute-start.9 = (bf16[1024,256]{1,0:T(8,128)(2,1)S(1)}, bf16[1024,256]{1,0:T(8,128)(2,1)S(1)}, u32[]{:S(2)}, u32[]{:S(2)}) collective-permute-start(bf16[1024,256]{1,0:T(8,128)(2,1)S(1)} %constant_dynamic-update-slice_fusion.4.p0.refs_0_), channel_id=1, source_target_pairs={{0,2},{1,3},{2,0},{3,1},{16,18},{17,19},{18,16},{19,17},{32,34},{3... | collective-permute-start | bytes 1572872 | tf_op jit(solution)/shard_map/ppermute | solution.py:49
  29.9 15.2 %collective-permute-start.10 = (bf16[1024,256]{1,0:T(8,128)(2,1)S(1)}, bf16[1024,256]{1,0:T(8,128)(2,1)S(1)}, u32[]{:S(2)}, u32[]{:S(2)}) collective-permute-start(bf16[1024,256]{1,0:T(8,128)(2,1)S(1)} %constant_dynamic-update-slice_fusion.4.p0.refs_0_), channel_id=1, source_target_pairs={{0,3},{1,2},{2,1},{3,0},{16,19},{17,18},{18,17},{19,16},{32,35},{3... | collective-permute-start | bytes 1572872 | tf_op jit(solution)/shard_map/ppermute | solution.py:49
  46.4 6.6 %collective-permute-start.11 = (bf16[512,256]{1,0:T(8,128)(2,1)S(1)}, bf16[512,256]{1,0:T(8,128)(2,1)S(1)}, u32[]{:S(2)}, u32[]{:S(2)}) collective-permute-start(bf16[512,256]{1,0:T(8,128)(2,1)S(1)} %shard_map.139.part), channel_id=1, source_target_pairs={{0,128},{128,0},{1,129},{129,1},{2,130},{130,2},{3,131},{131,3},{4... | collective-permute-start | bytes 786440 | tf_op jit(solution)/shard_map/ppermute | solution.py:35
  54.6 15.2 %collective-permute-start.15 = (bf16[1024,256]{1,0:T(8,128)(2,1)S(1)}, bf16[1024,256]{1,0:T(8,128)(2,1)S(1)}, u32[]{:S(2)}, u32[]{:S(2)}) collective-permute-start(bf16[1024,256]{1,0:T(8,128)(2,1)S(1)} %get-tuple-element.64), channel_id=1, source_target_pairs={{0,3},{1,2},{2,1},{3,0},{16,19},{17,18},{18,17},{19,16},{32,35},{3... | collective-permute-start | bytes 1572872 | tf_op jit(solution)/shard_map/ppermute | solution.py:49
  54.9 15.0 %collective-permute-start.14 = (bf16[1024,256]{1,0:T(8,128)(2,1)S(1)}, bf16[1024,256]{1,0:T(8,128)(2,1)S(1)}, u32[]{:S(2)}, u32[]{:S(2)}) collective-permute-start(bf16[1024,256]{1,0:T(8,128)(2,1)S(1)} %get-tuple-element.63), channel_id=1, source_target_pairs={{0,2},{1,3},{2,0},{3,1},{16,18},{17,19},{18,16},{19,17},{32,34},{3... | collective-permute-start | bytes 1572872 | tf_op jit(solution)/shard_map/ppermute | solution.py:49
  55.0 15.4 %collective-permute-start.13 = (bf16[1024,256]{1,0:T(8,128)(2,1)S(1)}, bf16[1024,256]{1,0:T(8,128)(2,1)S(1)}, u32[]{:S(2)}, u32[]{:S(2)}) collective-permute-start(bf16[1024,256]{1,0:T(8,128)(2,1)S(1)} %get-tuple-element.62), channel_id=1, source_target_pairs={{0,1},{1,0},{2,3},{3,2},{16,17},{17,16},{18,19},{19,18},{32,33},{3... | collective-permute-start | bytes 1572872 | tf_op jit(solution)/shard_map/ppermute | solution.py:49
  71.5 17.5 %all-to-all-start = ((bf16[16,64,256]{2,1,0:T(8,128)(2,1)}), bf16[16,64,256]{2,1,0:T(8,128)(2,1)}, u32[]{:S(2)}, u32[]{:S(2)}) async-start(bf16[16,64,256]{2,1,0:T(8,128)(2,1)} %bitcast.6), calls=%async_computation | async-start | bytes 1048576 | tf_op jit(solution)/shard_map/all_to_all | solution.py:39
  75.8 14.3 %collective-permute-start.16 = (bf16[2048,256]{1,0:T(8,128)(2,1)S(1)}, bf16[2048,256]{1,0:T(8,128)(2,1)S(1)}, u32[]{:S(2)}, u32[]{:S(2)}) collective-permute-start(bf16[2048,256]{1,0:T(8,128)(2,1)S(1)} %copy-done.9), channel_id=1, source_target_pairs={{0,64},{64,0},{1,65},{65,1},{2,66},{66,2},{3,67},{67,3},{4,68},{68... | collective-permute-start | bytes 3145736 | tf_op jit(solution)/shard_map/ppermute | solution.py:31
  82.3 7.8 %collective-permute-start.17 = (bf16[512,256]{1,0:T(8,128)(2,1)S(1)}, bf16[512,256]{1,0:T(8,128)(2,1)S(1)}, u32[]{:S(2)}, u32[]{:S(2)}) collective-permute-start(bf16[512,256]{1,0:T(8,128)(2,1)S(1)} %get-tuple-element.68.feat), channel_id=1, source_target_pairs={{0,64},{64,0},{1,65},{65,1},{2,66},{66,2},{3,67},{67,3},{4,68},{68... | collective-permute-start | bytes 786440 | tf_op jit(solution)/shard_map/ppermute | solution.py:31
  82.4 2.6 %collective-permute-start.18 = (bf16[1,32]{1,0:T(2,128)(2,1)S(1)}, bf16[1,32]{1,0:T(2,128)(2,1)S(1)}, u32[]{:S(2)}, u32[]{:S(2)}) collective-permute-start(bf16[1,32]{1,0:T(2,128)(2,1)S(1)} %copy-done.11), channel_id=1, source_target_pairs={{0,64},{64,0},{1,65},{65,1},{2,66},{66,2},{3,67},{67,3},{4,68},{68... | collective-permute-start | bytes 200 | tf_op jit(solution)/shard_map/ppermute | solution.py:31
  90.1 38.5 %copy-start.6 = (bf16[2048,256]{1,0:T(8,128)(2,1)}, bf16[2048,256]{1,0:T(8,128)(2,1)S(1)}, u32[]{:S(2)}) copy-start(bf16[2048,256]{1,0:T(8,128)(2,1)S(1)} %collective-permute-done.16.acts_b) | copy-start | bytes 3145732
  107.6 14.8 %collective-permute-start.22 = (bf16[1024,128]{1,0:T(8,128)(2,1)S(1)}, bf16[1024,128]{1,0:T(8,128)(2,1)S(1)}, u32[]{:S(2)}, u32[]{:S(2)}) collective-permute-start(bf16[1024,128]{1,0:T(8,128)(2,1)S(1)} %get-tuple-element.80.p0.refs_4_), channel_id=1, source_target_pairs={{0,1},{1,0},{2,3},{3,2},{16,17},{17,16},{18,19},{19,18},{32,33},{3... | collective-permute-start | bytes 786440 | tf_op jit(solution)/shard_map/ppermute | solution.py:49
  108.0 17.2 %collective-permute-start.23 = (bf16[1024,128]{1,0:T(8,128)(2,1)S(1)}, bf16[1024,128]{1,0:T(8,128)(2,1)S(1)}, u32[]{:S(2)}, u32[]{:S(2)}) collective-permute-start(bf16[1024,128]{1,0:T(8,128)(2,1)S(1)} %get-tuple-element.80.p0.refs_4_), channel_id=1, source_target_pairs={{0,2},{1,3},{2,0},{3,1},{16,18},{17,19},{18,16},{19,17},{32,34},{3... | collective-permute-start | bytes 786440 | tf_op jit(solution)/shard_map/ppermute | solution.py:49
  110.4 14.7 %collective-permute-start.24 = (bf16[1024,128]{1,0:T(8,128)(2,1)S(1)}, bf16[1024,128]{1,0:T(8,128)(2,1)S(1)}, u32[]{:S(2)}, u32[]{:S(2)}) collective-permute-start(bf16[1024,128]{1,0:T(8,128)(2,1)S(1)} %get-tuple-element.80.p0.refs_4_), channel_id=1, source_target_pairs={{0,3},{1,2},{2,1},{3,0},{16,19},{17,18},{18,17},{19,16},{32,35},{3... | collective-permute-start | bytes 786440 | tf_op jit(solution)/shard_map/ppermute | solution.py:49
  111.6 10.0 %collective-permute-start.25 = (f32[32]{0:T(128)S(1)}, f32[32]{0:T(128)S(1)}, u32[]{:S(2)}, u32[]{:S(2)}) collective-permute-start(f32[32]{0:T(128)S(1)} %slice.7), channel_id=1, source_target_pairs={{0,64},{64,0},{1,65},{65,1},{2,66},{66,2},{3,67},{67,3},{4,68},{68... | collective-permute-start | bytes 392 | tf_op jit(solution)/shard_map/ppermute | solution.py:31
  120.8 8.9 %collective-permute-start.19 = (bf16[1024,128]{1,0:T(8,128)(2,1)S(1)}, bf16[1024,128]{1,0:T(8,128)(2,1)S(1)}, u32[]{:S(2)}, u32[]{:S(2)}) collective-permute-start(bf16[1024,128]{1,0:T(8,128)(2,1)S(1)} %get-tuple-element.76.p0.refs_0_), channel_id=1, source_target_pairs={{0,1},{1,0},{2,3},{3,2},{16,17},{17,16},{18,19},{19,18},{32,33},{3... | collective-permute-start | bytes 786440 | tf_op jit(solution)/shard_map/ppermute | solution.py:49
  121.6 8.1 %collective-permute-start.20 = (bf16[1024,128]{1,0:T(8,128)(2,1)S(1)}, bf16[1024,128]{1,0:T(8,128)(2,1)S(1)}, u32[]{:S(2)}, u32[]{:S(2)}) collective-permute-start(bf16[1024,128]{1,0:T(8,128)(2,1)S(1)} %get-tuple-element.76.p0.refs_0_), channel_id=1, source_target_pairs={{0,2},{1,3},{2,0},{3,1},{16,18},{17,19},{18,16},{19,17},{32,34},{3... | collective-permute-start | bytes 786440 | tf_op jit(solution)/shard_map/ppermute | solution.py:49
  122.4 9.5 %collective-permute-start.21 = (bf16[1024,128]{1,0:T(8,128)(2,1)S(1)}, bf16[1024,128]{1,0:T(8,128)(2,1)S(1)}, u32[]{:S(2)}, u32[]{:S(2)}) collective-permute-start(bf16[1024,128]{1,0:T(8,128)(2,1)S(1)} %get-tuple-element.76.p0.refs_0_), channel_id=1, source_target_pairs={{0,3},{1,2},{2,1},{3,0},{16,19},{17,18},{18,17},{19,16},{32,35},{3... | collective-permute-start | bytes 786440 | tf_op jit(solution)/shard_map/ppermute | solution.py:49
  128.6 6.7 %collective-permute-start.27 = (bf16[512,128]{1,0:T(8,128)(2,1)S(1)}, bf16[512,128]{1,0:T(8,128)(2,1)S(1)}, u32[]{:S(2)}, u32[]{:S(2)}) collective-permute-start(bf16[512,128]{1,0:T(8,128)(2,1)S(1)} %shard_map.145), channel_id=1, source_target_pairs={{0,128},{128,0},{1,129},{129,1},{2,130},{130,2},{3,131},{131,3},{4... | collective-permute-start | bytes 393224 | tf_op jit(solution)/shard_map/ppermute | solution.py:35
  133.2 4.4 %collective-permute-start.26 = (bf16[512,128]{1,0:T(8,128)(2,1)S(1)}, bf16[512,128]{1,0:T(8,128)(2,1)S(1)}, u32[]{:S(2)}, u32[]{:S(2)}) collective-permute-start(bf16[512,128]{1,0:T(8,128)(2,1)S(1)} %shard_map.144), channel_id=1, source_target_pairs={{0,128},{128,0},{1,129},{129,1},{2,130},{130,2},{3,131},{131,3},{4... | collective-permute-start | bytes 393224 | tf_op jit(solution)/shard_map/ppermute | solution.py:35
  137.9 2.9 %collective-permute-start.28 = (bf16[512,256]{1,0:T(8,128)(2,1)S(1)}, bf16[512,256]{1,0:T(8,128)(2,1)S(1)}, u32[]{:S(2)}, u32[]{:S(2)}) collective-permute-start(bf16[512,256]{1,0:T(8,128)(2,1)S(1)} %multiply_convert_fusion.grad), channel_id=1, source_target_pairs={{0,64},{64,0},{1,65},{65,1},{2,66},{66,2},{3,67},{67,3},{4,68},{68... | collective-permute-start | bytes 786440 | tf_op jit(solution)/shard_map/ppermute | solution.py:31
  139.6 3.9 %collective-permute-start.29 = (bf16[2048,256]{1,0:T(8,128)(2,1)S(1)}, bf16[2048,256]{1,0:T(8,128)(2,1)S(1)}, u32[]{:S(2)}, u32[]{:S(2)}) collective-permute-start(bf16[2048,256]{1,0:T(8,128)(2,1)S(1)} %get-tuple-element.91), channel_id=1, source_target_pairs={{0,64},{64,0},{1,65},{65,1},{2,66},{66,2},{3,67},{67,3},{4,68},{68... | collective-permute-start | bytes 3145736 | tf_op jit(solution)/shard_map/ppermute | solution.py:31
  (11 other events, 65.0 us)
